TPU v7x, 32 devices: a whole 2x2x4 slice. The times are simulated.
32 devices in a mesh: dp: 8 (over y, x, core), ctx: 4 (over z).
Axes of the slice: x: 2, y: 2, z: 4, core: 2. Of those that a mesh axis runs over, the one named last changes fastest.
Arguments:
- value: bfloat16 [8, 512, 512], P('dp', 'ctx'), may hold values from -6 to 6
- gate_one: bfloat16 [8, 512, 512], P('dp', 'ctx'), may hold values from -6 to 6
- gate_two: bfloat16 [8, 512, 512], P('dp', 'ctx'), may hold values from -6 to 6
- filters: bfloat16 [2, 512, 512], replicated, may hold values from -0.25 to 0.25
- out_weight: bfloat16 [512, 512], replicated, may hold values from -0.25 to 0.25
- grad_out: bfloat16 [8, 512, 512], P('dp', 'ctx'), may hold values from -6 to 6
Outputs:
- mixed: bfloat16 [8, 512, 512], P('dp', 'ctx')
- grad_value: bfloat16 [8, 512, 512], P('dp', 'ctx')
- grad_gate_one: bfloat16 [8, 512, 512], P('dp', 'ctx')
- grad_gate_two: bfloat16 [8, 512, 512], P('dp', 'ctx')
- filter_grad: float32 [2, 512, 512], P(None, 'ctx', 'dp')
- weight_grad: float32 [512, 512], P('dp', 'ctx')
All inputs are finite; a program needn't handle non-finite values.
Results may differ from a plain program's by a relative error of at most 0.019.
Values may be sent and summed in bfloat16 or wider, within the bound.
No kernel may reach another device: no remote copies, remote signals or barrier semaphores. Data moves between devices by JAX's collectives and lax.ppermute only.
A program may use at most 128 MiB of HBM per device.

v0:
```python
import math

import jax
import jax.numpy as jnp
from jax import lax
from jax.sharding import PartitionSpec as P


def make_tables(block):
    period = 2 * block
    freq_bins = jnp.concatenate(
        [jnp.arange(block + 1, dtype=jnp.int32), jnp.arange(1, block, dtype=jnp.int32)]
    )
    sine_rows = jnp.arange(period, dtype=jnp.int32) > block
    inputs = jnp.arange(block, dtype=jnp.int32)
    turns = freq_bins[:, None] * inputs[None, :] % period
    radians = turns.astype(jnp.float32) * (2.0 * math.pi / period)
    forward = jnp.where(sine_rows[:, None], jnp.sin(radians), jnp.cos(radians))
    moments = jnp.arange(period, dtype=jnp.int32)
    turns_back = moments[:, None] * freq_bins[None, :] % period
    radians_back = turns_back.astype(jnp.float32) * (2.0 * math.pi / period)
    border_bins = (freq_bins == 0) | (freq_bins == block)
    weights = jnp.where(border_bins, 1.0, 2.0) / period
    inverse = (
        jnp.where(sine_rows[None, :], jnp.sin(radians_back), jnp.cos(radians_back))
        * weights[None, :]
    )
    parity = jnp.where(freq_bins % 2 == 0, 1.0, -1.0).astype(jnp.float32)[:, None]
    return (forward, inverse, parity)


def to_spectra(blocks, table):
    return jnp.einsum(
        "fb,...bd->...fd", table, blocks.astype(jnp.float32), precision=lax.Precision.HIGHEST
    )


def from_spectra(table, spectra):
    return jnp.einsum("tf,...fd->...td", table, spectra, precision=lax.Precision.HIGHEST)


def spectral_product(left, right, block, conj_left):
    left_real = left[..., : block + 1, :]
    left_imag = left[..., block + 1 :, :]
    right_real = right[..., : block + 1, :]
    right_imag = right[..., block + 1 :, :]
    if conj_left:
        left_imag = -left_imag
    cross = left_imag * right_imag
    border = jnp.zeros_like(cross[..., :1, :])
    real_part = left_real * right_real - jnp.concatenate([border, cross, border], axis=-2)
    imag_part = left_real[..., 1:block, :] * right_imag + left_imag * right_real[..., 1:block, :]
    return jnp.concatenate([real_part, imag_part], axis=-2)


def on_device(value, gate_one, gate_two, filters, out_weight, grad_out):
    rows = value.shape[1]
    width = value.shape[2]
    seq_count = lax.axis_size("ctx")
    data_count = lax.axis_size("dp")
    position = lax.axis_index("ctx")
    block = math.gcd(rows, 128)
    own_blocks = rows // block
    lag_blocks = own_blocks * seq_count
    forward, inverse, parity = make_tables(block)
    low_rows = inverse[:block]
    high_rows = inverse[block:]
    first_block = position * own_blocks
    own_start = position * rows
    filter_blocks = filters.reshape(2, lag_blocks, block, width)
    filter_spectra = to_spectra(filter_blocks, forward)
    padded_filters = jnp.concatenate([jnp.zeros_like(filter_spectra), filter_spectra], axis=1)

    def piece_spectra_of(piece):
        count = piece.shape[0] // block
        return to_spectra(piece.reshape(count, block, width), forward)

    def causal(source, padded_filter):
        initial = jnp.zeros((own_blocks + 1, 2 * block, width), jnp.float32)
        piece = lax.all_gather(source, "ctx", axis=0, tiled=True)
        start = jnp.int32(0)

        def work(total):
            piece_spectra = piece_spectra_of(piece)
            count = piece_spectra.shape[0]
            start_block = start // block
            last_block = start_block + count - 1
            terms_list = []
            for index in range(own_blocks + 1):
                out_block = first_block - 1 + index
                anchor = jnp.maximum(out_block, 0)
                window = lax.dynamic_slice_in_dim(
                    padded_filter, lag_blocks + anchor - last_block, count, 0
                )
                window = jnp.flip(window, 0)
                summed_term = jnp.sum(spectral_product(window, piece_spectra, block, False), axis=0)
                if index == 0:
                    summed_term = summed_term * (out_block >= 0).astype(jnp.float32)
                terms_list.append(summed_term)
            return total + jnp.stack(terms_list)

        summed = lax.cond(start < own_start + rows, work, lambda total: total, initial)
        lower = from_spectra(low_rows, summed[1:])
        upper = from_spectra(high_rows, summed[:-1])
        return (lower + upper).reshape(rows, width)

    def anti_owner(source, grad_rows, padded_filter):
        filter_spectrum = padded_filter[lag_blocks:]
        whole_source, whole_grad = (
            lax.all_gather(source, "ctx", axis=0, tiled=True),
            lax.all_gather(grad_rows, "ctx", axis=0, tiled=True),
        )
        source_spectra = piece_spectra_of(whole_source)
        grad_spectra = piece_spectra_of(whole_grad)
        following = (
            jnp.concatenate([grad_spectra[1:], jnp.zeros_like(grad_spectra[:1])], axis=0) * parity
        )
        combined = grad_spectra + following
        padded = jnp.concatenate([combined, jnp.zeros_like(combined)], axis=0)

        def one_block(offset):
            window = lax.dynamic_slice_in_dim(padded, offset, lag_blocks, 0)
            grad_piece = jnp.sum(spectral_product(filter_spectrum, window, block, True), axis=0)
            lag_piece = jnp.sum(spectral_product(source_spectra, window, block, True), axis=0)
            return (grad_piece, lag_piece)

        grad_parts, lag_parts = lax.map(
            one_block, first_block + jnp.arange(own_blocks, dtype=jnp.int32)
        )
        grad_part = from_spectra(low_rows, grad_parts).reshape(rows, width)
        lag_part = from_spectra(low_rows, lag_parts).reshape(rows, width)
        return (grad_part, lag_part)

    def backward(source, grad_rows, padded_filter):
        return anti_owner(source, grad_rows, padded_filter)

    value_rows = value[0]
    gate_first = gate_one[0].astype(jnp.float32)
    gate_second = gate_two[0].astype(jnp.float32)
    cotangent = grad_out[0]
    first_conv = causal(value_rows, padded_filters[0])
    mixed_input = (gate_first * first_conv).astype(jnp.bfloat16)
    second_conv = causal(mixed_input, padded_filters[1])
    gated = (gate_second * second_conv).astype(jnp.bfloat16)
    mixed = jnp.dot(gated, out_weight, preferred_element_type=jnp.float32).astype(jnp.bfloat16)
    grad_gated = lax.dot_general(
        cotangent, out_weight, (((1,), (1,)), ((), ())), preferred_element_type=jnp.float32
    )
    grad_gate_two = (grad_gated * second_conv).astype(jnp.bfloat16)
    grad_second = (grad_gated * gate_second).astype(jnp.bfloat16)
    grad_mixed, lag_second = backward(mixed_input, grad_second, padded_filters[1])
    grad_gate_one = (grad_mixed * first_conv).astype(jnp.bfloat16)
    grad_first = (grad_mixed * gate_first).astype(jnp.bfloat16)
    grad_value_full, lag_first = backward(value_rows, grad_first, padded_filters[0])
    grad_value = grad_value_full.astype(jnp.bfloat16)
    own_lags = jnp.stack([lag_first, lag_second])
    filter_grad = (
        lax.psum_scatter(
            own_lags.astype(jnp.bfloat16), "dp", scatter_dimension=2, tiled=True
        ).astype(jnp.float32)
        / data_count
    )
    weight_part = lax.psum_scatter(
        lax.dot_general(
            gated, cotangent, (((0,), (0,)), ((), ())), preferred_element_type=jnp.float32
        ).astype(jnp.bfloat16),
        "dp",
        scatter_dimension=0,
        tiled=True,
    )
    weight_grad = (
        lax.psum_scatter(weight_part, "ctx", scatter_dimension=1, tiled=True).astype(jnp.float32)
        / data_count
    )
    return (
        mixed[None],
        grad_value[None],
        grad_gate_one[None],
        grad_gate_two[None],
        filter_grad,
        weight_grad,
    )


def solution(mesh):
    return jax.shard_map(
        on_device,
        mesh=mesh,
        in_specs=(
            P("dp", "ctx", None),
            P("dp", "ctx", None),
            P("dp", "ctx", None),
            P(),
            P(),
            P("dp", "ctx", None),
        ),
        out_specs=(
            P("dp", "ctx", None),
            P("dp", "ctx", None),
            P("dp", "ctx", None),
            P("dp", "ctx", None),
            P(None, "ctx", "dp"),
            P("dp", "ctx"),
        ),
        check_vma=False,
    )
```

profile of v0, /device:TPU:0, one launch (start us, length us, event | category | flops | bytes accessed | tf_op | source)
XLA Modules:
  0.0 194.1 jit_solution(16005092052501717183)
XLA Ops:
  7.4 1.1 copy.23
  9.1 1.0 copy.24
  10.1 1.1 select_multiply_fusion
  11.2 17.6 %all-gather = bf16[1,512,512]{2,1,0:T(8,128)(2,1)S(1)} all-gather(bf16[1,128,512]{2,1,0:T(8,128)(2,1)} %param.10), channel_id=2, replica_groups=mesh['dp'=8,'ctx'=4] {'ctx'}, dimensions={1}, use_global_device_ids=true | all-gather | bytes 655360 | tf_op jit(solution)/shard_map/all_gather | solution.py:80
  28.8 2.4 %convolution_bitcast_fusion.2 = f32[2,4,256,512]{3,2,1,0:T(8,128)S(1)} fusion(bf16[2,4,128,512]{3,2,1,0:T(8,128)(2,1)S(1)} %bitcast.151, s32[256]{0:T(256)S(1)} %get-tuple-element.103, pred[256]{0:T(512)(128)(4,1)S(1)} %iota_compare_fusion), kind=kOutput, calls=%fused_computation.50 | convolution fusion | flops 1611104256 | bytes 5244160 | tf_op jit(solution)/shard_map/fb,...bd->...fd/dot_general | solution.py:33
  31.1 4.5 %concatenate.92 = f32[2,8,256,512]{3,2,1,0:T(8,128)} pad(f32[2,4,256,512]{3,2,1,0:T(8,128)S(1)} %convolution_bitcast_fusion.2, f32[]{:T(128)} %constant.162.clone.1), padding=0_0x4_0x0_0x0_0 | pad | bytes 12582916 | tf_op jit(solution)/shard_map/concatenate | solution.py:72
  35.6 7.5 %conditional.2 = (f32[2,256,512]{2,1,0:T(8,128)S(1)}) conditional(s32[]{:T(128)} %convert_element_type.91, () %tuple.25, (f32[2,8,256,512]{3,2,1,0:T(8,128)}, s32[]{:T(128)}, bf16[512,512]{1,0:T(8,128)(2,1)S(1)}, f32[256,128]{1,0:T(8,128)S(1)}) %tuple.80), branch_computations={%region_0.1_spmd, %region_1.4_spmd} | conditional | flops 811728896 | bytes 58253476 | solution.py:102
  35.6 2.9 %slice.174 = f32[1,8,256,512]{3,2,1,0:T(8,128)S(1)} slice(f32[2,8,256,512]{3,2,1,0:T(8,128)} %get-tuple-element.61), slice={[0:1], [0:8], [0:256], [0:512]} | slice | bytes 8388608 | tf_op jit(solution)/shard_map/slice | solution.py:141
  39.8 1.1 convolution_bitcast_fusion
  40.8 0.8 reverse_multiply_fusion.1
  43.1 1.0 fusion.24
  44.1 1.7 fusion.27
  45.8 15.2 %all-gather.1 = bf16[1,512,512]{1,2,0:T(8,128)(2,1)S(1)} all-gather(bf16[1,128,512]{1,2,0:T(8,128)(2,1)S(1)} %get-tuple-element.158), channel_id=3, replica_groups=mesh['dp'=8,'ctx'=4] {'ctx'}, dimensions={1}, use_global_device_ids=true | all-gather | bytes 655360 | tf_op jit(solution)/shard_map/all_gather | solution.py:80
  61.0 7.6 %conditional.3 = (f32[2,256,512]{2,1,0:T(8,128)S(1)}) conditional(s32[]{:T(128)} %convert_element_type.91, () %tuple.24, (f32[2,8,256,512]{3,2,1,0:T(8,128)}, s32[]{:T(128)}, bf16[512,512]{0,1:T(8,128)(2,1)S(1)}, f32[256,128]{1,0:T(8,128)S(1)}) %tuple.79), branch_computations={%region_4.5_spmd, %region_5.8_spmd} | conditional | flops 811728896 | bytes 59302052 | solution.py:102
  61.2 1.1 convolution_bitcast_fusion.1
  62.3 2.7 %slice.190 = f32[1,8,256,512]{3,2,1,0:T(8,128)S(1)} slice(f32[2,8,256,512]{3,2,1,0:T(8,128)} %get-tuple-element.72), slice={[1:2], [0:8], [0:256], [0:512]} | slice | bytes 8388608 | tf_op jit(solution)/shard_map/slice | solution.py:143
  66.2 0.9 reverse_multiply_fusion.3
  68.6 1.0 fusion.23
  69.6 1.0 convolution_add_fusion
  70.6 1.1 convolution_convert_fusion
  71.8 4.6 %slice_bitcast_fusion = (f32[4,256,512]{2,1,0:T(8,128)}, f32[4,256,512]{2,1,0:T(8,128)}) fusion(f32[2,4,256,512]{3,2,1,0:T(8,128)} %copy-done.2), kind=kLoop, calls=%fused_computation.51 | loop fusion | bytes 8388608 | tf_op jit(solution)/shard_map/slice | solution.py:108
  76.7 2.9 %convolution_bitcast_fusion.4 = f32[4,256,512]{2,1,0:T(8,128)} fusion(bf16[4,128,512]{2,1,0:T(8,128)(2,1)S(1)} %bitcast.154, s32[256]{0:T(256)S(1)} %get-tuple-element.103, pred[256]{0:T(512)(128)(4,1)S(1)} %iota_compare_fusion), kind=kOutput, calls=%fused_computation.60 | convolution fusion | flops 805797888 | bytes 2622720 | tf_op jit(solution)/shard_map/fb,...bd->...fd/dot_general | solution.py:33
  79.5 1.0 fusion.42
  80.5 14.3 %all_gather.16 = bf16[512,512]{0,1:T(8,128)(2,1)S(1)} all-gather(bf16[128,512]{0,1:T(8,128)(2,1)S(1)} %get-tuple-element.155), channel_id=1, replica_groups=mesh['dp'=8,'ctx'=4] {'ctx'}, dimensions={0}, use_global_device_ids=true | all-gather | bytes 655360 | tf_op jit(solution)/shard_map/all_gather | solution.py:111
  95.1 3.0 %convolution_bitcast_fusion.3 = f32[4,256,512]{2,1,0:T(8,128)} fusion(bf16[4,128,512]{2,1,0:T(8,128)(2,1)S(1)} %bitcast.156, s32[256]{0:T(256)S(1)} %get-tuple-element.103, pred[256]{0:T(512)(128)(4,1)S(1)} %iota_compare_fusion), kind=kOutput, calls=%fused_computation.59 | convolution fusion | flops 805797888 | bytes 2622720 | tf_op jit(solution)/shard_map/fb,...bd->...fd/dot_general | solution.py:33
  98.0 1.6 convolution_bitcast_fusion.6
  99.7 1.3 slice.294
  101.0 1.8 multiply_add_fusion.5
  103.7 1.2 fusion.22
  106.7 1.7 multiply_convert_fusion
  108.3 14.1 %all-gather.2 = bf16[1,512,512]{1,2,0:T(8,128)(2,1)S(1)} all-gather(bf16[1,128,512]{1,2,0:T(8,128)(2,1)S(1)} %get-tuple-element.157), channel_id=4, replica_groups=mesh['dp'=8,'ctx'=4] {'ctx'}, dimensions={1}, use_global_device_ids=true | all-gather | bytes 655360 | tf_op jit(solution)/shard_map/all_gather | solution.py:111
  122.6 1.6 convolution_bitcast_fusion.5
  124.7 1.3 copy-done.3
  126.6 2.1 %fusion.21 = (f32[4,127,512]{2,1,0:T(8,128)S(1)}, f32[4,127,512]{2,1,0:T(8,128)S(1)}, f32[4,127,512]{2,1,0:T(8,128)}, f32[4,127,512]{2,1,0:T(8,128)S(1)}) fusion(f32[4,256,512]{2,1,0:T(8,128)S(1)} %copy-done.3, s32[]{:T(128)S(6)} %select_n.74, s32[]{:T(128)S(6)} %add.189, f32[4,256,512]{2,1,0:T(8,128)S(1)} %multiply_add_fusion.4, s32[]{:T(128)S(6)} %add.190, ...), kind=kLoop, calls=%fused_computation.98 | loop fusion | flops 2600960 | bytes 10420236 | tf_op jit(solution)/shard_map/while/body/eval_jaxpr/mul | solution.py:49
  129.7 1.0 fusion.10
  130.7 1.0 fusion.9
  131.7 0.7 pad_maximum_fusion.18
  132.5 0.8 copy.33
  133.3 0.8 copy.32
  134.1 1.6 maximum_reduce_fusion.5
  135.7 1.0 fusion.8
  136.7 0.8 copy.31
  137.5 0.9 fusion.7
  138.4 1.6 copy.39
  140.1 24.6 %reduce-scatter.6.cloned.1.call-done = bf16[2,128,64]{1,2,0:T(8,128)(2,1)} async-done(((bf16[2,128,512]{1,2,0:T(8,128)(2,1)}), bf16[2,128,64]{1,2,0:T(8,128)(2,1)}) %reduce-scatter.6.cloned.1.call-update) | async-done | bytes 32784 | tf_op jit(solution)/shard_map/reduce_scatter | solution.py:158
  164.6 1.4 convert_multiply_fusion.3
  166.0 20.1 %reduce-scatter.10.cloned.1.call-done = bf16[128,64]{1,0:T(8,128)(2,1)} async-done(((bf16[512,64]{1,0:T(8,128)(2,1)}), bf16[128,64]{1,0:T(8,128)(2,1)}) %reduce-scatter.10.cloned.1.call-update) | async-done | bytes 16400
  186.1 0.8 copy.40
  (78 shorter events, 12.2 us)
Async XLA Ops:
  7.2 21.6 %copy-start = (bf16[2,512,512]{2,1,0:T(8,128)(2,1)S(1)}, bf16[2,512,512]{2,1,0:T(8,128)(2,1)}, u32[]{:S(2)}) copy-start(bf16[2,512,512]{2,1,0:T(8,128)(2,1)} %param.13) | copy-start | bytes 3145732
  7.2 131.2 %reduce-scatter.8.cloned.1.call-start = ((), (), s32[]{:S(2)}) async-start(), calls=%async_computation.4 | async-start | bytes 589824 | tf_op jit(solution)/shard_map/reduce_scatter | solution.py:163
  10.1 34.0 %copy-start.11 = (bf16[1,128,512]{1,2,0:T(8,128)(2,1)}, bf16[1,128,512]{1,2,0:T(8,128)(2,1)S(1)}, u32[]{:S(2)}) copy-start(bf16[1,128,512]{1,2,0:T(8,128)(2,1)S(1)} %copy.24) | copy-start | bytes 393220
  31.1 4.5 %copy-start.2 = (f32[2,4,256,512]{3,2,1,0:T(8,128)}, f32[2,4,256,512]{3,2,1,0:T(8,128)S(1)}, u32[]{:S(2)}) copy-start(f32[2,4,256,512]{3,2,1,0:T(8,128)S(1)} %convolution_bitcast_fusion.2) | copy-start | bytes 12582916
  68.6 2.0 %copy-start.16 = (bf16[1,128,512]{2,1,0:T(8,128)(2,1)S(1)}, bf16[1,128,512]{2,1,0:T(8,128)(2,1)}, u32[]{:S(2)}) copy-start(bf16[1,128,512]{2,1,0:T(8,128)(2,1)} %param.15) | copy-start | bytes 393220
  70.6 8.9 %copy-start.7 = (f32[512,128]{1,0:T(8,128)}, f32[512,128]{1,0:T(8,128)S(1)}, u32[]{:S(2)}) copy-start(f32[512,128]{1,0:T(8,128)S(1)} %convolution_add_fusion) | copy-start | bytes 786436
  71.8 92.8 %reduce-scatter.6.cloned.1.call-start = ((), (), s32[]{:S(2)}) async-start(), calls=%async_computation.3 | async-start | bytes 294912 | tf_op jit(solution)/shard_map/reduce_scatter | solution.py:158
  76.5 3.1 %copy-start.9 = (bf16[512,512]{1,0:T(8,128)(2,1)S(1)}, bf16[512,512]{1,0:T(8,128)(2,1)}, u32[]{:S(2)}) copy-start(bf16[512,512]{1,0:T(8,128)(2,1)} %param.14) | copy-start | bytes 1572868
  101.0 2.1 %copy-start.4 = (f32[4,256,512]{2,1,0:T(8,128)S(1)}, f32[4,256,512]{2,1,0:T(8,128)}, u32[]{:S(2)}) copy-start(f32[4,256,512]{2,1,0:T(8,128)} %convolution_bitcast_fusion.3) | copy-start | bytes 6291460
  101.0 2.7 %copy-start.6 = (f32[4,256,512]{2,1,0:T(8,128)S(1)}, f32[4,256,512]{2,1,0:T(8,128)}, u32[]{:S(2)}) copy-start(f32[4,256,512]{2,1,0:T(8,128)} %get-tuple-element.144) | copy-start | bytes 6291460
  105.6 0.9 copy-start.12
  105.7 1.0 copy-start.13
  124.4 1.6 copy-start.3
  124.4 2.2 %copy-start.5 = (f32[4,256,512]{2,1,0:T(8,128)S(1)}, f32[4,256,512]{2,1,0:T(8,128)}, u32[]{:S(2)}) copy-start(f32[4,256,512]{2,1,0:T(8,128)} %get-tuple-element.145) | copy-start | bytes 6291460
  129.4 3.1 %copy-start.14 = (bf16[1,128,512]{1,2,0:T(8,128)(2,1)S(1)}, bf16[1,128,512]{1,2,0:T(8,128)(2,1)}, u32[]{:S(2)}) copy-start(bf16[1,128,512]{1,2,0:T(8,128)(2,1)} %get-tuple-element.154) | copy-start | bytes 393220
  129.4 3.9 %copy-start.15 = (bf16[1,128,512]{1,2,0:T(8,128)(2,1)S(1)}, bf16[1,128,512]{1,2,0:T(8,128)(2,1)}, u32[]{:S(2)}) copy-start(bf16[1,128,512]{1,2,0:T(8,128)(2,1)} %get-tuple-element.156) | copy-start | bytes 393220
  132.5 53.6 %reduce-scatter.10.cloned.1.call-start = ((), (), s32[]{:S(2)}) async-start(), calls=%async_computation.5 | async-start | bytes 163840
  132.5 5.0 %copy-start.8 = (f32[512,128]{1,0:T(8,128)S(1)}, f32[512,128]{1,0:T(8,128)}, u32[]{:S(2)}) copy-start(f32[512,128]{1,0:T(8,128)} %copy-done.7) | copy-start | bytes 786436
  132.5 5.0 %copy-start.10 = (bf16[512,512]{1,0:T(8,128)(2,1)S(1)}, bf16[512,512]{1,0:T(8,128)(2,1)}, u32[]{:S(2)}) copy-start(bf16[512,512]{1,0:T(8,128)(2,1)} %param.14) | copy-start | bytes 1572868
  134.1 53.5 %copy-start.1 = (bf16[2,512,512]{2,1,0:T(8,128)(2,1)S(1)}, bf16[2,512,512]{2,1,0:T(8,128)(2,1)}, u32[]{:S(2)}) copy-start(bf16[2,512,512]{2,1,0:T(8,128)(2,1)} %param.13) | copy-start | bytes 3145732
Sparse Core Ops, SparseCore 0:
  71.9 34.6 reduce-scatter.7
  132.6 31.9 reduce-scatter.5
  166.9 19.1 reduce-scatter.9
where the time goes:
time: 195 us; the launch traced here: 194 us
  blocking collectives  61.2 us (31%)
  waiting for transfers between devices  44.7 us (23%)
  local copies, waits for them, and re-layouts  29.6 us (15%)
  matrix products  25.9 us (13%)
  other arithmetic  18.2 us (9%)
  between operations  14.1 us (7%)
    all_gather x2, blocking collectives, causal(): piece = lax.all_gather(source, 'ctx', axis=0, tiled=True)  32.8 us
    all_gather x2, blocking collectives, anti_owner(): lax.all_gather(grad_rows, 'ctx', axis=0, tiled=True)  28.4 us
    reduce_scatter x1, waiting for transfers between devices, on_device(): lax.psum_scatter(own_lags.astype(jnp.bfloat16), 'dp', scatter_dimension=2...  24.6 us
    unnamed x4, waiting for transfers between devices  20.1 us
    dot_general x7, matrix products, to_spectra(): jnp.einsum('fb,...bd->...fd', table, blocks.astype(jnp.float32), precisio...  13.6 us
    unnamed x41, local copies, waits for them, and re-layouts  10.2 us
    dot_general x8, matrix products, from_spectra(): jnp.einsum('tf,...fd->...td', table, spectra, precision=lax.Precision.HIG...  9.32 us
    mul x4, other arithmetic, spectral_product(): cross = left_imag * right_imag  4.95 us
  transfers between devices with their start and end apart: 3, of which 2 were waited for; matrix products, arithmetic and copies ran while one was open for 19% of the time, Pallas kernels for 0%

commit v1 on v0

v1 whole, which is shorter than its diff:
```python
import functools
import math

import jax
import jax.numpy as jnp
import ml_dtypes
import numpy as np
from jax import lax
from jax.experimental import pallas as pl
from jax.experimental.pallas import tpu as pltpu
from jax.sharding import PartitionSpec as P

F32 = jnp.float32
BF16 = jnp.bfloat16


def split_table(table):
    high = table.astype(ml_dtypes.bfloat16)
    low = (table - high.astype(np.float64)).astype(ml_dtypes.bfloat16)
    return high, low


@functools.lru_cache(maxsize=None)
def make_tables(length):
    period = 2 * length
    bins = np.arange(length)
    moments = np.arange(length)
    radians = (bins[:, None] * moments[None, :] % period) * (2.0 * math.pi / period)
    cosines, sines = np.cos(radians), -np.sin(radians)
    sines[0] = np.where(moments % 2 == 0, 1.0, -1.0)
    forward = np.concatenate([cosines, sines], axis=0)
    weights = np.full((period,), 2.0 / period)
    weights[0] = weights[length] = 1.0 / period
    inverse = forward.T * weights[None, :]
    return split_table(forward), split_table(inverse)


def product(left, right, conj_left):
    half = left.shape[0] // 2
    left_re, left_im = left[:half], left[half:]
    right_re, right_im = right[:half], right[half:]
    border = lax.broadcasted_iota(jnp.int32, left_re.shape, 0) == 0
    cross = left_im * right_im
    straight = left_re * right_re
    if conj_left:
        real = straight + jnp.where(border, 0.0, cross)
        imag = left_re * right_im - left_im * right_re
    else:
        real = straight - jnp.where(border, 0.0, cross)
        imag = left_re * right_im + left_im * right_re
    return jnp.concatenate([real, jnp.where(border, cross, imag)], axis=0)


def mxu(left, right):
    return jnp.dot(left, right, preferred_element_type=F32)


def to_spectrum(high, low, stream):
    return mxu(high[...], stream) + mxu(low[...], stream)


def from_spectrum(high, spectrum):
    return mxu(high[...], spectrum.astype(BF16))


def pick_columns(ref, index, width, count):
    if width % 128 == 0:
        return ref[:, pl.ds(pl.multiple_of(index * width, width), width)]
    whole = ref[...]
    out = whole[:, :width]
    for other in range(1, count):
        out = jnp.where(index == other, whole[:, other * width : (other + 1) * width], out)
    return out


def pick_rows(ref, index, rows):
    return ref[pl.ds(pl.multiple_of(index * rows, rows), rows), :]


def put_rows(ref, index, rows, block):
    ref[pl.ds(pl.multiple_of(index * rows, rows), rows), :] = block


def call(kernel, out_shape, args, scratch=(), flops=0, limit=16):
    vmem = pl.BlockSpec(memory_space=pltpu.VMEM)
    total = sum(math.prod(a.shape) * a.dtype.itemsize for a in args)
    return pl.pallas_call(
        kernel,
        out_shape=out_shape,
        in_specs=[vmem] * len(args),
        out_specs=jax.tree.map(lambda _: vmem, out_shape),
        scratch_shapes=list(scratch),
        compiler_params=pltpu.CompilerParams(vmem_limit_bytes=limit * 2**20),
        cost_estimate=pl.CostEstimate(flops=flops, bytes_accessed=total, transcendentals=0),
    )(*args)


def on_device(value, gate_one, gate_two, filters, out_weight, grad_out):
    rows, width = value.shape[1:]
    seq = lax.axis_size("ctx")
    data = lax.axis_size("dp")
    here = lax.axis_index("ctx")
    length = rows * seq
    cols = width // seq
    limit = 16 if length <= 512 else 56
    (fwd_high, fwd_low), (inv_high, _) = make_tables(length)
    fwd_high, fwd_low, inv_high = map(jnp.asarray, (fwd_high, fwd_low, inv_high))
    table_flops = 2 * 2 * length * length * cols

    def ahead(step):
        return lax.rem(lax.axis_index("ctx") + step, seq)

    def behind(step):
        return lax.rem(lax.axis_index("ctx") + seq - step, seq)

    def around(blocks):
        out = [blocks[0]]
        for step in range(1, seq):
            pairs = [(i, (i + step) % seq) for i in range(seq)]
            out.append(lax.ppermute(blocks[step], "ctx", pairs))
        return out

    value, gate_one, gate_two, cotangent = value[0], gate_one[0], gate_two[0], grad_out[0]

    def pack_kernel(value_ref, gate_ref, *outs):
        for step, out in enumerate(outs):
            out[0] = pick_columns(value_ref, ahead(step), cols, seq)
            out[1] = pick_columns(gate_ref, ahead(step), cols, seq)

    pair = jax.ShapeDtypeStruct((2, rows, cols), BF16)
    single = jax.ShapeDtypeStruct((rows, cols), BF16)
    with jax.named_scope("pack_value"):
        sends = call(pack_kernel, [pair] * seq, (value, gate_one))
    value_parts = around(sends)

    def grad_kernel(cot_ref, weight_ref, gate_ref, grad_ref, *rest):
        outs, scratch = rest[:-1], rest[-1]
        grad = lax.dot_general(
            cot_ref[...], weight_ref[...], (((1,), (1,)), ((), ())), preferred_element_type=F32
        )
        grad_ref[...] = grad
        scratch[...] = grad * gate_ref[...].astype(F32)
        for step, out in enumerate(outs):
            out[...] = pick_columns(scratch, ahead(step), cols, seq).astype(BF16)

    with jax.named_scope("grad_second"):
        grad_gated, *sends = call(
            grad_kernel,
            [jax.ShapeDtypeStruct((rows, width), F32)] + [single] * seq,
            (cotangent, out_weight, gate_two),
            scratch=[pltpu.VMEM((rows, width), F32)],
            flops=2 * rows * width * width,
        )
    grad_parts = around(sends)

    def filter_kernel(filters_ref, high, low, out):
        for index in range(2):
            out[index] = to_spectrum(high, low, filters_ref[index])

    with jax.named_scope("filter_spectra"):
        own_filters = lax.dynamic_slice_in_dim(filters, here * cols, cols, 2)
        spectra = call(
            filter_kernel,
            jax.ShapeDtypeStruct((2, 2 * length, cols), F32),
            (own_filters, fwd_high, fwd_low),
            flops=4 * table_flops,
            limit=limit,
        )

    def forward_kernel(*refs):
        parts, refs = refs[:seq], refs[seq:]
        filt, high, low, back, first_ref, value_spec, mixed_spec = refs[:7]
        outs, (stream, second) = refs[7:-2], refs[-2:]
        for step, part in enumerate(parts):
            put_rows(stream, behind(step), rows, part[0])
        value_spec[...] = to_spectrum(high, low, stream[...])
        first_ref[...] = from_spectrum(back, product(filt[0], value_spec[...], False))
        for step, part in enumerate(parts):
            gated = part[1].astype(F32) * pick_rows(first_ref, behind(step), rows)
            put_rows(stream, behind(step), rows, gated.astype(BF16))
        mixed_spec[...] = to_spectrum(high, low, stream[...])
        second[...] = from_spectrum(back, product(filt[1], mixed_spec[...], False))
        for step, out in enumerate(outs):
            out[...] = pick_rows(second, ahead(step), rows).astype(BF16)

    stream_f32 = jax.ShapeDtypeStruct((length, cols), F32)
    spectrum_f32 = jax.ShapeDtypeStruct((2 * length, cols), F32)
    with jax.named_scope("forward_convolutions"):
        first_conv, value_spectrum, mixed_spectrum, *sends = call(
            forward_kernel,
            [stream_f32, spectrum_f32, spectrum_f32] + [single] * seq,
            (*value_parts, spectra, fwd_high, fwd_low, inv_high),
            scratch=[pltpu.VMEM((length, cols), BF16), pltpu.VMEM((length, cols), F32)],
            flops=6 * table_flops,
            limit=limit,
        )
    second_parts = around(sends)

    per_ctx = data // seq
    fine = cols // per_ctx
    packed = fine == 64 and per_ctx == 2

    def backward_kernel(*refs):
        parts, values, refs = refs[:seq], refs[seq : 2 * seq], refs[2 * seq :]
        filt, first_ref, value_spec, mixed_spec, high, low, back, lags = refs[:8]
        outs, (stream, wide, total) = refs[8:-3], refs[-3:]
        for step, part in enumerate(parts):
            put_rows(stream, behind(step), rows, part[...])
        spectrum = to_spectrum(high, low, stream[...])
        wide[:, :cols] = product(filt[1], spectrum, True).astype(BF16)
        wide[:, cols:] = product(mixed_spec[...], spectrum, True).astype(BF16)
        both = mxu(back[...], wide[...])
        total[...] = both[:, :cols]
        lag_second = both[:, cols:]
        for step, part in enumerate(values):
            grad = pick_rows(total, behind(step), rows)
            put_rows(stream, behind(step), rows, (grad * part[1].astype(F32)).astype(BF16))
        for step, out in enumerate(outs):
            grad = pick_rows(total, ahead(step), rows) * pick_rows(first_ref, ahead(step), rows)
            out[0] = grad.astype(BF16)
        spectrum = to_spectrum(high, low, stream[...])
        wide[:, :cols] = product(filt[0], spectrum, True).astype(BF16)
        wide[:, cols:] = product(value_spec[...], spectrum, True).astype(BF16)
        both = mxu(back[...], wide[...])
        total[...] = both[:, :cols]
        lag_first = both[:, cols:]
        for step, out in enumerate(outs):
            out[1] = pick_rows(total, ahead(step), rows).astype(BF16)
        if packed:
            low_lanes = lax.broadcasted_iota(jnp.int32, lag_first.shape, 1) < fine
            turned_first = pltpu.roll(lag_first, fine, axis=1)
            turned_second = pltpu.roll(lag_second, fine, axis=1)
            lags[0] = jnp.where(low_lanes, lag_first, turned_second).astype(BF16)
            lags[1] = jnp.where(low_lanes, turned_first, lag_second).astype(BF16)
        else:
            lags[0] = lag_first.astype(BF16)
            lags[1] = lag_second.astype(BF16)

    with jax.named_scope("backward_convolutions"):
        lags, *sends = call(
            backward_kernel,
            [jax.ShapeDtypeStruct((2, length, cols), BF16)] + [pair] * seq,
            (
                *grad_parts,
                *value_parts,
                spectra,
                first_conv,
                value_spectrum,
                mixed_spectrum,
                fwd_high,
                fwd_low,
                inv_high,
            ),
            scratch=[
                pltpu.VMEM((length, cols), BF16),
                pltpu.VMEM((2 * length, 2 * cols), BF16),
                pltpu.VMEM((length, cols), F32),
            ],
            flops=8 * table_flops,
            limit=limit,
        )
    result_parts = around(sends)

    def gated_kernel(*refs):
        parts, (gate_ref, cot_ref, second_ref, gated_ref, weight_ref) = refs[:seq], refs[seq:]
        for step, part in enumerate(parts):
            if cols % 128 == 0:
                start = pl.multiple_of(behind(step) * cols, cols)
                second_ref[:, pl.ds(start, cols)] = part[...]
            else:
                for index in range(seq):

                    @pl.when(behind(step) == index)
                    def _():
                        second_ref[:, index * cols : (index + 1) * cols] = part[...]

        gated = (gate_ref[...].astype(F32) * second_ref[...].astype(F32)).astype(BF16)
        gated_ref[...] = gated
        weight_ref[...] = lax.dot_general(
            gated, cot_ref[...], (((0,), (0,)), ((), ())), preferred_element_type=F32
        ).astype(BF16)

    wide_bf16 = jax.ShapeDtypeStruct((rows, width), BF16)
    with jax.named_scope("weight_partial"):
        second_conv, gated, weight_part = call(
            gated_kernel,
            [wide_bf16, wide_bf16, jax.ShapeDtypeStruct((width, width), BF16)],
            (*second_parts, gate_two, cotangent),
            flops=2 * rows * width * width,
        )
    mixed = mxu(gated, out_weight).astype(BF16)
    grad_gate_two = (grad_gated * second_conv.astype(F32)).astype(BF16)

    core = lax.rem(lax.axis_index("dp"), 2)
    chip = lax.div(lax.axis_index("dp"), 2)
    chips = data // 2

    def over_documents(terms):
        shape = terms.shape[1:]
        by_core = terms.reshape(chips, 2, *shape)
        kept = lax.dynamic_index_in_dim(by_core, core, 1, keepdims=False)
        given = lax.dynamic_index_in_dim(by_core, 1 - core, 1, keepdims=False)
        swap = [(i, i ^ 1) for i in range(data)]
        kept = kept.astype(F32) + lax.ppermute(given, "dp", swap).astype(F32)
        total = lax.dynamic_index_in_dim(kept, chip, 0, keepdims=False)
        for step in range(1, chips):
            pairs = [(i, (i + 2 * step) % data) for i in range(data)]
            block = lax.dynamic_index_in_dim(kept, lax.rem(chip + step, chips), 0, keepdims=False)
            total = total + lax.ppermute(block.astype(BF16), "dp", pairs).astype(F32)
        return total

    if packed:
        lag_terms = lags.reshape(2, seq, rows, cols).transpose(1, 0, 2, 3)
    else:
        lag_terms = lags.reshape(2, seq, rows, per_ctx, fine).transpose(1, 3, 2, 0, 4)
    lag_terms = lag_terms.reshape(data, rows, 2 * fine)
    lag_sum = over_documents(lag_terms)
    weight_sum = over_documents(weight_part.reshape(data, width // data, width))

    pairs = []
    for i in range(data):
        for j in range(seq):
            pairs.append((i * seq + j, (per_ctx * j + i % per_ctx) * seq + i // per_ctx))
    lag_own = lax.ppermute(lag_sum.astype(BF16), ("dp", "ctx"), pairs)
    filter_grad = lag_own.reshape(rows, 2, fine).transpose(1, 0, 2).astype(F32) / data

    weight_blocks = weight_sum.reshape(width // data, seq, cols)
    total = lax.dynamic_index_in_dim(weight_blocks, here, 1, keepdims=False)
    for step in range(1, seq):
        block = lax.dynamic_index_in_dim(weight_blocks, ahead(step), 1, keepdims=False)
        ring = [(i, (i + step) % seq) for i in range(seq)]
        total = total + lax.ppermute(block.astype(BF16), "ctx", ring).astype(F32)
    weight_grad = total / data

    def unpack_kernel(*refs):
        parts, (gate_ref, value_ref) = refs[:seq], refs[seq:]
        for step, part in enumerate(parts):
            if cols % 128 == 0:
                start = pl.multiple_of(behind(step) * cols, cols)
                gate_ref[:, pl.ds(start, cols)] = part[0]
                value_ref[:, pl.ds(start, cols)] = part[1]
            else:
                for index in range(seq):

                    @pl.when(behind(step) == index)
                    def _():
                        gate_ref[:, index * cols : (index + 1) * cols] = part[0]
                        value_ref[:, index * cols : (index + 1) * cols] = part[1]

    with jax.named_scope("unpack_results"):
        grad_gate_one, grad_value = call(unpack_kernel, [wide_bf16, wide_bf16], result_parts)
    return (
        mixed[None],
        grad_value[None],
        grad_gate_one[None],
        grad_gate_two[None],
        filter_grad,
        weight_grad,
    )


def solution(mesh):
    stream = P("dp", "ctx", None)
    return jax.shard_map(
        on_device,
        mesh=mesh,
        in_specs=(stream, stream, stream, P(), P(), stream),
        out_specs=(stream, stream, stream, stream, P(None, "ctx", "dp"), P("dp", "ctx")),
        check_vma=False,
    )
```

time: 195 us -> 65.7 us (0.34)
  blocking collectives: 61.2 us -> 0 us
  waiting for transfers between devices: 44.7 us -> 6.76 us
  starting transfers between devices: 0.12 us -> 37.8 us
  matrix products: 25.9 us -> 0.89 us
  local copies, waits for them, and re-layouts: 29.6 us -> 7.1 us
  other arithmetic: 18.2 us -> 1.47 us
  between operations: 14.1 us -> 0.96 us
  Pallas kernels: 0 us -> 10.4 us
    all_gather x4 -> x0, blocking collectives: 61.2 us -> none  [the longest x2 32.8 us: causal(): piece = lax.all_gather(source, 'ctx', axis=0, tiled=True)]
    ppermute x0 -> x24, starting transfers between devices: none -> 37.8 us  [the longest x12 19.9 us: around(): out.append(lax.ppermute(blocks[step], 'ctx', pairs))]
    dot_general x18 -> x1, matrix products: 25.9 us -> 0.89 us  [mxu(): return jnp.dot(left, right, preferred_element_type=F32)]
    reduce_scatter x2 -> x0, waiting for transfers between devices: 24.6 us -> none  [the longest x1 24.6 us: on_device(): lax.psum_scatter(own_lags.astype(jnp.bfloat16), 'dp', scatter_dimension=2...]
    unnamed x4 -> x0, waiting for transfers between devices: 20.1 us -> none
    slice x11 -> x0, local copies, waits for them, and re-layouts: 13.1 us -> none  [the longest x1 4.62 us: anti_owner(): filter_spectrum = padded_filter[lag_blocks:]]
    pallas_call x0 -> x7, Pallas kernels: none -> 10.4 us  [call(): pl.pallas_call(kernel, out_shape=out_shape, in_specs=[vmem] * len(args),...]
    ppermute x0 -> x24, waiting for transfers between devices: none -> 6.76 us  [the longest x3 4.48 us: on_device(): total = total + lax.ppermute(block.astype(BF16), 'ctx', ring).astype(F32)]
  transfers between devices with their start and end apart: 3 -> 24, of which waited for: 2 -> 6; matrix products, arithmetic and copies ran while one was open for 19% -> 4% of each run, Pallas kernels for 0% -> 16%
where the time goes in v1:
time: 65.7 us; the launch traced here: 65.4 us
  starting transfers between devices  37.8 us (58%)
  Pallas kernels  10.4 us (16%)
  local copies, waits for them, and re-layouts  7.1 us (11%)
  waiting for transfers between devices  6.76 us (10%)
  other arithmetic  1.47 us (2%)
  between operations  0.96 us (1%)
  matrix products  0.89 us (1%)
    ppermute x12, starting transfers between devices, around(): out.append(lax.ppermute(blocks[step], 'ctx', pairs))  19.9 us
    ppermute x6, starting transfers between devices, over_documents(): total = total + lax.ppermute(block.astype(BF16), 'dp', pairs).astype(F32)  12.2 us
    pallas_call x7, Pallas kernels, call(): pl.pallas_call(kernel, out_shape=out_shape, in_specs=[vmem] * len(args),...  10.4 us
    unnamed x27, local copies, waits for them, and re-layouts  6.06 us
    ppermute x3, starting transfers between devices, on_device(): total = total + lax.ppermute(block.astype(BF16), 'ctx', ring).astype(F32)  4.51 us
    ppermute x3, waiting for transfers between devices, on_device(): total = total + lax.ppermute(block.astype(BF16), 'ctx', ring).astype(F32)  4.48 us
    ppermute x6, waiting for transfers between devices, over_documents(): total = total + lax.ppermute(block.astype(BF16), 'dp', pairs).astype(F32)  2.25 us
  transfers between devices with their start and end apart: 24, of which 6 were waited for; matrix products, arithmetic and copies ran while one was open for 4% of the time, Pallas kernels for 16%

profile of v1, /device:TPU:0, one launch (start us, length us, event | category | flops | bytes accessed | tf_op | source)
XLA Modules:
  0.0 65.4 jit_solution(3435139285659039537)
XLA Ops:
  0.6 0.0 copy-start
  0.7 1.0 %copy-done.10 = bf16[1,128,512]{2,1,0:T(8,128)(2,1)S(1)} copy-done((bf16[1,128,512]{2,1,0:T(8,128)(2,1)S(1)}, bf16[1,128,512]{2,1,0:T(8,128)(2,1)}, u32[]{:S(2)}) %copy-start.10) | copy-done | bytes 131096
  1.7 0.9 %copy-done.11 = bf16[1,128,512]{2,1,0:T(8,128)(2,1)S(1)} copy-done((bf16[1,128,512]{2,1,0:T(8,128)(2,1)S(1)}, bf16[1,128,512]{2,1,0:T(8,128)(2,1)}, u32[]{:S(2)}) %copy-start.11) | copy-done | bytes 131096
  2.7 3.1 %collective-permute-start = (bf16[2,128,128]{2,1,0:T(8,128)(2,1)S(1)}, bf16[2,128,128]{2,1,0:T(8,128)(2,1)S(1)}, u32[]{:S(2)}, u32[]{:S(2)}) collective-permute-start(bf16[2,128,128]{2,1,0:T(8,128)(2,1)S(1)} %get-tuple-element.33), channel_id=1, source_target_pairs={{0,1},{1,2},{2,3},{3,0},{4,5},{5,6},{6,7},{7,4},{8,9},{9,10},{10,1... | collective-permute-start | bytes 196616 | tf_op jit(solution)/shard_map/ppermute | solution.py:120
  5.7 2.6 %collective-permute-start.1 = (bf16[2,128,128]{2,1,0:T(8,128)(2,1)S(1)}, bf16[2,128,128]{2,1,0:T(8,128)(2,1)S(1)}, u32[]{:S(2)}, u32[]{:S(2)}) collective-permute-start(bf16[2,128,128]{2,1,0:T(8,128)(2,1)S(1)} %get-tuple-element.34), channel_id=1, source_target_pairs={{0,2},{1,3},{2,0},{3,1},{4,6},{5,7},{6,4},{7,5},{8,10},{9,11},{10,... | collective-permute-start | bytes 196616 | tf_op jit(solution)/shard_map/ppermute | solution.py:120
  8.3 1.3 %collective-permute-start.2 = (bf16[2,128,128]{2,1,0:T(8,128)(2,1)S(1)}, bf16[2,128,128]{2,1,0:T(8,128)(2,1)S(1)}, u32[]{:S(2)}, u32[]{:S(2)}) collective-permute-start(bf16[2,128,128]{2,1,0:T(8,128)(2,1)S(1)} %get-tuple-element.35), channel_id=1, source_target_pairs={{0,3},{1,0},{2,1},{3,2},{4,7},{5,4},{6,5},{7,6},{8,11},{9,8},{10,9... | collective-permute-start | bytes 196616 | tf_op jit(solution)/shard_map/ppermute | solution.py:120
  9.7 1.0 %copy-done.4 = bf16[512,512]{1,0:T(8,128)(2,1)S(1)} copy-done((bf16[512,512]{1,0:T(8,128)(2,1)S(1)}, bf16[512,512]{1,0:T(8,128)(2,1)}, u32[]{:S(2)}) %copy-start.4) | copy-done | bytes 524312
  10.7 0.9 %copy-done.6 = bf16[1,128,512]{2,1,0:T(8,128)(2,1)S(1)} copy-done((bf16[1,128,512]{2,1,0:T(8,128)(2,1)S(1)}, bf16[1,128,512]{2,1,0:T(8,128)(2,1)}, u32[]{:S(2)}) %copy-start.6) | copy-done | bytes 131096
  11.6 0.9 %copy-done.8 = bf16[1,128,512]{2,1,0:T(8,128)(2,1)S(1)} copy-done((bf16[1,128,512]{2,1,0:T(8,128)(2,1)S(1)}, bf16[1,128,512]{2,1,0:T(8,128)(2,1)}, u32[]{:S(2)}) %copy-start.8) | copy-done | bytes 131096
  12.5 0.4 grad_second.1
  12.9 0.7 %collective-permute-start.6 = (bf16[128,128]{1,0:T(8,128)(2,1)S(1)}, bf16[128,128]{1,0:T(8,128)(2,1)S(1)}, u32[]{:S(2)}, u32[]{:S(2)}) collective-permute-start(bf16[128,128]{1,0:T(8,128)(2,1)S(1)} %get-tuple-element.42), channel_id=1, source_target_pairs={{0,1},{1,2},{2,3},{3,0},{4,5},{5,6},{6,7},{7,4},{8,9},{9,10},{10,1... | collective-permute-start | bytes 98312 | tf_op jit(solution)/shard_map/ppermute | solution.py:120
  13.6 0.3 collective-permute-start.7
  14.1 1.2 %copy-done.2 = bf16[1024,512]{1,0:T(8,128)(2,1)S(1)} copy-done((bf16[1024,512]{1,0:T(8,128)(2,1)S(1)}, bf16[1024,512]{1,0:T(8,128)(2,1)}, u32[]{:S(2)}) %copy-start.2) | copy-done | bytes 1048600
  15.3 1.2 %filter_spectra.1.refs_4_.refs_8_ = f32[2,1024,128]{2,1,0:T(8,128)S(1)} custom-call(bf16[2,512,128]{2,1,0:T(8,128)(2,1)S(1)} %constant_dynamic-slice_fusion.1.filters_ref, bf16[1024,512]{1,0:T(8,128)(2,1)S(1)} %copy-done.2, bf16[1024,512]{1,0:T(8,128)(2,1)S(1)} %copy-done.1), custom_call_target="tpu_custom_call" | custom-call | flops 536870912 | bytes 2359296 | tf_op jit(solution)/shard_map/filter_spectra/pallas_call | solution.py:87
  16.6 2.9 %collective-permute-start.8 = (bf16[128,128]{1,0:T(8,128)(2,1)S(1)}, bf16[128,128]{1,0:T(8,128)(2,1)S(1)}, u32[]{:S(2)}, u32[]{:S(2)}) collective-permute-start(bf16[128,128]{1,0:T(8,128)(2,1)S(1)} %get-tuple-element.44), channel_id=1, source_target_pairs={{0,3},{1,0},{2,1},{3,2},{4,7},{5,4},{6,5},{7,6},{8,11},{9,8},{10,9... | collective-permute-start | bytes 98312 | tf_op jit(solution)/shard_map/ppermute | solution.py:120
  19.4 3.7 %forward_convolutions.1 = (f32[512,128]{1,0:T(8,128)S(1)}, f32[1024,128]{1,0:T(8,128)S(1)}, f32[1024,128]{1,0:T(8,128)S(1)}, bf16[128,128]{1,0:T(8,128)(2,1)S(1)...) custom-call(bf16[2,128,128]{2,1,0:T(8,128)(2,1)S(1)} %get-tuple-element.32.refs_0_.refs_4, ...), custom_call_target="tpu_custom_call" | custom-call | flops 805306368 | bytes 4456448 | tf_op jit(solution)/shard_map/forward_convolutions/pallas_call | solution.py:87
  23.2 0.6 collective-permute-start.3
  23.8 1.5 %collective-permute-start.4 = (bf16[128,128]{1,0:T(8,128)(2,1)S(1)}, bf16[128,128]{1,0:T(8,128)(2,1)S(1)}, u32[]{:S(2)}, u32[]{:S(2)}) collective-permute-start(bf16[128,128]{1,0:T(8,128)(2,1)S(1)} %get-tuple-element.38), channel_id=1, source_target_pairs={{0,2},{1,3},{2,0},{3,1},{4,6},{5,7},{6,4},{7,5},{8,10},{9,11},{10,... | collective-permute-start | bytes 98312 | tf_op jit(solution)/shard_map/ppermute | solution.py:120
  25.3 2.8 %collective-permute-start.5 = (bf16[128,128]{1,0:T(8,128)(2,1)S(1)}, bf16[128,128]{1,0:T(8,128)(2,1)S(1)}, u32[]{:S(2)}, u32[]{:S(2)}) collective-permute-start(bf16[128,128]{1,0:T(8,128)(2,1)S(1)} %get-tuple-element.39), channel_id=1, source_target_pairs={{0,3},{1,0},{2,1},{3,2},{4,7},{5,4},{6,5},{7,6},{8,11},{9,8},{10,9... | collective-permute-start | bytes 98312 | tf_op jit(solution)/shard_map/ppermute | solution.py:120
  28.2 3.9 %backward_convolutions.1 = (bf16[2,512,128]{2,1,0:T(8,128)(2,1)S(1)}, bf16[2,128,128]{2,1,0:T(8,128)(2,1)S(1)}, bf16[2,128,128]{2,1,0:T(8,128)(2,1)S(1)}, bf16[2...) custom-call(bf16[128,128]{1,0:T(8,128)(2,1)S(1)} %get-tuple-element.41.refs_0_, ...), custom_call_target="tpu_custom_call" | custom-call | flops 1073741824 | bytes 5898240 | tf_op jit(solution)/shard_map/backward_convolutions/pallas_call | solution.py:87
  32.1 0.1 collective-permute-start.9
  32.2 1.0 %collective-permute-start.10 = (bf16[2,128,128]{2,1,0:T(8,128)(2,1)S(1)}, bf16[2,128,128]{2,1,0:T(8,128)(2,1)S(1)}, u32[]{:S(2)}, u32[]{:S(2)}) collective-permute-start(bf16[2,128,128]{2,1,0:T(8,128)(2,1)S(1)} %get-tuple-element.50), channel_id=1, source_target_pairs={{0,2},{1,3},{2,0},{3,1},{4,6},{5,7},{6,4},{7,5},{8,10},{9,11},{10,... | collective-permute-start | bytes 196616 | tf_op jit(solution)/shard_map/ppermute | solution.py:120
  33.2 2.9 %collective-permute-start.11 = (bf16[2,128,128]{2,1,0:T(8,128)(2,1)S(1)}, bf16[2,128,128]{2,1,0:T(8,128)(2,1)S(1)}, u32[]{:S(2)}, u32[]{:S(2)}) collective-permute-start(bf16[2,128,128]{2,1,0:T(8,128)(2,1)S(1)} %get-tuple-element.51), channel_id=1, source_target_pairs={{0,3},{1,0},{2,1},{3,2},{4,7},{5,4},{6,5},{7,6},{8,11},{9,8},{10,9... | collective-permute-start | bytes 196616 | tf_op jit(solution)/shard_map/ppermute | solution.py:120
  36.1 0.4 weight_partial.1
  36.5 0.6 collective-permute-start.17
  37.1 0.7 %fusion.1 = bf16[1,128,512]{2,1,0:T(8,128)(2,1)} fusion(f32[128,512]{1,0:T(8,128)S(1)} %get-tuple-element.54, bf16[128,512]{1,0:T(8,128)(2,1)S(1)} %get-tuple-element.55), kind=kLoop, calls=%fused_computation.6 | loop fusion | flops 196608 | bytes 524288 | tf_op jit(solution)/shard_map/broadcast_in_dim | solution.py:356
  37.8 1.5 %collective-permute-start.13 = (bf16[128,128]{1,0:T(8,128)(2,1)S(1)}, bf16[128,128]{1,0:T(8,128)(2,1)S(1)}, u32[]{:S(2)}, u32[]{:S(2)}) collective-permute-start(bf16[128,128]{1,0:T(8,128)(2,1)S(1)} %get-tuple-element.61), channel_id=1, source_target_pairs={{0,8},{4,12},{8,16},{12,20},{16,24},{20,28},{24,0},{28,4},{1,9},{5... | collective-permute-start | bytes 98312 | tf_op jit(solution)/shard_map/ppermute | solution.py:309
  39.4 1.4 %collective-permute-start.15 = (bf16[128,128]{1,0:T(8,128)(2,1)S(1)}, bf16[128,128]{1,0:T(8,128)(2,1)S(1)}, u32[]{:S(2)}, u32[]{:S(2)}) collective-permute-start(bf16[128,128]{1,0:T(8,128)(2,1)S(1)} %get-tuple-element.62), channel_id=1, source_target_pairs={{0,24},{4,28},{8,0},{12,4},{16,8},{20,12},{24,16},{28,20},{1,25},{... | collective-permute-start | bytes 98312 | tf_op jit(solution)/shard_map/ppermute | solution.py:309
  40.8 1.5 %collective-permute-start.14 = (bf16[128,128]{1,0:T(8,128)(2,1)S(1)}, bf16[128,128]{1,0:T(8,128)(2,1)S(1)}, u32[]{:S(2)}, u32[]{:S(2)}) collective-permute-start(bf16[128,128]{1,0:T(8,128)(2,1)S(1)} %get-tuple-element.63), channel_id=1, source_target_pairs={{0,16},{4,20},{8,24},{12,28},{16,0},{20,4},{24,8},{28,12},{1,17},{... | collective-permute-start | bytes 98312 | tf_op jit(solution)/shard_map/ppermute | solution.py:309
  42.3 0.9 %fusion = bf16[1,128,512]{2,1,0:T(8,128)(2,1)} fusion(bf16[128,512]{1,0:T(8,128)(2,1)S(1)} %get-tuple-element.40, bf16[512,512]{1,0:T(8,128)(2,1)S(1)} %copy-done.5), kind=kOutput, calls=%fused_computation.1 | convolution fusion | flops 67174400 | bytes 786432 | tf_op jit(solution)/shard_map/dot_general | solution.py:55
  43.2 0.7 %unpack_results.1 = (bf16[128,512]{1,0:T(8,128)(2,1)}, bf16[128,512]{1,0:T(8,128)(2,1)}) custom-call(bf16[2,128,128]{2,1,0:T(8,128)(2,1)S(1)} %get-tuple-element.48.refs_0_, bf16[2,128,128]{2,1,0:T(8,128)(2,1)S(1)} %collective-permute-done.9.refs_1_, bf16[2,128,128]{2,1,0:T(8,128)(2,1)S(1)} %collective-permute-done.10.refs_2_, ...), custom_call_target="tpu_custom_call" | custom-call | bytes 262144 | tf_op jit(solution)/shard_map/unpack_results/pallas_call | solution.py:87
  44.0 0.7 %collective-permute-done.14 = bf16[128,128]{1,0:T(8,128)(2,1)S(1)} collective-permute-done((bf16[128,128]{1,0:T(8,128)(2,1)S(1)}, bf16[128,128]{1,0:T(8,128)(2,1)S(1)}, u32[]{:S(2)}, u32[]{:S(2)}) %collective-permute-start.14) | collective-permute-done | bytes 32800 | tf_op jit(solution)/shard_map/ppermute | solution.py:309
  44.8 0.7 %collective-permute-start.16 = (bf16[128,128]{1,0:T(8,128)(2,1)S(1)}, bf16[128,128]{1,0:T(8,128)(2,1)S(1)}, u32[]{:S(2)}, u32[]{:S(2)}) collective-permute-start(bf16[128,128]{1,0:T(8,128)(2,1)S(1)} %fusion.9), channel_id=1, source_target_pairs={{0,0},{1,8},{2,16},{3,24},{4,4},{5,12},{6,20},{7,28},{8,1},{9,9},{... | collective-permute-start | bytes 98312 | tf_op jit(solution)/shard_map/ppermute | solution.py:324
  45.4 0.1 convert_add_fusion
  45.6 3.7 %collective-permute-start.18 = (bf16[64,512]{1,0:T(8,128)(2,1)S(1)}, bf16[64,512]{1,0:T(8,128)(2,1)S(1)}, u32[]{:S(2)}, u32[]{:S(2)}) collective-permute-start(bf16[64,512]{1,0:T(8,128)(2,1)S(1)} %get-tuple-element.58), channel_id=1, source_target_pairs={{0,8},{4,12},{8,16},{12,20},{16,24},{20,28},{24,0},{28,4},{1,9},{5... | collective-permute-start | bytes 196616 | tf_op jit(solution)/shard_map/ppermute | solution.py:309
  49.3 0.7 %collective-permute-start.20 = (bf16[64,512]{1,0:T(8,128)(2,1)S(1)}, bf16[64,512]{1,0:T(8,128)(2,1)S(1)}, u32[]{:S(2)}, u32[]{:S(2)}) collective-permute-start(bf16[64,512]{1,0:T(8,128)(2,1)S(1)} %get-tuple-element.59), channel_id=1, source_target_pairs={{0,24},{4,28},{8,0},{12,4},{16,8},{20,12},{24,16},{28,20},{1,25},{... | collective-permute-start | bytes 196616 | tf_op jit(solution)/shard_map/ppermute | solution.py:309
  49.9 3.3 %collective-permute-start.19 = (bf16[64,512]{1,0:T(8,128)(2,1)S(1)}, bf16[64,512]{1,0:T(8,128)(2,1)S(1)}, u32[]{:S(2)}, u32[]{:S(2)}) collective-permute-start(bf16[64,512]{1,0:T(8,128)(2,1)S(1)} %get-tuple-element.60), channel_id=1, source_target_pairs={{0,16},{4,20},{8,24},{12,28},{16,0},{20,4},{24,8},{28,12},{1,17},{... | collective-permute-start | bytes 196616 | tf_op jit(solution)/shard_map/ppermute | solution.py:309
  53.3 0.7 %copy.25 = f32[128,128]{0,1:T(8,128)} copy(f32[128,128]{1,0:T(8,128)S(1)} %convert_multiply_fusion) | data formatting | bytes 131072 | tf_op jit(solution)/shard_map/div | solution.py:325
  54.0 0.7 %collective-permute-done.20 = bf16[64,512]{1,0:T(8,128)(2,1)S(1)} collective-permute-done((bf16[64,512]{1,0:T(8,128)(2,1)S(1)}, bf16[64,512]{1,0:T(8,128)(2,1)S(1)}, u32[]{:S(2)}, u32[]{:S(2)}) %collective-permute-start.20) | collective-permute-done | bytes 65568 | tf_op jit(solution)/shard_map/ppermute | solution.py:309
  54.8 0.8 %collective-permute-done.19 = bf16[64,512]{1,0:T(8,128)(2,1)S(1)} collective-permute-done((bf16[64,512]{1,0:T(8,128)(2,1)S(1)}, bf16[64,512]{1,0:T(8,128)(2,1)S(1)}, u32[]{:S(2)}, u32[]{:S(2)}) %collective-permute-start.19) | collective-permute-done | bytes 65568 | tf_op jit(solution)/shard_map/ppermute | solution.py:309
  55.6 0.1 dynamic-slice_convert_fusion.8
  55.8 2.5 %collective-permute-start.22 = (bf16[64,128]{1,0:T(8,128)(2,1)S(1)}, bf16[64,128]{1,0:T(8,128)(2,1)S(1)}, u32[]{:S(2)}, u32[]{:S(2)}) collective-permute-start(bf16[64,128]{1,0:T(8,128)(2,1)S(1)} %bitcast.79), channel_id=1, source_target_pairs={{0,2},{1,3},{2,0},{3,1},{4,6},{5,7},{6,4},{7,5},{8,10},{9,11},{10,... | collective-permute-start | bytes 49160 | tf_op jit(solution)/shard_map/ppermute | solution.py:332
  58.2 1.0 %collective-permute-start.23 = (bf16[64,128]{1,0:T(8,128)(2,1)S(1)}, bf16[64,128]{1,0:T(8,128)(2,1)S(1)}, u32[]{:S(2)}, u32[]{:S(2)}) collective-permute-start(bf16[64,128]{1,0:T(8,128)(2,1)S(1)} %bitcast.78), channel_id=1, source_target_pairs={{0,3},{1,0},{2,1},{3,2},{4,7},{5,4},{6,5},{7,6},{8,11},{9,8},{10,9... | collective-permute-start | bytes 49160 | tf_op jit(solution)/shard_map/ppermute | solution.py:332
  59.2 1.0 %collective-permute-start.21 = (bf16[64,128]{1,0:T(8,128)(2,1)S(1)}, bf16[64,128]{1,0:T(8,128)(2,1)S(1)}, u32[]{:S(2)}, u32[]{:S(2)}) collective-permute-start(bf16[64,128]{1,0:T(8,128)(2,1)S(1)} %bitcast.77), channel_id=1, source_target_pairs={{0,1},{1,2},{2,3},{3,0},{4,5},{5,6},{6,7},{7,4},{8,9},{9,10},{10,1... | collective-permute-start | bytes 49160 | tf_op jit(solution)/shard_map/ppermute | solution.py:332
  60.3 0.2 collective-permute-done.22
  60.5 1.5 %collective-permute-done.23 = bf16[64,128]{1,0:T(8,128)(2,1)S(1)} collective-permute-done((bf16[64,128]{1,0:T(8,128)(2,1)S(1)}, bf16[64,128]{1,0:T(8,128)(2,1)S(1)}, u32[]{:S(2)}, u32[]{:S(2)}) %collective-permute-start.23) | collective-permute-done | bytes 16416 | tf_op jit(solution)/shard_map/ppermute | solution.py:332
  62.0 2.8 %collective-permute-done.21 = bf16[64,128]{1,0:T(8,128)(2,1)S(1)} collective-permute-done((bf16[64,128]{1,0:T(8,128)(2,1)S(1)}, bf16[64,128]{1,0:T(8,128)(2,1)S(1)}, u32[]{:S(2)}, u32[]{:S(2)}) %collective-permute-start.21) | collective-permute-done | bytes 16416 | tf_op jit(solution)/shard_map/ppermute | solution.py:332
  64.8 0.6 add_multiply_fusion
  (51 shorter events, 0.4 us)
Async XLA Ops:
  0.6 13.3 %copy-start = (bf16[2,512,512]{2,1,0:T(8,128)(2,1)S(1)}, bf16[2,512,512]{2,1,0:T(8,128)(2,1)}, u32[]{:S(2)}) copy-start(bf16[2,512,512]{2,1,0:T(8,128)(2,1)} %param.12) | copy-start | bytes 3145732
  0.6 13.4 %copy-start.1 = (bf16[1024,512]{1,0:T(8,128)(2,1)S(1)}, bf16[1024,512]{1,0:T(8,128)(2,1)}, u32[]{:S(2)}) copy-start(bf16[1024,512]{1,0:T(8,128)(2,1)} %constant.94.clone.low.refs_6_.refs_13_) | copy-start | bytes 3145732
  0.7 1.1 %copy-start.10 = (bf16[1,128,512]{2,1,0:T(8,128)(2,1)S(1)}, bf16[1,128,512]{2,1,0:T(8,128)(2,1)}, u32[]{:S(2)}) copy-start(bf16[1,128,512]{2,1,0:T(8,128)(2,1)} %param.9) | copy-start | bytes 393220
  1.7 0.9 %copy-start.11 = (bf16[1,128,512]{2,1,0:T(8,128)(2,1)S(1)}, bf16[1,128,512]{2,1,0:T(8,128)(2,1)}, u32[]{:S(2)}) copy-start(bf16[1,128,512]{2,1,0:T(8,128)(2,1)} %param.10) | copy-start | bytes 393220
  2.7 13.9 %collective-permute-start = (bf16[2,128,128]{2,1,0:T(8,128)(2,1)S(1)}, bf16[2,128,128]{2,1,0:T(8,128)(2,1)S(1)}, u32[]{:S(2)}, u32[]{:S(2)}) collective-permute-start(bf16[2,128,128]{2,1,0:T(8,128)(2,1)S(1)} %get-tuple-element.33), channel_id=1, source_target_pairs={{0,1},{1,2},{2,3},{3,0},{4,5},{5,6},{6,7},{7,4},{8,9},{9,10},{10,1... | collective-permute-start | bytes 196616 | tf_op jit(solution)/shard_map/ppermute | solution.py:120
  5.7 13.7 %collective-permute-start.1 = (bf16[2,128,128]{2,1,0:T(8,128)(2,1)S(1)}, bf16[2,128,128]{2,1,0:T(8,128)(2,1)S(1)}, u32[]{:S(2)}, u32[]{:S(2)}) collective-permute-start(bf16[2,128,128]{2,1,0:T(8,128)(2,1)S(1)} %get-tuple-element.34), channel_id=1, source_target_pairs={{0,2},{1,3},{2,0},{3,1},{4,6},{5,7},{6,4},{7,5},{8,10},{9,11},{10,... | collective-permute-start | bytes 196616 | tf_op jit(solution)/shard_map/ppermute | solution.py:120
  8.3 11.1 %collective-permute-start.2 = (bf16[2,128,128]{2,1,0:T(8,128)(2,1)S(1)}, bf16[2,128,128]{2,1,0:T(8,128)(2,1)S(1)}, u32[]{:S(2)}, u32[]{:S(2)}) collective-permute-start(bf16[2,128,128]{2,1,0:T(8,128)(2,1)S(1)} %get-tuple-element.35), channel_id=1, source_target_pairs={{0,3},{1,0},{2,1},{3,2},{4,7},{5,4},{6,5},{7,6},{8,11},{9,8},{10,9... | collective-permute-start | bytes 196616 | tf_op jit(solution)/shard_map/ppermute | solution.py:120
  9.7 1.0 %copy-start.4 = (bf16[512,512]{1,0:T(8,128)(2,1)S(1)}, bf16[512,512]{1,0:T(8,128)(2,1)}, u32[]{:S(2)}) copy-start(bf16[512,512]{1,0:T(8,128)(2,1)} %weight_ref.1) | copy-start | bytes 1572868
  10.7 0.9 %copy-start.6 = (bf16[1,128,512]{2,1,0:T(8,128)(2,1)S(1)}, bf16[1,128,512]{2,1,0:T(8,128)(2,1)}, u32[]{:S(2)}) copy-start(bf16[1,128,512]{2,1,0:T(8,128)(2,1)} %param.11) | copy-start | bytes 393220
  11.6 0.9 %copy-start.8 = (bf16[1,128,512]{2,1,0:T(8,128)(2,1)S(1)}, bf16[1,128,512]{2,1,0:T(8,128)(2,1)}, u32[]{:S(2)}) copy-start(bf16[1,128,512]{2,1,0:T(8,128)(2,1)} %param.14) | copy-start | bytes 393220
  12.9 12.4 %collective-permute-start.6 = (bf16[128,128]{1,0:T(8,128)(2,1)S(1)}, bf16[128,128]{1,0:T(8,128)(2,1)S(1)}, u32[]{:S(2)}, u32[]{:S(2)}) collective-permute-start(bf16[128,128]{1,0:T(8,128)(2,1)S(1)} %get-tuple-element.42), channel_id=1, source_target_pairs={{0,1},{1,2},{2,3},{3,0},{4,5},{5,6},{6,7},{7,4},{8,9},{9,10},{10,1... | collective-permute-start | bytes 98312 | tf_op jit(solution)/shard_map/ppermute | solution.py:120
  13.6 14.6 %collective-permute-start.7 = (bf16[128,128]{1,0:T(8,128)(2,1)S(1)}, bf16[128,128]{1,0:T(8,128)(2,1)S(1)}, u32[]{:S(2)}, u32[]{:S(2)}) collective-permute-start(bf16[128,128]{1,0:T(8,128)(2,1)S(1)} %get-tuple-element.43), channel_id=1, source_target_pairs={{0,2},{1,3},{2,0},{3,1},{4,6},{5,7},{6,4},{7,5},{8,10},{9,11},{10,... | collective-permute-start | bytes 98312 | tf_op jit(solution)/shard_map/ppermute | solution.py:120
  14.1 1.2 %copy-start.2 = (bf16[1024,512]{1,0:T(8,128)(2,1)S(1)}, bf16[1024,512]{1,0:T(8,128)(2,1)}, u32[]{:S(2)}) copy-start(bf16[1024,512]{1,0:T(8,128)(2,1)} %constant.93.clone.high.refs_5_.refs_12_) | copy-start | bytes 3145732
  15.3 4.1 %copy-start.3 = (bf16[512,1024]{1,0:T(8,128)(2,1)S(1)}, bf16[512,1024]{1,0:T(8,128)(2,1)}, u32[]{:S(2)}) copy-start(bf16[512,1024]{1,0:T(8,128)(2,1)} %constant.95.clone.refs_7_.refs_14_) | copy-start | bytes 3145732
  16.6 11.6 %collective-permute-start.8 = (bf16[128,128]{1,0:T(8,128)(2,1)S(1)}, bf16[128,128]{1,0:T(8,128)(2,1)S(1)}, u32[]{:S(2)}, u32[]{:S(2)}) collective-permute-start(bf16[128,128]{1,0:T(8,128)(2,1)S(1)} %get-tuple-element.44), channel_id=1, source_target_pairs={{0,3},{1,0},{2,1},{3,2},{4,7},{5,4},{6,5},{7,6},{8,11},{9,8},{10,9... | collective-permute-start | bytes 98312 | tf_op jit(solution)/shard_map/ppermute | solution.py:120
  23.2 10.0 %collective-permute-start.3 = (bf16[128,128]{1,0:T(8,128)(2,1)S(1)}, bf16[128,128]{1,0:T(8,128)(2,1)S(1)}, u32[]{:S(2)}, u32[]{:S(2)}) collective-permute-start(bf16[128,128]{1,0:T(8,128)(2,1)S(1)} %get-tuple-element.37), channel_id=1, source_target_pairs={{0,1},{1,2},{2,3},{3,0},{4,5},{5,6},{6,7},{7,4},{8,9},{9,10},{10,1... | collective-permute-start | bytes 98312 | tf_op jit(solution)/shard_map/ppermute | solution.py:120
  23.8 12.2 %collective-permute-start.4 = (bf16[128,128]{1,0:T(8,128)(2,1)S(1)}, bf16[128,128]{1,0:T(8,128)(2,1)S(1)}, u32[]{:S(2)}, u32[]{:S(2)}) collective-permute-start(bf16[128,128]{1,0:T(8,128)(2,1)S(1)} %get-tuple-element.38), channel_id=1, source_target_pairs={{0,2},{1,3},{2,0},{3,1},{4,6},{5,7},{6,4},{7,5},{8,10},{9,11},{10,... | collective-permute-start | bytes 98312 | tf_op jit(solution)/shard_map/ppermute | solution.py:120
  25.3 10.7 %collective-permute-start.5 = (bf16[128,128]{1,0:T(8,128)(2,1)S(1)}, bf16[128,128]{1,0:T(8,128)(2,1)S(1)}, u32[]{:S(2)}, u32[]{:S(2)}) collective-permute-start(bf16[128,128]{1,0:T(8,128)(2,1)S(1)} %get-tuple-element.39), channel_id=1, source_target_pairs={{0,3},{1,0},{2,1},{3,2},{4,7},{5,4},{6,5},{7,6},{8,11},{9,8},{10,9... | collective-permute-start | bytes 98312 | tf_op jit(solution)/shard_map/ppermute | solution.py:120
  32.1 7.3 %collective-permute-start.9 = (bf16[2,128,128]{2,1,0:T(8,128)(2,1)S(1)}, bf16[2,128,128]{2,1,0:T(8,128)(2,1)S(1)}, u32[]{:S(2)}, u32[]{:S(2)}) collective-permute-start(bf16[2,128,128]{2,1,0:T(8,128)(2,1)S(1)} %get-tuple-element.49), channel_id=1, source_target_pairs={{0,1},{1,2},{2,3},{3,0},{4,5},{5,6},{6,7},{7,4},{8,9},{9,10},{10,1... | collective-permute-start | bytes 196616 | tf_op jit(solution)/shard_map/ppermute | solution.py:120
  32.2 8.6 %collective-permute-start.10 = (bf16[2,128,128]{2,1,0:T(8,128)(2,1)S(1)}, bf16[2,128,128]{2,1,0:T(8,128)(2,1)S(1)}, u32[]{:S(2)}, u32[]{:S(2)}) collective-permute-start(bf16[2,128,128]{2,1,0:T(8,128)(2,1)S(1)} %get-tuple-element.50), channel_id=1, source_target_pairs={{0,2},{1,3},{2,0},{3,1},{4,6},{5,7},{6,4},{7,5},{8,10},{9,11},{10,... | collective-permute-start | bytes 196616 | tf_op jit(solution)/shard_map/ppermute | solution.py:120
  33.1 2.9 %copy-start.7 = (bf16[1,128,512]{2,1,0:T(8,128)(2,1)S(1)}, bf16[1,128,512]{2,1,0:T(8,128)(2,1)}, u32[]{:S(2)}) copy-start(bf16[1,128,512]{2,1,0:T(8,128)(2,1)} %param.11) | copy-start | bytes 393220
  33.1 3.0 %copy-start.9 = (bf16[1,128,512]{2,1,0:T(8,128)(2,1)S(1)}, bf16[1,128,512]{2,1,0:T(8,128)(2,1)}, u32[]{:S(2)}) copy-start(bf16[1,128,512]{2,1,0:T(8,128)(2,1)} %param.14) | copy-start | bytes 393220
  33.2 10.1 %collective-permute-start.11 = (bf16[2,128,128]{2,1,0:T(8,128)(2,1)S(1)}, bf16[2,128,128]{2,1,0:T(8,128)(2,1)S(1)}, u32[]{:S(2)}, u32[]{:S(2)}) collective-permute-start(bf16[2,128,128]{2,1,0:T(8,128)(2,1)S(1)} %get-tuple-element.51), channel_id=1, source_target_pairs={{0,3},{1,0},{2,1},{3,2},{4,7},{5,4},{6,5},{7,6},{8,11},{9,8},{10,9... | collective-permute-start | bytes 196616 | tf_op jit(solution)/shard_map/ppermute | solution.py:120
  36.1 1.7 %collective-permute-start.12 = (bf16[4,128,128]{2,1,0:T(8,128)(2,1)S(1)}, bf16[4,128,128]{2,1,0:T(8,128)(2,1)S(1)}, u32[]{:S(2)}, u32[]{:S(2)}) collective-permute-start(bf16[4,128,128]{2,1,0:T(8,128)(2,1)S(1)} %dynamic-slice_bitcast_fusion.1), channel_id=1, source_target_pairs={{0,4},{4,0},{8,12},{12,8},{16,20},{20,16},{24,28},{28,24},{1,5},{5... | collective-permute-start | bytes 393224 | tf_op jit(solution)/shard_map/ppermute | solution.py:304
  36.5 8.9 %collective-permute-start.17 = (bf16[4,64,512]{2,1,0:T(8,128)(2,1)S(1)}, bf16[4,64,512]{2,1,0:T(8,128)(2,1)S(1)}, u32[]{:S(2)}, u32[]{:S(2)}) collective-permute-start(bf16[4,64,512]{2,1,0:T(8,128)(2,1)S(1)} %dynamic-slice_bitcast_fusion), channel_id=1, source_target_pairs={{0,4},{4,0},{8,12},{12,8},{16,20},{20,16},{24,28},{28,24},{1,5},{5... | collective-permute-start | bytes 786440 | tf_op jit(solution)/shard_map/ppermute | solution.py:304
  37.1 5.3 %copy-start.5 = (bf16[512,512]{1,0:T(8,128)(2,1)S(1)}, bf16[512,512]{1,0:T(8,128)(2,1)}, u32[]{:S(2)}) copy-start(bf16[512,512]{1,0:T(8,128)(2,1)} %weight_ref.1) | copy-start | bytes 1572868
  37.8 6.2 %collective-permute-start.13 = (bf16[128,128]{1,0:T(8,128)(2,1)S(1)}, bf16[128,128]{1,0:T(8,128)(2,1)S(1)}, u32[]{:S(2)}, u32[]{:S(2)}) collective-permute-start(bf16[128,128]{1,0:T(8,128)(2,1)S(1)} %get-tuple-element.61), channel_id=1, source_target_pairs={{0,8},{4,12},{8,16},{12,20},{16,24},{20,28},{24,0},{28,4},{1,9},{5... | collective-permute-start | bytes 98312 | tf_op jit(solution)/shard_map/ppermute | solution.py:309
  39.4 4.6 %collective-permute-start.15 = (bf16[128,128]{1,0:T(8,128)(2,1)S(1)}, bf16[128,128]{1,0:T(8,128)(2,1)S(1)}, u32[]{:S(2)}, u32[]{:S(2)}) collective-permute-start(bf16[128,128]{1,0:T(8,128)(2,1)S(1)} %get-tuple-element.62), channel_id=1, source_target_pairs={{0,24},{4,28},{8,0},{12,4},{16,8},{20,12},{24,16},{28,20},{1,25},{... | collective-permute-start | bytes 98312 | tf_op jit(solution)/shard_map/ppermute | solution.py:309
  40.8 3.9 %collective-permute-start.14 = (bf16[128,128]{1,0:T(8,128)(2,1)S(1)}, bf16[128,128]{1,0:T(8,128)(2,1)S(1)}, u32[]{:S(2)}, u32[]{:S(2)}) collective-permute-start(bf16[128,128]{1,0:T(8,128)(2,1)S(1)} %get-tuple-element.63), channel_id=1, source_target_pairs={{0,16},{4,20},{8,24},{12,28},{16,0},{20,4},{24,8},{28,12},{1,17},{... | collective-permute-start | bytes 98312 | tf_op jit(solution)/shard_map/ppermute | solution.py:309
  44.8 8.5 %collective-permute-start.16 = (bf16[128,128]{1,0:T(8,128)(2,1)S(1)}, bf16[128,128]{1,0:T(8,128)(2,1)S(1)}, u32[]{:S(2)}, u32[]{:S(2)}) collective-permute-start(bf16[128,128]{1,0:T(8,128)(2,1)S(1)} %fusion.9), channel_id=1, source_target_pairs={{0,0},{1,8},{2,16},{3,24},{4,4},{5,12},{6,20},{7,28},{8,1},{9,9},{... | collective-permute-start | bytes 98312 | tf_op jit(solution)/shard_map/ppermute | solution.py:324
  45.6 8.5 %collective-permute-start.18 = (bf16[64,512]{1,0:T(8,128)(2,1)S(1)}, bf16[64,512]{1,0:T(8,128)(2,1)S(1)}, u32[]{:S(2)}, u32[]{:S(2)}) collective-permute-start(bf16[64,512]{1,0:T(8,128)(2,1)S(1)} %get-tuple-element.58), channel_id=1, source_target_pairs={{0,8},{4,12},{8,16},{12,20},{16,24},{20,28},{24,0},{28,4},{1,9},{5... | collective-permute-start | bytes 196616 | tf_op jit(solution)/shard_map/ppermute | solution.py:309
  49.3 5.5 %collective-permute-start.20 = (bf16[64,512]{1,0:T(8,128)(2,1)S(1)}, bf16[64,512]{1,0:T(8,128)(2,1)S(1)}, u32[]{:S(2)}, u32[]{:S(2)}) collective-permute-start(bf16[64,512]{1,0:T(8,128)(2,1)S(1)} %get-tuple-element.59), channel_id=1, source_target_pairs={{0,24},{4,28},{8,0},{12,4},{16,8},{20,12},{24,16},{28,20},{1,25},{... | collective-permute-start | bytes 196616 | tf_op jit(solution)/shard_map/ppermute | solution.py:309
  49.9 5.6 %collective-permute-start.19 = (bf16[64,512]{1,0:T(8,128)(2,1)S(1)}, bf16[64,512]{1,0:T(8,128)(2,1)S(1)}, u32[]{:S(2)}, u32[]{:S(2)}) collective-permute-start(bf16[64,512]{1,0:T(8,128)(2,1)S(1)} %get-tuple-element.60), channel_id=1, source_target_pairs={{0,16},{4,20},{8,24},{12,28},{16,0},{20,4},{24,8},{28,12},{1,17},{... | collective-permute-start | bytes 196616 | tf_op jit(solution)/shard_map/ppermute | solution.py:309
  55.8 4.7 %collective-permute-start.22 = (bf16[64,128]{1,0:T(8,128)(2,1)S(1)}, bf16[64,128]{1,0:T(8,128)(2,1)S(1)}, u32[]{:S(2)}, u32[]{:S(2)}) collective-permute-start(bf16[64,128]{1,0:T(8,128)(2,1)S(1)} %bitcast.79), channel_id=1, source_target_pairs={{0,2},{1,3},{2,0},{3,1},{4,6},{5,7},{6,4},{7,5},{8,10},{9,11},{10,... | collective-permute-start | bytes 49160 | tf_op jit(solution)/shard_map/ppermute | solution.py:332
  58.2 3.7 %collective-permute-start.23 = (bf16[64,128]{1,0:T(8,128)(2,1)S(1)}, bf16[64,128]{1,0:T(8,128)(2,1)S(1)}, u32[]{:S(2)}, u32[]{:S(2)}) collective-permute-start(bf16[64,128]{1,0:T(8,128)(2,1)S(1)} %bitcast.78), channel_id=1, source_target_pairs={{0,3},{1,0},{2,1},{3,2},{4,7},{5,4},{6,5},{7,6},{8,11},{9,8},{10,9... | collective-permute-start | bytes 49160 | tf_op jit(solution)/shard_map/ppermute | solution.py:332
  59.2 5.5 %collective-permute-start.21 = (bf16[64,128]{1,0:T(8,128)(2,1)S(1)}, bf16[64,128]{1,0:T(8,128)(2,1)S(1)}, u32[]{:S(2)}, u32[]{:S(2)}) collective-permute-start(bf16[64,128]{1,0:T(8,128)(2,1)S(1)} %bitcast.77), channel_id=1, source_target_pairs={{0,1},{1,2},{2,3},{3,0},{4,5},{5,6},{6,7},{7,4},{8,9},{9,10},{10,1... | collective-permute-start | bytes 49160 | tf_op jit(solution)/shard_map/ppermute | solution.py:332

commit v2 on v1

v2 whole, which is shorter than its diff:
```python
import functools
import math

import jax
import jax.numpy as jnp
import ml_dtypes
import numpy as np
from jax import lax
from jax.experimental import pallas as pl
from jax.experimental.pallas import tpu as pltpu
from jax.sharding import PartitionSpec as P

F32 = jnp.float32
BF16 = jnp.bfloat16


def split_table(table):
    high = table.astype(ml_dtypes.bfloat16)
    low = (table - high.astype(np.float64)).astype(ml_dtypes.bfloat16)
    return jnp.asarray(high), jnp.asarray(low)


@functools.lru_cache(maxsize=None)
def table_values(block):
    period = 2 * block
    bins = np.arange(block)
    radians = (bins[:, None] * bins[None, :] % period) * (2.0 * math.pi / period)
    cosines, sines = np.cos(radians), -np.sin(radians)
    sines[0] = np.where(bins % 2 == 0, 1.0, -1.0)
    forward = np.concatenate([cosines, sines], axis=0)
    weights = np.full((period,), 2.0 / period)
    weights[0] = weights[block] = 1.0 / period
    return forward, forward.T * weights[None, :]


def mxu(left, right):
    return jnp.dot(left, right, preferred_element_type=F32)


def beside(stream, block):
    return jnp.concatenate(
        [stream[i : i + block] for i in range(0, stream.shape[0], block)], axis=1
    )


def to_spectra(high, low, stream):
    blocks = beside(stream, high.shape[1])
    return mxu(high[...], blocks) + mxu(low[...], blocks)


def from_spectra(high, spectra):
    return mxu(high[...], spectra.astype(BF16))


def parity(shape):
    row = lax.broadcasted_iota(jnp.int32, shape, 0)
    return jnp.where(row % 2 == 0, 1.0, -1.0)


def with_previous(spectra, cols):
    sign = parity((spectra.shape[0], cols))
    out = [spectra[:, :cols]]
    for i in range(cols, spectra.shape[1], cols):
        out.append(spectra[:, i : i + cols] + sign * spectra[:, i - cols : i])
    return jnp.concatenate(out, axis=1)


def sum_of_products(terms, conj_left):
    half = terms[0][0].shape[0] // 2
    border = lax.broadcasted_iota(jnp.int32, (half, terms[0][0].shape[1]), 0) == 0
    straight = cross = imag = 0.0
    for left, right in terms:
        left_re, left_im, right_re, right_im = left[:half], left[half:], right[:half], right[half:]
        straight += left_re * right_re
        cross += left_im * right_im
        if conj_left:
            imag += left_re * right_im - left_im * right_re
        else:
            imag += left_re * right_im + left_im * right_re
    inner = jnp.where(border, 0.0, cross)
    real = straight + inner if conj_left else straight - inner
    return jnp.concatenate([real, jnp.where(border, cross, imag)], axis=0)


def columns(ref, index, cols):
    return ref[:, index * cols : (index + 1) * cols]


def causal_product(filt, spectra, cols):
    count = spectra.shape[1] // cols
    out = []
    for i in range(count):
        terms = [(columns(filt, i - a, cols), columns(spectra, a, cols)) for a in range(i + 1)]
        out.append(sum_of_products(terms, False))
    return jnp.concatenate(out, axis=1)


def anti_product(left, spectra, cols):
    count = spectra.shape[1] // cols
    out = []
    for i in range(count):
        terms = [
            (columns(left, a - i, cols), columns(spectra, a, cols)) for a in range(i, count)
        ]
        out.append(sum_of_products(terms, True))
    return jnp.concatenate(out, axis=1)


def pick_columns(ref, index, width, count):
    if width % 128 == 0:
        return ref[:, pl.ds(pl.multiple_of(index * width, width), width)]
    whole = ref[...]
    out = whole[:, :width]
    for other in range(1, count):
        out = jnp.where(index == other, whole[:, other * width : (other + 1) * width], out)
    return out


def put_columns(ref, index, width, count, block):
    if width % 128 == 0:
        ref[:, pl.ds(pl.multiple_of(index * width, width), width)] = block
        return
    for other in range(count):

        @pl.when(index == other)
        def _():
            ref[:, other * width : (other + 1) * width] = block


def pick_rows(ref, index, rows):
    return ref[pl.ds(pl.multiple_of(index * rows, rows), rows), :]


def put_rows(ref, index, rows, block):
    ref[pl.ds(pl.multiple_of(index * rows, rows), rows), :] = block


def call(kernel, outs, args, scratch=(), flops=0, limit=16, anywhere=False):
    vmem = pl.BlockSpec(memory_space=pltpu.VMEM)
    source = pl.BlockSpec(memory_space=pl.ANY) if anywhere else vmem
    total = sum(math.prod(a.shape) * a.dtype.itemsize for a in args)
    return pl.pallas_call(
        kernel,
        out_shape=[jax.ShapeDtypeStruct(shape, dtype) for shape, dtype in outs],
        in_specs=[source] * len(args),
        out_specs=[vmem] * len(outs),
        scratch_shapes=list(scratch),
        compiler_params=pltpu.CompilerParams(vmem_limit_bytes=limit * 2**20),
        cost_estimate=pl.CostEstimate(flops=flops, bytes_accessed=total, transcendentals=0),
    )(*args)


def on_device(value, gate_one, gate_two, filters, out_weight, grad_out):
    rows, width = value.shape[1:]
    seq = lax.axis_size("ctx")
    data = lax.axis_size("dp")
    length = rows * seq
    cols = width // seq
    block = math.gcd(length, 256)
    per_ctx = data // seq
    fine = cols // per_ctx
    chips = data // 2
    own_rows = width // data
    fast = cols == 128 and per_ctx == 2 and rows % (width // cols) == 0
    limit = 16 if length <= 512 else 48
    forward, inverse = table_values(block)
    (fwd_high, fwd_low), (inv_high, _) = split_table(forward), split_table(inverse)
    spectra_shape = (2 * block, length // block * cols)
    table_flops = 4 * block * length * cols

    def ahead(step):
        return lax.rem(lax.axis_index("ctx") + step, seq)

    def behind(step):
        return lax.rem(lax.axis_index("ctx") + seq - step, seq)

    def around(blocks):
        out = [blocks[0]]
        for step in range(1, seq):
            pairs = [(i, (i + step) % seq) for i in range(seq)]
            out.append(lax.ppermute(blocks[step], "ctx", pairs))
        return out

    def load_kernel(value_ref, gate_ref, *refs):
        sources, refs = refs[:3], refs[3:]
        outs, copies, (whole, sems) = refs[:seq], refs[seq : seq + 3], refs[seq + 3 :]
        started = []
        if cols % 128 == 0:
            for step, out in enumerate(outs):
                lanes = pl.ds(pl.multiple_of(ahead(step) * cols, cols), cols)
                started.append((value_ref.at[0, :, lanes], out.at[0]))
                started.append((gate_ref.at[0, :, lanes], out.at[1]))
        else:
            started.append((value_ref.at[0], whole.at[0]))
            started.append((gate_ref.at[0], whole.at[1]))
        for source, copy in zip(sources, copies):
            started.append((source.at[0] if len(source.shape) == 3 else source, copy))
        started = [
            pltpu.make_async_copy(source, target, sems.at[index])
            for index, (source, target) in enumerate(started)
        ]
        for copy in started:
            copy.start()
        for copy in started:
            copy.wait()
        if cols % 128 != 0:
            for step, out in enumerate(outs):
                for index in range(2):
                    out[index] = pick_columns(whole.at[index], ahead(step), cols, seq)

    pair, single = ((2, rows, cols), BF16), ((rows, cols), BF16)
    wide_bf16, wide_f32 = ((rows, width), BF16), ((rows, width), F32)
    with jax.named_scope("load"):
        *sends, cotangent, weight, gate = call(
            load_kernel,
            [pair] * seq + [wide_bf16, ((width, width), BF16), wide_bf16],
            (value, gate_one, grad_out, out_weight, gate_two),
            scratch=[pltpu.VMEM((2, rows, width), BF16), pltpu.SemaphoreType.DMA((2 * seq + 3,))],
            anywhere=True,
        )
    value_parts = around(sends)

    def grad_kernel(cot_ref, weight_ref, gate_ref, grad_ref, *rest):
        outs, scratch = rest[:-1], rest[-1]
        grad = lax.dot_general(
            cot_ref[...], weight_ref[...], (((1,), (1,)), ((), ())), preferred_element_type=F32
        )
        grad_ref[...] = grad
        scratch[...] = grad * gate_ref[...].astype(F32)
        for step, out in enumerate(outs):
            out[...] = pick_columns(scratch, ahead(step), cols, seq).astype(BF16)

    with jax.named_scope("grad_second"):
        grad_gated, *sends = call(
            grad_kernel,
            [wide_f32] + [single] * seq,
            (cotangent, weight, gate),
            scratch=[pltpu.VMEM((rows, width), F32)],
            flops=2 * rows * width * width,
        )
    grad_parts = around(sends)

    def filter_kernel(filters_ref, high, low, out):
        for index in range(2):
            out[index] = with_previous(to_spectra(high, low, filters_ref[index]), cols)

    with jax.named_scope("filter_spectra"):
        own_filters = lax.dynamic_slice_in_dim(filters, lax.axis_index("ctx") * cols, cols, 2)
        (filter_spectra,) = call(
            filter_kernel,
            [((2, *spectra_shape), F32)],
            (own_filters, fwd_high, fwd_low),
            flops=4 * table_flops,
            limit=limit,
        )

    def forward_kernel(*refs):
        parts, refs = refs[:seq], refs[seq:]
        filt, high, low, back, first_ref, value_spec, mixed_spec = refs[:7]
        outs, (stream, second) = refs[7:-2], refs[-2:]
        for step, part in enumerate(parts):
            put_rows(stream, behind(step), rows, part[0])
        spectra = to_spectra(high, low, stream[...])
        value_spec[...] = with_previous(spectra, cols)
        conv = from_spectra(back, causal_product(filt[0], spectra, cols))
        for i in range(length // block):
            first_ref[i * block : (i + 1) * block] = columns(conv, i, cols)
        for step, part in enumerate(parts):
            gated = part[1].astype(F32) * pick_rows(first_ref, behind(step), rows)
            put_rows(stream, behind(step), rows, gated.astype(BF16))
        spectra = to_spectra(high, low, stream[...])
        mixed_spec[...] = with_previous(spectra, cols)
        conv = from_spectra(back, causal_product(filt[1], spectra, cols))
        for i in range(length // block):
            second[i * block : (i + 1) * block] = columns(conv, i, cols)
        for step, out in enumerate(outs):
            out[...] = pick_rows(second, ahead(step), rows).astype(BF16)

    with jax.named_scope("forward_convolutions"):
        first_conv, value_spectra, mixed_spectra, *sends = call(
            forward_kernel,
            [((length, cols), F32), (spectra_shape, F32), (spectra_shape, F32)] + [single] * seq,
            (*value_parts, filter_spectra, fwd_high, fwd_low, inv_high),
            scratch=[pltpu.VMEM((length, cols), BF16), pltpu.VMEM((length, cols), F32)],
            flops=6 * table_flops,
            limit=limit,
        )
    second_parts = around(sends)

    def backward_kernel(*refs):
        parts, values, refs = refs[:seq], refs[seq : 2 * seq], refs[2 * seq :]
        filt, first_ref, value_spec, mixed_spec, high, low, back = refs[:7]
        lags, gate_grad, value_grad, stream, total = refs[7:]
        count = length // block
        for step, part in enumerate(parts):
            put_rows(stream, behind(step), rows, part[...])

        def both(left, other):
            spectra = to_spectra(high, low, stream[...])
            grads = anti_product(left, spectra, cols)
            terms = anti_product(other, spectra, cols)
            return from_spectra(back, jnp.concatenate([grads, terms], axis=1))

        def put_lags(index, out):
            for i in range(count):
                piece = columns(out, count + i, cols)
                lags[index, i * block : (i + 1) * block] = piece

        out = both(filt[1], mixed_spec[...])
        for i in range(count):
            total[i * block : (i + 1) * block] = columns(out, i, cols)
        put_lags(1, out)
        for step, part in enumerate(values):
            grad = pick_rows(total, behind(step), rows)
            put_rows(stream, behind(step), rows, (grad * part[1].astype(F32)).astype(BF16))
        gate_grad[...] = (total[...] * first_ref[...]).astype(BF16)
        out = both(filt[0], value_spec[...])
        for i in range(count):
            value_grad[i * block : (i + 1) * block] = columns(out, i, cols).astype(BF16)
        put_lags(0, out)

    with jax.named_scope("backward_convolutions"):
        lags, gate_grad, value_grad = call(
            backward_kernel,
            [((2, length, cols), F32), ((length, cols), BF16), ((length, cols), BF16)],
            (
                *grad_parts,
                *value_parts,
                filter_spectra,
                first_conv,
                value_spectra,
                mixed_spectra,
                fwd_high,
                fwd_low,
                inv_high,
            ),
            scratch=[pltpu.VMEM((length, cols), BF16), pltpu.VMEM((length, cols), F32)],
            flops=8 * table_flops,
            limit=limit,
        )

    core = lax.rem(lax.axis_index("dp"), 2)
    chip = lax.div(lax.axis_index("dp"), 2)
    lag_rows = rows * cols // width if fast else 0
    term_shape = (chips, own_rows + lag_rows, width)

    def gated_kernel(*refs):
        parts, refs = refs[:seq], refs[seq:]
        gate_ref, cot_ref, lags, second_ref, gated_ref = refs[:5]
        for step, part in enumerate(parts):
            put_columns(second_ref, behind(step), cols, seq, part[...])
        gated = (gate_ref[...].astype(F32) * second_ref[...].astype(F32)).astype(BF16)
        gated_ref[...] = gated
        partial = lax.dot_general(
            gated, cot_ref[...], (((0,), (0,)), ((), ())), preferred_element_type=F32
        )
        if not fast:
            refs[5][...] = partial
            return
        kept, given, whole, packed = refs[5:]
        whole[...] = partial
        lower = lax.broadcasted_iota(jnp.int32, (length, cols), 1) < fine
        packed[0] = jnp.where(lower, lags[0], pltpu.roll(lags[1], fine, axis=1))
        packed[1] = jnp.where(lower, pltpu.roll(lags[0], fine, axis=1), lags[1])
        own_core = lax.rem(lax.axis_index("dp"), 2)
        for out, which in ((kept, own_core), (given, 1 - own_core)):
            for index in range(chips):
                start = pl.multiple_of((2 * index + which) * own_rows, own_rows)
                out[index, :own_rows] = whole[pl.ds(start, own_rows), :].astype(out.dtype)
                for part in range(width // cols):
                    first = index * rows + part * lag_rows
                    out[index, own_rows:, part * cols : (part + 1) * cols] = packed[
                        which, first : first + lag_rows
                    ].astype(out.dtype)

    with jax.named_scope("weight_partial"):
        second_conv, gated, *terms = call(
            gated_kernel,
            [wide_bf16, wide_bf16]
            + ([(term_shape, F32), (term_shape, BF16)] if fast else [((width, width), F32)]),
            (*second_parts, gate, cotangent, lags),
            scratch=[pltpu.VMEM((width, width), F32), pltpu.VMEM((2, length, cols), F32)]
            if fast
            else [],
            flops=2 * rows * width * width,
            limit=limit,
        )

    if not fast:
        lag_terms = lags.reshape(2, seq, rows, per_ctx, fine).transpose(1, 3, 2, 0, 4)
        terms = jnp.concatenate(
            [
                terms[0].reshape(data, own_rows, width),
                lag_terms.reshape(data, rows * 2 * fine // width, width),
            ],
            axis=1,
        )
        by_core = terms.reshape(chips, 2, *terms.shape[1:])
        kept = lax.dynamic_index_in_dim(by_core, core, 1, keepdims=False)
        given = lax.dynamic_index_in_dim(by_core, 1 - core, 1, keepdims=False).astype(BF16)
        lag_rows = rows * 2 * fine // width
    else:
        kept, given = terms
    taken = lax.ppermute(given, "dp", [(i, i ^ 1) for i in range(data)])

    def chip_kernel(kept_ref, taken_ref, own, *outs):
        place = lax.div(lax.axis_index("dp"), 2)
        own[...] = kept_ref[place] + taken_ref[place].astype(F32)
        for step, out in enumerate(outs, 1):
            there = lax.rem(place + step, chips)
            out[...] = (kept_ref[there] + taken_ref[there].astype(F32)).astype(BF16)

    term = (own_rows + lag_rows, width)
    with jax.named_scope("core_sum"):
        own_term, *sends = call(
            chip_kernel,
            [(term, F32)] + [(term, BF16)] * (chips - 1),
            (kept, taken),
            limit=limit,
        )
    chip_terms = []
    for step, block_out in enumerate(sends, 1):
        pairs = [(i, (i + 2 * step) % data) for i in range(data)]
        chip_terms.append(lax.ppermute(block_out, "dp", pairs))

    def mixed_kernel(*refs):
        gated_ref, weight_ref, grad_ref, second_ref, gate_grad, value_grad, _ = refs[:7]
        mixed_ref, gate_ref, outs = refs[7], refs[8], refs[9:]
        mixed_ref[...] = mxu(gated_ref[...], weight_ref[...]).astype(BF16)
        gate_ref[...] = (grad_ref[...] * second_ref[...].astype(F32)).astype(BF16)
        for step, out in enumerate(outs):
            out[0] = pick_rows(gate_grad, ahead(step), rows)
            out[1] = pick_rows(value_grad, ahead(step), rows)

    with jax.named_scope("mixed"):
        mixed, grad_gate_two, *sends = call(
            mixed_kernel,
            [wide_bf16, wide_bf16] + [pair] * seq,
            (gated, weight, grad_gated, second_conv, gate_grad, value_grad, own_term),
            flops=2 * rows * width * width,
            limit=limit,
        )
    result_parts = around(sends)

    if fast:

        def place_kernel(own, *refs):
            arrived, outs, lag, total = refs[: chips - 1], refs[chips - 1 : -2], refs[-2], refs[-1]
            summed = own[...]
            for part in arrived:
                summed = summed + part[...].astype(F32)
            total[...] = summed[:own_rows]
            for step, out in enumerate(outs):
                out[...] = pick_columns(total, ahead(step), cols, seq).astype(out.dtype)
            for part in range(width // cols):
                piece = summed[own_rows:, part * cols : (part + 1) * cols]
                lag[part * lag_rows : (part + 1) * lag_rows] = piece.astype(BF16)

        small = (own_rows, cols)
        with jax.named_scope("chip_sum"):
            *sends, lag_sum = call(
                place_kernel,
                [(small, F32)] + [(small, BF16)] * (seq - 1) + [((rows, 2 * fine), BF16)],
                (own_term, *chip_terms),
                scratch=[pltpu.VMEM((own_rows, width), F32)],
            )
    else:
        total = own_term
        for part in chip_terms:
            total = total + part.astype(F32)
        weight_blocks = total[:own_rows].reshape(own_rows, seq, cols)
        sends = [
            lax.dynamic_index_in_dim(weight_blocks, ahead(step), 1, keepdims=False)
            for step in range(seq)
        ]
        sends = sends[:1] + [part.astype(BF16) for part in sends[1:]]
        lag_sum = total[own_rows:].reshape(rows, 2 * fine).astype(BF16)
    weight_terms = around(sends)
    pairs = []
    for i in range(data):
        for j in range(seq):
            pairs.append((i * seq + j, (per_ctx * j + i % per_ctx) * seq + i // per_ctx))
    lag_own = lax.ppermute(lag_sum, ("dp", "ctx"), pairs)

    def unpack_kernel(*refs):
        parts, (gate_ref, value_ref) = refs[:seq], refs[seq:]
        for step, part in enumerate(parts):
            put_columns(gate_ref, behind(step), cols, seq, part[0])
            put_columns(value_ref, behind(step), cols, seq, part[1])

    with jax.named_scope("unpack_results"):
        grad_gate_one, grad_value = call(unpack_kernel, [wide_bf16, wide_bf16], result_parts)

    if fast:

        def final_kernel(lag_ref, *refs):
            arrived, (filter_ref, weight_ref) = refs[:seq], refs[seq:]
            lag = lag_ref[...].astype(F32) * (1.0 / data)
            filter_ref[0] = lag[:, :fine]
            filter_ref[1] = pltpu.roll(lag, fine, axis=1)[:, :fine]
            total = arrived[0][...]
            for part in arrived[1:]:
                total = total + part[...].astype(F32)
            weight_ref[...] = total * (1.0 / data)

        with jax.named_scope("means"):
            filter_grad, weight_grad = call(
                final_kernel,
                [((2, rows, fine), F32), ((own_rows, cols), F32)],
                (lag_own, *weight_terms),
            )
    else:
        filter_grad = lag_own.reshape(rows, 2, fine).transpose(1, 0, 2).astype(F32) / data
        weight_grad = sum(part.astype(F32) for part in weight_terms) / data
    return (
        mixed[None],
        grad_value[None],
        grad_gate_one[None],
        grad_gate_two[None],
        filter_grad,
        weight_grad,
    )


def solution(mesh):
    stream = P("dp", "ctx", None)
    return jax.shard_map(
        on_device,
        mesh=mesh,
        in_specs=(stream, stream, stream, P(), P(), stream),
        out_specs=(stream, stream, stream, stream, P(None, "ctx", "dp"), P("dp", "ctx")),
        check_vma=False,
    )
```

time: 65.7 us -> 52.7 us (0.80)
  starting transfers between devices: 37.8 us -> 34.3 us
  waiting for transfers between devices: 6.76 us -> 3.36 us
  Pallas kernels: 10.4 us -> 7.52 us
  other arithmetic: 1.47 us -> 0 us
  matrix products: 0.89 us -> 0 us
    ppermute x12 -> x5, starting transfers between devices: 17.9 us -> 5.23 us  [the longest x3 4.5 us: on_device(): chip_terms.append(lax.ppermute(block_out, 'dp', pairs))]
    ppermute x12 -> x15, starting transfers between devices: 19.9 us -> 29.1 us  [around(): out.append(lax.ppermute(blocks[step], 'ctx', pairs))]
    ppermute x12 -> x5, waiting for transfers between devices: 6.73 us -> 1.72 us  [the longest x1 1.71 us: on_device(): taken = lax.ppermute(given, 'dp', [(i, i ^ 1) for i in range(data)])]
    pallas_call x7 -> x11, Pallas kernels: 10.4 us -> 7.52 us  [call(): pl.pallas_call(kernel, out_shape=[jax.ShapeDtypeStruct(shape, dtype) for...]
    ppermute x12 -> x15, waiting for transfers between devices: 0.03 us -> 1.64 us  [around(): out.append(lax.ppermute(blocks[step], 'ctx', pairs))]
    dot_general x1 -> x0, matrix products: 0.89 us -> none  [mxu(): return jnp.dot(left, right, preferred_element_type=F32)]
    div x1 -> x0, local copies, waits for them, and re-layouts: 0.73 us -> none  [on_device(): lag_own.reshape(rows, 2, fine).transpose(1, 0, 2).astype(F32) / data]
    broadcast_in_dim x1 -> x0, other arithmetic: 0.68 us -> none  [on_device(): grad_gate_two[None]]
  transfers between devices with their start and end apart: 24 -> 20, of which waited for: 6 -> 2; matrix products, arithmetic and copies ran while one was open for 4% -> 0% of each run, Pallas kernels for 16% -> 11%
where the time goes in v2:
time: 52.7 us; the launch traced here: 52.5 us
  starting transfers between devices  34.3 us (65%)
  Pallas kernels  7.52 us (14%)
  local copies, waits for them, and re-layouts  6.49 us (12%)
  waiting for transfers between devices  3.36 us (6%)
  between operations  0.78 us (1%)
    ppermute x15, starting transfers between devices, around(): out.append(lax.ppermute(blocks[step], 'ctx', pairs))  29.1 us
    pallas_call x11, Pallas kernels, call(): pl.pallas_call(kernel, out_shape=[jax.ShapeDtypeStruct(shape, dtype) for...  7.52 us
    unnamed x19, local copies, waits for them, and re-layouts  6.45 us
    ppermute x3, starting transfers between devices, on_device(): chip_terms.append(lax.ppermute(block_out, 'dp', pairs))  4.5 us
    ppermute x1, waiting for transfers between devices, on_device(): taken = lax.ppermute(given, 'dp', [(i, i ^ 1) for i in range(data)])  1.71 us
    ppermute x15, waiting for transfers between devices, around(): out.append(lax.ppermute(blocks[step], 'ctx', pairs))  1.64 us
  transfers between devices with their start and end apart: 20, of which 2 were waited for; matrix products, arithmetic and copies ran while one was open for 0% of the time, Pallas kernels for 11%

profile of v2, /device:TPU:0, one launch (start us, length us, event | category | flops | bytes accessed | tf_op | source)
XLA Modules:
  0.0 52.5 jit_solution(15978660703127254563)
XLA Ops:
  0.6 0.0 copy-start
  0.7 1.1 %copy-done.4 = bf16[512,512]{1,0:T(8,128)(2,1)S(1)} copy-done((bf16[512,512]{1,0:T(8,128)(2,1)S(1)}, bf16[512,512]{1,0:T(8,128)(2,1)}, u32[]{:S(2)}) %copy-start.4) | copy-done | bytes 524312
  1.8 0.9 %copy-done.5 = bf16[1,128,512]{2,1,0:T(8,128)(2,1)S(1)} copy-done((bf16[1,128,512]{2,1,0:T(8,128)(2,1)S(1)}, bf16[1,128,512]{2,1,0:T(8,128)(2,1)}, u32[]{:S(2)}) %copy-start.5) | copy-done | bytes 131096
  2.7 0.9 %copy-done.6 = bf16[1,128,512]{2,1,0:T(8,128)(2,1)S(1)} copy-done((bf16[1,128,512]{2,1,0:T(8,128)(2,1)S(1)}, bf16[1,128,512]{2,1,0:T(8,128)(2,1)}, u32[]{:S(2)}) %copy-start.6) | copy-done | bytes 131096
  3.6 0.9 %copy-done.7 = bf16[1,128,512]{2,1,0:T(8,128)(2,1)S(1)} copy-done((bf16[1,128,512]{2,1,0:T(8,128)(2,1)S(1)}, bf16[1,128,512]{2,1,0:T(8,128)(2,1)}, u32[]{:S(2)}) %copy-start.7) | copy-done | bytes 131096
  4.5 0.9 %copy-done.8 = bf16[1,128,512]{2,1,0:T(8,128)(2,1)S(1)} copy-done((bf16[1,128,512]{2,1,0:T(8,128)(2,1)S(1)}, bf16[1,128,512]{2,1,0:T(8,128)(2,1)}, u32[]{:S(2)}) %copy-start.8) | copy-done | bytes 131096
  5.4 0.5 %load.1 = (bf16[2,128,128]{2,1,0:T(8,128)(2,1)S(1)}, bf16[2,128,128]{2,1,0:T(8,128)(2,1)S(1)}, bf16[2,128,128]{2,1,0:T(8,128)(2,1)S(1)}, bf16[2,128,128]{2,1,0:T...) custom-call(bf16[1,128,512]{2,1,0:T(8,128)(2,1)S(1)} %copy-done.5, ...), custom_call_target="tpu_custom_call" | custom-call | bytes 1048576 | tf_op jit(solution)/shard_map/load/pallas_call | solution.py:142
  5.9 3.1 %collective-permute-start = (bf16[2,128,128]{2,1,0:T(8,128)(2,1)S(1)}, bf16[2,128,128]{2,1,0:T(8,128)(2,1)S(1)}, u32[]{:S(2)}, u32[]{:S(2)}) collective-permute-start(bf16[2,128,128]{2,1,0:T(8,128)(2,1)S(1)} %get-tuple-element.52), channel_id=1, source_target_pairs={{0,1},{1,2},{2,3},{3,0},{4,5},{5,6},{6,7},{7,4},{8,9},{9,10},{10,1... | collective-permute-start | bytes 196616 | tf_op jit(solution)/shard_map/ppermute | solution.py:181
  9.0 2.6 %collective-permute-start.1 = (bf16[2,128,128]{2,1,0:T(8,128)(2,1)S(1)}, bf16[2,128,128]{2,1,0:T(8,128)(2,1)S(1)}, u32[]{:S(2)}, u32[]{:S(2)}) collective-permute-start(bf16[2,128,128]{2,1,0:T(8,128)(2,1)S(1)} %get-tuple-element.53), channel_id=1, source_target_pairs={{0,2},{1,3},{2,0},{3,1},{4,6},{5,7},{6,4},{7,5},{8,10},{9,11},{10,... | collective-permute-start | bytes 196616 | tf_op jit(solution)/shard_map/ppermute | solution.py:181
  11.6 1.3 %collective-permute-start.2 = (bf16[2,128,128]{2,1,0:T(8,128)(2,1)S(1)}, bf16[2,128,128]{2,1,0:T(8,128)(2,1)S(1)}, u32[]{:S(2)}, u32[]{:S(2)}) collective-permute-start(bf16[2,128,128]{2,1,0:T(8,128)(2,1)S(1)} %get-tuple-element.54), channel_id=1, source_target_pairs={{0,3},{1,0},{2,1},{3,2},{4,7},{5,4},{6,5},{7,6},{8,11},{9,8},{10,9... | collective-permute-start | bytes 196616 | tf_op jit(solution)/shard_map/ppermute | solution.py:181
  13.0 0.4 grad_second.1
  13.3 0.7 %collective-permute-start.6 = (bf16[128,128]{1,0:T(8,128)(2,1)S(1)}, bf16[128,128]{1,0:T(8,128)(2,1)S(1)}, u32[]{:S(2)}, u32[]{:S(2)}) collective-permute-start(bf16[128,128]{1,0:T(8,128)(2,1)S(1)} %get-tuple-element.63), channel_id=1, source_target_pairs={{0,1},{1,2},{2,3},{3,0},{4,5},{5,6},{6,7},{7,4},{8,9},{9,10},{10,1... | collective-permute-start | bytes 98312 | tf_op jit(solution)/shard_map/ppermute | solution.py:181
  14.1 0.3 collective-permute-start.7
  14.4 0.9 %copy-done.1 = bf16[512,256]{1,0:T(8,128)(2,1)S(1)} copy-done((bf16[512,256]{1,0:T(8,128)(2,1)S(1)}, bf16[512,256]{1,0:T(8,128)(2,1)}, u32[]{:S(2)}) %copy-start.1) | copy-done | bytes 262168
  15.3 0.1 copy-done.2
  15.4 0.4 filter_spectra.1.refs_4_.refs_8_
  15.9 2.9 %collective-permute-start.8 = (bf16[128,128]{1,0:T(8,128)(2,1)S(1)}, bf16[128,128]{1,0:T(8,128)(2,1)S(1)}, u32[]{:S(2)}, u32[]{:S(2)}) collective-permute-start(bf16[128,128]{1,0:T(8,128)(2,1)S(1)} %get-tuple-element.65), channel_id=1, source_target_pairs={{0,3},{1,0},{2,1},{3,2},{4,7},{5,4},{6,5},{7,6},{8,11},{9,8},{10,9... | collective-permute-start | bytes 98312 | tf_op jit(solution)/shard_map/ppermute | solution.py:181
  18.7 0.0 collective-permute-done.1.refs_2_.refs_6_
  18.8 1.5 %forward_convolutions.1 = (f32[512,128]{1,0:T(8,128)S(1)}, f32[512,256]{1,0:T(8,128)S(1)}, f32[512,256]{1,0:T(8,128)S(1)}, bf16[128,128]{1,0:T(8,128)(2,1)S(1)},...) custom-call(bf16[2,128,128]{2,1,0:T(8,128)(2,1)S(1)} %get-tuple-element.51.refs_0_.refs_4_,, ...), custom_call_target="tpu_custom_call" | custom-call | flops 402653184 | bytes 2097152 | tf_op jit(solution)/shard_map/forward_convolutions/pallas_call | solution.py:142
  20.3 1.0 %collective-permute-start.3 = (bf16[128,128]{1,0:T(8,128)(2,1)S(1)}, bf16[128,128]{1,0:T(8,128)(2,1)S(1)}, u32[]{:S(2)}, u32[]{:S(2)}) collective-permute-start(bf16[128,128]{1,0:T(8,128)(2,1)S(1)} %get-tuple-element.56), channel_id=1, source_target_pairs={{0,1},{1,2},{2,3},{3,0},{4,5},{5,6},{6,7},{7,4},{8,9},{9,10},{10,1... | collective-permute-start | bytes 98312 | tf_op jit(solution)/shard_map/ppermute | solution.py:181
  21.3 1.6 %collective-permute-start.4 = (bf16[128,128]{1,0:T(8,128)(2,1)S(1)}, bf16[128,128]{1,0:T(8,128)(2,1)S(1)}, u32[]{:S(2)}, u32[]{:S(2)}) collective-permute-start(bf16[128,128]{1,0:T(8,128)(2,1)S(1)} %get-tuple-element.57), channel_id=1, source_target_pairs={{0,2},{1,3},{2,0},{3,1},{4,6},{5,7},{6,4},{7,5},{8,10},{9,11},{10,... | collective-permute-start | bytes 98312 | tf_op jit(solution)/shard_map/ppermute | solution.py:181
  22.9 2.4 %collective-permute-start.5 = (bf16[128,128]{1,0:T(8,128)(2,1)S(1)}, bf16[128,128]{1,0:T(8,128)(2,1)S(1)}, u32[]{:S(2)}, u32[]{:S(2)}) collective-permute-start(bf16[128,128]{1,0:T(8,128)(2,1)S(1)} %get-tuple-element.58), channel_id=1, source_target_pairs={{0,3},{1,0},{2,1},{3,2},{4,7},{5,4},{6,5},{7,6},{8,11},{9,8},{10,9... | collective-permute-start | bytes 98312 | tf_op jit(solution)/shard_map/ppermute | solution.py:181
  25.3 1.7 %backward_convolutions.1 = (f32[2,512,128]{2,1,0:T(8,128)S(1)}, bf16[512,128]{1,0:T(8,128)(2,1)S(1)}, bf16[512,128]{1,0:T(8,128)(2,1)S(1)}) custom-call(bf16[128,128]{1,0:T(8,128)(2,1)S(1)} %get-tuple-element.62.refs_0_, bf16[128,128]{1,0:T(8,128)(2,1)S(1)} %collective-permute-done.6.refs_1_, bf16[128,128]{1,0:T(8,128)(2,1)S(1)} %collective-permute-done.7.refs_2_, ...), custom_call_target="tpu_custom_call" | custom-call | flops 536870912 | bytes 3538944 | tf_op jit(solution)/shard_map/backward_convolutions/pallas_call | solution.py:142
  27.0 0.0 collective-permute-done.4.refs_2_
  27.0 0.0 collective-permute-done.5.refs_3_
  27.0 0.6 %weight_partial.1 = (bf16[128,512]{1,0:T(8,128)(2,1)S(1)}, bf16[128,512]{1,0:T(8,128)(2,1)S(1)}, f32[4,96,512]{2,1,0:T(8,128)S(1)}, bf16[4,96,512]{2,1,0:T(8,128)(2,1)S(1)}) custom-call(bf16[128,128]{1,0:T(8,128)(2,1)S(1)} %get-tuple-element.55.refs_0_, bf16[128,128]{1,0:T(8,128)(2,1)S(1)} %collective-permute-done.3.refs_1_, ...), custom_call_target="tpu_custom_call" | custom-call | flops 67108864 | bytes 917504 | tf_op jit(solution)/shard_map/weight_partial/pallas_call | solution.py:142
  27.6 0.1 collective-permute-start.9
  27.7 1.7 %collective-permute-done.9.taken_ref = bf16[4,96,512]{2,1,0:T(8,128)(2,1)S(1)} collective-permute-done((bf16[4,96,512]{2,1,0:T(8,128)(2,1)S(1)}, bf16[4,96,512]{2,1,0:T(8,128)(2,1)S(1)}, u32[]{:S(2)}, u32[]{:S(2)}) %collective-permute-start.9) | collective-permute-done | bytes 393248 | tf_op jit(solution)/shard_map/ppermute | solution.py:404
  29.4 0.1 core_sum.1
  29.5 1.5 %collective-permute-start.13 = (bf16[96,512]{1,0:T(8,128)(2,1)S(1)}, bf16[96,512]{1,0:T(8,128)(2,1)S(1)}, u32[]{:S(2)}, u32[]{:S(2)}) collective-permute-start(bf16[96,512]{1,0:T(8,128)(2,1)S(1)} %get-tuple-element.86), channel_id=1, source_target_pairs={{0,8},{4,12},{8,16},{12,20},{16,24},{20,28},{24,0},{28,4},{1,9},{5... | collective-permute-start | bytes 294920 | tf_op jit(solution)/shard_map/ppermute | solution.py:424
  31.0 1.5 %collective-permute-start.14 = (bf16[96,512]{1,0:T(8,128)(2,1)S(1)}, bf16[96,512]{1,0:T(8,128)(2,1)S(1)}, u32[]{:S(2)}, u32[]{:S(2)}) collective-permute-start(bf16[96,512]{1,0:T(8,128)(2,1)S(1)} %get-tuple-element.87), channel_id=1, source_target_pairs={{0,16},{4,20},{8,24},{12,28},{16,0},{20,4},{24,8},{28,12},{1,17},{... | collective-permute-start | bytes 294920 | tf_op jit(solution)/shard_map/ppermute | solution.py:424
  32.5 1.4 %collective-permute-start.15 = (bf16[96,512]{1,0:T(8,128)(2,1)S(1)}, bf16[96,512]{1,0:T(8,128)(2,1)S(1)}, u32[]{:S(2)}, u32[]{:S(2)}) collective-permute-start(bf16[96,512]{1,0:T(8,128)(2,1)S(1)} %get-tuple-element.88), channel_id=1, source_target_pairs={{0,24},{4,28},{8,0},{12,4},{16,8},{20,12},{24,16},{28,20},{1,25},{... | collective-permute-start | bytes 294920 | tf_op jit(solution)/shard_map/ppermute | solution.py:424
  34.0 0.9 %mixed.1 = (bf16[128,512]{1,0:T(8,128)(2,1)}, bf16[128,512]{1,0:T(8,128)(2,1)}, bf16[2,128,128]{2,1,0:T(8,128)(2,1)S(1)}, bf16[2,128,128]{2,1,0:T(8,128)(2,1)S(1...) custom-call(bf16[128,512]{1,0:T(8,128)(2,1)S(1)} %get-tuple-element.70.refs_0_, ...), custom_call_target="tpu_custom_call" | custom-call | flops 67108864 | bytes 1507328 | tf_op jit(solution)/shard_map/mixed/pallas_call | solution.py:142
  34.9 1.6 %collective-permute-start.10 = (bf16[2,128,128]{2,1,0:T(8,128)(2,1)S(1)}, bf16[2,128,128]{2,1,0:T(8,128)(2,1)S(1)}, u32[]{:S(2)}, u32[]{:S(2)}) collective-permute-start(bf16[2,128,128]{2,1,0:T(8,128)(2,1)S(1)} %get-tuple-element.80), channel_id=1, source_target_pairs={{0,1},{1,2},{2,3},{3,0},{4,5},{5,6},{6,7},{7,4},{8,9},{9,10},{10,1... | collective-permute-start | bytes 196616 | tf_op jit(solution)/shard_map/ppermute | solution.py:181
  36.5 2.9 %collective-permute-start.11 = (bf16[2,128,128]{2,1,0:T(8,128)(2,1)S(1)}, bf16[2,128,128]{2,1,0:T(8,128)(2,1)S(1)}, u32[]{:S(2)}, u32[]{:S(2)}) collective-permute-start(bf16[2,128,128]{2,1,0:T(8,128)(2,1)S(1)} %get-tuple-element.81), channel_id=1, source_target_pairs={{0,2},{1,3},{2,0},{3,1},{4,6},{5,7},{6,4},{7,5},{8,10},{9,11},{10,... | collective-permute-start | bytes 196616 | tf_op jit(solution)/shard_map/ppermute | solution.py:181
  39.4 0.0 collective-permute-done.13.refs_0_
  39.4 0.5 collective-permute-start.12
  39.9 0.0 collective-permute-done.14.refs_1_
  39.9 0.0 collective-permute-done.15.refs_2_
  39.9 0.1 chip_sum.1
  40.0 0.7 %collective-permute-start.16 = (bf16[128,128]{1,0:T(8,128)(2,1)S(1)}, bf16[128,128]{1,0:T(8,128)(2,1)S(1)}, u32[]{:S(2)}, u32[]{:S(2)}) collective-permute-start(bf16[128,128]{1,0:T(8,128)(2,1)S(1)} %get-tuple-element.89), channel_id=1, source_target_pairs={{0,0},{1,8},{2,16},{3,24},{4,4},{5,12},{6,20},{7,28},{8,1},{9,9},{... | collective-permute-start | bytes 98312 | tf_op jit(solution)/shard_map/ppermute | solution.py:483
  40.6 2.9 %collective-permute-start.17 = (bf16[64,128]{1,0:T(8,128)(2,1)S(1)}, bf16[64,128]{1,0:T(8,128)(2,1)S(1)}, u32[]{:S(2)}, u32[]{:S(2)}) collective-permute-start(bf16[64,128]{1,0:T(8,128)(2,1)S(1)} %get-tuple-element.91), channel_id=1, source_target_pairs={{0,1},{1,2},{2,3},{3,0},{4,5},{5,6},{6,7},{7,4},{8,9},{9,10},{10,1... | collective-permute-start | bytes 49160 | tf_op jit(solution)/shard_map/ppermute | solution.py:181
  43.5 3.8 %collective-permute-start.18 = (bf16[64,128]{1,0:T(8,128)(2,1)S(1)}, bf16[64,128]{1,0:T(8,128)(2,1)S(1)}, u32[]{:S(2)}, u32[]{:S(2)}) collective-permute-start(bf16[64,128]{1,0:T(8,128)(2,1)S(1)} %get-tuple-element.92), channel_id=1, source_target_pairs={{0,2},{1,3},{2,0},{3,1},{4,6},{5,7},{6,4},{7,5},{8,10},{9,11},{10,... | collective-permute-start | bytes 49160 | tf_op jit(solution)/shard_map/ppermute | solution.py:181
  47.4 1.4 %collective-permute-start.19 = (bf16[64,128]{1,0:T(8,128)(2,1)S(1)}, bf16[64,128]{1,0:T(8,128)(2,1)S(1)}, u32[]{:S(2)}, u32[]{:S(2)}) collective-permute-start(bf16[64,128]{1,0:T(8,128)(2,1)S(1)} %get-tuple-element.93), channel_id=1, source_target_pairs={{0,3},{1,0},{2,1},{3,2},{4,7},{5,4},{6,5},{7,6},{8,11},{9,8},{10,9... | collective-permute-start | bytes 49160 | tf_op jit(solution)/shard_map/ppermute | solution.py:181
  48.8 0.7 %unpack_results.1 = (bf16[128,512]{1,0:T(8,128)(2,1)}, bf16[128,512]{1,0:T(8,128)(2,1)}) custom-call(bf16[2,128,128]{2,1,0:T(8,128)(2,1)S(1)} %get-tuple-element.79.refs_0_, bf16[2,128,128]{2,1,0:T(8,128)(2,1)S(1)} %collective-permute-done.10.refs_1_, bf16[2,128,128]{2,1,0:T(8,128)(2,1)S(1)} %collective-permute-done.11.refs_2_, ...), custom_call_target="tpu_custom_call" | custom-call | bytes 262144 | tf_op jit(solution)/shard_map/unpack_results/pallas_call | solution.py:142
  49.5 1.6 %collective-permute-done.19.refs_3_ = bf16[64,128]{1,0:T(8,128)(2,1)S(1)} collective-permute-done((bf16[64,128]{1,0:T(8,128)(2,1)S(1)}, bf16[64,128]{1,0:T(8,128)(2,1)S(1)}, u32[]{:S(2)}, u32[]{:S(2)}) %collective-permute-start.19) | collective-permute-done | bytes 16416 | tf_op jit(solution)/shard_map/ppermute | solution.py:181
  51.1 0.6 %means.1 = (f32[2,128,64]{2,1,0:T(8,128)S(1)}, f32[64,128]{1,0:T(8,128)}) custom-call(bf16[128,128]{1,0:T(8,128)(2,1)S(1)} %collective-permute-done.16.lag_ref, f32[64,128]{1,0:T(8,128)S(1)} %get-tuple-element.90.refs_0_, bf16[64,128]{1,0:T(8,128)(2,1)S(1)} %collective-permute-done.17.refs_1_, bf16[64,128]{1,0:T(8,128)(2,1)S(1)} %collective-permute-done.18.refs_2_, ...), custom_call_target="tpu_custom_call" | custom-call | bytes 114688 | tf_op jit(solution)/shard_map/means/pallas_call | solution.py:142
  51.8 0.7 %copy.15 = f32[2,128,64]{1,2,0:T(8,128)} copy(f32[2,128,64]{2,1,0:T(8,128)S(1)} %get-tuple-element.100) | data formatting | bytes 131072
  (23 shorter events, 0.1 us)
Async XLA Ops:
  0.6 13.8 %copy-start = (bf16[2,512,512]{2,1,0:T(8,128)(2,1)S(1)}, bf16[2,512,512]{2,1,0:T(8,128)(2,1)}, u32[]{:S(2)}) copy-start(bf16[2,512,512]{2,1,0:T(8,128)(2,1)} %param.12) | copy-start | bytes 3145732
  0.6 1.1 %copy-start.4 = (bf16[512,512]{1,0:T(8,128)(2,1)S(1)}, bf16[512,512]{1,0:T(8,128)(2,1)}, u32[]{:S(2)}) copy-start(bf16[512,512]{1,0:T(8,128)(2,1)} %refs_1_.1) | copy-start | bytes 1572868
  1.8 0.9 %copy-start.5 = (bf16[1,128,512]{2,1,0:T(8,128)(2,1)S(1)}, bf16[1,128,512]{2,1,0:T(8,128)(2,1)}, u32[]{:S(2)}) copy-start(bf16[1,128,512]{2,1,0:T(8,128)(2,1)} %value_ref.1) | copy-start | bytes 393220
  2.7 0.9 %copy-start.6 = (bf16[1,128,512]{2,1,0:T(8,128)(2,1)S(1)}, bf16[1,128,512]{2,1,0:T(8,128)(2,1)}, u32[]{:S(2)}) copy-start(bf16[1,128,512]{2,1,0:T(8,128)(2,1)} %gate_ref.1) | copy-start | bytes 393220
  3.6 0.9 %copy-start.7 = (bf16[1,128,512]{2,1,0:T(8,128)(2,1)S(1)}, bf16[1,128,512]{2,1,0:T(8,128)(2,1)}, u32[]{:S(2)}) copy-start(bf16[1,128,512]{2,1,0:T(8,128)(2,1)} %refs_0_.1) | copy-start | bytes 393220
  4.5 0.9 %copy-start.8 = (bf16[1,128,512]{2,1,0:T(8,128)(2,1)S(1)}, bf16[1,128,512]{2,1,0:T(8,128)(2,1)}, u32[]{:S(2)}) copy-start(bf16[1,128,512]{2,1,0:T(8,128)(2,1)} %refs_2_.1) | copy-start | bytes 393220
  5.9 9.9 %collective-permute-start = (bf16[2,128,128]{2,1,0:T(8,128)(2,1)S(1)}, bf16[2,128,128]{2,1,0:T(8,128)(2,1)S(1)}, u32[]{:S(2)}, u32[]{:S(2)}) collective-permute-start(bf16[2,128,128]{2,1,0:T(8,128)(2,1)S(1)} %get-tuple-element.52), channel_id=1, source_target_pairs={{0,1},{1,2},{2,3},{3,0},{4,5},{5,6},{6,7},{7,4},{8,9},{9,10},{10,1... | collective-permute-start | bytes 196616 | tf_op jit(solution)/shard_map/ppermute | solution.py:181
  9.0 9.7 %collective-permute-start.1 = (bf16[2,128,128]{2,1,0:T(8,128)(2,1)S(1)}, bf16[2,128,128]{2,1,0:T(8,128)(2,1)S(1)}, u32[]{:S(2)}, u32[]{:S(2)}) collective-permute-start(bf16[2,128,128]{2,1,0:T(8,128)(2,1)S(1)} %get-tuple-element.53), channel_id=1, source_target_pairs={{0,2},{1,3},{2,0},{3,1},{4,6},{5,7},{6,4},{7,5},{8,10},{9,11},{10,... | collective-permute-start | bytes 196616 | tf_op jit(solution)/shard_map/ppermute | solution.py:181
  11.6 7.1 %collective-permute-start.2 = (bf16[2,128,128]{2,1,0:T(8,128)(2,1)S(1)}, bf16[2,128,128]{2,1,0:T(8,128)(2,1)S(1)}, u32[]{:S(2)}, u32[]{:S(2)}) collective-permute-start(bf16[2,128,128]{2,1,0:T(8,128)(2,1)S(1)} %get-tuple-element.54), channel_id=1, source_target_pairs={{0,3},{1,0},{2,1},{3,2},{4,7},{5,4},{6,5},{7,6},{8,11},{9,8},{10,9... | collective-permute-start | bytes 196616 | tf_op jit(solution)/shard_map/ppermute | solution.py:181
  13.3 9.6 %collective-permute-start.6 = (bf16[128,128]{1,0:T(8,128)(2,1)S(1)}, bf16[128,128]{1,0:T(8,128)(2,1)S(1)}, u32[]{:S(2)}, u32[]{:S(2)}) collective-permute-start(bf16[128,128]{1,0:T(8,128)(2,1)S(1)} %get-tuple-element.63), channel_id=1, source_target_pairs={{0,1},{1,2},{2,3},{3,0},{4,5},{5,6},{6,7},{7,4},{8,9},{9,10},{10,1... | collective-permute-start | bytes 98312 | tf_op jit(solution)/shard_map/ppermute | solution.py:181
  14.1 11.2 %collective-permute-start.7 = (bf16[128,128]{1,0:T(8,128)(2,1)S(1)}, bf16[128,128]{1,0:T(8,128)(2,1)S(1)}, u32[]{:S(2)}, u32[]{:S(2)}) collective-permute-start(bf16[128,128]{1,0:T(8,128)(2,1)S(1)} %get-tuple-element.64), channel_id=1, source_target_pairs={{0,2},{1,3},{2,0},{3,1},{4,6},{5,7},{6,4},{7,5},{8,10},{9,11},{10,... | collective-permute-start | bytes 98312 | tf_op jit(solution)/shard_map/ppermute | solution.py:181
  14.4 1.0 %copy-start.1 = (bf16[512,256]{1,0:T(8,128)(2,1)S(1)}, bf16[512,256]{1,0:T(8,128)(2,1)}, u32[]{:S(2)}) copy-start(bf16[512,256]{1,0:T(8,128)(2,1)} %constant.17.clone.low.refs_6_.refs_13_) | copy-start | bytes 786436
  14.4 1.0 %copy-start.2 = (bf16[512,256]{1,0:T(8,128)(2,1)S(1)}, bf16[512,256]{1,0:T(8,128)(2,1)}, u32[]{:S(2)}) copy-start(bf16[512,256]{1,0:T(8,128)(2,1)} %constant.16.clone.high.refs_5_.refs_12_) | copy-start | bytes 786436
  15.4 3.3 %copy-start.3 = (bf16[256,512]{1,0:T(8,128)(2,1)S(1)}, bf16[256,512]{1,0:T(8,128)(2,1)}, u32[]{:S(2)}) copy-start(bf16[256,512]{1,0:T(8,128)(2,1)} %constant.18.clone.refs_7_.refs_14_) | copy-start | bytes 786436
  15.9 9.4 %collective-permute-start.8 = (bf16[128,128]{1,0:T(8,128)(2,1)S(1)}, bf16[128,128]{1,0:T(8,128)(2,1)S(1)}, u32[]{:S(2)}, u32[]{:S(2)}) collective-permute-start(bf16[128,128]{1,0:T(8,128)(2,1)S(1)} %get-tuple-element.65), channel_id=1, source_target_pairs={{0,3},{1,0},{2,1},{3,2},{4,7},{5,4},{6,5},{7,6},{8,11},{9,8},{10,9... | collective-permute-start | bytes 98312 | tf_op jit(solution)/shard_map/ppermute | solution.py:181
  20.3 6.7 %collective-permute-start.3 = (bf16[128,128]{1,0:T(8,128)(2,1)S(1)}, bf16[128,128]{1,0:T(8,128)(2,1)S(1)}, u32[]{:S(2)}, u32[]{:S(2)}) collective-permute-start(bf16[128,128]{1,0:T(8,128)(2,1)S(1)} %get-tuple-element.56), channel_id=1, source_target_pairs={{0,1},{1,2},{2,3},{3,0},{4,5},{5,6},{6,7},{7,4},{8,9},{9,10},{10,1... | collective-permute-start | bytes 98312 | tf_op jit(solution)/shard_map/ppermute | solution.py:181
  21.3 5.7 %collective-permute-start.4 = (bf16[128,128]{1,0:T(8,128)(2,1)S(1)}, bf16[128,128]{1,0:T(8,128)(2,1)S(1)}, u32[]{:S(2)}, u32[]{:S(2)}) collective-permute-start(bf16[128,128]{1,0:T(8,128)(2,1)S(1)} %get-tuple-element.57), channel_id=1, source_target_pairs={{0,2},{1,3},{2,0},{3,1},{4,6},{5,7},{6,4},{7,5},{8,10},{9,11},{10,... | collective-permute-start | bytes 98312 | tf_op jit(solution)/shard_map/ppermute | solution.py:181
  22.9 4.1 %collective-permute-start.5 = (bf16[128,128]{1,0:T(8,128)(2,1)S(1)}, bf16[128,128]{1,0:T(8,128)(2,1)S(1)}, u32[]{:S(2)}, u32[]{:S(2)}) collective-permute-start(bf16[128,128]{1,0:T(8,128)(2,1)S(1)} %get-tuple-element.58), channel_id=1, source_target_pairs={{0,3},{1,0},{2,1},{3,2},{4,7},{5,4},{6,5},{7,6},{8,11},{9,8},{10,9... | collective-permute-start | bytes 98312 | tf_op jit(solution)/shard_map/ppermute | solution.py:181
  27.6 1.8 %collective-permute-start.9 = (bf16[4,96,512]{2,1,0:T(8,128)(2,1)S(1)}, bf16[4,96,512]{2,1,0:T(8,128)(2,1)S(1)}, u32[]{:S(2)}, u32[]{:S(2)}) collective-permute-start(bf16[4,96,512]{2,1,0:T(8,128)(2,1)S(1)} %get-tuple-element.76), channel_id=1, source_target_pairs={{0,4},{4,0},{8,12},{12,8},{16,20},{20,16},{24,28},{28,24},{1,5},{5... | collective-permute-start | bytes 1179656 | tf_op jit(solution)/shard_map/ppermute | solution.py:404
  29.5 9.9 %collective-permute-start.13 = (bf16[96,512]{1,0:T(8,128)(2,1)S(1)}, bf16[96,512]{1,0:T(8,128)(2,1)S(1)}, u32[]{:S(2)}, u32[]{:S(2)}) collective-permute-start(bf16[96,512]{1,0:T(8,128)(2,1)S(1)} %get-tuple-element.86), channel_id=1, source_target_pairs={{0,8},{4,12},{8,16},{12,20},{16,24},{20,28},{24,0},{28,4},{1,9},{5... | collective-permute-start | bytes 294920 | tf_op jit(solution)/shard_map/ppermute | solution.py:424
  31.0 8.9 %collective-permute-start.14 = (bf16[96,512]{1,0:T(8,128)(2,1)S(1)}, bf16[96,512]{1,0:T(8,128)(2,1)S(1)}, u32[]{:S(2)}, u32[]{:S(2)}) collective-permute-start(bf16[96,512]{1,0:T(8,128)(2,1)S(1)} %get-tuple-element.87), channel_id=1, source_target_pairs={{0,16},{4,20},{8,24},{12,28},{16,0},{20,4},{24,8},{28,12},{1,17},{... | collective-permute-start | bytes 294920 | tf_op jit(solution)/shard_map/ppermute | solution.py:424
  32.5 7.4 %collective-permute-start.15 = (bf16[96,512]{1,0:T(8,128)(2,1)S(1)}, bf16[96,512]{1,0:T(8,128)(2,1)S(1)}, u32[]{:S(2)}, u32[]{:S(2)}) collective-permute-start(bf16[96,512]{1,0:T(8,128)(2,1)S(1)} %get-tuple-element.88), channel_id=1, source_target_pairs={{0,24},{4,28},{8,0},{12,4},{16,8},{20,12},{24,16},{28,20},{1,25},{... | collective-permute-start | bytes 294920 | tf_op jit(solution)/shard_map/ppermute | solution.py:424
  34.9 8.7 %collective-permute-start.10 = (bf16[2,128,128]{2,1,0:T(8,128)(2,1)S(1)}, bf16[2,128,128]{2,1,0:T(8,128)(2,1)S(1)}, u32[]{:S(2)}, u32[]{:S(2)}) collective-permute-start(bf16[2,128,128]{2,1,0:T(8,128)(2,1)S(1)} %get-tuple-element.80), channel_id=1, source_target_pairs={{0,1},{1,2},{2,3},{3,0},{4,5},{5,6},{6,7},{7,4},{8,9},{9,10},{10,1... | collective-permute-start | bytes 196616 | tf_op jit(solution)/shard_map/ppermute | solution.py:181
  36.5 10.9 %collective-permute-start.11 = (bf16[2,128,128]{2,1,0:T(8,128)(2,1)S(1)}, bf16[2,128,128]{2,1,0:T(8,128)(2,1)S(1)}, u32[]{:S(2)}, u32[]{:S(2)}) collective-permute-start(bf16[2,128,128]{2,1,0:T(8,128)(2,1)S(1)} %get-tuple-element.81), channel_id=1, source_target_pairs={{0,2},{1,3},{2,0},{3,1},{4,6},{5,7},{6,4},{7,5},{8,10},{9,11},{10,... | collective-permute-start | bytes 196616 | tf_op jit(solution)/shard_map/ppermute | solution.py:181
  39.4 9.3 %collective-permute-start.12 = (bf16[2,128,128]{2,1,0:T(8,128)(2,1)S(1)}, bf16[2,128,128]{2,1,0:T(8,128)(2,1)S(1)}, u32[]{:S(2)}, u32[]{:S(2)}) collective-permute-start(bf16[2,128,128]{2,1,0:T(8,128)(2,1)S(1)} %get-tuple-element.82), channel_id=1, source_target_pairs={{0,3},{1,0},{2,1},{3,2},{4,7},{5,4},{6,5},{7,6},{8,11},{9,8},{10,9... | collective-permute-start | bytes 196616 | tf_op jit(solution)/shard_map/ppermute | solution.py:181
  40.0 11.1 %collective-permute-start.16 = (bf16[128,128]{1,0:T(8,128)(2,1)S(1)}, bf16[128,128]{1,0:T(8,128)(2,1)S(1)}, u32[]{:S(2)}, u32[]{:S(2)}) collective-permute-start(bf16[128,128]{1,0:T(8,128)(2,1)S(1)} %get-tuple-element.89), channel_id=1, source_target_pairs={{0,0},{1,8},{2,16},{3,24},{4,4},{5,12},{6,20},{7,28},{8,1},{9,9},{... | collective-permute-start | bytes 98312 | tf_op jit(solution)/shard_map/ppermute | solution.py:483
  40.6 8.9 %collective-permute-start.17 = (bf16[64,128]{1,0:T(8,128)(2,1)S(1)}, bf16[64,128]{1,0:T(8,128)(2,1)S(1)}, u32[]{:S(2)}, u32[]{:S(2)}) collective-permute-start(bf16[64,128]{1,0:T(8,128)(2,1)S(1)} %get-tuple-element.91), channel_id=1, source_target_pairs={{0,1},{1,2},{2,3},{3,0},{4,5},{5,6},{6,7},{7,4},{8,9},{9,10},{10,1... | collective-permute-start | bytes 49160 | tf_op jit(solution)/shard_map/ppermute | solution.py:181
  43.5 6.0 %collective-permute-start.18 = (bf16[64,128]{1,0:T(8,128)(2,1)S(1)}, bf16[64,128]{1,0:T(8,128)(2,1)S(1)}, u32[]{:S(2)}, u32[]{:S(2)}) collective-permute-start(bf16[64,128]{1,0:T(8,128)(2,1)S(1)} %get-tuple-element.92), channel_id=1, source_target_pairs={{0,2},{1,3},{2,0},{3,1},{4,6},{5,7},{6,4},{7,5},{8,10},{9,11},{10,... | collective-permute-start | bytes 49160 | tf_op jit(solution)/shard_map/ppermute | solution.py:181
  47.4 3.7 %collective-permute-start.19 = (bf16[64,128]{1,0:T(8,128)(2,1)S(1)}, bf16[64,128]{1,0:T(8,128)(2,1)S(1)}, u32[]{:S(2)}, u32[]{:S(2)}) collective-permute-start(bf16[64,128]{1,0:T(8,128)(2,1)S(1)} %get-tuple-element.93), channel_id=1, source_target_pairs={{0,3},{1,0},{2,1},{3,2},{4,7},{5,4},{6,5},{7,6},{8,11},{9,8},{10,9... | collective-permute-start | bytes 49160 | tf_op jit(solution)/shard_map/ppermute | solution.py:181

commit v3 on v2

--- a/solution.py
+++ b/solution.py
@@ -135,9 +135,9 @@
     ref[pl.ds(pl.multiple_of(index * rows, rows), rows), :] = block
 
 
-def call(kernel, outs, args, scratch=(), flops=0, limit=16, anywhere=False):
+def call(kernel, outs, args, scratch=(), flops=0, limit=16, in_hbm=False):
     vmem = pl.BlockSpec(memory_space=pltpu.VMEM)
-    source = pl.BlockSpec(memory_space=pl.ANY) if anywhere else vmem
+    source = pl.BlockSpec(memory_space=pltpu.HBM) if in_hbm else vmem
     total = sum(math.prod(a.shape) * a.dtype.itemsize for a in args)
     return pl.pallas_call(
         kernel,
@@ -161,7 +161,7 @@
     fine = cols // per_ctx
     chips = data // 2
     own_rows = width // data
-    fast = cols == 128 and per_ctx == 2 and rows % (width // cols) == 0
+    fast = cols == 128 and per_ctx == 2 and chips == seq and seq & (seq - 1) == 0
     limit = 16 if length <= 512 else 48
     forward, inverse = table_values(block)
     (fwd_high, fwd_low), (inv_high, _) = split_table(forward), split_table(inverse)
@@ -173,6 +173,9 @@
 
     def behind(step):
         return lax.rem(lax.axis_index("ctx") + seq - step, seq)
+
+    def held(place):
+        return place ^ lax.div(lax.axis_index("dp"), 2) if fast else place
 
     def around(blocks):
         out = [blocks[0]]
@@ -181,71 +184,69 @@
             out.append(lax.ppermute(blocks[step], "ctx", pairs))
         return out
 
-    def load_kernel(value_ref, gate_ref, *refs):
-        sources, refs = refs[:3], refs[3:]
-        outs, copies, (whole, sems) = refs[:seq], refs[seq : seq + 3], refs[seq + 3 :]
-        started = []
+    def load_kernel(*refs):
+        value_ref, gate_ref, cot_arg, weight_arg, gate_arg = refs[:5]
+        outs, refs = refs[5 : 5 + seq], refs[5 + seq :]
+        cot_ref, weight_ref, gate_two_ref, grad_ref, second, whole, sems = refs
+        started = [
+            (cot_arg.at[0], cot_ref),
+            (weight_arg, weight_ref),
+            (gate_arg.at[0], gate_two_ref),
+        ]
         if cols % 128 == 0:
             for step, out in enumerate(outs):
-                lanes = pl.ds(pl.multiple_of(ahead(step) * cols, cols), cols)
-                started.append((value_ref.at[0, :, lanes], out.at[0]))
-                started.append((gate_ref.at[0, :, lanes], out.at[1]))
+                start = pl.multiple_of(held(ahead(step)) * cols, cols)
+                started.append((value_ref.at[0, :, pl.ds(start, cols)], out.at[0]))
+                started.append((gate_ref.at[0, :, pl.ds(start, cols)], out.at[1]))
         else:
             started.append((value_ref.at[0], whole.at[0]))
             started.append((gate_ref.at[0], whole.at[1]))
-        for source, copy in zip(sources, copies):
-            started.append((source.at[0] if len(source.shape) == 3 else source, copy))
         started = [
             pltpu.make_async_copy(source, target, sems.at[index])
             for index, (source, target) in enumerate(started)
         ]
         for copy in started:
             copy.start()
-        for copy in started:
+        for copy in started[:3]:
+            copy.wait()
+        grad = lax.dot_general(
+            cot_ref[...], weight_ref[...], (((1,), (1,)), ((), ())), preferred_element_type=F32
+        )
+        grad_ref[...] = grad
+        second[...] = grad * gate_two_ref[...].astype(F32)
+        for step, out in enumerate(outs):
+            out[2] = pick_columns(second, held(ahead(step)), cols, seq).astype(BF16)
+        for copy in started[3:]:
             copy.wait()
         if cols % 128 != 0:
             for step, out in enumerate(outs):
                 for index in range(2):
-                    out[index] = pick_columns(whole.at[index], ahead(step), cols, seq)
-
-    pair, single = ((2, rows, cols), BF16), ((rows, cols), BF16)
+                    out[index] = pick_columns(whole.at[index], held(ahead(step)), cols, seq)
+
+    triple, pair = [((count, rows, cols), BF16) for count in (3, 2)]
+    single = ((rows, cols), BF16)
     wide_bf16, wide_f32 = ((rows, width), BF16), ((rows, width), F32)
     with jax.named_scope("load"):
-        *sends, cotangent, weight, gate = call(
+        *sends, cotangent, weight, gate, grad_gated = call(
             load_kernel,
-            [pair] * seq + [wide_bf16, ((width, width), BF16), wide_bf16],
+            [triple] * seq + [wide_bf16, ((width, width), BF16), wide_bf16, wide_f32],
             (value, gate_one, grad_out, out_weight, gate_two),
-            scratch=[pltpu.VMEM((2, rows, width), BF16), pltpu.SemaphoreType.DMA((2 * seq + 3,))],
-            anywhere=True,
-        )
-    value_parts = around(sends)
-
-    def grad_kernel(cot_ref, weight_ref, gate_ref, grad_ref, *rest):
-        outs, scratch = rest[:-1], rest[-1]
-        grad = lax.dot_general(
-            cot_ref[...], weight_ref[...], (((1,), (1,)), ((), ())), preferred_element_type=F32
-        )
-        grad_ref[...] = grad
-        scratch[...] = grad * gate_ref[...].astype(F32)
-        for step, out in enumerate(outs):
-            out[...] = pick_columns(scratch, ahead(step), cols, seq).astype(BF16)
-
-    with jax.named_scope("grad_second"):
-        grad_gated, *sends = call(
-            grad_kernel,
-            [wide_f32] + [single] * seq,
-            (cotangent, weight, gate),
-            scratch=[pltpu.VMEM((rows, width), F32)],
+            scratch=[
+                pltpu.VMEM((rows, width), F32),
+                pltpu.VMEM((2, rows, width), BF16),
+                pltpu.SemaphoreType.DMA((2 * seq + 3,)),
+            ],
             flops=2 * rows * width * width,
-        )
-    grad_parts = around(sends)
+            in_hbm=True,
+        )
+    parts_in = around(sends)
 
     def filter_kernel(filters_ref, high, low, out):
         for index in range(2):
             out[index] = with_previous(to_spectra(high, low, filters_ref[index]), cols)
 
     with jax.named_scope("filter_spectra"):
-        own_filters = lax.dynamic_slice_in_dim(filters, lax.axis_index("ctx") * cols, cols, 2)
+        own_filters = lax.dynamic_slice_in_dim(filters, held(lax.axis_index("ctx")) * cols, cols, 2)
         (filter_spectra,) = call(
             filter_kernel,
             [((2, *spectra_shape), F32)],
@@ -280,7 +281,7 @@
         first_conv, value_spectra, mixed_spectra, *sends = call(
             forward_kernel,
             [((length, cols), F32), (spectra_shape, F32), (spectra_shape, F32)] + [single] * seq,
-            (*value_parts, filter_spectra, fwd_high, fwd_low, inv_high),
+            (*parts_in, filter_spectra, fwd_high, fwd_low, inv_high),
             scratch=[pltpu.VMEM((length, cols), BF16), pltpu.VMEM((length, cols), F32)],
             flops=6 * table_flops,
             limit=limit,
@@ -288,12 +289,12 @@
     second_parts = around(sends)
 
     def backward_kernel(*refs):
-        parts, values, refs = refs[:seq], refs[seq : 2 * seq], refs[2 * seq :]
+        parts, refs = refs[:seq], refs[seq:]
         filt, first_ref, value_spec, mixed_spec, high, low, back = refs[:7]
         lags, gate_grad, value_grad, stream, total = refs[7:]
         count = length // block
         for step, part in enumerate(parts):
-            put_rows(stream, behind(step), rows, part[...])
+            put_rows(stream, behind(step), rows, part[2])
 
         def both(left, other):
             spectra = to_spectra(high, low, stream[...])
@@ -310,7 +311,7 @@
         for i in range(count):
             total[i * block : (i + 1) * block] = columns(out, i, cols)
         put_lags(1, out)
-        for step, part in enumerate(values):
+        for step, part in enumerate(parts):
             grad = pick_rows(total, behind(step), rows)
             put_rows(stream, behind(step), rows, (grad * part[1].astype(F32)).astype(BF16))
         gate_grad[...] = (total[...] * first_ref[...]).astype(BF16)
@@ -324,8 +325,7 @@
             backward_kernel,
             [((2, length, cols), F32), ((length, cols), BF16), ((length, cols), BF16)],
             (
-                *grad_parts,
-                *value_parts,
+                *parts_in,
                 filter_spectra,
                 first_conv,
                 value_spectra,
@@ -341,14 +341,13 @@
 
     core = lax.rem(lax.axis_index("dp"), 2)
     chip = lax.div(lax.axis_index("dp"), 2)
-    lag_rows = rows * cols // width if fast else 0
-    term_shape = (chips, own_rows + lag_rows, width)
+    term_shape = (width // 2 + rows, width)
 
     def gated_kernel(*refs):
         parts, refs = refs[:seq], refs[seq:]
         gate_ref, cot_ref, lags, second_ref, gated_ref = refs[:5]
         for step, part in enumerate(parts):
-            put_columns(second_ref, behind(step), cols, seq, part[...])
+            put_columns(second_ref, held(behind(step)), cols, seq, part[...])
         gated = (gate_ref[...].astype(F32) * second_ref[...].astype(F32)).astype(BF16)
         gated_ref[...] = gated
         partial = lax.dot_general(
@@ -366,12 +365,11 @@
         for out, which in ((kept, own_core), (given, 1 - own_core)):
             for index in range(chips):
                 start = pl.multiple_of((2 * index + which) * own_rows, own_rows)
-                out[index, :own_rows] = whole[pl.ds(start, own_rows), :].astype(out.dtype)
-                for part in range(width // cols):
-                    first = index * rows + part * lag_rows
-                    out[index, own_rows:, part * cols : (part + 1) * cols] = packed[
-                        which, first : first + lag_rows
-                    ].astype(out.dtype)
+                piece = whole[pl.ds(start, own_rows), :]
+                out[index * own_rows : (index + 1) * own_rows] = piece.astype(out.dtype)
+            for index in range(seq):
+                piece = packed[which, index * rows : (index + 1) * rows]
+                out[width // 2 :, index * cols : (index + 1) * cols] = piece.astype(out.dtype)
 
     with jax.named_scope("weight_partial"):
         second_conv, gated, *terms = call(
@@ -388,40 +386,55 @@
 
     if not fast:
         lag_terms = lags.reshape(2, seq, rows, per_ctx, fine).transpose(1, 3, 2, 0, 4)
+        lag_rows = rows * 2 * fine // width
         terms = jnp.concatenate(
             [
                 terms[0].reshape(data, own_rows, width),
-                lag_terms.reshape(data, rows * 2 * fine // width, width),
+                lag_terms.reshape(data, lag_rows, width),
             ],
             axis=1,
         )
         by_core = terms.reshape(chips, 2, *terms.shape[1:])
         kept = lax.dynamic_index_in_dim(by_core, core, 1, keepdims=False)
         given = lax.dynamic_index_in_dim(by_core, 1 - core, 1, keepdims=False).astype(BF16)
-        lag_rows = rows * 2 * fine // width
+        given, kept = (a.reshape(-1, width) for a in (given, kept))
     else:
         kept, given = terms
+        lag_rows = 0
     taken = lax.ppermute(given, "dp", [(i, i ^ 1) for i in range(data)])
+    term_rows = own_rows + lag_rows
 
     def chip_kernel(kept_ref, taken_ref, own, *outs):
         place = lax.div(lax.axis_index("dp"), 2)
-        own[...] = kept_ref[place] + taken_ref[place].astype(F32)
-        for step, out in enumerate(outs, 1):
-            there = lax.rem(place + step, chips)
-            out[...] = (kept_ref[there] + taken_ref[there].astype(F32)).astype(BF16)
-
-    term = (own_rows + lag_rows, width)
+
+        def summed(index):
+            start = pl.multiple_of(index * term_rows, term_rows)
+            taken = taken_ref[pl.ds(start, term_rows), :]
+            return kept_ref[pl.ds(start, term_rows), :] + taken.astype(F32)
+
+        own[...] = summed(place)
+        for step in range(1, chips):
+            outs[step - 1][...] = summed(place ^ step).astype(BF16)
+        if fast:
+            outs[-1][...] = (kept_ref[width // 2 :] + taken_ref[width // 2 :].astype(F32)).astype(
+                BF16
+            )
+
+    term = (term_rows, width)
     with jax.named_scope("core_sum"):
         own_term, *sends = call(
             chip_kernel,
-            [(term, F32)] + [(term, BF16)] * (chips - 1),
+            [(term, F32)] + [(term, BF16)] * (chips - 1) + [((rows, width), BF16)] * fast,
             (kept, taken),
             limit=limit,
         )
     chip_terms = []
-    for step, block_out in enumerate(sends, 1):
-        pairs = [(i, (i + 2 * step) % data) for i in range(data)]
-        chip_terms.append(lax.ppermute(block_out, "dp", pairs))
+    for step in range(1, chips):
+        pairs = [(i, i ^ (2 * step)) for i in range(data)]
+        chip_terms.append(lax.ppermute(sends[step - 1], "dp", pairs))
+    if fast:
+        pairs = [(i * seq + j, (i ^ (2 * j)) * seq + j) for i in range(data) for j in range(seq)]
+        lag_term = lax.ppermute(sends[-1], ("dp", "ctx"), pairs)
 
     def mixed_kernel(*refs):
         gated_ref, weight_ref, grad_ref, second_ref, gate_grad, value_grad, _ = refs[:7]
@@ -444,24 +457,22 @@
 
     if fast:
 
-        def place_kernel(own, *refs):
-            arrived, outs, lag, total = refs[: chips - 1], refs[chips - 1 : -2], refs[-2], refs[-1]
+        def place_kernel(own, lag, *refs):
+            arrived, outs, total = refs[: chips - 1], refs[chips - 1 : -1], refs[-1]
             summed = own[...]
             for part in arrived:
                 summed = summed + part[...].astype(F32)
-            total[...] = summed[:own_rows]
+            total[...] = summed
             for step, out in enumerate(outs):
-                out[...] = pick_columns(total, ahead(step), cols, seq).astype(out.dtype)
-            for part in range(width // cols):
-                piece = summed[own_rows:, part * cols : (part + 1) * cols]
-                lag[part * lag_rows : (part + 1) * lag_rows] = piece.astype(BF16)
-
-        small = (own_rows, cols)
+                out[:own_rows] = pick_columns(total, ahead(step), cols, seq).astype(out.dtype)
+                out[own_rows:] = pick_columns(lag, ahead(step), cols, seq).astype(out.dtype)
+
+        small = (own_rows + rows, cols)
         with jax.named_scope("chip_sum"):
-            *sends, lag_sum = call(
+            sends = call(
                 place_kernel,
-                [(small, F32)] + [(small, BF16)] * (seq - 1) + [((rows, 2 * fine), BF16)],
-                (own_term, *chip_terms),
+                [(small, F32)] + [(small, BF16)] * (seq - 1),
+                (own_term, lag_term, *chip_terms),
                 scratch=[pltpu.VMEM((own_rows, width), F32)],
             )
     else:
@@ -475,43 +486,43 @@
         ]
         sends = sends[:1] + [part.astype(BF16) for part in sends[1:]]
         lag_sum = total[own_rows:].reshape(rows, 2 * fine).astype(BF16)
-    weight_terms = around(sends)
-    pairs = []
-    for i in range(data):
-        for j in range(seq):
-            pairs.append((i * seq + j, (per_ctx * j + i % per_ctx) * seq + i // per_ctx))
-    lag_own = lax.ppermute(lag_sum, ("dp", "ctx"), pairs)
+        pairs = []
+        for i in range(data):
+            for j in range(seq):
+                pairs.append((i * seq + j, (per_ctx * j + i % per_ctx) * seq + i // per_ctx))
+        lag_own = lax.ppermute(lag_sum, ("dp", "ctx"), pairs)
+    last_terms = around(sends)
 
     def unpack_kernel(*refs):
         parts, (gate_ref, value_ref) = refs[:seq], refs[seq:]
         for step, part in enumerate(parts):
-            put_columns(gate_ref, behind(step), cols, seq, part[0])
-            put_columns(value_ref, behind(step), cols, seq, part[1])
+            put_columns(gate_ref, held(behind(step)), cols, seq, part[0])
+            put_columns(value_ref, held(behind(step)), cols, seq, part[1])
 
     with jax.named_scope("unpack_results"):
         grad_gate_one, grad_value = call(unpack_kernel, [wide_bf16, wide_bf16], result_parts)
 
     if fast:
 
-        def final_kernel(lag_ref, *refs):
+        def final_kernel(*refs):
             arrived, (filter_ref, weight_ref) = refs[:seq], refs[seq:]
-            lag = lag_ref[...].astype(F32) * (1.0 / data)
-            filter_ref[0] = lag[:, :fine]
-            filter_ref[1] = pltpu.roll(lag, fine, axis=1)[:, :fine]
             total = arrived[0][...]
             for part in arrived[1:]:
                 total = total + part[...].astype(F32)
-            weight_ref[...] = total * (1.0 / data)
+            total = total * (1.0 / data)
+            weight_ref[...] = total[:own_rows]
+            turned = total[own_rows:].T
+            filter_ref[0] = turned[:fine]
+            filter_ref[1] = turned[fine:]
 
         with jax.named_scope("means"):
             filter_grad, weight_grad = call(
-                final_kernel,
-                [((2, rows, fine), F32), ((own_rows, cols), F32)],
-                (lag_own, *weight_terms),
+                final_kernel, [((2, fine, rows), F32), ((own_rows, cols), F32)], last_terms
             )
+        filter_grad = jnp.swapaxes(filter_grad, 1, 2)
     else:
         filter_grad = lag_own.reshape(rows, 2, fine).transpose(1, 0, 2).astype(F32) / data
-        weight_grad = sum(part.astype(F32) for part in weight_terms) / data
+        weight_grad = sum(part.astype(F32) for part in last_terms) / data
     return (
         mixed[None],
         grad_value[None],

time: 52.7 us -> 52.2 us (level)
  waiting for transfers between devices: 3.36 us -> 8.57 us
  starting transfers between devices: 34.3 us -> 29.3 us
  local copies, waits for them, and re-layouts: 6.49 us -> 5.77 us
    ppermute x15 -> x12, waiting for transfers between devices: 1.64 us -> 6.85 us  [around(): out.append(lax.ppermute(blocks[step], 'ctx', pairs))]
    ppermute x15 -> x12, starting transfers between devices: 29.1 us -> 25 us  [around(): out.append(lax.ppermute(blocks[step], 'ctx', pairs))]
    ppermute x4, starting transfers between devices: 5.16 us -> 4.22 us  [the longest x3 3.55 us: on_device(): chip_terms.append(lax.ppermute(sends[step - 1], 'dp', pairs))]
    unnamed x19 -> x18, local copies, waits for them, and re-layouts: 6.45 us -> 5.74 us
    pallas_call x11 -> x10, Pallas kernels: 7.52 us -> 7.56 us  [call(): pl.pallas_call(kernel, out_shape=[jax.ShapeDtypeStruct(shape, dtype) for...]
  transfers between devices with their start and end apart: 20 -> 17, of which waited for: 2 -> 7; matrix products, arithmetic and copies ran while one was open for 0% -> 0% of each run, Pallas kernels for 11% -> 7%
where the time goes in v3:
time: 52.2 us; the launch traced here: 52 us
  starting transfers between devices  29.3 us (56%)
  waiting for transfers between devices  8.57 us (16%)
  Pallas kernels  7.56 us (14%)
  local copies, waits for them, and re-layouts  5.77 us (11%)
  between operations  0.75 us (1%)
    ppermute x12, starting transfers between devices, around(): out.append(lax.ppermute(blocks[step], 'ctx', pairs))  25 us
    pallas_call x10, Pallas kernels, call(): pl.pallas_call(kernel, out_shape=[jax.ShapeDtypeStruct(shape, dtype) for...  7.56 us
    ppermute x12, waiting for transfers between devices, around(): out.append(lax.ppermute(blocks[step], 'ctx', pairs))  6.85 us
    unnamed x18, local copies, waits for them, and re-layouts  5.74 us
    ppermute x3, starting transfers between devices, on_device(): chip_terms.append(lax.ppermute(sends[step - 1], 'dp', pairs))  3.55 us
    ppermute x1, waiting for transfers between devices, on_device(): taken = lax.ppermute(given, 'dp', [(i, i ^ 1) for i in range(data)])  1.71 us
  transfers between devices with their start and end apart: 17, of which 7 were waited for; matrix products, arithmetic and copies ran while one was open for 0% of the time, Pallas kernels for 7%

profile of v3, /device:TPU:0, one launch (start us, length us, event | category | flops | bytes accessed | tf_op | source)
XLA Modules:
  0.0 52.0 jit_solution(5126537060489739507)
XLA Ops:
  0.6 0.0 copy-start
  0.7 1.1 %copy-done.4 = bf16[512,512]{1,0:T(8,128)(2,1)S(1)} copy-done((bf16[512,512]{1,0:T(8,128)(2,1)S(1)}, bf16[512,512]{1,0:T(8,128)(2,1)}, u32[]{:S(2)}) %copy-start.4) | copy-done | bytes 524312
  1.8 0.9 %copy-done.5 = bf16[1,128,512]{2,1,0:T(8,128)(2,1)S(1)} copy-done((bf16[1,128,512]{2,1,0:T(8,128)(2,1)S(1)}, bf16[1,128,512]{2,1,0:T(8,128)(2,1)}, u32[]{:S(2)}) %copy-start.5) | copy-done | bytes 131096
  2.7 0.9 %copy-done.6 = bf16[1,128,512]{2,1,0:T(8,128)(2,1)S(1)} copy-done((bf16[1,128,512]{2,1,0:T(8,128)(2,1)S(1)}, bf16[1,128,512]{2,1,0:T(8,128)(2,1)}, u32[]{:S(2)}) %copy-start.6) | copy-done | bytes 131096
  3.6 0.9 %copy-done.7 = bf16[1,128,512]{2,1,0:T(8,128)(2,1)S(1)} copy-done((bf16[1,128,512]{2,1,0:T(8,128)(2,1)S(1)}, bf16[1,128,512]{2,1,0:T(8,128)(2,1)}, u32[]{:S(2)}) %copy-start.7) | copy-done | bytes 131096
  4.5 0.9 %copy-done.8 = bf16[1,128,512]{2,1,0:T(8,128)(2,1)S(1)} copy-done((bf16[1,128,512]{2,1,0:T(8,128)(2,1)S(1)}, bf16[1,128,512]{2,1,0:T(8,128)(2,1)}, u32[]{:S(2)}) %copy-start.8) | copy-done | bytes 131096
  5.4 0.9 %load.1 = (bf16[3,128,128]{2,1,0:T(8,128)(2,1)S(1)}, bf16[3,128,128]{2,1,0:T(8,128)(2,1)S(1)}, bf16[3,128,128]{2,1,0:T(8,128)(2,1)S(1)}, bf16[3,128,128]{2,1,0:T...) custom-call(bf16[1,128,512]{2,1,0:T(8,128)(2,1)S(1)} %copy-done.5, ...), custom_call_target="tpu_custom_call" | custom-call | flops 67108864 | bytes 1048576 | tf_op jit(solution)/shard_map/load/pallas_call | solution.py:142
  6.3 3.1 %collective-permute-start = (bf16[3,128,128]{2,1,0:T(8,128)(2,1)S(1)}, bf16[3,128,128]{2,1,0:T(8,128)(2,1)S(1)}, u32[]{:S(2)}, u32[]{:S(2)}) collective-permute-start(bf16[3,128,128]{2,1,0:T(8,128)(2,1)S(1)} %get-tuple-element.48), channel_id=1, source_target_pairs={{0,1},{1,2},{2,3},{3,0},{4,5},{5,6},{6,7},{7,4},{8,9},{9,10},{10,1... | collective-permute-start | bytes 294920 | tf_op jit(solution)/shard_map/ppermute | solution.py:184
  9.3 2.6 %collective-permute-start.1 = (bf16[3,128,128]{2,1,0:T(8,128)(2,1)S(1)}, bf16[3,128,128]{2,1,0:T(8,128)(2,1)S(1)}, u32[]{:S(2)}, u32[]{:S(2)}) collective-permute-start(bf16[3,128,128]{2,1,0:T(8,128)(2,1)S(1)} %get-tuple-element.49), channel_id=1, source_target_pairs={{0,2},{1,3},{2,0},{3,1},{4,6},{5,7},{6,4},{7,5},{8,10},{9,11},{10,... | collective-permute-start | bytes 294920 | tf_op jit(solution)/shard_map/ppermute | solution.py:184
  11.9 1.3 %collective-permute-start.2 = (bf16[3,128,128]{2,1,0:T(8,128)(2,1)S(1)}, bf16[3,128,128]{2,1,0:T(8,128)(2,1)S(1)}, u32[]{:S(2)}, u32[]{:S(2)}) collective-permute-start(bf16[3,128,128]{2,1,0:T(8,128)(2,1)S(1)} %get-tuple-element.50), channel_id=1, source_target_pairs={{0,3},{1,0},{2,1},{3,2},{4,7},{5,4},{6,5},{7,6},{8,11},{9,8},{10,9... | collective-permute-start | bytes 294920 | tf_op jit(solution)/shard_map/ppermute | solution.py:184
  13.3 0.9 %copy-done.1 = bf16[512,256]{1,0:T(8,128)(2,1)S(1)} copy-done((bf16[512,256]{1,0:T(8,128)(2,1)S(1)}, bf16[512,256]{1,0:T(8,128)(2,1)}, u32[]{:S(2)}) %copy-start.1) | copy-done | bytes 262168
  14.2 0.1 copy-done.2
  14.3 0.4 filter_spectra.1.refs_4_
  14.8 0.3 collective-permute-done.refs_1_
  15.0 3.5 %collective-permute-done.1.refs_2_ = bf16[3,128,128]{2,1,0:T(8,128)(2,1)S(1)} collective-permute-done((bf16[3,128,128]{2,1,0:T(8,128)(2,1)S(1)}, bf16[3,128,128]{2,1,0:T(8,128)(2,1)S(1)}, u32[]{:S(2)}, u32[]{:S(2)}) %collective-permute-start.1) | collective-permute-done | bytes 98336 | tf_op jit(solution)/shard_map/ppermute | solution.py:184
  18.5 0.0 collective-permute-done.2.refs_3_
  18.6 1.5 %forward_convolutions.1 = (f32[512,128]{1,0:T(8,128)S(1)}, f32[512,256]{1,0:T(8,128)S(1)}, f32[512,256]{1,0:T(8,128)S(1)}, bf16[128,128]{1,0:T(8,128)(2,1)S(1)},...) custom-call(bf16[3,128,128]{2,1,0:T(8,128)(2,1)S(1)} %get-tuple-element.47.refs_0_, ...), custom_call_target="tpu_custom_call" | custom-call | flops 402653184 | bytes 2228224 | tf_op jit(solution)/shard_map/forward_convolutions/pallas_call | solution.py:142
  20.0 2.6 %collective-permute-start.3 = (bf16[128,128]{1,0:T(8,128)(2,1)S(1)}, bf16[128,128]{1,0:T(8,128)(2,1)S(1)}, u32[]{:S(2)}, u32[]{:S(2)}) collective-permute-start(bf16[128,128]{1,0:T(8,128)(2,1)S(1)} %get-tuple-element.52), channel_id=1, source_target_pairs={{0,1},{1,2},{2,3},{3,0},{4,5},{5,6},{6,7},{7,4},{8,9},{9,10},{10,1... | collective-permute-start | bytes 98312 | tf_op jit(solution)/shard_map/ppermute | solution.py:184
  22.7 1.6 %collective-permute-start.4 = (bf16[128,128]{1,0:T(8,128)(2,1)S(1)}, bf16[128,128]{1,0:T(8,128)(2,1)S(1)}, u32[]{:S(2)}, u32[]{:S(2)}) collective-permute-start(bf16[128,128]{1,0:T(8,128)(2,1)S(1)} %get-tuple-element.53), channel_id=1, source_target_pairs={{0,2},{1,3},{2,0},{3,1},{4,6},{5,7},{6,4},{7,5},{8,10},{9,11},{10,... | collective-permute-start | bytes 98312 | tf_op jit(solution)/shard_map/ppermute | solution.py:184
  24.3 0.8 %collective-permute-start.5 = (bf16[128,128]{1,0:T(8,128)(2,1)S(1)}, bf16[128,128]{1,0:T(8,128)(2,1)S(1)}, u32[]{:S(2)}, u32[]{:S(2)}) collective-permute-start(bf16[128,128]{1,0:T(8,128)(2,1)S(1)} %get-tuple-element.54), channel_id=1, source_target_pairs={{0,3},{1,0},{2,1},{3,2},{4,7},{5,4},{6,5},{7,6},{8,11},{9,8},{10,9... | collective-permute-start | bytes 98312 | tf_op jit(solution)/shard_map/ppermute | solution.py:184
  25.1 1.7 %backward_convolutions.1 = (f32[2,512,128]{2,1,0:T(8,128)S(1)}, bf16[512,128]{1,0:T(8,128)(2,1)S(1)}, bf16[512,128]{1,0:T(8,128)(2,1)S(1)}) custom-call(bf16[3,128,128]{2,1,0:T(8,128)(2,1)S(1)} %get-tuple-element.47.refs_0_, bf16[3,128,128]{2,1,0:T(8,128)(2,1)S(1)} %collective-permute-done.refs_1_, bf16[3,128,128]{2,1,0:T(8,128)(2,1)S(1)} %collective-permute-done.1.refs_2_, ...), custom_call_target="tpu_custom_call" | custom-call | flops 536870912 | bytes 3538944 | tf_op jit(solution)/shard_map/backward_convolutions/pallas_call | solution.py:142
  26.8 0.0 collective-permute-done.3.refs_1_
  26.8 0.8 %collective-permute-done.4.refs_2_ = bf16[128,128]{1,0:T(8,128)(2,1)S(1)} collective-permute-done((bf16[128,128]{1,0:T(8,128)(2,1)S(1)}, bf16[128,128]{1,0:T(8,128)(2,1)S(1)}, u32[]{:S(2)}, u32[]{:S(2)}) %collective-permute-start.4) | collective-permute-done | bytes 32800 | tf_op jit(solution)/shard_map/ppermute | solution.py:184
  27.6 0.6 %collective-permute-done.5.refs_3_ = bf16[128,128]{1,0:T(8,128)(2,1)S(1)} collective-permute-done((bf16[128,128]{1,0:T(8,128)(2,1)S(1)}, bf16[128,128]{1,0:T(8,128)(2,1)S(1)}, u32[]{:S(2)}, u32[]{:S(2)}) %collective-permute-start.5) | collective-permute-done | bytes 32800 | tf_op jit(solution)/shard_map/ppermute | solution.py:184
  28.2 0.6 %weight_partial.1 = (bf16[128,512]{1,0:T(8,128)(2,1)S(1)}, bf16[128,512]{1,0:T(8,128)(2,1)S(1)}, f32[384,512]{1,0:T(8,128)S(1)}, bf16[384,512]{1,0:T(8,128)(2,1)S(1)}) custom-call(bf16[128,128]{1,0:T(8,128)(2,1)S(1)} %get-tuple-element.51.refs_0_, bf16[128,128]{1,0:T(8,128)(2,1)S(1)} %collective-permute-done.3.refs_1_, ...), custom_call_target="tpu_custom_call" | custom-call | flops 67108864 | bytes 917504 | tf_op jit(solution)/shard_map/weight_partial/pallas_call | solution.py:142
  28.8 0.1 collective-permute-start.6
  28.9 1.7 %collective-permute-done.6.taken_ref = bf16[384,512]{1,0:T(8,128)(2,1)S(1)} collective-permute-done((bf16[384,512]{1,0:T(8,128)(2,1)S(1)}, bf16[384,512]{1,0:T(8,128)(2,1)S(1)}, u32[]{:S(2)}, u32[]{:S(2)}) %collective-permute-start.6) | collective-permute-done | bytes 393248 | tf_op jit(solution)/shard_map/ppermute | solution.py:404
  30.6 0.1 core_sum.1
  30.6 0.7 %collective-permute-start.10 = (bf16[128,512]{1,0:T(8,128)(2,1)S(1)}, bf16[128,512]{1,0:T(8,128)(2,1)S(1)}, u32[]{:S(2)}, u32[]{:S(2)}) collective-permute-start(bf16[128,512]{1,0:T(8,128)(2,1)S(1)} %get-tuple-element.78), channel_id=1, source_target_pairs={{0,0},{1,9},{2,18},{3,27},{4,4},{5,13},{6,22},{7,31},{8,8},{9,1},{... | collective-permute-start | bytes 393224 | tf_op jit(solution)/shard_map/ppermute | solution.py:437
  31.3 1.6 %collective-permute-start.11 = (bf16[64,512]{1,0:T(8,128)(2,1)S(1)}, bf16[64,512]{1,0:T(8,128)(2,1)S(1)}, u32[]{:S(2)}, u32[]{:S(2)}) collective-permute-start(bf16[64,512]{1,0:T(8,128)(2,1)S(1)} %get-tuple-element.79), channel_id=1, source_target_pairs={{0,8},{4,12},{8,0},{12,4},{16,24},{20,28},{24,16},{28,20},{1,9},{5... | collective-permute-start | bytes 196616 | tf_op jit(solution)/shard_map/ppermute | solution.py:434
  32.9 1.5 %collective-permute-start.12 = (bf16[64,512]{1,0:T(8,128)(2,1)S(1)}, bf16[64,512]{1,0:T(8,128)(2,1)S(1)}, u32[]{:S(2)}, u32[]{:S(2)}) collective-permute-start(bf16[64,512]{1,0:T(8,128)(2,1)S(1)} %get-tuple-element.80), channel_id=1, source_target_pairs={{0,16},{4,20},{8,24},{12,28},{16,0},{20,4},{24,8},{28,12},{1,17},{... | collective-permute-start | bytes 196616 | tf_op jit(solution)/shard_map/ppermute | solution.py:434
  34.4 0.5 collective-permute-start.13
  34.9 0.9 %mixed.1 = (bf16[128,512]{1,0:T(8,128)(2,1)}, bf16[128,512]{1,0:T(8,128)(2,1)}, bf16[2,128,128]{2,1,0:T(8,128)(2,1)S(1)}, bf16[2,128,128]{2,1,0:T(8,128)(2,1)S(1...) custom-call(bf16[128,512]{1,0:T(8,128)(2,1)S(1)} %get-tuple-element.61.refs_0_, ...), custom_call_target="tpu_custom_call" | custom-call | flops 67108864 | bytes 1441792 | tf_op jit(solution)/shard_map/mixed/pallas_call | solution.py:142
  35.8 3.0 %collective-permute-start.7 = (bf16[2,128,128]{2,1,0:T(8,128)(2,1)S(1)}, bf16[2,128,128]{2,1,0:T(8,128)(2,1)S(1)}, u32[]{:S(2)}, u32[]{:S(2)}) collective-permute-start(bf16[2,128,128]{2,1,0:T(8,128)(2,1)S(1)} %get-tuple-element.72), channel_id=1, source_target_pairs={{0,1},{1,2},{2,3},{3,0},{4,5},{5,6},{6,7},{7,4},{8,9},{9,10},{10,1... | collective-permute-start | bytes 196616 | tf_op jit(solution)/shard_map/ppermute | solution.py:184
  38.8 3.8 %collective-permute-start.8 = (bf16[2,128,128]{2,1,0:T(8,128)(2,1)S(1)}, bf16[2,128,128]{2,1,0:T(8,128)(2,1)S(1)}, u32[]{:S(2)}, u32[]{:S(2)}) collective-permute-start(bf16[2,128,128]{2,1,0:T(8,128)(2,1)S(1)} %get-tuple-element.73), channel_id=1, source_target_pairs={{0,2},{1,3},{2,0},{3,1},{4,6},{5,7},{6,4},{7,5},{8,10},{9,11},{10,... | collective-permute-start | bytes 196616 | tf_op jit(solution)/shard_map/ppermute | solution.py:184
  42.6 0.0 collective-permute-done.12.refs_1_
  42.6 1.1 %collective-permute-start.9 = (bf16[2,128,128]{2,1,0:T(8,128)(2,1)S(1)}, bf16[2,128,128]{2,1,0:T(8,128)(2,1)S(1)}, u32[]{:S(2)}, u32[]{:S(2)}) collective-permute-start(bf16[2,128,128]{2,1,0:T(8,128)(2,1)S(1)} %get-tuple-element.74), channel_id=1, source_target_pairs={{0,3},{1,0},{2,1},{3,2},{4,7},{5,4},{6,5},{7,6},{8,11},{9,8},{10,9... | collective-permute-start | bytes 196616 | tf_op jit(solution)/shard_map/ppermute | solution.py:184
  43.8 0.0 collective-permute-done.13.refs_2_
  43.8 0.0 collective-permute-done.10.lag
  43.8 0.1 chip_sum.1
  43.8 1.0 %collective-permute-start.14 = (bf16[192,128]{1,0:T(8,128)(2,1)S(1)}, bf16[192,128]{1,0:T(8,128)(2,1)S(1)}, u32[]{:S(2)}, u32[]{:S(2)}) collective-permute-start(bf16[192,128]{1,0:T(8,128)(2,1)S(1)} %get-tuple-element.83), channel_id=1, source_target_pairs={{0,1},{1,2},{2,3},{3,0},{4,5},{5,6},{6,7},{7,4},{8,9},{9,10},{10,1... | collective-permute-start | bytes 147464 | tf_op jit(solution)/shard_map/ppermute | solution.py:184
  44.8 1.2 %collective-permute-start.15 = (bf16[192,128]{1,0:T(8,128)(2,1)S(1)}, bf16[192,128]{1,0:T(8,128)(2,1)S(1)}, u32[]{:S(2)}, u32[]{:S(2)}) collective-permute-start(bf16[192,128]{1,0:T(8,128)(2,1)S(1)} %get-tuple-element.84), channel_id=1, source_target_pairs={{0,2},{1,3},{2,0},{3,1},{4,6},{5,7},{6,4},{7,5},{8,10},{9,11},{10,... | collective-permute-start | bytes 147464 | tf_op jit(solution)/shard_map/ppermute | solution.py:184
  46.0 2.8 %collective-permute-start.16 = (bf16[192,128]{1,0:T(8,128)(2,1)S(1)}, bf16[192,128]{1,0:T(8,128)(2,1)S(1)}, u32[]{:S(2)}, u32[]{:S(2)}) collective-permute-start(bf16[192,128]{1,0:T(8,128)(2,1)S(1)} %get-tuple-element.85), channel_id=1, source_target_pairs={{0,3},{1,0},{2,1},{3,2},{4,7},{5,4},{6,5},{7,6},{8,11},{9,8},{10,9... | collective-permute-start | bytes 147464 | tf_op jit(solution)/shard_map/ppermute | solution.py:184
  48.8 0.0 collective-permute-done.8.refs_2_
  48.8 0.8 %unpack_results.1 = (bf16[128,512]{1,0:T(8,128)(2,1)}, bf16[128,512]{1,0:T(8,128)(2,1)}) custom-call(bf16[2,128,128]{2,1,0:T(8,128)(2,1)S(1)} %get-tuple-element.71.refs_0_, bf16[2,128,128]{2,1,0:T(8,128)(2,1)S(1)} %collective-permute-done.7.refs_1_, bf16[2,128,128]{2,1,0:T(8,128)(2,1)S(1)} %collective-permute-done.8.refs_2_, ...), custom_call_target="tpu_custom_call" | custom-call | bytes 262144 | tf_op jit(solution)/shard_map/unpack_results/pallas_call | solution.py:142
  49.6 0.3 collective-permute-done.14.refs_1_
  49.9 1.4 %collective-permute-done.15.refs_2_ = bf16[192,128]{1,0:T(8,128)(2,1)S(1)} collective-permute-done((bf16[192,128]{1,0:T(8,128)(2,1)S(1)}, bf16[192,128]{1,0:T(8,128)(2,1)S(1)}, u32[]{:S(2)}, u32[]{:S(2)}) %collective-permute-start.15) | collective-permute-done | bytes 49184 | tf_op jit(solution)/shard_map/ppermute | solution.py:184
  51.2 0.7 %means.1 = (f32[2,64,128]{2,1,0:T(8,128)}, f32[64,128]{1,0:T(8,128)}) custom-call(f32[192,128]{1,0:T(8,128)S(1)} %get-tuple-element.82.refs_0_, bf16[192,128]{1,0:T(8,128)(2,1)S(1)} %collective-permute-done.14.refs_1_, bf16[192,128]{1,0:T(8,128)(2,1)S(1)} %collective-permute-done.15.refs_2_, bf16[192,128]{1,0:T(8,128)(2,1)S(1)} %collective-permute-done.16.refs_3_), custom_call_target="tpu_custom_call" | custom-call | bytes 245760 | tf_op jit(solution)/shard_map/means/pallas_call | solution.py:142
  (15 shorter events, 0.1 us)
Async XLA Ops:
  0.6 12.6 %copy-start = (bf16[2,512,512]{2,1,0:T(8,128)(2,1)S(1)}, bf16[2,512,512]{2,1,0:T(8,128)(2,1)}, u32[]{:S(2)}) copy-start(bf16[2,512,512]{2,1,0:T(8,128)(2,1)} %param.12) | copy-start | bytes 3145732
  0.6 1.1 %copy-start.4 = (bf16[512,512]{1,0:T(8,128)(2,1)S(1)}, bf16[512,512]{1,0:T(8,128)(2,1)}, u32[]{:S(2)}) copy-start(bf16[512,512]{1,0:T(8,128)(2,1)} %refs_3_.1) | copy-start | bytes 1572868
  1.8 0.9 %copy-start.5 = (bf16[1,128,512]{2,1,0:T(8,128)(2,1)S(1)}, bf16[1,128,512]{2,1,0:T(8,128)(2,1)}, u32[]{:S(2)}) copy-start(bf16[1,128,512]{2,1,0:T(8,128)(2,1)} %refs_0_.1) | copy-start | bytes 393220
  2.7 0.9 %copy-start.6 = (bf16[1,128,512]{2,1,0:T(8,128)(2,1)S(1)}, bf16[1,128,512]{2,1,0:T(8,128)(2,1)}, u32[]{:S(2)}) copy-start(bf16[1,128,512]{2,1,0:T(8,128)(2,1)} %refs_1_.1) | copy-start | bytes 393220
  3.6 0.9 %copy-start.7 = (bf16[1,128,512]{2,1,0:T(8,128)(2,1)S(1)}, bf16[1,128,512]{2,1,0:T(8,128)(2,1)}, u32[]{:S(2)}) copy-start(bf16[1,128,512]{2,1,0:T(8,128)(2,1)} %refs_2_.1) | copy-start | bytes 393220
  4.5 0.9 %copy-start.8 = (bf16[1,128,512]{2,1,0:T(8,128)(2,1)S(1)}, bf16[1,128,512]{2,1,0:T(8,128)(2,1)}, u32[]{:S(2)}) copy-start(bf16[1,128,512]{2,1,0:T(8,128)(2,1)} %refs_4_.1) | copy-start | bytes 393220
  6.3 8.8 %collective-permute-start = (bf16[3,128,128]{2,1,0:T(8,128)(2,1)S(1)}, bf16[3,128,128]{2,1,0:T(8,128)(2,1)S(1)}, u32[]{:S(2)}, u32[]{:S(2)}) collective-permute-start(bf16[3,128,128]{2,1,0:T(8,128)(2,1)S(1)} %get-tuple-element.48), channel_id=1, source_target_pairs={{0,1},{1,2},{2,3},{3,0},{4,5},{5,6},{6,7},{7,4},{8,9},{9,10},{10,1... | collective-permute-start | bytes 294920 | tf_op jit(solution)/shard_map/ppermute | solution.py:184
  9.3 9.2 %collective-permute-start.1 = (bf16[3,128,128]{2,1,0:T(8,128)(2,1)S(1)}, bf16[3,128,128]{2,1,0:T(8,128)(2,1)S(1)}, u32[]{:S(2)}, u32[]{:S(2)}) collective-permute-start(bf16[3,128,128]{2,1,0:T(8,128)(2,1)S(1)} %get-tuple-element.49), channel_id=1, source_target_pairs={{0,2},{1,3},{2,0},{3,1},{4,6},{5,7},{6,4},{7,5},{8,10},{9,11},{10,... | collective-permute-start | bytes 294920 | tf_op jit(solution)/shard_map/ppermute | solution.py:184
  11.9 6.6 %collective-permute-start.2 = (bf16[3,128,128]{2,1,0:T(8,128)(2,1)S(1)}, bf16[3,128,128]{2,1,0:T(8,128)(2,1)S(1)}, u32[]{:S(2)}, u32[]{:S(2)}) collective-permute-start(bf16[3,128,128]{2,1,0:T(8,128)(2,1)S(1)} %get-tuple-element.50), channel_id=1, source_target_pairs={{0,3},{1,0},{2,1},{3,2},{4,7},{5,4},{6,5},{7,6},{8,11},{9,8},{10,9... | collective-permute-start | bytes 294920 | tf_op jit(solution)/shard_map/ppermute | solution.py:184
  13.3 1.0 %copy-start.1 = (bf16[512,256]{1,0:T(8,128)(2,1)S(1)}, bf16[512,256]{1,0:T(8,128)(2,1)}, u32[]{:S(2)}) copy-start(bf16[512,256]{1,0:T(8,128)(2,1)} %constant.26.clone.low.refs_6_.refs_9_) | copy-start | bytes 786436
  13.3 1.0 %copy-start.2 = (bf16[512,256]{1,0:T(8,128)(2,1)S(1)}, bf16[512,256]{1,0:T(8,128)(2,1)}, u32[]{:S(2)}) copy-start(bf16[512,256]{1,0:T(8,128)(2,1)} %constant.25.clone.high.refs_5_.refs_8_) | copy-start | bytes 786436
  14.3 4.2 %copy-start.3 = (bf16[256,512]{1,0:T(8,128)(2,1)S(1)}, bf16[256,512]{1,0:T(8,128)(2,1)}, u32[]{:S(2)}) copy-start(bf16[256,512]{1,0:T(8,128)(2,1)} %constant.27.clone.refs_7_.refs_10_) | copy-start | bytes 786436
  20.0 6.7 %collective-permute-start.3 = (bf16[128,128]{1,0:T(8,128)(2,1)S(1)}, bf16[128,128]{1,0:T(8,128)(2,1)S(1)}, u32[]{:S(2)}, u32[]{:S(2)}) collective-permute-start(bf16[128,128]{1,0:T(8,128)(2,1)S(1)} %get-tuple-element.52), channel_id=1, source_target_pairs={{0,1},{1,2},{2,3},{3,0},{4,5},{5,6},{6,7},{7,4},{8,9},{9,10},{10,1... | collective-permute-start | bytes 98312 | tf_op jit(solution)/shard_map/ppermute | solution.py:184
  22.7 4.9 %collective-permute-start.4 = (bf16[128,128]{1,0:T(8,128)(2,1)S(1)}, bf16[128,128]{1,0:T(8,128)(2,1)S(1)}, u32[]{:S(2)}, u32[]{:S(2)}) collective-permute-start(bf16[128,128]{1,0:T(8,128)(2,1)S(1)} %get-tuple-element.53), channel_id=1, source_target_pairs={{0,2},{1,3},{2,0},{3,1},{4,6},{5,7},{6,4},{7,5},{8,10},{9,11},{10,... | collective-permute-start | bytes 98312 | tf_op jit(solution)/shard_map/ppermute | solution.py:184
  24.3 3.9 %collective-permute-start.5 = (bf16[128,128]{1,0:T(8,128)(2,1)S(1)}, bf16[128,128]{1,0:T(8,128)(2,1)S(1)}, u32[]{:S(2)}, u32[]{:S(2)}) collective-permute-start(bf16[128,128]{1,0:T(8,128)(2,1)S(1)} %get-tuple-element.54), channel_id=1, source_target_pairs={{0,3},{1,0},{2,1},{3,2},{4,7},{5,4},{6,5},{7,6},{8,11},{9,8},{10,9... | collective-permute-start | bytes 98312 | tf_op jit(solution)/shard_map/ppermute | solution.py:184
  28.8 1.8 %collective-permute-start.6 = (bf16[384,512]{1,0:T(8,128)(2,1)S(1)}, bf16[384,512]{1,0:T(8,128)(2,1)S(1)}, u32[]{:S(2)}, u32[]{:S(2)}) collective-permute-start(bf16[384,512]{1,0:T(8,128)(2,1)S(1)} %get-tuple-element.68), channel_id=1, source_target_pairs={{0,4},{4,0},{8,12},{12,8},{16,20},{20,16},{24,28},{28,24},{1,5},{5... | collective-permute-start | bytes 1179656 | tf_op jit(solution)/shard_map/ppermute | solution.py:404
  30.6 13.1 %collective-permute-start.10 = (bf16[128,512]{1,0:T(8,128)(2,1)S(1)}, bf16[128,512]{1,0:T(8,128)(2,1)S(1)}, u32[]{:S(2)}, u32[]{:S(2)}) collective-permute-start(bf16[128,512]{1,0:T(8,128)(2,1)S(1)} %get-tuple-element.78), channel_id=1, source_target_pairs={{0,0},{1,9},{2,18},{3,27},{4,4},{5,13},{6,22},{7,31},{8,8},{9,1},{... | collective-permute-start | bytes 393224 | tf_op jit(solution)/shard_map/ppermute | solution.py:437
  31.3 7.5 %collective-permute-start.11 = (bf16[64,512]{1,0:T(8,128)(2,1)S(1)}, bf16[64,512]{1,0:T(8,128)(2,1)S(1)}, u32[]{:S(2)}, u32[]{:S(2)}) collective-permute-start(bf16[64,512]{1,0:T(8,128)(2,1)S(1)} %get-tuple-element.79), channel_id=1, source_target_pairs={{0,8},{4,12},{8,0},{12,4},{16,24},{20,28},{24,16},{28,20},{1,9},{5... | collective-permute-start | bytes 196616 | tf_op jit(solution)/shard_map/ppermute | solution.py:434
  32.9 9.8 %collective-permute-start.12 = (bf16[64,512]{1,0:T(8,128)(2,1)S(1)}, bf16[64,512]{1,0:T(8,128)(2,1)S(1)}, u32[]{:S(2)}, u32[]{:S(2)}) collective-permute-start(bf16[64,512]{1,0:T(8,128)(2,1)S(1)} %get-tuple-element.80), channel_id=1, source_target_pairs={{0,16},{4,20},{8,24},{12,28},{16,0},{20,4},{24,8},{28,12},{1,17},{... | collective-permute-start | bytes 196616 | tf_op jit(solution)/shard_map/ppermute | solution.py:434
  34.4 9.4 %collective-permute-start.13 = (bf16[64,512]{1,0:T(8,128)(2,1)S(1)}, bf16[64,512]{1,0:T(8,128)(2,1)S(1)}, u32[]{:S(2)}, u32[]{:S(2)}) collective-permute-start(bf16[64,512]{1,0:T(8,128)(2,1)S(1)} %get-tuple-element.81), channel_id=1, source_target_pairs={{0,24},{4,28},{8,16},{12,20},{16,8},{20,12},{24,0},{28,4},{1,25},{... | collective-permute-start | bytes 196616 | tf_op jit(solution)/shard_map/ppermute | solution.py:434
  35.8 10.2 %collective-permute-start.7 = (bf16[2,128,128]{2,1,0:T(8,128)(2,1)S(1)}, bf16[2,128,128]{2,1,0:T(8,128)(2,1)S(1)}, u32[]{:S(2)}, u32[]{:S(2)}) collective-permute-start(bf16[2,128,128]{2,1,0:T(8,128)(2,1)S(1)} %get-tuple-element.72), channel_id=1, source_target_pairs={{0,1},{1,2},{2,3},{3,0},{4,5},{5,6},{6,7},{7,4},{8,9},{9,10},{10,1... | collective-permute-start | bytes 196616 | tf_op jit(solution)/shard_map/ppermute | solution.py:184
  38.8 10.0 %collective-permute-start.8 = (bf16[2,128,128]{2,1,0:T(8,128)(2,1)S(1)}, bf16[2,128,128]{2,1,0:T(8,128)(2,1)S(1)}, u32[]{:S(2)}, u32[]{:S(2)}) collective-permute-start(bf16[2,128,128]{2,1,0:T(8,128)(2,1)S(1)} %get-tuple-element.73), channel_id=1, source_target_pairs={{0,2},{1,3},{2,0},{3,1},{4,6},{5,7},{6,4},{7,5},{8,10},{9,11},{10,... | collective-permute-start | bytes 196616 | tf_op jit(solution)/shard_map/ppermute | solution.py:184
  42.6 6.2 %collective-permute-start.9 = (bf16[2,128,128]{2,1,0:T(8,128)(2,1)S(1)}, bf16[2,128,128]{2,1,0:T(8,128)(2,1)S(1)}, u32[]{:S(2)}, u32[]{:S(2)}) collective-permute-start(bf16[2,128,128]{2,1,0:T(8,128)(2,1)S(1)} %get-tuple-element.74), channel_id=1, source_target_pairs={{0,3},{1,0},{2,1},{3,2},{4,7},{5,4},{6,5},{7,6},{8,11},{9,8},{10,9... | collective-permute-start | bytes 196616 | tf_op jit(solution)/shard_map/ppermute | solution.py:184
  43.8 6.0 %collective-permute-start.14 = (bf16[192,128]{1,0:T(8,128)(2,1)S(1)}, bf16[192,128]{1,0:T(8,128)(2,1)S(1)}, u32[]{:S(2)}, u32[]{:S(2)}) collective-permute-start(bf16[192,128]{1,0:T(8,128)(2,1)S(1)} %get-tuple-element.83), channel_id=1, source_target_pairs={{0,1},{1,2},{2,3},{3,0},{4,5},{5,6},{6,7},{7,4},{8,9},{9,10},{10,1... | collective-permute-start | bytes 147464 | tf_op jit(solution)/shard_map/ppermute | solution.py:184
  44.8 6.4 %collective-permute-start.15 = (bf16[192,128]{1,0:T(8,128)(2,1)S(1)}, bf16[192,128]{1,0:T(8,128)(2,1)S(1)}, u32[]{:S(2)}, u32[]{:S(2)}) collective-permute-start(bf16[192,128]{1,0:T(8,128)(2,1)S(1)} %get-tuple-element.84), channel_id=1, source_target_pairs={{0,2},{1,3},{2,0},{3,1},{4,6},{5,7},{6,4},{7,5},{8,10},{9,11},{10,... | collective-permute-start | bytes 147464 | tf_op jit(solution)/shard_map/ppermute | solution.py:184
  46.0 5.3 %collective-permute-start.16 = (bf16[192,128]{1,0:T(8,128)(2,1)S(1)}, bf16[192,128]{1,0:T(8,128)(2,1)S(1)}, u32[]{:S(2)}, u32[]{:S(2)}) collective-permute-start(bf16[192,128]{1,0:T(8,128)(2,1)S(1)} %get-tuple-element.85), channel_id=1, source_target_pairs={{0,3},{1,0},{2,1},{3,2},{4,7},{5,4},{6,5},{7,6},{8,11},{9,8},{10,9... | collective-permute-start | bytes 147464 | tf_op jit(solution)/shard_map/ppermute | solution.py:184

commit v4 on v3

--- a/solution.py
+++ b/solution.py
@@ -145,7 +145,7 @@
         in_specs=[source] * len(args),
         out_specs=[vmem] * len(outs),
         scratch_shapes=list(scratch),
-        compiler_params=pltpu.CompilerParams(vmem_limit_bytes=limit * 2**20),
+        compiler_params=pltpu.CompilerParams(vmem_limit_bytes=int(limit * 2**20)),
         cost_estimate=pl.CostEstimate(flops=flops, bytes_accessed=total, transcendentals=0),
     )(*args)
 
@@ -161,8 +161,9 @@
     fine = cols // per_ctx
     chips = data // 2
     own_rows = width // data
-    fast = cols == 128 and per_ctx == 2 and chips == seq and seq & (seq - 1) == 0
+    fast = cols == 128 and per_ctx == 2 and chips == seq == 4
     limit = 16 if length <= 512 else 48
+    load_limit = 53.5
     forward, inverse = table_values(block)
     (fwd_high, fwd_low), (inv_high, _) = split_table(forward), split_table(inverse)
     spectra_shape = (2 * block, length // block * cols)
@@ -184,10 +185,15 @@
             out.append(lax.ppermute(blocks[step], "ctx", pairs))
         return out
 
+    def grad_gated(cot_ref, weight_ref):
+        return lax.dot_general(
+            cot_ref[...], weight_ref[...], (((1,), (1,)), ((), ())), preferred_element_type=F32
+        )
+
     def load_kernel(*refs):
         value_ref, gate_ref, cot_arg, weight_arg, gate_arg = refs[:5]
         outs, refs = refs[5 : 5 + seq], refs[5 + seq :]
-        cot_ref, weight_ref, gate_two_ref, grad_ref, second, whole, sems = refs
+        cot_ref, weight_ref, gate_two_ref, second, whole, sems = refs
         started = [
             (cot_arg.at[0], cot_ref),
             (weight_arg, weight_ref),
@@ -209,11 +215,7 @@
             copy.start()
         for copy in started[:3]:
             copy.wait()
-        grad = lax.dot_general(
-            cot_ref[...], weight_ref[...], (((1,), (1,)), ((), ())), preferred_element_type=F32
-        )
-        grad_ref[...] = grad
-        second[...] = grad * gate_two_ref[...].astype(F32)
+        second[...] = grad_gated(cot_ref, weight_ref) * gate_two_ref[...].astype(F32)
         for step, out in enumerate(outs):
             out[2] = pick_columns(second, held(ahead(step)), cols, seq).astype(BF16)
         for copy in started[3:]:
@@ -225,19 +227,23 @@
 
     triple, pair = [((count, rows, cols), BF16) for count in (3, 2)]
     single = ((rows, cols), BF16)
-    wide_bf16, wide_f32 = ((rows, width), BF16), ((rows, width), F32)
+    wide_bf16 = ((rows, width), BF16)
     with jax.named_scope("load"):
-        *sends, cotangent, weight, gate, grad_gated = call(
+        sends = call(
             load_kernel,
-            [triple] * seq + [wide_bf16, ((width, width), BF16), wide_bf16, wide_f32],
+            [triple] * seq,
             (value, gate_one, grad_out, out_weight, gate_two),
             scratch=[
+                pltpu.VMEM((rows, width), BF16),
+                pltpu.VMEM((width, width), BF16),
+                pltpu.VMEM((rows, width), BF16),
                 pltpu.VMEM((rows, width), F32),
                 pltpu.VMEM((2, rows, width), BF16),
                 pltpu.SemaphoreType.DMA((2 * seq + 3,)),
             ],
             flops=2 * rows * width * width,
             in_hbm=True,
+            limit=load_limit,
         )
     parts_in = around(sends)
 
@@ -288,10 +294,19 @@
         )
     second_parts = around(sends)
 
+    def put_result(outs, index, total):
+        if not fast:
+            for step, out in enumerate(outs):
+                out[index] = pick_rows(total, ahead(step), rows).astype(BF16)
+            return
+        for far in range(4):
+            place = lax.axis_index("ctx") ^ far
+            outs[far % 2][far // 2 * 2 + index] = pick_rows(total, place, rows).astype(BF16)
+
     def backward_kernel(*refs):
         parts, refs = refs[:seq], refs[seq:]
         filt, first_ref, value_spec, mixed_spec, high, low, back = refs[:7]
-        lags, gate_grad, value_grad, stream, total = refs[7:]
+        lags, *outs, stream, total = refs[7:]
         count = length // block
         for step, part in enumerate(parts):
             put_rows(stream, behind(step), rows, part[2])
@@ -314,16 +329,18 @@
         for step, part in enumerate(parts):
             grad = pick_rows(total, behind(step), rows)
             put_rows(stream, behind(step), rows, (grad * part[1].astype(F32)).astype(BF16))
-        gate_grad[...] = (total[...] * first_ref[...]).astype(BF16)
+        total[...] = total[...] * first_ref[...]
+        put_result(outs, 0, total)
         out = both(filt[0], value_spec[...])
         for i in range(count):
-            value_grad[i * block : (i + 1) * block] = columns(out, i, cols).astype(BF16)
+            total[i * block : (i + 1) * block] = columns(out, i, cols)
+        put_result(outs, 1, total)
         put_lags(0, out)
 
     with jax.named_scope("backward_convolutions"):
-        lags, gate_grad, value_grad = call(
+        lags, *sends_home = call(
             backward_kernel,
-            [((2, length, cols), F32), ((length, cols), BF16), ((length, cols), BF16)],
+            [((2, length, cols), F32)] + ([((4, rows, cols), BF16)] * 2 if fast else [pair] * seq),
             (
                 *parts_in,
                 filter_spectra,
@@ -339,6 +356,9 @@
             limit=limit,
         )
 
+    def home_core(core):
+        return jnp.where(lax.axis_index("ctx") == 0, 1 - core, core)
+
     core = lax.rem(lax.axis_index("dp"), 2)
     chip = lax.div(lax.axis_index("dp"), 2)
     term_shape = (width // 2 + rows, width)
@@ -362,13 +382,14 @@
         packed[0] = jnp.where(lower, lags[0], pltpu.roll(lags[1], fine, axis=1))
         packed[1] = jnp.where(lower, pltpu.roll(lags[0], fine, axis=1), lags[1])
         own_core = lax.rem(lax.axis_index("dp"), 2)
-        for out, which in ((kept, own_core), (given, 1 - own_core)):
+        turn = home_core(own_core)
+        for out, which, lag_which in ((kept, own_core, turn), (given, 1 - own_core, 1 - turn)):
             for index in range(chips):
                 start = pl.multiple_of((2 * index + which) * own_rows, own_rows)
                 piece = whole[pl.ds(start, own_rows), :]
                 out[index * own_rows : (index + 1) * own_rows] = piece.astype(out.dtype)
             for index in range(seq):
-                piece = packed[which, index * rows : (index + 1) * rows]
+                piece = packed[lag_which, index * rows : (index + 1) * rows]
                 out[width // 2 :, index * cols : (index + 1) * cols] = piece.astype(out.dtype)
 
     with jax.named_scope("weight_partial"):
@@ -376,7 +397,7 @@
             gated_kernel,
             [wide_bf16, wide_bf16]
             + ([(term_shape, F32), (term_shape, BF16)] if fast else [((width, width), F32)]),
-            (*second_parts, gate, cotangent, lags),
+            (*second_parts, gate_two[0], grad_out[0], lags),
             scratch=[pltpu.VMEM((width, width), F32), pltpu.VMEM((2, length, cols), F32)]
             if fast
             else [],
@@ -433,31 +454,47 @@
         pairs = [(i, i ^ (2 * step)) for i in range(data)]
         chip_terms.append(lax.ppermute(sends[step - 1], "dp", pairs))
     if fast:
-        pairs = [(i * seq + j, (i ^ (2 * j)) * seq + j) for i in range(data) for j in range(seq)]
+        pairs = []
+        for i in range(data):
+            pairs.append((i * seq, (i ^ 1) * seq))
+            pairs += [(i * seq + j, (i ^ (2 * j)) * seq + j) for j in range(1, seq)]
         lag_term = lax.ppermute(sends[-1], ("dp", "ctx"), pairs)
 
-    def mixed_kernel(*refs):
-        gated_ref, weight_ref, grad_ref, second_ref, gate_grad, value_grad, _ = refs[:7]
-        mixed_ref, gate_ref, outs = refs[7], refs[8], refs[9:]
+    def across(far):
+        return [(i, i ^ far) for i in range(seq)]
+
+    if fast:
+        stays, goes = sends_home
+        near = lax.ppermute(goes, "ctx", across(1))
+
+        def turn_kernel(stays_ref, near_ref, _, out):
+            out[:2] = stays_ref[2:]
+            out[2:] = near_ref[2:]
+
+        with jax.named_scope("turn"):
+            (goes,) = call(turn_kernel, [((4, rows, cols), BF16)], (stays, near, chip_terms[0]))
+        home = [stays, near, lax.ppermute(goes, "ctx", across(2))]
+    else:
+        home = around(sends_home)
+
+    def mixed_kernel(gated_ref, weight_ref, cot_ref, second_ref, mixed_ref, gate_ref, mark):
+        mark[...] = jnp.zeros_like(mark)
         mixed_ref[...] = mxu(gated_ref[...], weight_ref[...]).astype(BF16)
-        gate_ref[...] = (grad_ref[...] * second_ref[...].astype(F32)).astype(BF16)
-        for step, out in enumerate(outs):
-            out[0] = pick_rows(gate_grad, ahead(step), rows)
-            out[1] = pick_rows(value_grad, ahead(step), rows)
+        grad = grad_gated(cot_ref, weight_ref)
+        gate_ref[...] = (grad * second_ref[...].astype(F32)).astype(BF16)
 
     with jax.named_scope("mixed"):
-        mixed, grad_gate_two, *sends = call(
+        mixed, grad_gate_two, mark = call(
             mixed_kernel,
-            [wide_bf16, wide_bf16] + [pair] * seq,
-            (gated, weight, grad_gated, second_conv, gate_grad, value_grad, own_term),
-            flops=2 * rows * width * width,
+            [wide_bf16, wide_bf16, ((8, 128), F32)],
+            (gated, out_weight, grad_out[0], second_conv),
+            flops=4 * rows * width * width,
             limit=limit,
         )
-    result_parts = around(sends)
 
     if fast:
 
-        def place_kernel(own, lag, *refs):
+        def place_kernel(mark, own, lag, *refs):
             arrived, outs, total = refs[: chips - 1], refs[chips - 1 : -1], refs[-1]
             summed = own[...]
             for part in arrived:
@@ -472,7 +509,7 @@
             sends = call(
                 place_kernel,
                 [(small, F32)] + [(small, BF16)] * (seq - 1),
-                (own_term, lag_term, *chip_terms),
+                (mark, own_term, lag_term, *chip_terms),
                 scratch=[pltpu.VMEM((own_rows, width), F32)],
             )
     else:
@@ -494,13 +531,19 @@
     last_terms = around(sends)
 
     def unpack_kernel(*refs):
-        parts, (gate_ref, value_ref) = refs[:seq], refs[seq:]
-        for step, part in enumerate(parts):
-            put_columns(gate_ref, held(behind(step)), cols, seq, part[0])
-            put_columns(value_ref, held(behind(step)), cols, seq, part[1])
+        parts, (gate_ref, value_ref) = refs[:-2], refs[-2:]
+        if fast:
+            stays_ref, near_ref, far_ref = parts
+            blocks = [(stays_ref, 0), (near_ref, 0), (far_ref, 0), (far_ref, 2)]
+            blocks = [(lax.axis_index("ctx") ^ far, *block) for far, block in enumerate(blocks)]
+        else:
+            blocks = [(behind(step), part, 0) for step, part in enumerate(parts)]
+        for place, part, first in blocks:
+            put_columns(gate_ref, held(place), cols, seq, part[first])
+            put_columns(value_ref, held(place), cols, seq, part[first + 1])
 
     with jax.named_scope("unpack_results"):
-        grad_gate_one, grad_value = call(unpack_kernel, [wide_bf16, wide_bf16], result_parts)
+        grad_gate_one, grad_value = call(unpack_kernel, [wide_bf16, wide_bf16], home)
 
     if fast:
 

time: 52.2 us -> 48.2 us (0.923)
  starting transfers between devices: 29.3 us -> 23.1 us
  waiting for transfers between devices: 8.57 us -> 14.6 us
  local copies, waits for them, and re-layouts: 5.77 us -> 1.05 us
  Pallas kernels: 7.56 us -> 8.57 us
    ppermute x12 -> x9, starting transfers between devices: 25 us -> 16.6 us  [around(): out.append(lax.ppermute(blocks[step], 'ctx', pairs))]
    unnamed x18 -> x14, local copies, waits for them, and re-layouts: 5.74 us -> 1.01 us
    ppermute x3, waiting for transfers between devices: 0.01 us -> 2.87 us  [on_device(): chip_terms.append(lax.ppermute(sends[step - 1], 'dp', pairs))]
    ppermute x0 -> x2, waiting for transfers between devices: none -> 2.58 us  [the longest x1 2.57 us: on_device(): near = lax.ppermute(goes, 'ctx', across(1))]
    ppermute x0 -> x2, starting transfers between devices: none -> 1.96 us  [the longest x1 1.6 us: on_device(): home = [stays, near, lax.ppermute(goes, 'ctx', across(2))]]
    pallas_call x10 -> x11, Pallas kernels: 7.56 us -> 8.57 us  [call(): pl.pallas_call(kernel, out_shape=[jax.ShapeDtypeStruct(shape, dtype) for...]
    ppermute x3, starting transfers between devices: 3.55 us -> 4.5 us  [on_device(): chip_terms.append(lax.ppermute(sends[step - 1], 'dp', pairs))]
    ppermute x12 -> x9, waiting for transfers between devices: 6.85 us -> 7.79 us  [around(): out.append(lax.ppermute(blocks[step], 'ctx', pairs))]
  transfers between devices with their start and end apart: 17 -> 16, of which waited for: 7 -> 11; matrix products, arithmetic and copies ran while one was open for 0% -> 0% of each run, Pallas kernels for 7% -> 8%
where the time goes in v4:
time: 48.2 us; the launch traced here: 48 us
  starting transfers between devices  23.1 us (48%)
  waiting for transfers between devices  14.6 us (30%)
  Pallas kernels  8.57 us (18%)
  local copies, waits for them, and re-layouts  1.05 us (2%)
  between operations  0.72 us (1%)
    ppermute x9, starting transfers between devices, around(): out.append(lax.ppermute(blocks[step], 'ctx', pairs))  16.6 us
    pallas_call x11, Pallas kernels, call(): pl.pallas_call(kernel, out_shape=[jax.ShapeDtypeStruct(shape, dtype) for...  8.57 us
    ppermute x9, waiting for transfers between devices, around(): out.append(lax.ppermute(blocks[step], 'ctx', pairs))  7.79 us
    ppermute x3, starting transfers between devices, on_device(): chip_terms.append(lax.ppermute(sends[step - 1], 'dp', pairs))  4.5 us
    ppermute x3, waiting for transfers between devices, on_device(): chip_terms.append(lax.ppermute(sends[step - 1], 'dp', pairs))  2.87 us
    ppermute x1, waiting for transfers between devices, on_device(): near = lax.ppermute(goes, 'ctx', across(1))  2.57 us
    ppermute x1, starting transfers between devices, on_device(): home = [stays, near, lax.ppermute(goes, 'ctx', across(2))]  1.6 us
    ppermute x1, waiting for transfers between devices, on_device(): taken = lax.ppermute(given, 'dp', [(i, i ^ 1) for i in range(data)])  1.35 us
  transfers between devices with their start and end apart: 16, of which 11 were waited for; matrix products, arithmetic and copies ran while one was open for 0% of the time, Pallas kernels for 8%

profile of v4, /device:TPU:0, one launch (start us, length us, event | category | flops | bytes accessed | tf_op | source)
XLA Modules:
  0.0 48.0 jit_solution(6469460725745650650)
XLA Ops:
  0.6 0.0 copy-start
  0.6 1.7 %load.1 = (bf16[3,128,128]{2,1,0:T(8,128)(2,1)S(1)}, bf16[3,128,128]{2,1,0:T(8,128)(2,1)S(1)}, bf16[3,128,128]{2,1,0:T(8,128)(2,1)S(1)}, bf16[3,128,128]{2,1,0:T(8,128)(2,1)S(1)}) custom-call(bf16[1,128,512]{2,1,0:T(8,128)(2,1)} %refs_0_.1, bf16[1,128,512]{2,1,0:T(8,128)(2,1)} %refs_1_.1, bf16[1,128,512]{2,1,0:T(8,128)(2,1)} %refs_2_.1, ...), custom_call_target="tpu_custom_call" | custom-call | flops 67108864 | bytes 1048576 | tf_op jit(solution)/shard_map/load/pallas_call | solution.py:142
  2.3 3.1 %collective-permute-start = (bf16[3,128,128]{2,1,0:T(8,128)(2,1)S(1)}, bf16[3,128,128]{2,1,0:T(8,128)(2,1)S(1)}, u32[]{:S(2)}, u32[]{:S(2)}) collective-permute-start(bf16[3,128,128]{2,1,0:T(8,128)(2,1)S(1)} %get-tuple-element.41), channel_id=1, source_target_pairs={{0,1},{1,2},{2,3},{3,0},{4,5},{5,6},{6,7},{7,4},{8,9},{9,10},{10,1... | collective-permute-start | bytes 294920 | tf_op jit(solution)/shard_map/ppermute | solution.py:185
  5.4 2.6 %collective-permute-start.1 = (bf16[3,128,128]{2,1,0:T(8,128)(2,1)S(1)}, bf16[3,128,128]{2,1,0:T(8,128)(2,1)S(1)}, u32[]{:S(2)}, u32[]{:S(2)}) collective-permute-start(bf16[3,128,128]{2,1,0:T(8,128)(2,1)S(1)} %get-tuple-element.42), channel_id=1, source_target_pairs={{0,2},{1,3},{2,0},{3,1},{4,6},{5,7},{6,4},{7,5},{8,10},{9,11},{10,... | collective-permute-start | bytes 294920 | tf_op jit(solution)/shard_map/ppermute | solution.py:185
  8.0 1.3 %collective-permute-start.2 = (bf16[3,128,128]{2,1,0:T(8,128)(2,1)S(1)}, bf16[3,128,128]{2,1,0:T(8,128)(2,1)S(1)}, u32[]{:S(2)}, u32[]{:S(2)}) collective-permute-start(bf16[3,128,128]{2,1,0:T(8,128)(2,1)S(1)} %get-tuple-element.43), channel_id=1, source_target_pairs={{0,3},{1,0},{2,1},{3,2},{4,7},{5,4},{6,5},{7,6},{8,11},{9,8},{10,9... | collective-permute-start | bytes 294920 | tf_op jit(solution)/shard_map/ppermute | solution.py:185
  9.3 0.0 copy-done
  9.4 0.9 %copy-done.1 = bf16[512,256]{1,0:T(8,128)(2,1)S(1)} copy-done((bf16[512,256]{1,0:T(8,128)(2,1)S(1)}, bf16[512,256]{1,0:T(8,128)(2,1)}, u32[]{:S(2)}) %copy-start.1) | copy-done | bytes 262168
  10.3 0.1 copy-done.2
  10.4 0.4 filter_spectra.1.refs_4_
  10.8 0.3 collective-permute-done.refs_1_
  11.1 3.5 %collective-permute-done.1.refs_2_ = bf16[3,128,128]{2,1,0:T(8,128)(2,1)S(1)} collective-permute-done((bf16[3,128,128]{2,1,0:T(8,128)(2,1)S(1)}, bf16[3,128,128]{2,1,0:T(8,128)(2,1)S(1)}, u32[]{:S(2)}, u32[]{:S(2)}) %collective-permute-start.1) | collective-permute-done | bytes 98336 | tf_op jit(solution)/shard_map/ppermute | solution.py:185
  14.6 0.0 collective-permute-done.2.refs_3_
  14.6 0.0 copy-done.5
  14.6 1.5 %forward_convolutions.1 = (f32[512,128]{1,0:T(8,128)S(1)}, f32[512,256]{1,0:T(8,128)S(1)}, f32[512,256]{1,0:T(8,128)S(1)}, bf16[128,128]{1,0:T(8,128)(2,1)S(1)},...) custom-call(bf16[3,128,128]{2,1,0:T(8,128)(2,1)S(1)} %get-tuple-element.40.refs_0_, ...), custom_call_target="tpu_custom_call" | custom-call | flops 402653184 | bytes 2228224 | tf_op jit(solution)/shard_map/forward_convolutions/pallas_call | solution.py:142
  16.1 2.6 %collective-permute-start.3 = (bf16[128,128]{1,0:T(8,128)(2,1)S(1)}, bf16[128,128]{1,0:T(8,128)(2,1)S(1)}, u32[]{:S(2)}, u32[]{:S(2)}) collective-permute-start(bf16[128,128]{1,0:T(8,128)(2,1)S(1)} %get-tuple-element.45), channel_id=1, source_target_pairs={{0,1},{1,2},{2,3},{3,0},{4,5},{5,6},{6,7},{7,4},{8,9},{9,10},{10,1... | collective-permute-start | bytes 98312 | tf_op jit(solution)/shard_map/ppermute | solution.py:185
  18.7 1.6 %collective-permute-start.4 = (bf16[128,128]{1,0:T(8,128)(2,1)S(1)}, bf16[128,128]{1,0:T(8,128)(2,1)S(1)}, u32[]{:S(2)}, u32[]{:S(2)}) collective-permute-start(bf16[128,128]{1,0:T(8,128)(2,1)S(1)} %get-tuple-element.46), channel_id=1, source_target_pairs={{0,2},{1,3},{2,0},{3,1},{4,6},{5,7},{6,4},{7,5},{8,10},{9,11},{10,... | collective-permute-start | bytes 98312 | tf_op jit(solution)/shard_map/ppermute | solution.py:185
  20.3 0.8 %collective-permute-start.5 = (bf16[128,128]{1,0:T(8,128)(2,1)S(1)}, bf16[128,128]{1,0:T(8,128)(2,1)S(1)}, u32[]{:S(2)}, u32[]{:S(2)}) collective-permute-start(bf16[128,128]{1,0:T(8,128)(2,1)S(1)} %get-tuple-element.47), channel_id=1, source_target_pairs={{0,3},{1,0},{2,1},{3,2},{4,7},{5,4},{6,5},{7,6},{8,11},{9,8},{10,9... | collective-permute-start | bytes 98312 | tf_op jit(solution)/shard_map/ppermute | solution.py:185
  21.2 1.7 %backward_convolutions.1 = (f32[2,512,128]{2,1,0:T(8,128)S(1)}, bf16[4,128,128]{2,1,0:T(8,128)(2,1)S(1)}, bf16[4,128,128]{2,1,0:T(8,128)(2,1)S(1)}) custom-call(bf16[3,128,128]{2,1,0:T(8,128)(2,1)S(1)} %get-tuple-element.40.refs_0_, bf16[3,128,128]{2,1,0:T(8,128)(2,1)S(1)} %collective-permute-done.refs_1_, ...), custom_call_target="tpu_custom_call" | custom-call | flops 536870912 | bytes 3538944 | tf_op jit(solution)/shard_map/backward_convolutions/pallas_call | solution.py:142
  22.8 0.0 collective-permute-done.3.refs_1_
  22.9 0.8 %collective-permute-done.4.refs_2_ = bf16[128,128]{1,0:T(8,128)(2,1)S(1)} collective-permute-done((bf16[128,128]{1,0:T(8,128)(2,1)S(1)}, bf16[128,128]{1,0:T(8,128)(2,1)S(1)}, u32[]{:S(2)}, u32[]{:S(2)}) %collective-permute-start.4) | collective-permute-done | bytes 32800 | tf_op jit(solution)/shard_map/ppermute | solution.py:185
  23.6 0.6 %collective-permute-done.5.refs_3_ = bf16[128,128]{1,0:T(8,128)(2,1)S(1)} collective-permute-done((bf16[128,128]{1,0:T(8,128)(2,1)S(1)}, bf16[128,128]{1,0:T(8,128)(2,1)S(1)}, u32[]{:S(2)}, u32[]{:S(2)}) %collective-permute-start.5) | collective-permute-done | bytes 32800 | tf_op jit(solution)/shard_map/ppermute | solution.py:185
  24.2 0.0 copy-done.4
  24.3 0.6 %weight_partial.1 = (bf16[128,512]{1,0:T(8,128)(2,1)S(1)}, bf16[128,512]{1,0:T(8,128)(2,1)S(1)}, f32[384,512]{1,0:T(8,128)S(1)}, bf16[384,512]{1,0:T(8,128)(2,1)S(1)}) custom-call(bf16[128,128]{1,0:T(8,128)(2,1)S(1)} %get-tuple-element.44.refs_0_, bf16[128,128]{1,0:T(8,128)(2,1)S(1)} %collective-permute-done.3.refs_1_, ...), custom_call_target="tpu_custom_call" | custom-call | flops 67108864 | bytes 917504 | tf_op jit(solution)/shard_map/weight_partial/pallas_call | solution.py:142
  24.9 0.1 collective-permute-start.7
  24.9 0.4 collective-permute-start.6
  25.3 1.3 %collective-permute-done.7.taken_ref = bf16[384,512]{1,0:T(8,128)(2,1)S(1)} collective-permute-done((bf16[384,512]{1,0:T(8,128)(2,1)S(1)}, bf16[384,512]{1,0:T(8,128)(2,1)S(1)}, u32[]{:S(2)}, u32[]{:S(2)}) %collective-permute-start.7) | collective-permute-done | bytes 393248 | tf_op jit(solution)/shard_map/ppermute | solution.py:425
  26.6 0.1 core_sum.1
  26.7 1.6 %collective-permute-start.8 = (bf16[64,512]{1,0:T(8,128)(2,1)S(1)}, bf16[64,512]{1,0:T(8,128)(2,1)S(1)}, u32[]{:S(2)}, u32[]{:S(2)}) collective-permute-start(bf16[64,512]{1,0:T(8,128)(2,1)S(1)} %get-tuple-element.59), channel_id=1, source_target_pairs={{0,8},{4,12},{8,0},{12,4},{16,24},{20,28},{24,16},{28,20},{1,9},{5... | collective-permute-start | bytes 196616 | tf_op jit(solution)/shard_map/ppermute | solution.py:455
  28.3 0.0 collective-permute-start.10
  28.3 2.6 %collective-permute-done.6.near_ref.refs_1_ = bf16[4,128,128]{2,1,0:T(8,128)(2,1)S(1)} collective-permute-done((bf16[4,128,128]{2,1,0:T(8,128)(2,1)S(1)}, bf16[4,128,128]{2,1,0:T(8,128)(2,1)S(1)}, u32[]{:S(2)}, u32[]{:S(2)}) %collective-permute-start.6) | collective-permute-done | bytes 131104 | tf_op jit(solution)/shard_map/ppermute | solution.py:468
  30.8 0.2 collective-permute-done.8._.refs_0_
  31.1 1.6 %collective-permute-start.9 = (bf16[4,128,128]{2,1,0:T(8,128)(2,1)S(1)}, bf16[4,128,128]{2,1,0:T(8,128)(2,1)S(1)}, u32[]{:S(2)}, u32[]{:S(2)}) collective-permute-start(bf16[4,128,128]{2,1,0:T(8,128)(2,1)S(1)} %turn.1), channel_id=1, source_target_pairs={{0,2},{1,3},{2,0},{3,1},{4,6},{5,7},{6,4},{7,5},{8,10},{9,11},{10,... | collective-permute-start | bytes 393224 | tf_op jit(solution)/shard_map/ppermute | solution.py:476
  32.7 1.5 %collective-permute-start.11 = (bf16[64,512]{1,0:T(8,128)(2,1)S(1)}, bf16[64,512]{1,0:T(8,128)(2,1)S(1)}, u32[]{:S(2)}, u32[]{:S(2)}) collective-permute-start(bf16[64,512]{1,0:T(8,128)(2,1)S(1)} %get-tuple-element.66), channel_id=1, source_target_pairs={{0,16},{4,20},{8,24},{12,28},{16,0},{20,4},{24,8},{28,12},{1,17},{... | collective-permute-start | bytes 196616 | tf_op jit(solution)/shard_map/ppermute | solution.py:455
  34.2 1.4 %collective-permute-start.12 = (bf16[64,512]{1,0:T(8,128)(2,1)S(1)}, bf16[64,512]{1,0:T(8,128)(2,1)S(1)}, u32[]{:S(2)}, u32[]{:S(2)}) collective-permute-start(bf16[64,512]{1,0:T(8,128)(2,1)S(1)} %get-tuple-element.67), channel_id=1, source_target_pairs={{0,24},{4,28},{8,16},{12,20},{16,8},{20,12},{24,0},{28,4},{1,25},{... | collective-permute-start | bytes 196616 | tf_op jit(solution)/shard_map/ppermute | solution.py:455
  35.6 1.1 %mixed.1 = (bf16[128,512]{1,0:T(8,128)(2,1)}, bf16[128,512]{1,0:T(8,128)(2,1)}, f32[8,128]{1,0:T(8,128)S(1)}) custom-call(bf16[128,512]{1,0:T(8,128)(2,1)S(1)} %get-tuple-element.52.gated_ref, bf16[512,512]{1,0:T(8,128)(2,1)S(1)} %copy-done.3, bf16[128,512]{1,0:T(8,128)(2,1)S(1)} %bitcast.8, bf16[128,512]{1,0:T(8,128)(2,1)S(1)} %get-tuple-element.53.second_ref), custom_call_target="tpu_custom_call" | custom-call | flops 134217728 | bytes 917504 | tf_op jit(solution)/shard_map/mixed/pallas_call | solution.py:142
  36.7 1.0 %collective-permute-done.11.refs_1_ = bf16[64,512]{1,0:T(8,128)(2,1)S(1)} collective-permute-done((bf16[64,512]{1,0:T(8,128)(2,1)S(1)}, bf16[64,512]{1,0:T(8,128)(2,1)S(1)}, u32[]{:S(2)}, u32[]{:S(2)}) %collective-permute-start.11) | collective-permute-done | bytes 65568 | tf_op jit(solution)/shard_map/ppermute | solution.py:455
  37.6 1.7 %collective-permute-done.12.refs_2_ = bf16[64,512]{1,0:T(8,128)(2,1)S(1)} collective-permute-done((bf16[64,512]{1,0:T(8,128)(2,1)S(1)}, bf16[64,512]{1,0:T(8,128)(2,1)S(1)}, u32[]{:S(2)}, u32[]{:S(2)}) %collective-permute-start.12) | collective-permute-done | bytes 65568 | tf_op jit(solution)/shard_map/ppermute | solution.py:455
  39.3 0.0 collective-permute-done.10.lag
  39.3 0.1 chip_sum.1
  39.4 2.1 %collective-permute-start.13 = (bf16[192,128]{1,0:T(8,128)(2,1)S(1)}, bf16[192,128]{1,0:T(8,128)(2,1)S(1)}, u32[]{:S(2)}, u32[]{:S(2)}) collective-permute-start(bf16[192,128]{1,0:T(8,128)(2,1)S(1)} %get-tuple-element.69), channel_id=1, source_target_pairs={{0,1},{1,2},{2,3},{3,0},{4,5},{5,6},{6,7},{7,4},{8,9},{9,10},{10,1... | collective-permute-start | bytes 147464 | tf_op jit(solution)/shard_map/ppermute | solution.py:185
  41.5 0.1 collective-permute-start.14
  41.6 2.3 %collective-permute-start.15 = (bf16[192,128]{1,0:T(8,128)(2,1)S(1)}, bf16[192,128]{1,0:T(8,128)(2,1)S(1)}, u32[]{:S(2)}, u32[]{:S(2)}) collective-permute-start(bf16[192,128]{1,0:T(8,128)(2,1)S(1)} %get-tuple-element.71), channel_id=1, source_target_pairs={{0,3},{1,0},{2,1},{3,2},{4,7},{5,4},{6,5},{7,6},{8,11},{9,8},{10,9... | collective-permute-start | bytes 147464 | tf_op jit(solution)/shard_map/ppermute | solution.py:185
  43.9 1.4 %collective-permute-done.13.refs_1_ = bf16[192,128]{1,0:T(8,128)(2,1)S(1)} collective-permute-done((bf16[192,128]{1,0:T(8,128)(2,1)S(1)}, bf16[192,128]{1,0:T(8,128)(2,1)S(1)}, u32[]{:S(2)}, u32[]{:S(2)}) %collective-permute-start.13) | collective-permute-done | bytes 49184 | tf_op jit(solution)/shard_map/ppermute | solution.py:185
  45.4 1.2 %collective-permute-done.14.refs_2_ = bf16[192,128]{1,0:T(8,128)(2,1)S(1)} collective-permute-done((bf16[192,128]{1,0:T(8,128)(2,1)S(1)}, bf16[192,128]{1,0:T(8,128)(2,1)S(1)}, u32[]{:S(2)}, u32[]{:S(2)}) %collective-permute-start.14) | collective-permute-done | bytes 49184 | tf_op jit(solution)/shard_map/ppermute | solution.py:185
  46.5 0.0 collective-permute-done.15.refs_3_
  46.5 0.7 %means.1 = (f32[2,64,128]{2,1,0:T(8,128)}, f32[64,128]{1,0:T(8,128)}) custom-call(f32[192,128]{1,0:T(8,128)S(1)} %get-tuple-element.68.refs_0_, bf16[192,128]{1,0:T(8,128)(2,1)S(1)} %collective-permute-done.13.refs_1_, bf16[192,128]{1,0:T(8,128)(2,1)S(1)} %collective-permute-done.14.refs_2_, bf16[192,128]{1,0:T(8,128)(2,1)S(1)} %collective-permute-done.15.refs_3_), custom_call_target="tpu_custom_call" | custom-call | bytes 245760 | tf_op jit(solution)/shard_map/means/pallas_call | solution.py:142
  47.3 0.0 collective-permute-done.9.refs_2_
  47.3 0.8 %unpack_results.1 = (bf16[128,512]{1,0:T(8,128)(2,1)}, bf16[128,512]{1,0:T(8,128)(2,1)}) custom-call(bf16[4,128,128]{2,1,0:T(8,128)(2,1)S(1)} %get-tuple-element.55.stays_ref.refs_0_, bf16[4,128,128]{2,1,0:T(8,128)(2,1)S(1)} %collective-permute-done.6.near_ref.refs_1_, bf16[4,128,128]{2,1,0:T(8,128)(2,1)S(1)} %collective-permute-done.9.refs_2_), custom_call_target="tpu_custom_call" | custom-call | bytes 393216 | tf_op jit(solution)/shard_map/unpack_results/pallas_call | solution.py:142
  (10 shorter events, 0.1 us)
Async XLA Ops:
  0.6 8.7 %copy-start = (bf16[2,512,512]{2,1,0:T(8,128)(2,1)S(1)}, bf16[2,512,512]{2,1,0:T(8,128)(2,1)}, u32[]{:S(2)}) copy-start(bf16[2,512,512]{2,1,0:T(8,128)(2,1)} %param.12) | copy-start | bytes 3145732
  2.3 8.7 %collective-permute-start = (bf16[3,128,128]{2,1,0:T(8,128)(2,1)S(1)}, bf16[3,128,128]{2,1,0:T(8,128)(2,1)S(1)}, u32[]{:S(2)}, u32[]{:S(2)}) collective-permute-start(bf16[3,128,128]{2,1,0:T(8,128)(2,1)S(1)} %get-tuple-element.41), channel_id=1, source_target_pairs={{0,1},{1,2},{2,3},{3,0},{4,5},{5,6},{6,7},{7,4},{8,9},{9,10},{10,1... | collective-permute-start | bytes 294920 | tf_op jit(solution)/shard_map/ppermute | solution.py:185
  5.4 9.2 %collective-permute-start.1 = (bf16[3,128,128]{2,1,0:T(8,128)(2,1)S(1)}, bf16[3,128,128]{2,1,0:T(8,128)(2,1)S(1)}, u32[]{:S(2)}, u32[]{:S(2)}) collective-permute-start(bf16[3,128,128]{2,1,0:T(8,128)(2,1)S(1)} %get-tuple-element.42), channel_id=1, source_target_pairs={{0,2},{1,3},{2,0},{3,1},{4,6},{5,7},{6,4},{7,5},{8,10},{9,11},{10,... | collective-permute-start | bytes 294920 | tf_op jit(solution)/shard_map/ppermute | solution.py:185
  8.0 6.6 %collective-permute-start.2 = (bf16[3,128,128]{2,1,0:T(8,128)(2,1)S(1)}, bf16[3,128,128]{2,1,0:T(8,128)(2,1)S(1)}, u32[]{:S(2)}, u32[]{:S(2)}) collective-permute-start(bf16[3,128,128]{2,1,0:T(8,128)(2,1)S(1)} %get-tuple-element.43), channel_id=1, source_target_pairs={{0,3},{1,0},{2,1},{3,2},{4,7},{5,4},{6,5},{7,6},{8,11},{9,8},{10,9... | collective-permute-start | bytes 294920 | tf_op jit(solution)/shard_map/ppermute | solution.py:185
  9.3 1.0 %copy-start.1 = (bf16[512,256]{1,0:T(8,128)(2,1)S(1)}, bf16[512,256]{1,0:T(8,128)(2,1)}, u32[]{:S(2)}) copy-start(bf16[512,256]{1,0:T(8,128)(2,1)} %constant.25.clone.high.refs_5_.refs_8_) | copy-start | bytes 786436
  9.3 1.0 %copy-start.2 = (bf16[512,256]{1,0:T(8,128)(2,1)S(1)}, bf16[512,256]{1,0:T(8,128)(2,1)}, u32[]{:S(2)}) copy-start(bf16[512,256]{1,0:T(8,128)(2,1)} %constant.26.clone.low.refs_6_.refs_9_) | copy-start | bytes 786436
  10.4 4.2 %copy-start.5 = (bf16[256,512]{1,0:T(8,128)(2,1)S(1)}, bf16[256,512]{1,0:T(8,128)(2,1)}, u32[]{:S(2)}) copy-start(bf16[256,512]{1,0:T(8,128)(2,1)} %constant.27.clone.refs_7_.refs_10_) | copy-start | bytes 786436
  16.1 6.7 %collective-permute-start.3 = (bf16[128,128]{1,0:T(8,128)(2,1)S(1)}, bf16[128,128]{1,0:T(8,128)(2,1)S(1)}, u32[]{:S(2)}, u32[]{:S(2)}) collective-permute-start(bf16[128,128]{1,0:T(8,128)(2,1)S(1)} %get-tuple-element.45), channel_id=1, source_target_pairs={{0,1},{1,2},{2,3},{3,0},{4,5},{5,6},{6,7},{7,4},{8,9},{9,10},{10,1... | collective-permute-start | bytes 98312 | tf_op jit(solution)/shard_map/ppermute | solution.py:185
  18.7 4.9 %collective-permute-start.4 = (bf16[128,128]{1,0:T(8,128)(2,1)S(1)}, bf16[128,128]{1,0:T(8,128)(2,1)S(1)}, u32[]{:S(2)}, u32[]{:S(2)}) collective-permute-start(bf16[128,128]{1,0:T(8,128)(2,1)S(1)} %get-tuple-element.46), channel_id=1, source_target_pairs={{0,2},{1,3},{2,0},{3,1},{4,6},{5,7},{6,4},{7,5},{8,10},{9,11},{10,... | collective-permute-start | bytes 98312 | tf_op jit(solution)/shard_map/ppermute | solution.py:185
  20.3 3.9 %collective-permute-start.5 = (bf16[128,128]{1,0:T(8,128)(2,1)S(1)}, bf16[128,128]{1,0:T(8,128)(2,1)S(1)}, u32[]{:S(2)}, u32[]{:S(2)}) collective-permute-start(bf16[128,128]{1,0:T(8,128)(2,1)S(1)} %get-tuple-element.47), channel_id=1, source_target_pairs={{0,3},{1,0},{2,1},{3,2},{4,7},{5,4},{6,5},{7,6},{8,11},{9,8},{10,9... | collective-permute-start | bytes 98312 | tf_op jit(solution)/shard_map/ppermute | solution.py:185
  21.1 3.1 %copy-start.4 = (bf16[1,128,512]{2,1,0:T(8,128)(2,1)S(1)}, bf16[1,128,512]{2,1,0:T(8,128)(2,1)}, u32[]{:S(2)}) copy-start(bf16[1,128,512]{2,1,0:T(8,128)(2,1)} %refs_2_.1) | copy-start | bytes 393220
  21.2 3.1 %copy-start.6 = (bf16[1,128,512]{2,1,0:T(8,128)(2,1)S(1)}, bf16[1,128,512]{2,1,0:T(8,128)(2,1)}, u32[]{:S(2)}) copy-start(bf16[1,128,512]{2,1,0:T(8,128)(2,1)} %refs_4_.1) | copy-start | bytes 393220
  24.9 1.8 %collective-permute-start.7 = (bf16[384,512]{1,0:T(8,128)(2,1)S(1)}, bf16[384,512]{1,0:T(8,128)(2,1)S(1)}, u32[]{:S(2)}, u32[]{:S(2)}) collective-permute-start(bf16[384,512]{1,0:T(8,128)(2,1)S(1)} %get-tuple-element.58), channel_id=1, source_target_pairs={{0,4},{4,0},{8,12},{12,8},{16,20},{20,16},{24,28},{28,24},{1,5},{5... | collective-permute-start | bytes 1179656 | tf_op jit(solution)/shard_map/ppermute | solution.py:425
  24.9 5.9 %collective-permute-start.6 = (bf16[4,128,128]{2,1,0:T(8,128)(2,1)S(1)}, bf16[4,128,128]{2,1,0:T(8,128)(2,1)S(1)}, u32[]{:S(2)}, u32[]{:S(2)}) collective-permute-start(bf16[4,128,128]{2,1,0:T(8,128)(2,1)S(1)} %get-tuple-element.56), channel_id=1, source_target_pairs={{0,1},{1,0},{2,3},{3,2},{4,5},{5,4},{6,7},{7,6},{8,9},{9,8},{10,11... | collective-permute-start | bytes 393224 | tf_op jit(solution)/shard_map/ppermute | solution.py:468
  26.6 9.0 %copy-start.3 = (bf16[512,512]{1,0:T(8,128)(2,1)S(1)}, bf16[512,512]{1,0:T(8,128)(2,1)}, u32[]{:S(2)}) copy-start(bf16[512,512]{1,0:T(8,128)(2,1)} %weight_ref.1) | copy-start | bytes 1572868
  26.7 4.3 %collective-permute-start.8 = (bf16[64,512]{1,0:T(8,128)(2,1)S(1)}, bf16[64,512]{1,0:T(8,128)(2,1)S(1)}, u32[]{:S(2)}, u32[]{:S(2)}) collective-permute-start(bf16[64,512]{1,0:T(8,128)(2,1)S(1)} %get-tuple-element.59), channel_id=1, source_target_pairs={{0,8},{4,12},{8,0},{12,4},{16,24},{20,28},{24,16},{28,20},{1,9},{5... | collective-permute-start | bytes 196616 | tf_op jit(solution)/shard_map/ppermute | solution.py:455
  28.3 11.1 %collective-permute-start.10 = (bf16[128,512]{1,0:T(8,128)(2,1)S(1)}, bf16[128,512]{1,0:T(8,128)(2,1)S(1)}, u32[]{:S(2)}, u32[]{:S(2)}) collective-permute-start(bf16[128,512]{1,0:T(8,128)(2,1)S(1)} %get-tuple-element.65), channel_id=1, source_target_pairs={{0,4},{1,9},{2,18},{3,27},{4,0},{5,13},{6,22},{7,31},{8,12},{9,1},... | collective-permute-start | bytes 393224 | tf_op jit(solution)/shard_map/ppermute | solution.py:461
  31.1 16.2 %collective-permute-start.9 = (bf16[4,128,128]{2,1,0:T(8,128)(2,1)S(1)}, bf16[4,128,128]{2,1,0:T(8,128)(2,1)S(1)}, u32[]{:S(2)}, u32[]{:S(2)}) collective-permute-start(bf16[4,128,128]{2,1,0:T(8,128)(2,1)S(1)} %turn.1), channel_id=1, source_target_pairs={{0,2},{1,3},{2,0},{3,1},{4,6},{5,7},{6,4},{7,5},{8,10},{9,11},{10,... | collective-permute-start | bytes 393224 | tf_op jit(solution)/shard_map/ppermute | solution.py:476
  32.7 5.0 %collective-permute-start.11 = (bf16[64,512]{1,0:T(8,128)(2,1)S(1)}, bf16[64,512]{1,0:T(8,128)(2,1)S(1)}, u32[]{:S(2)}, u32[]{:S(2)}) collective-permute-start(bf16[64,512]{1,0:T(8,128)(2,1)S(1)} %get-tuple-element.66), channel_id=1, source_target_pairs={{0,16},{4,20},{8,24},{12,28},{16,0},{20,4},{24,8},{28,12},{1,17},{... | collective-permute-start | bytes 196616 | tf_op jit(solution)/shard_map/ppermute | solution.py:455
  34.2 5.2 %collective-permute-start.12 = (bf16[64,512]{1,0:T(8,128)(2,1)S(1)}, bf16[64,512]{1,0:T(8,128)(2,1)S(1)}, u32[]{:S(2)}, u32[]{:S(2)}) collective-permute-start(bf16[64,512]{1,0:T(8,128)(2,1)S(1)} %get-tuple-element.67), channel_id=1, source_target_pairs={{0,24},{4,28},{8,16},{12,20},{16,8},{20,12},{24,0},{28,4},{1,25},{... | collective-permute-start | bytes 196616 | tf_op jit(solution)/shard_map/ppermute | solution.py:455
  39.4 5.9 %collective-permute-start.13 = (bf16[192,128]{1,0:T(8,128)(2,1)S(1)}, bf16[192,128]{1,0:T(8,128)(2,1)S(1)}, u32[]{:S(2)}, u32[]{:S(2)}) collective-permute-start(bf16[192,128]{1,0:T(8,128)(2,1)S(1)} %get-tuple-element.69), channel_id=1, source_target_pairs={{0,1},{1,2},{2,3},{3,0},{4,5},{5,6},{6,7},{7,4},{8,9},{9,10},{10,1... | collective-permute-start | bytes 147464 | tf_op jit(solution)/shard_map/ppermute | solution.py:185
  41.5 5.0 %collective-permute-start.14 = (bf16[192,128]{1,0:T(8,128)(2,1)S(1)}, bf16[192,128]{1,0:T(8,128)(2,1)S(1)}, u32[]{:S(2)}, u32[]{:S(2)}) collective-permute-start(bf16[192,128]{1,0:T(8,128)(2,1)S(1)} %get-tuple-element.70), channel_id=1, source_target_pairs={{0,2},{1,3},{2,0},{3,1},{4,6},{5,7},{6,4},{7,5},{8,10},{9,11},{10,... | collective-permute-start | bytes 147464 | tf_op jit(solution)/shard_map/ppermute | solution.py:185
  41.6 4.9 %collective-permute-start.15 = (bf16[192,128]{1,0:T(8,128)(2,1)S(1)}, bf16[192,128]{1,0:T(8,128)(2,1)S(1)}, u32[]{:S(2)}, u32[]{:S(2)}) collective-permute-start(bf16[192,128]{1,0:T(8,128)(2,1)S(1)} %get-tuple-element.71), channel_id=1, source_target_pairs={{0,3},{1,0},{2,1},{3,2},{4,7},{5,4},{6,5},{7,6},{8,11},{9,8},{10,9... | collective-permute-start | bytes 147464 | tf_op jit(solution)/shard_map/ppermute | solution.py:185

commit v5 on v4

--- a/solution.py
+++ b/solution.py
@@ -301,7 +301,7 @@
             return
         for far in range(4):
             place = lax.axis_index("ctx") ^ far
-            outs[far % 2][far // 2 * 2 + index] = pick_rows(total, place, rows).astype(BF16)
+            outs[far // 2][far % 2 * 2 + index] = pick_rows(total, place, rows).astype(BF16)
 
     def backward_kernel(*refs):
         parts, refs = refs[:seq], refs[seq:]
@@ -460,23 +460,6 @@
             pairs += [(i * seq + j, (i ^ (2 * j)) * seq + j) for j in range(1, seq)]
         lag_term = lax.ppermute(sends[-1], ("dp", "ctx"), pairs)
 
-    def across(far):
-        return [(i, i ^ far) for i in range(seq)]
-
-    if fast:
-        stays, goes = sends_home
-        near = lax.ppermute(goes, "ctx", across(1))
-
-        def turn_kernel(stays_ref, near_ref, _, out):
-            out[:2] = stays_ref[2:]
-            out[2:] = near_ref[2:]
-
-        with jax.named_scope("turn"):
-            (goes,) = call(turn_kernel, [((4, rows, cols), BF16)], (stays, near, chip_terms[0]))
-        home = [stays, near, lax.ppermute(goes, "ctx", across(2))]
-    else:
-        home = around(sends_home)
-
     def mixed_kernel(gated_ref, weight_ref, cot_ref, second_ref, mixed_ref, gate_ref, mark):
         mark[...] = jnp.zeros_like(mark)
         mixed_ref[...] = mxu(gated_ref[...], weight_ref[...]).astype(BF16)
@@ -491,6 +474,25 @@
             flops=4 * rows * width * width,
             limit=limit,
         )
+
+    def across(far):
+        return [(i, i ^ far) for i in range(seq)]
+
+    if fast:
+        stays, goes = sends_home
+        near = lax.ppermute(goes, "ctx", across(2))
+
+        def turn_kernel(stays_ref, near_ref, *refs):
+            refs[-1][:2] = stays_ref[2:]
+            refs[-1][2:] = near_ref[2:]
+
+        with jax.named_scope("turn"):
+            (goes,) = call(
+                turn_kernel, [((4, rows, cols), BF16)], (stays, near, mark, *chip_terms)
+            )
+        far = lax.ppermute(goes, "ctx", across(1))
+    else:
+        home = around(sends_home)
 
     if fast:
 
@@ -530,25 +532,20 @@
         lag_own = lax.ppermute(lag_sum, ("dp", "ctx"), pairs)
     last_terms = around(sends)
 
-    def unpack_kernel(*refs):
-        parts, (gate_ref, value_ref) = refs[:-2], refs[-2:]
-        if fast:
-            stays_ref, near_ref, far_ref = parts
-            blocks = [(stays_ref, 0), (near_ref, 0), (far_ref, 0), (far_ref, 2)]
-            blocks = [(lax.axis_index("ctx") ^ far, *block) for far, block in enumerate(blocks)]
-        else:
-            blocks = [(behind(step), part, 0) for step, part in enumerate(parts)]
+    def unpack(blocks, gate_ref, value_ref):
         for place, part, first in blocks:
             put_columns(gate_ref, held(place), cols, seq, part[first])
             put_columns(value_ref, held(place), cols, seq, part[first + 1])
 
-    with jax.named_scope("unpack_results"):
-        grad_gate_one, grad_value = call(unpack_kernel, [wide_bf16, wide_bf16], home)
-
     if fast:
 
         def final_kernel(*refs):
-            arrived, (filter_ref, weight_ref) = refs[:seq], refs[seq:]
+            arrived, (stays_ref, near_ref, far_ref) = refs[:4], refs[4:7]
+            filter_ref, weight_ref, gate_ref, value_ref = refs[7:]
+            here = lax.axis_index("ctx")
+            blocks = [(here, stays_ref, 0), (here ^ 2, near_ref, 0)]
+            blocks += [(here ^ 1, far_ref, 0), (here ^ 3, far_ref, 2)]
+            unpack(blocks, gate_ref, value_ref)
             total = arrived[0][...]
             for part in arrived[1:]:
                 total = total + part[...].astype(F32)
@@ -559,11 +556,19 @@
             filter_ref[1] = turned[fine:]
 
         with jax.named_scope("means"):
-            filter_grad, weight_grad = call(
-                final_kernel, [((2, fine, rows), F32), ((own_rows, cols), F32)], last_terms
+            filter_grad, weight_grad, grad_gate_one, grad_value = call(
+                final_kernel,
+                [((2, fine, rows), F32), ((own_rows, cols), F32), wide_bf16, wide_bf16],
+                (*last_terms, stays, near, far),
             )
         filter_grad = jnp.swapaxes(filter_grad, 1, 2)
     else:
+
+        def unpack_kernel(*refs):
+            unpack([(behind(step), part, 0) for step, part in enumerate(refs[:-2])], *refs[-2:])
+
+        with jax.named_scope("unpack_results"):
+            grad_gate_one, grad_value = call(unpack_kernel, [wide_bf16, wide_bf16], home)
         filter_grad = lag_own.reshape(rows, 2, fine).transpose(1, 0, 2).astype(F32) / data
         weight_grad = sum(part.astype(F32) for part in last_terms) / data
     return (

time: 48.2 us -> 45.4 us (0.942)
  waiting for transfers between devices: 14.6 us -> 11.7 us
  starting transfers between devices: 23.1 us -> 24 us
  Pallas kernels: 8.57 us -> 7.84 us
    ppermute x3, waiting for transfers between devices: 2.87 us -> 0.43 us  [on_device(): chip_terms.append(lax.ppermute(sends[step - 1], 'dp', pairs))]
    ppermute x2, starting transfers between devices: 1.96 us -> 3.71 us  [the longest x1 2.34 us: on_device(): far = lax.ppermute(goes, 'ctx', across(1))]
    ppermute x1, waiting for transfers between devices: 1.35 us -> 0.34 us  [on_device(): taken = lax.ppermute(given, 'dp', [(i, i ^ 1) for i in range(data)])]
    ppermute x3, starting transfers between devices: 4.5 us -> 3.55 us  [on_device(): chip_terms.append(lax.ppermute(sends[step - 1], 'dp', pairs))]
    pallas_call x11 -> x10, Pallas kernels: 8.57 us -> 7.84 us  [call(): pl.pallas_call(kernel, out_shape=[jax.ShapeDtypeStruct(shape, dtype) for...]
    ppermute x2, waiting for transfers between devices: 2.58 us -> 3.19 us  [the longest x1 3.19 us: on_device(): near = lax.ppermute(goes, 'ctx', across(2))]
  transfers between devices with their start and end apart: 16 -> 16, of which waited for: 11 -> 9; matrix products, arithmetic and copies ran while one was open for 0% -> 0% of each run, Pallas kernels for 8% -> 7%
where the time goes in v5:
time: 45.4 us; the launch traced here: 45.2 us
  starting transfers between devices  24 us (53%)
  waiting for transfers between devices  11.7 us (26%)
  Pallas kernels  7.84 us (17%)
  local copies, waits for them, and re-layouts  1.05 us (2%)
  between operations  0.72 us (2%)
    ppermute x9, starting transfers between devices, around(): out.append(lax.ppermute(blocks[step], 'ctx', pairs))  16.6 us
    pallas_call x10, Pallas kernels, call(): pl.pallas_call(kernel, out_shape=[jax.ShapeDtypeStruct(shape, dtype) for...  7.84 us
    ppermute x9, waiting for transfers between devices, around(): out.append(lax.ppermute(blocks[step], 'ctx', pairs))  7.68 us
    ppermute x3, starting transfers between devices, on_device(): chip_terms.append(lax.ppermute(sends[step - 1], 'dp', pairs))  3.55 us
    ppermute x1, waiting for transfers between devices, on_device(): near = lax.ppermute(goes, 'ctx', across(2))  3.19 us
    ppermute x1, starting transfers between devices, on_device(): far = lax.ppermute(goes, 'ctx', across(1))  2.34 us
    ppermute x1, starting transfers between devices, on_device(): near = lax.ppermute(goes, 'ctx', across(2))  1.37 us
    unnamed x14, local copies, waits for them, and re-layouts  1.01 us
  transfers between devices with their start and end apart: 16, of which 9 were waited for; matrix products, arithmetic and copies ran while one was open for 0% of the time, Pallas kernels for 7%

profile of v5, /device:TPU:0, one launch (start us, length us, event | category | flops | bytes accessed | tf_op | source)
XLA Modules:
  0.0 45.2 jit_solution(18167662848494323742)
XLA Ops:
  0.6 0.0 copy-start
  0.6 1.7 %load.1 = (bf16[3,128,128]{2,1,0:T(8,128)(2,1)S(1)}, bf16[3,128,128]{2,1,0:T(8,128)(2,1)S(1)}, bf16[3,128,128]{2,1,0:T(8,128)(2,1)S(1)}, bf16[3,128,128]{2,1,0:T(8,128)(2,1)S(1)}) custom-call(bf16[1,128,512]{2,1,0:T(8,128)(2,1)} %refs_0_.1, bf16[1,128,512]{2,1,0:T(8,128)(2,1)} %refs_1_.1, bf16[1,128,512]{2,1,0:T(8,128)(2,1)} %refs_2_.1, ...), custom_call_target="tpu_custom_call" | custom-call | flops 67108864 | bytes 1048576 | tf_op jit(solution)/shard_map/load/pallas_call | solution.py:142
  2.3 3.1 %collective-permute-start = (bf16[3,128,128]{2,1,0:T(8,128)(2,1)S(1)}, bf16[3,128,128]{2,1,0:T(8,128)(2,1)S(1)}, u32[]{:S(2)}, u32[]{:S(2)}) collective-permute-start(bf16[3,128,128]{2,1,0:T(8,128)(2,1)S(1)} %get-tuple-element.41), channel_id=1, source_target_pairs={{0,1},{1,2},{2,3},{3,0},{4,5},{5,6},{6,7},{7,4},{8,9},{9,10},{10,1... | collective-permute-start | bytes 294920 | tf_op jit(solution)/shard_map/ppermute | solution.py:185
  5.4 2.6 %collective-permute-start.1 = (bf16[3,128,128]{2,1,0:T(8,128)(2,1)S(1)}, bf16[3,128,128]{2,1,0:T(8,128)(2,1)S(1)}, u32[]{:S(2)}, u32[]{:S(2)}) collective-permute-start(bf16[3,128,128]{2,1,0:T(8,128)(2,1)S(1)} %get-tuple-element.42), channel_id=1, source_target_pairs={{0,2},{1,3},{2,0},{3,1},{4,6},{5,7},{6,4},{7,5},{8,10},{9,11},{10,... | collective-permute-start | bytes 294920 | tf_op jit(solution)/shard_map/ppermute | solution.py:185
  8.0 1.3 %collective-permute-start.2 = (bf16[3,128,128]{2,1,0:T(8,128)(2,1)S(1)}, bf16[3,128,128]{2,1,0:T(8,128)(2,1)S(1)}, u32[]{:S(2)}, u32[]{:S(2)}) collective-permute-start(bf16[3,128,128]{2,1,0:T(8,128)(2,1)S(1)} %get-tuple-element.43), channel_id=1, source_target_pairs={{0,3},{1,0},{2,1},{3,2},{4,7},{5,4},{6,5},{7,6},{8,11},{9,8},{10,9... | collective-permute-start | bytes 294920 | tf_op jit(solution)/shard_map/ppermute | solution.py:185
  9.3 0.0 copy-done
  9.4 0.9 %copy-done.1 = bf16[512,256]{1,0:T(8,128)(2,1)S(1)} copy-done((bf16[512,256]{1,0:T(8,128)(2,1)S(1)}, bf16[512,256]{1,0:T(8,128)(2,1)}, u32[]{:S(2)}) %copy-start.1) | copy-done | bytes 262168
  10.3 0.1 copy-done.2
  10.4 0.4 filter_spectra.1.refs_4_
  10.8 0.3 collective-permute-done.refs_1_
  11.1 3.5 %collective-permute-done.1.refs_2_ = bf16[3,128,128]{2,1,0:T(8,128)(2,1)S(1)} collective-permute-done((bf16[3,128,128]{2,1,0:T(8,128)(2,1)S(1)}, bf16[3,128,128]{2,1,0:T(8,128)(2,1)S(1)}, u32[]{:S(2)}, u32[]{:S(2)}) %collective-permute-start.1) | collective-permute-done | bytes 98336 | tf_op jit(solution)/shard_map/ppermute | solution.py:185
  14.6 0.0 collective-permute-done.2.refs_3_
  14.6 0.0 copy-done.5
  14.6 1.5 %forward_convolutions.1 = (f32[512,128]{1,0:T(8,128)S(1)}, f32[512,256]{1,0:T(8,128)S(1)}, f32[512,256]{1,0:T(8,128)S(1)}, bf16[128,128]{1,0:T(8,128)(2,1)S(1)},...) custom-call(bf16[3,128,128]{2,1,0:T(8,128)(2,1)S(1)} %get-tuple-element.40.refs_0_, ...), custom_call_target="tpu_custom_call" | custom-call | flops 402653184 | bytes 2228224 | tf_op jit(solution)/shard_map/forward_convolutions/pallas_call | solution.py:142
  16.1 2.6 %collective-permute-start.3 = (bf16[128,128]{1,0:T(8,128)(2,1)S(1)}, bf16[128,128]{1,0:T(8,128)(2,1)S(1)}, u32[]{:S(2)}, u32[]{:S(2)}) collective-permute-start(bf16[128,128]{1,0:T(8,128)(2,1)S(1)} %get-tuple-element.45), channel_id=1, source_target_pairs={{0,1},{1,2},{2,3},{3,0},{4,5},{5,6},{6,7},{7,4},{8,9},{9,10},{10,1... | collective-permute-start | bytes 98312 | tf_op jit(solution)/shard_map/ppermute | solution.py:185
  18.7 1.6 %collective-permute-start.4 = (bf16[128,128]{1,0:T(8,128)(2,1)S(1)}, bf16[128,128]{1,0:T(8,128)(2,1)S(1)}, u32[]{:S(2)}, u32[]{:S(2)}) collective-permute-start(bf16[128,128]{1,0:T(8,128)(2,1)S(1)} %get-tuple-element.46), channel_id=1, source_target_pairs={{0,2},{1,3},{2,0},{3,1},{4,6},{5,7},{6,4},{7,5},{8,10},{9,11},{10,... | collective-permute-start | bytes 98312 | tf_op jit(solution)/shard_map/ppermute | solution.py:185
  20.3 0.8 %collective-permute-start.5 = (bf16[128,128]{1,0:T(8,128)(2,1)S(1)}, bf16[128,128]{1,0:T(8,128)(2,1)S(1)}, u32[]{:S(2)}, u32[]{:S(2)}) collective-permute-start(bf16[128,128]{1,0:T(8,128)(2,1)S(1)} %get-tuple-element.47), channel_id=1, source_target_pairs={{0,3},{1,0},{2,1},{3,2},{4,7},{5,4},{6,5},{7,6},{8,11},{9,8},{10,9... | collective-permute-start | bytes 98312 | tf_op jit(solution)/shard_map/ppermute | solution.py:185
  21.2 1.7 %backward_convolutions.1 = (f32[2,512,128]{2,1,0:T(8,128)S(1)}, bf16[4,128,128]{2,1,0:T(8,128)(2,1)S(1)}, bf16[4,128,128]{2,1,0:T(8,128)(2,1)S(1)}) custom-call(bf16[3,128,128]{2,1,0:T(8,128)(2,1)S(1)} %get-tuple-element.40.refs_0_, bf16[3,128,128]{2,1,0:T(8,128)(2,1)S(1)} %collective-permute-done.refs_1_, ...), custom_call_target="tpu_custom_call" | custom-call | flops 536870912 | bytes 3538944 | tf_op jit(solution)/shard_map/backward_convolutions/pallas_call | solution.py:142
  22.8 0.0 collective-permute-done.3.refs_1_
  22.9 0.8 %collective-permute-done.4.refs_2_ = bf16[128,128]{1,0:T(8,128)(2,1)S(1)} collective-permute-done((bf16[128,128]{1,0:T(8,128)(2,1)S(1)}, bf16[128,128]{1,0:T(8,128)(2,1)S(1)}, u32[]{:S(2)}, u32[]{:S(2)}) %collective-permute-start.4) | collective-permute-done | bytes 32800 | tf_op jit(solution)/shard_map/ppermute | solution.py:185
  23.6 0.6 %collective-permute-done.5.refs_3_ = bf16[128,128]{1,0:T(8,128)(2,1)S(1)} collective-permute-done((bf16[128,128]{1,0:T(8,128)(2,1)S(1)}, bf16[128,128]{1,0:T(8,128)(2,1)S(1)}, u32[]{:S(2)}, u32[]{:S(2)}) %collective-permute-start.5) | collective-permute-done | bytes 32800 | tf_op jit(solution)/shard_map/ppermute | solution.py:185
  24.2 0.0 copy-done.4
  24.2 0.0 copy-done.6
  24.3 0.6 %weight_partial.1 = (bf16[128,512]{1,0:T(8,128)(2,1)S(1)}, bf16[128,512]{1,0:T(8,128)(2,1)S(1)}, f32[384,512]{1,0:T(8,128)S(1)}, bf16[384,512]{1,0:T(8,128)(2,1)S(1)}) custom-call(bf16[128,128]{1,0:T(8,128)(2,1)S(1)} %get-tuple-element.44.refs_0_, bf16[128,128]{1,0:T(8,128)(2,1)S(1)} %collective-permute-done.3.refs_1_, ...), custom_call_target="tpu_custom_call" | custom-call | flops 67108864 | bytes 917504 | tf_op jit(solution)/shard_map/weight_partial/pallas_call | solution.py:142
  24.8 0.1 collective-permute-start.6
  24.9 1.4 %collective-permute-start.14 = (bf16[4,128,128]{2,1,0:T(8,128)(2,1)S(1)}, bf16[4,128,128]{2,1,0:T(8,128)(2,1)S(1)}, u32[]{:S(2)}, u32[]{:S(2)}) collective-permute-start(bf16[4,128,128]{2,1,0:T(8,128)(2,1)S(1)} %get-tuple-element.68), channel_id=1, source_target_pairs={{0,2},{1,3},{2,0},{3,1},{4,6},{5,7},{6,4},{7,5},{8,10},{9,11},{10,... | collective-permute-start | bytes 393224 | tf_op jit(solution)/shard_map/ppermute | solution.py:483
  26.3 0.3 collective-permute-done.6.taken_ref
  26.6 0.1 core_sum.1
  26.7 1.6 %collective-permute-start.8 = (bf16[64,512]{1,0:T(8,128)(2,1)S(1)}, bf16[64,512]{1,0:T(8,128)(2,1)S(1)}, u32[]{:S(2)}, u32[]{:S(2)}) collective-permute-start(bf16[64,512]{1,0:T(8,128)(2,1)S(1)} %get-tuple-element.60), channel_id=1, source_target_pairs={{0,8},{4,12},{8,0},{12,4},{16,24},{20,28},{24,16},{28,20},{1,9},{5... | collective-permute-start | bytes 196616 | tf_op jit(solution)/shard_map/ppermute | solution.py:455
  28.3 1.5 %collective-permute-start.9 = (bf16[64,512]{1,0:T(8,128)(2,1)S(1)}, bf16[64,512]{1,0:T(8,128)(2,1)S(1)}, u32[]{:S(2)}, u32[]{:S(2)}) collective-permute-start(bf16[64,512]{1,0:T(8,128)(2,1)S(1)} %get-tuple-element.61), channel_id=1, source_target_pairs={{0,16},{4,20},{8,24},{12,28},{16,0},{20,4},{24,8},{28,12},{1,17},{... | collective-permute-start | bytes 196616 | tf_op jit(solution)/shard_map/ppermute | solution.py:455
  29.8 0.5 %collective-permute-start.10 = (bf16[64,512]{1,0:T(8,128)(2,1)S(1)}, bf16[64,512]{1,0:T(8,128)(2,1)S(1)}, u32[]{:S(2)}, u32[]{:S(2)}) collective-permute-start(bf16[64,512]{1,0:T(8,128)(2,1)S(1)} %get-tuple-element.62), channel_id=1, source_target_pairs={{0,24},{4,28},{8,16},{12,20},{16,8},{20,12},{24,0},{28,4},{1,25},{... | collective-permute-start | bytes 196616 | tf_op jit(solution)/shard_map/ppermute | solution.py:455
  30.3 0.0 collective-permute-start.7
  30.3 1.1 %mixed.1 = (bf16[128,512]{1,0:T(8,128)(2,1)}, bf16[128,512]{1,0:T(8,128)(2,1)}, f32[8,128]{1,0:T(8,128)S(1)}) custom-call(bf16[128,512]{1,0:T(8,128)(2,1)S(1)} %get-tuple-element.52.gated_ref, bf16[512,512]{1,0:T(8,128)(2,1)S(1)} %copy-done.3, bf16[128,512]{1,0:T(8,128)(2,1)S(1)} %bitcast.8, bf16[128,512]{1,0:T(8,128)(2,1)S(1)} %get-tuple-element.53.second_ref), custom_call_target="tpu_custom_call" | custom-call | flops 134217728 | bytes 917504 | tf_op jit(solution)/shard_map/mixed/pallas_call | solution.py:142
  31.3 3.2 %collective-permute-done.14.near_ref.refs_5_ = bf16[4,128,128]{2,1,0:T(8,128)(2,1)S(1)} collective-permute-done((bf16[4,128,128]{2,1,0:T(8,128)(2,1)S(1)}, bf16[4,128,128]{2,1,0:T(8,128)(2,1)S(1)}, u32[]{:S(2)}, u32[]{:S(2)}) %collective-permute-start.14) | collective-permute-done | bytes 131104 | tf_op jit(solution)/shard_map/ppermute | solution.py:483
  34.5 0.0 collective-permute-done.8.refs_0_.refs_1_
  34.5 0.0 collective-permute-done.9.refs_1_.refs_2_
  34.5 0.4 collective-permute-done.10.refs_2_.refs_3_
  35.0 2.3 %collective-permute-start.15 = (bf16[4,128,128]{2,1,0:T(8,128)(2,1)S(1)}, bf16[4,128,128]{2,1,0:T(8,128)(2,1)S(1)}, u32[]{:S(2)}, u32[]{:S(2)}) collective-permute-start(bf16[4,128,128]{2,1,0:T(8,128)(2,1)S(1)} %turn.1), channel_id=1, source_target_pairs={{0,1},{1,0},{2,3},{3,2},{4,5},{5,4},{6,7},{7,6},{8,9},{9,8},{10,11... | collective-permute-start | bytes 393224 | tf_op jit(solution)/shard_map/ppermute | solution.py:493
  37.3 0.0 collective-permute-done.7.lag
  37.3 0.1 chip_sum.1
  37.4 0.4 collective-permute-start.11
  37.8 2.6 %collective-permute-start.12 = (bf16[192,128]{1,0:T(8,128)(2,1)S(1)}, bf16[192,128]{1,0:T(8,128)(2,1)S(1)}, u32[]{:S(2)}, u32[]{:S(2)}) collective-permute-start(bf16[192,128]{1,0:T(8,128)(2,1)S(1)} %get-tuple-element.65), channel_id=1, source_target_pairs={{0,2},{1,3},{2,0},{3,1},{4,6},{5,7},{6,4},{7,5},{8,10},{9,11},{10,... | collective-permute-start | bytes 147464 | tf_op jit(solution)/shard_map/ppermute | solution.py:185
  40.4 1.6 %collective-permute-start.13 = (bf16[192,128]{1,0:T(8,128)(2,1)S(1)}, bf16[192,128]{1,0:T(8,128)(2,1)S(1)}, u32[]{:S(2)}, u32[]{:S(2)}) collective-permute-start(bf16[192,128]{1,0:T(8,128)(2,1)S(1)} %get-tuple-element.66), channel_id=1, source_target_pairs={{0,3},{1,0},{2,1},{3,2},{4,7},{5,4},{6,5},{7,6},{8,11},{9,8},{10,9... | collective-permute-start | bytes 147464 | tf_op jit(solution)/shard_map/ppermute | solution.py:185
  42.0 1.4 %collective-permute-done.11.refs_1_ = bf16[192,128]{1,0:T(8,128)(2,1)S(1)} collective-permute-done((bf16[192,128]{1,0:T(8,128)(2,1)S(1)}, bf16[192,128]{1,0:T(8,128)(2,1)S(1)}, u32[]{:S(2)}, u32[]{:S(2)}) %collective-permute-start.11) | collective-permute-done | bytes 49184 | tf_op jit(solution)/shard_map/ppermute | solution.py:185
  43.3 0.0 collective-permute-done.12.refs_2_
  43.3 1.1 %collective-permute-done.13.refs_3_ = bf16[192,128]{1,0:T(8,128)(2,1)S(1)} collective-permute-done((bf16[192,128]{1,0:T(8,128)(2,1)S(1)}, bf16[192,128]{1,0:T(8,128)(2,1)S(1)}, u32[]{:S(2)}, u32[]{:S(2)}) %collective-permute-start.13) | collective-permute-done | bytes 49184 | tf_op jit(solution)/shard_map/ppermute | solution.py:185
  44.5 0.0 collective-permute-done.15.refs_6_
  44.5 0.8 %means.1 = (f32[2,64,128]{2,1,0:T(8,128)}, f32[64,128]{1,0:T(8,128)}, bf16[128,512]{1,0:T(8,128)(2,1)}, bf16[128,512]{1,0:T(8,128)(2,1)}) custom-call(f32[192,128]{1,0:T(8,128)S(1)} %get-tuple-element.63.refs_0_, bf16[192,128]{1,0:T(8,128)(2,1)S(1)} %collective-permute-done.11.refs_1_, bf16[192,128]{1,0:T(8,128)(2,1)S(1)} %collective-permute-done.12.refs_2_, ...), custom_call_target="tpu_custom_call" | custom-call | bytes 638976 | tf_op jit(solution)/shard_map/means/pallas_call | solution.py:142
  (9 shorter events, 0.1 us)
Async XLA Ops:
  0.6 8.7 %copy-start = (bf16[2,512,512]{2,1,0:T(8,128)(2,1)S(1)}, bf16[2,512,512]{2,1,0:T(8,128)(2,1)}, u32[]{:S(2)}) copy-start(bf16[2,512,512]{2,1,0:T(8,128)(2,1)} %param.12) | copy-start | bytes 3145732
  2.3 8.7 %collective-permute-start = (bf16[3,128,128]{2,1,0:T(8,128)(2,1)S(1)}, bf16[3,128,128]{2,1,0:T(8,128)(2,1)S(1)}, u32[]{:S(2)}, u32[]{:S(2)}) collective-permute-start(bf16[3,128,128]{2,1,0:T(8,128)(2,1)S(1)} %get-tuple-element.41), channel_id=1, source_target_pairs={{0,1},{1,2},{2,3},{3,0},{4,5},{5,6},{6,7},{7,4},{8,9},{9,10},{10,1... | collective-permute-start | bytes 294920 | tf_op jit(solution)/shard_map/ppermute | solution.py:185
  5.4 9.2 %collective-permute-start.1 = (bf16[3,128,128]{2,1,0:T(8,128)(2,1)S(1)}, bf16[3,128,128]{2,1,0:T(8,128)(2,1)S(1)}, u32[]{:S(2)}, u32[]{:S(2)}) collective-permute-start(bf16[3,128,128]{2,1,0:T(8,128)(2,1)S(1)} %get-tuple-element.42), channel_id=1, source_target_pairs={{0,2},{1,3},{2,0},{3,1},{4,6},{5,7},{6,4},{7,5},{8,10},{9,11},{10,... | collective-permute-start | bytes 294920 | tf_op jit(solution)/shard_map/ppermute | solution.py:185
  8.0 6.6 %collective-permute-start.2 = (bf16[3,128,128]{2,1,0:T(8,128)(2,1)S(1)}, bf16[3,128,128]{2,1,0:T(8,128)(2,1)S(1)}, u32[]{:S(2)}, u32[]{:S(2)}) collective-permute-start(bf16[3,128,128]{2,1,0:T(8,128)(2,1)S(1)} %get-tuple-element.43), channel_id=1, source_target_pairs={{0,3},{1,0},{2,1},{3,2},{4,7},{5,4},{6,5},{7,6},{8,11},{9,8},{10,9... | collective-permute-start | bytes 294920 | tf_op jit(solution)/shard_map/ppermute | solution.py:185
  9.3 1.0 %copy-start.1 = (bf16[512,256]{1,0:T(8,128)(2,1)S(1)}, bf16[512,256]{1,0:T(8,128)(2,1)}, u32[]{:S(2)}) copy-start(bf16[512,256]{1,0:T(8,128)(2,1)} %constant.25.clone.high.refs_5_.refs_8_) | copy-start | bytes 786436
  9.3 1.0 %copy-start.2 = (bf16[512,256]{1,0:T(8,128)(2,1)S(1)}, bf16[512,256]{1,0:T(8,128)(2,1)}, u32[]{:S(2)}) copy-start(bf16[512,256]{1,0:T(8,128)(2,1)} %constant.26.clone.low.refs_6_.refs_9_) | copy-start | bytes 786436
  10.4 4.2 %copy-start.5 = (bf16[256,512]{1,0:T(8,128)(2,1)S(1)}, bf16[256,512]{1,0:T(8,128)(2,1)}, u32[]{:S(2)}) copy-start(bf16[256,512]{1,0:T(8,128)(2,1)} %constant.27.clone.refs_7_.refs_10_) | copy-start | bytes 786436
  16.1 6.7 %collective-permute-start.3 = (bf16[128,128]{1,0:T(8,128)(2,1)S(1)}, bf16[128,128]{1,0:T(8,128)(2,1)S(1)}, u32[]{:S(2)}, u32[]{:S(2)}) collective-permute-start(bf16[128,128]{1,0:T(8,128)(2,1)S(1)} %get-tuple-element.45), channel_id=1, source_target_pairs={{0,1},{1,2},{2,3},{3,0},{4,5},{5,6},{6,7},{7,4},{8,9},{9,10},{10,1... | collective-permute-start | bytes 98312 | tf_op jit(solution)/shard_map/ppermute | solution.py:185
  18.7 4.9 %collective-permute-start.4 = (bf16[128,128]{1,0:T(8,128)(2,1)S(1)}, bf16[128,128]{1,0:T(8,128)(2,1)S(1)}, u32[]{:S(2)}, u32[]{:S(2)}) collective-permute-start(bf16[128,128]{1,0:T(8,128)(2,1)S(1)} %get-tuple-element.46), channel_id=1, source_target_pairs={{0,2},{1,3},{2,0},{3,1},{4,6},{5,7},{6,4},{7,5},{8,10},{9,11},{10,... | collective-permute-start | bytes 98312 | tf_op jit(solution)/shard_map/ppermute | solution.py:185
  20.3 3.9 %collective-permute-start.5 = (bf16[128,128]{1,0:T(8,128)(2,1)S(1)}, bf16[128,128]{1,0:T(8,128)(2,1)S(1)}, u32[]{:S(2)}, u32[]{:S(2)}) collective-permute-start(bf16[128,128]{1,0:T(8,128)(2,1)S(1)} %get-tuple-element.47), channel_id=1, source_target_pairs={{0,3},{1,0},{2,1},{3,2},{4,7},{5,4},{6,5},{7,6},{8,11},{9,8},{10,9... | collective-permute-start | bytes 98312 | tf_op jit(solution)/shard_map/ppermute | solution.py:185
  21.1 3.1 %copy-start.4 = (bf16[1,128,512]{2,1,0:T(8,128)(2,1)S(1)}, bf16[1,128,512]{2,1,0:T(8,128)(2,1)}, u32[]{:S(2)}) copy-start(bf16[1,128,512]{2,1,0:T(8,128)(2,1)} %refs_2_.1) | copy-start | bytes 393220
  21.2 3.1 %copy-start.6 = (bf16[1,128,512]{2,1,0:T(8,128)(2,1)S(1)}, bf16[1,128,512]{2,1,0:T(8,128)(2,1)}, u32[]{:S(2)}) copy-start(bf16[1,128,512]{2,1,0:T(8,128)(2,1)} %refs_4_.1) | copy-start | bytes 393220
  24.8 1.8 %collective-permute-start.6 = (bf16[384,512]{1,0:T(8,128)(2,1)S(1)}, bf16[384,512]{1,0:T(8,128)(2,1)S(1)}, u32[]{:S(2)}, u32[]{:S(2)}) collective-permute-start(bf16[384,512]{1,0:T(8,128)(2,1)S(1)} %get-tuple-element.57), channel_id=1, source_target_pairs={{0,4},{4,0},{8,12},{12,8},{16,20},{20,16},{24,28},{28,24},{1,5},{5... | collective-permute-start | bytes 1179656 | tf_op jit(solution)/shard_map/ppermute | solution.py:425
  24.9 9.6 %collective-permute-start.14 = (bf16[4,128,128]{2,1,0:T(8,128)(2,1)S(1)}, bf16[4,128,128]{2,1,0:T(8,128)(2,1)S(1)}, u32[]{:S(2)}, u32[]{:S(2)}) collective-permute-start(bf16[4,128,128]{2,1,0:T(8,128)(2,1)S(1)} %get-tuple-element.68), channel_id=1, source_target_pairs={{0,2},{1,3},{2,0},{3,1},{4,6},{5,7},{6,4},{7,5},{8,10},{9,11},{10,... | collective-permute-start | bytes 393224 | tf_op jit(solution)/shard_map/ppermute | solution.py:483
  26.6 3.6 %copy-start.3 = (bf16[512,512]{1,0:T(8,128)(2,1)S(1)}, bf16[512,512]{1,0:T(8,128)(2,1)}, u32[]{:S(2)}) copy-start(bf16[512,512]{1,0:T(8,128)(2,1)} %weight_ref.1) | copy-start | bytes 1572868
  26.7 7.8 %collective-permute-start.8 = (bf16[64,512]{1,0:T(8,128)(2,1)S(1)}, bf16[64,512]{1,0:T(8,128)(2,1)S(1)}, u32[]{:S(2)}, u32[]{:S(2)}) collective-permute-start(bf16[64,512]{1,0:T(8,128)(2,1)S(1)} %get-tuple-element.60), channel_id=1, source_target_pairs={{0,8},{4,12},{8,0},{12,4},{16,24},{20,28},{24,16},{28,20},{1,9},{5... | collective-permute-start | bytes 196616 | tf_op jit(solution)/shard_map/ppermute | solution.py:455
  28.3 6.3 %collective-permute-start.9 = (bf16[64,512]{1,0:T(8,128)(2,1)S(1)}, bf16[64,512]{1,0:T(8,128)(2,1)S(1)}, u32[]{:S(2)}, u32[]{:S(2)}) collective-permute-start(bf16[64,512]{1,0:T(8,128)(2,1)S(1)} %get-tuple-element.61), channel_id=1, source_target_pairs={{0,16},{4,20},{8,24},{12,28},{16,0},{20,4},{24,8},{28,12},{1,17},{... | collective-permute-start | bytes 196616 | tf_op jit(solution)/shard_map/ppermute | solution.py:455
  29.8 5.2 %collective-permute-start.10 = (bf16[64,512]{1,0:T(8,128)(2,1)S(1)}, bf16[64,512]{1,0:T(8,128)(2,1)S(1)}, u32[]{:S(2)}, u32[]{:S(2)}) collective-permute-start(bf16[64,512]{1,0:T(8,128)(2,1)S(1)} %get-tuple-element.62), channel_id=1, source_target_pairs={{0,24},{4,28},{8,16},{12,20},{16,8},{20,12},{24,0},{28,4},{1,25},{... | collective-permute-start | bytes 196616 | tf_op jit(solution)/shard_map/ppermute | solution.py:455
  30.3 7.0 %collective-permute-start.7 = (bf16[128,512]{1,0:T(8,128)(2,1)S(1)}, bf16[128,512]{1,0:T(8,128)(2,1)S(1)}, u32[]{:S(2)}, u32[]{:S(2)}) collective-permute-start(bf16[128,512]{1,0:T(8,128)(2,1)S(1)} %get-tuple-element.59), channel_id=1, source_target_pairs={{0,4},{1,9},{2,18},{3,27},{4,0},{5,13},{6,22},{7,31},{8,12},{9,1},... | collective-permute-start | bytes 393224 | tf_op jit(solution)/shard_map/ppermute | solution.py:461
  35.0 9.5 %collective-permute-start.15 = (bf16[4,128,128]{2,1,0:T(8,128)(2,1)S(1)}, bf16[4,128,128]{2,1,0:T(8,128)(2,1)S(1)}, u32[]{:S(2)}, u32[]{:S(2)}) collective-permute-start(bf16[4,128,128]{2,1,0:T(8,128)(2,1)S(1)} %turn.1), channel_id=1, source_target_pairs={{0,1},{1,0},{2,3},{3,2},{4,5},{5,4},{6,7},{7,6},{8,9},{9,8},{10,11... | collective-permute-start | bytes 393224 | tf_op jit(solution)/shard_map/ppermute | solution.py:493
  37.4 5.9 %collective-permute-start.11 = (bf16[192,128]{1,0:T(8,128)(2,1)S(1)}, bf16[192,128]{1,0:T(8,128)(2,1)S(1)}, u32[]{:S(2)}, u32[]{:S(2)}) collective-permute-start(bf16[192,128]{1,0:T(8,128)(2,1)S(1)} %get-tuple-element.64), channel_id=1, source_target_pairs={{0,1},{1,2},{2,3},{3,0},{4,5},{5,6},{6,7},{7,4},{8,9},{9,10},{10,1... | collective-permute-start | bytes 147464 | tf_op jit(solution)/shard_map/ppermute | solution.py:185
  37.8 5.5 %collective-permute-start.12 = (bf16[192,128]{1,0:T(8,128)(2,1)S(1)}, bf16[192,128]{1,0:T(8,128)(2,1)S(1)}, u32[]{:S(2)}, u32[]{:S(2)}) collective-permute-start(bf16[192,128]{1,0:T(8,128)(2,1)S(1)} %get-tuple-element.65), channel_id=1, source_target_pairs={{0,2},{1,3},{2,0},{3,1},{4,6},{5,7},{6,4},{7,5},{8,10},{9,11},{10,... | collective-permute-start | bytes 147464 | tf_op jit(solution)/shard_map/ppermute | solution.py:185
  40.4 4.1 %collective-permute-start.13 = (bf16[192,128]{1,0:T(8,128)(2,1)S(1)}, bf16[192,128]{1,0:T(8,128)(2,1)S(1)}, u32[]{:S(2)}, u32[]{:S(2)}) collective-permute-start(bf16[192,128]{1,0:T(8,128)(2,1)S(1)} %get-tuple-element.66), channel_id=1, source_target_pairs={{0,3},{1,0},{2,1},{3,2},{4,7},{5,4},{6,5},{7,6},{8,11},{9,8},{10,9... | collective-permute-start | bytes 147464 | tf_op jit(solution)/shard_map/ppermute | solution.py:185

commit v6 on v4

--- a/solution.py
+++ b/solution.py
@@ -225,8 +225,7 @@
                 for index in range(2):
                     out[index] = pick_columns(whole.at[index], held(ahead(step)), cols, seq)
 
-    triple, pair = [((count, rows, cols), BF16) for count in (3, 2)]
-    single = ((rows, cols), BF16)
+    triple = ((3, rows, cols), BF16)
     wide_bf16 = ((rows, width), BF16)
     with jax.named_scope("load"):
         sends = call(
@@ -247,19 +246,38 @@
         )
     parts_in = around(sends)
 
-    def filter_kernel(filters_ref, high, low, out):
+    def across(far):
+        return [(i, i ^ far) for i in range(seq)]
+
+    def filter_kernel(filters_ref, high, low, cot_ref, gate_ref, out, *beside):
+        if fast:
+            beside[0][:, :width] = cot_ref[...]
+            for index, far in enumerate((1, 3)):
+                piece = pick_columns(gate_ref, held(lax.axis_index("ctx") ^ far), cols, seq)
+                beside[0][:, width + index * cols : width + (index + 1) * cols] = piece
         for index in range(2):
             out[index] = with_previous(to_spectra(high, low, filters_ref[index]), cols)
 
     with jax.named_scope("filter_spectra"):
         own_filters = lax.dynamic_slice_in_dim(filters, held(lax.axis_index("ctx")) * cols, cols, 2)
-        (filter_spectra,) = call(
+        filter_spectra, *sends = call(
             filter_kernel,
-            [((2, *spectra_shape), F32)],
-            (own_filters, fwd_high, fwd_low),
+            [((2, *spectra_shape), F32)] + [((rows, width + 2 * cols), BF16)] * fast,
+            (own_filters, fwd_high, fwd_low, grad_out[0], gate_two[0]),
             flops=4 * table_flops,
             limit=limit,
         )
+    if fast:
+        beside_in = lax.ppermute(sends[0], "ctx", across(1))
+
+    def put_result(outs, index, total, arrays):
+        if len(outs) == seq:
+            for step, out in enumerate(outs):
+                out[index] = pick_rows(total, ahead(step), rows).astype(BF16)
+            return
+        for far in range(4):
+            piece = pick_rows(total, lax.axis_index("ctx") ^ far, rows).astype(BF16)
+            outs[far // 2][far % 2 * arrays + index] = piece
 
     def forward_kernel(*refs):
         parts, refs = refs[:seq], refs[seq:]
@@ -280,28 +298,23 @@
         conv = from_spectra(back, causal_product(filt[1], spectra, cols))
         for i in range(length // block):
             second[i * block : (i + 1) * block] = columns(conv, i, cols)
-        for step, out in enumerate(outs):
-            out[...] = pick_rows(second, ahead(step), rows).astype(BF16)
+        put_result(outs, 0, second, 1)
 
     with jax.named_scope("forward_convolutions"):
         first_conv, value_spectra, mixed_spectra, *sends = call(
             forward_kernel,
-            [((length, cols), F32), (spectra_shape, F32), (spectra_shape, F32)] + [single] * seq,
+            [((length, cols), F32), (spectra_shape, F32), (spectra_shape, F32)]
+            + ([((2, rows, cols), BF16)] * 2 if fast else [((1, rows, cols), BF16)] * seq),
             (*parts_in, filter_spectra, fwd_high, fwd_low, inv_high),
             scratch=[pltpu.VMEM((length, cols), BF16), pltpu.VMEM((length, cols), F32)],
             flops=6 * table_flops,
             limit=limit,
         )
-    second_parts = around(sends)
-
-    def put_result(outs, index, total):
-        if not fast:
-            for step, out in enumerate(outs):
-                out[index] = pick_rows(total, ahead(step), rows).astype(BF16)
-            return
-        for far in range(4):
-            place = lax.axis_index("ctx") ^ far
-            outs[far % 2][far // 2 * 2 + index] = pick_rows(total, place, rows).astype(BF16)
+    if fast:
+        second_stays, goes = sends
+        second_near = lax.ppermute(goes, "ctx", across(2))
+    else:
+        second_parts = around(sends)
 
     def backward_kernel(*refs):
         parts, refs = refs[:seq], refs[seq:]
@@ -330,17 +343,17 @@
             grad = pick_rows(total, behind(step), rows)
             put_rows(stream, behind(step), rows, (grad * part[1].astype(F32)).astype(BF16))
         total[...] = total[...] * first_ref[...]
-        put_result(outs, 0, total)
+        put_result(outs, 0, total, 2)
         out = both(filt[0], value_spec[...])
         for i in range(count):
             total[i * block : (i + 1) * block] = columns(out, i, cols)
-        put_result(outs, 1, total)
+        put_result(outs, 1, total, 2)
         put_lags(0, out)
 
     with jax.named_scope("backward_convolutions"):
         lags, *sends_home = call(
             backward_kernel,
-            [((2, length, cols), F32)] + ([((4, rows, cols), BF16)] * 2 if fast else [pair] * seq),
+            [((2, length, cols), F32)] + [((2, rows, cols), BF16)] * seq,
             (
                 *parts_in,
                 filter_spectra,
@@ -356,199 +369,131 @@
             limit=limit,
         )
 
-    def home_core(core):
-        return jnp.where(lax.axis_index("ctx") == 0, 1 - core, core)
-
-    core = lax.rem(lax.axis_index("dp"), 2)
-    chip = lax.div(lax.axis_index("dp"), 2)
-    term_shape = (width // 2 + rows, width)
-
-    def gated_kernel(*refs):
-        parts, refs = refs[:seq], refs[seq:]
-        gate_ref, cot_ref, lags, second_ref, gated_ref = refs[:5]
-        for step, part in enumerate(parts):
-            put_columns(second_ref, held(behind(step)), cols, seq, part[...])
-        gated = (gate_ref[...].astype(F32) * second_ref[...].astype(F32)).astype(BF16)
-        gated_ref[...] = gated
-        partial = lax.dot_general(
-            gated, cot_ref[...], (((0,), (0,)), ((), ())), preferred_element_type=F32
-        )
-        if not fast:
-            refs[5][...] = partial
-            return
-        kept, given, whole, packed = refs[5:]
-        whole[...] = partial
-        lower = lax.broadcasted_iota(jnp.int32, (length, cols), 1) < fine
-        packed[0] = jnp.where(lower, lags[0], pltpu.roll(lags[1], fine, axis=1))
-        packed[1] = jnp.where(lower, pltpu.roll(lags[0], fine, axis=1), lags[1])
-        own_core = lax.rem(lax.axis_index("dp"), 2)
-        turn = home_core(own_core)
-        for out, which, lag_which in ((kept, own_core, turn), (given, 1 - own_core, 1 - turn)):
-            for index in range(chips):
-                start = pl.multiple_of((2 * index + which) * own_rows, own_rows)
-                piece = whole[pl.ds(start, own_rows), :]
-                out[index * own_rows : (index + 1) * own_rows] = piece.astype(out.dtype)
-            for index in range(seq):
-                piece = packed[lag_which, index * rows : (index + 1) * rows]
-                out[width // 2 :, index * cols : (index + 1) * cols] = piece.astype(out.dtype)
-
-    with jax.named_scope("weight_partial"):
-        second_conv, gated, *terms = call(
-            gated_kernel,
-            [wide_bf16, wide_bf16]
-            + ([(term_shape, F32), (term_shape, BF16)] if fast else [((width, width), F32)]),
-            (*second_parts, gate_two[0], grad_out[0], lags),
-            scratch=[pltpu.VMEM((width, width), F32), pltpu.VMEM((2, length, cols), F32)]
-            if fast
-            else [],
-            flops=2 * rows * width * width,
-            limit=limit,
-        )
-
-    if not fast:
-        lag_terms = lags.reshape(2, seq, rows, per_ctx, fine).transpose(1, 3, 2, 0, 4)
-        lag_rows = rows * 2 * fine // width
-        terms = jnp.concatenate(
-            [
-                terms[0].reshape(data, own_rows, width),
-                lag_terms.reshape(data, lag_rows, width),
-            ],
-            axis=1,
-        )
-        by_core = terms.reshape(chips, 2, *terms.shape[1:])
-        kept = lax.dynamic_index_in_dim(by_core, core, 1, keepdims=False)
-        given = lax.dynamic_index_in_dim(by_core, 1 - core, 1, keepdims=False).astype(BF16)
-        given, kept = (a.reshape(-1, width) for a in (given, kept))
-    else:
-        kept, given = terms
-        lag_rows = 0
-    taken = lax.ppermute(given, "dp", [(i, i ^ 1) for i in range(data)])
-    term_rows = own_rows + lag_rows
-
-    def chip_kernel(kept_ref, taken_ref, own, *outs):
-        place = lax.div(lax.axis_index("dp"), 2)
-
-        def summed(index):
-            start = pl.multiple_of(index * term_rows, term_rows)
-            taken = taken_ref[pl.ds(start, term_rows), :]
-            return kept_ref[pl.ds(start, term_rows), :] + taken.astype(F32)
-
-        own[...] = summed(place)
-        for step in range(1, chips):
-            outs[step - 1][...] = summed(place ^ step).astype(BF16)
-        if fast:
-            outs[-1][...] = (kept_ref[width // 2 :] + taken_ref[width // 2 :].astype(F32)).astype(
-                BF16
+    if fast:
+        def gated_kernel(*refs):
+            stays_ref, near_ref, gate_ref, cot_ref, beside_ref, lags, *refs = refs
+            kept, given, turned, gated, cots, whole, packed = refs
+            turned[0] = stays_ref[1]
+            turned[1] = near_ref[1]
+            here = lax.axis_index("ctx")
+            cots[:rows] = cot_ref[...]
+            cots[rows:] = beside_ref[:, :width]
+            for index, ref in enumerate((stays_ref, near_ref)):
+                lanes = pl.ds(index * cols, cols)
+                gate = pick_columns(gate_ref, held(here ^ (2 * index)), cols, seq)
+                gated[:rows, lanes] = (gate.astype(F32) * ref[0].astype(F32)).astype(BF16)
+                gate = columns(beside_ref, width // cols + index, cols)
+                gated[rows:, lanes] = (gate.astype(F32) * ref[1].astype(F32)).astype(BF16)
+            whole[...] = lax.dot_general(
+                gated[...], cots[...], (((0,), (0,)), ((), ())), preferred_element_type=F32
             )
-
-    term = (term_rows, width)
-    with jax.named_scope("core_sum"):
-        own_term, *sends = call(
-            chip_kernel,
-            [(term, F32)] + [(term, BF16)] * (chips - 1) + [((rows, width), BF16)] * fast,
-            (kept, taken),
-            limit=limit,
-        )
-    chip_terms = []
-    for step in range(1, chips):
-        pairs = [(i, i ^ (2 * step)) for i in range(data)]
-        chip_terms.append(lax.ppermute(sends[step - 1], "dp", pairs))
-    if fast:
-        pairs = []
-        for i in range(data):
-            pairs.append((i * seq, (i ^ 1) * seq))
-            pairs += [(i * seq + j, (i ^ (2 * j)) * seq + j) for j in range(1, seq)]
-        lag_term = lax.ppermute(sends[-1], ("dp", "ctx"), pairs)
-
-    def across(far):
-        return [(i, i ^ far) for i in range(seq)]
-
-    if fast:
-        stays, goes = sends_home
-        near = lax.ppermute(goes, "ctx", across(1))
-
-        def turn_kernel(stays_ref, near_ref, _, out):
-            out[:2] = stays_ref[2:]
-            out[2:] = near_ref[2:]
-
-        with jax.named_scope("turn"):
-            (goes,) = call(turn_kernel, [((4, rows, cols), BF16)], (stays, near, chip_terms[0]))
-        home = [stays, near, lax.ppermute(goes, "ctx", across(2))]
-    else:
+            lower = lax.broadcasted_iota(jnp.int32, (length, cols), 1) < fine
+            packed[0] = jnp.where(lower, lags[0], pltpu.roll(lags[1], fine, axis=1))
+            packed[1] = jnp.where(lower, pltpu.roll(lags[0], fine, axis=1), lags[1])
+            own_core = lax.rem(lax.axis_index("dp"), 2)
+            first = jnp.where(here == 0, 1 - own_core, own_core)
+            second = jnp.where(here == 2, 1 - own_core, own_core)
+            for out, one, two in ((kept, first, second), (given, 1 - first, 1 - second)):
+                piece = whole[pl.ds(pl.multiple_of(one * own_rows, own_rows), own_rows), :]
+                out[:own_rows] = piece.astype(out.dtype)
+                for index in range(seq):
+                    piece = packed[one, index * rows : (index + 1) * rows]
+                    out[own_rows : own_rows + rows, index * cols : (index + 1) * cols] = (
+                        piece.astype(out.dtype)
+                    )
+                start = pl.multiple_of(cols + two * own_rows, own_rows)
+                out[own_rows + rows :] = whole[pl.ds(start, own_rows), :].astype(out.dtype)
+
+        term_shape = (2 * own_rows + rows, width)
+        with jax.named_scope("weight_partial"):
+            kept, given, goes_on = call(
+                gated_kernel,
+                [(term_shape, F32), (term_shape, BF16), ((2, rows, cols), BF16)],
+                (second_stays, second_near, gate_two[0], grad_out[0], beside_in, lags),
+                scratch=[
+                    pltpu.VMEM((2 * rows, 2 * cols), BF16),
+                    pltpu.VMEM((2 * rows, width), BF16),
+                    pltpu.VMEM((2 * cols, width), F32),
+                    pltpu.VMEM((2, length, cols), F32),
+                ],
+                limit=limit,
+            )
+        taken = lax.ppermute(given, "dp", [(i, i ^ 1) for i in range(data)])
+        second_far = lax.ppermute(goes_on, "ctx", across(1))
+
+        def core_kernel(kept_ref, taken_ref, one, two):
+            summed = (kept_ref[...] + taken_ref[...].astype(F32)).astype(BF16)
+            one[...] = summed[: own_rows + rows]
+            two[...] = summed[own_rows + rows :]
+
+        with jax.named_scope("core_sum"):
+            sends = call(
+                core_kernel,
+                [((own_rows + rows, width), BF16), ((own_rows, width), BF16)],
+                (kept, taken),
+                limit=limit,
+            )
+
+        def to_chip(block, other):
+            pairs = []
+            for i in range(data):
+                for j in range(seq):
+                    pairs.append((i * seq + j, (i ^ (2 * (j ^ other) or 1)) * seq + j))
+            return lax.ppermute(block, ("dp", "ctx"), pairs)
+
+        chip_terms = [to_chip(sends[0], 0), to_chip(sends[1], 2)]
+
         home = around(sends_home)
 
-    def mixed_kernel(gated_ref, weight_ref, cot_ref, second_ref, mixed_ref, gate_ref, mark):
-        mark[...] = jnp.zeros_like(mark)
-        mixed_ref[...] = mxu(gated_ref[...], weight_ref[...]).astype(BF16)
-        grad = grad_gated(cot_ref, weight_ref)
-        gate_ref[...] = (grad * second_ref[...].astype(F32)).astype(BF16)
-
-    with jax.named_scope("mixed"):
-        mixed, grad_gate_two, mark = call(
-            mixed_kernel,
-            [wide_bf16, wide_bf16, ((8, 128), F32)],
-            (gated, out_weight, grad_out[0], second_conv),
-            flops=4 * rows * width * width,
-            limit=limit,
-        )
-
-    if fast:
-
-        def place_kernel(mark, own, lag, *refs):
-            arrived, outs, total = refs[: chips - 1], refs[chips - 1 : -1], refs[-1]
-            summed = own[...]
-            for part in arrived:
-                summed = summed + part[...].astype(F32)
-            total[...] = summed
+        def place_kernel(one, two, *refs):
+            outs, total = refs[:-1], refs[-1]
+            total[...] = one[:own_rows].astype(F32) + two[...].astype(F32)
             for step, out in enumerate(outs):
                 out[:own_rows] = pick_columns(total, ahead(step), cols, seq).astype(out.dtype)
-                out[own_rows:] = pick_columns(lag, ahead(step), cols, seq).astype(out.dtype)
+                lag = pick_columns(one, ahead(step), cols, seq)[own_rows:]
+                out[own_rows:] = lag.astype(out.dtype)
 
         small = (own_rows + rows, cols)
         with jax.named_scope("chip_sum"):
             sends = call(
                 place_kernel,
                 [(small, F32)] + [(small, BF16)] * (seq - 1),
-                (mark, own_term, lag_term, *chip_terms),
+                chip_terms,
                 scratch=[pltpu.VMEM((own_rows, width), F32)],
             )
-    else:
-        total = own_term
-        for part in chip_terms:
-            total = total + part.astype(F32)
-        weight_blocks = total[:own_rows].reshape(own_rows, seq, cols)
-        sends = [
-            lax.dynamic_index_in_dim(weight_blocks, ahead(step), 1, keepdims=False)
-            for step in range(seq)
-        ]
-        sends = sends[:1] + [part.astype(BF16) for part in sends[1:]]
-        lag_sum = total[own_rows:].reshape(rows, 2 * fine).astype(BF16)
-        pairs = []
-        for i in range(data):
-            for j in range(seq):
-                pairs.append((i * seq + j, (per_ctx * j + i % per_ctx) * seq + i // per_ctx))
-        lag_own = lax.ppermute(lag_sum, ("dp", "ctx"), pairs)
-    last_terms = around(sends)
-
-    def unpack_kernel(*refs):
-        parts, (gate_ref, value_ref) = refs[:-2], refs[-2:]
-        if fast:
+        last_terms = around(sends)
+
+        def mixed_kernel(*refs):
+            parts, (gate_ref, weight_ref, cot_ref, mixed_ref, out, second) = refs[:3], refs[3:]
+            here = lax.axis_index("ctx")
             stays_ref, near_ref, far_ref = parts
-            blocks = [(stays_ref, 0), (near_ref, 0), (far_ref, 0), (far_ref, 2)]
-            blocks = [(lax.axis_index("ctx") ^ far, *block) for far, block in enumerate(blocks)]
-        else:
-            blocks = [(behind(step), part, 0) for step, part in enumerate(parts)]
-        for place, part, first in blocks:
-            put_columns(gate_ref, held(place), cols, seq, part[first])
-            put_columns(value_ref, held(place), cols, seq, part[first + 1])
-
-    with jax.named_scope("unpack_results"):
-        grad_gate_one, grad_value = call(unpack_kernel, [wide_bf16, wide_bf16], home)
-
-    if fast:
+            put_columns(second, held(here), cols, seq, stays_ref[0])
+            put_columns(second, held(here ^ 2), cols, seq, near_ref[0])
+            put_columns(second, held(here ^ 1), cols, seq, far_ref[0])
+            put_columns(second, held(here ^ 3), cols, seq, far_ref[1])
+            wide = second[...].astype(F32)
+            gated = (gate_ref[...].astype(F32) * wide).astype(BF16)
+            mixed_ref[...] = mxu(gated, weight_ref[...]).astype(BF16)
+            out[...] = (grad_gated(cot_ref, weight_ref) * wide).astype(BF16)
+
+        with jax.named_scope("mixed"):
+            mixed, grad_gate_two = call(
+                mixed_kernel,
+                [wide_bf16, wide_bf16],
+                (second_stays, second_near, second_far, gate_two[0], out_weight, grad_out[0]),
+                scratch=[pltpu.VMEM((rows, width), BF16)],
+                flops=4 * rows * width * width,
+                limit=limit,
+            )
+
+        order = (0, 3, 2, 1)
 
         def final_kernel(*refs):
-            arrived, (filter_ref, weight_ref) = refs[:seq], refs[seq:]
+            arrived, parts, refs = refs[:seq], refs[seq : 2 * seq], refs[2 * seq :]
+            filter_ref, weight_ref, gate_ref, value_ref = refs
+            for step, part in zip(order, parts):
+                put_columns(gate_ref, held(behind(step)), cols, seq, part[0])
+                put_columns(value_ref, held(behind(step)), cols, seq, part[1])
             total = arrived[0][...]
             for part in arrived[1:]:
                 total = total + part[...].astype(F32)
@@ -559,13 +504,119 @@
             filter_ref[1] = turned[fine:]
 
         with jax.named_scope("means"):
-            filter_grad, weight_grad = call(
-                final_kernel, [((2, fine, rows), F32), ((own_rows, cols), F32)], last_terms
+            filter_grad, weight_grad, grad_gate_one, grad_value = call(
+                final_kernel,
+                [((2, fine, rows), F32), ((own_rows, cols), F32), wide_bf16, wide_bf16],
+                (*last_terms, *(home[step] for step in order)),
             )
         filter_grad = jnp.swapaxes(filter_grad, 1, 2)
-    else:
-        filter_grad = lag_own.reshape(rows, 2, fine).transpose(1, 0, 2).astype(F32) / data
-        weight_grad = sum(part.astype(F32) for part in last_terms) / data
+        return (
+            mixed[None],
+            grad_value[None],
+            grad_gate_one[None],
+            grad_gate_two[None],
+            filter_grad,
+            weight_grad,
+        )
+
+    def gated_kernel(*refs):
+        parts, (gate_ref, cot_ref, second_ref, gated_ref, weight_ref) = refs[:seq], refs[seq:]
+        for step, part in enumerate(parts):
+            put_columns(second_ref, held(behind(step)), cols, seq, part[0])
+        gated = (gate_ref[...].astype(F32) * second_ref[...].astype(F32)).astype(BF16)
+        gated_ref[...] = gated
+        weight_ref[...] = lax.dot_general(
+            gated, cot_ref[...], (((0,), (0,)), ((), ())), preferred_element_type=F32
+        )
+
+    with jax.named_scope("weight_partial"):
+        second_conv, gated, weight_part = call(
+            gated_kernel,
+            [wide_bf16, wide_bf16, ((width, width), F32)],
+            (*second_parts, gate_two[0], grad_out[0]),
+            flops=2 * rows * width * width,
+            limit=limit,
+        )
+
+    core = lax.rem(lax.axis_index("dp"), 2)
+    lag_terms = lags.reshape(2, seq, rows, per_ctx, fine).transpose(1, 3, 2, 0, 4)
+    lag_rows = rows * 2 * fine // width
+    terms = jnp.concatenate(
+        [
+            weight_part.reshape(data, own_rows, width),
+            lag_terms.reshape(data, lag_rows, width),
+        ],
+        axis=1,
+    )
+    by_core = terms.reshape(chips, 2, *terms.shape[1:])
+    kept = lax.dynamic_index_in_dim(by_core, core, 1, keepdims=False)
+    given = lax.dynamic_index_in_dim(by_core, 1 - core, 1, keepdims=False).astype(BF16)
+    given, kept = (a.reshape(-1, width) for a in (given, kept))
+    taken = lax.ppermute(given, "dp", [(i, i ^ 1) for i in range(data)])
+    term_rows = own_rows + lag_rows
+
+    def chip_kernel(kept_ref, taken_ref, own, *outs):
+        place = lax.div(lax.axis_index("dp"), 2)
+
+        def summed(index):
+            start = pl.multiple_of(index * term_rows, term_rows)
+            taken = taken_ref[pl.ds(start, term_rows), :]
+            return kept_ref[pl.ds(start, term_rows), :] + taken.astype(F32)
+
+        own[...] = summed(place)
+        for step in range(1, chips):
+            outs[step - 1][...] = summed(place ^ step).astype(BF16)
+
+    term = (term_rows, width)
+    with jax.named_scope("core_sum"):
+        total, *sends = call(
+            chip_kernel,
+            [(term, F32)] + [(term, BF16)] * (chips - 1),
+            (kept, taken),
+            limit=limit,
+        )
+    for step in range(1, chips):
+        pairs = [(i, i ^ (2 * step)) for i in range(data)]
+        total = total + lax.ppermute(sends[step - 1], "dp", pairs).astype(F32)
+
+    def mixed_kernel(gated_ref, weight_ref, cot_ref, second_ref, mixed_ref, gate_ref):
+        mixed_ref[...] = mxu(gated_ref[...], weight_ref[...]).astype(BF16)
+        grad = grad_gated(cot_ref, weight_ref)
+        gate_ref[...] = (grad * second_ref[...].astype(F32)).astype(BF16)
+
+    with jax.named_scope("mixed"):
+        mixed, grad_gate_two = call(
+            mixed_kernel,
+            [wide_bf16, wide_bf16],
+            (gated, out_weight, grad_out[0], second_conv),
+            flops=4 * rows * width * width,
+            limit=limit,
+        )
+    home = around(sends_home)
+
+    weight_blocks = total[:own_rows].reshape(own_rows, seq, cols)
+    sends = [
+        lax.dynamic_index_in_dim(weight_blocks, ahead(step), 1, keepdims=False)
+        for step in range(seq)
+    ]
+    last_terms = around(sends[:1] + [part.astype(BF16) for part in sends[1:]])
+    lag_sum = total[own_rows:].reshape(rows, 2 * fine).astype(BF16)
+    pairs = []
+    for i in range(data):
+        for j in range(seq):
+            pairs.append((i * seq + j, (per_ctx * j + i % per_ctx) * seq + i // per_ctx))
+    lag_own = lax.ppermute(lag_sum, ("dp", "ctx"), pairs)
+
+    def unpack_kernel(*refs):
+        parts, (gate_ref, value_ref) = refs[:-2], refs[-2:]
+        for step, part in enumerate(parts):
+            put_columns(gate_ref, held(behind(step)), cols, seq, part[0])
+            put_columns(value_ref, held(behind(step)), cols, seq, part[1])
+
+    with jax.named_scope("unpack_results"):
+        grad_gate_one, grad_value = call(unpack_kernel, [wide_bf16, wide_bf16], home)
+    filter_grad = lag_own.reshape(rows, 2, fine).transpose(1, 0, 2).astype(F32) / data
+    weight_grad = sum(part.astype(F32) for part in last_terms) / data
     return (
         mixed[None],
         grad_value[None],

time: 48.2 us -> 43.1 us (0.89)
  waiting for transfers between devices: 14.6 us -> 9.28 us
  starting transfers between devices: 23.1 us -> 24.2 us
  Pallas kernels: 8.57 us -> 7.65 us
    ppermute x9, starting transfers between devices: 16.6 us -> 20.6 us  [around(): out.append(lax.ppermute(blocks[step], 'ctx', pairs))]
    ppermute x9, waiting for transfers between devices: 7.79 us -> 4.58 us  [around(): out.append(lax.ppermute(blocks[step], 'ctx', pairs))]
    ppermute x6 -> x5, starting transfers between devices: 6.46 us -> 3.55 us  [the longest x2 1.73 us: to_chip(): return lax.ppermute(block, ('dp', 'ctx'), pairs)]
    ppermute x6 -> x5, waiting for transfers between devices: 5.45 us -> 3.18 us  [the longest x1 3.17 us: on_device(): second_near = lax.ppermute(goes, 'ctx', across(2))]
    pallas_call x11 -> x9, Pallas kernels: 8.57 us -> 7.65 us  [call(): pl.pallas_call(kernel, out_shape=[jax.ShapeDtypeStruct(shape, dtype) for...]
  transfers between devices with their start and end apart: 16 -> 15, of which waited for: 11 -> 6; matrix products, arithmetic and copies ran while one was open for 0% -> 0% of each run, Pallas kernels for 8% -> 11%
where the time goes in v6:
time: 43.1 us; the launch traced here: 43 us
  starting transfers between devices  24.2 us (56%)
  waiting for transfers between devices  9.28 us (22%)
  Pallas kernels  7.65 us (18%)
  local copies, waits for them, and re-layouts  1.03 us (2%)
  between operations  0.75 us (2%)
    ppermute x9, starting transfers between devices, around(): out.append(lax.ppermute(blocks[step], 'ctx', pairs))  20.6 us
    pallas_call x9, Pallas kernels, call(): pl.pallas_call(kernel, out_shape=[jax.ShapeDtypeStruct(shape, dtype) for...  7.65 us
    ppermute x9, waiting for transfers between devices, around(): out.append(lax.ppermute(blocks[step], 'ctx', pairs))  4.58 us
    ppermute x1, waiting for transfers between devices, on_device(): second_near = lax.ppermute(goes, 'ctx', across(2))  3.17 us
    ppermute x2, starting transfers between devices, to_chip(): return lax.ppermute(block, ('dp', 'ctx'), pairs)  1.73 us
    ppermute x1, waiting for transfers between devices, on_device(): taken = lax.ppermute(given, 'dp', [(i, i ^ 1) for i in range(data)])  1.52 us
    ppermute x1, starting transfers between devices, on_device(): second_near = lax.ppermute(goes, 'ctx', across(2))  1.07 us
    unnamed x14, local copies, waits for them, and re-layouts  0.99 us
  transfers between devices with their start and end apart: 15, of which 6 were waited for; matrix products, arithmetic and copies ran while one was open for 0% of the time, Pallas kernels for 11%

profile of v6, /device:TPU:0, one launch (start us, length us, event | category | flops | bytes accessed | tf_op | source)
XLA Modules:
  0.0 43.0 jit_solution(13178989898529240315)
XLA Ops:
  0.6 0.0 copy-start
  0.6 0.0 copy-start.4
  0.7 0.0 copy-start.5
  0.7 1.7 %load.1 = (bf16[3,128,128]{2,1,0:T(8,128)(2,1)S(1)}, bf16[3,128,128]{2,1,0:T(8,128)(2,1)S(1)}, bf16[3,128,128]{2,1,0:T(8,128)(2,1)S(1)}, bf16[3,128,128]{2,1,0:T(8,128)(2,1)S(1)}) custom-call(bf16[1,128,512]{2,1,0:T(8,128)(2,1)} %refs_0_.1, bf16[1,128,512]{2,1,0:T(8,128)(2,1)} %refs_1_.1, bf16[1,128,512]{2,1,0:T(8,128)(2,1)} %refs_2_.1, ...), custom_call_target="tpu_custom_call" | custom-call | flops 67108864 | bytes 1048576 | tf_op jit(solution)/shard_map/load/pallas_call | solution.py:142
  2.4 3.1 %collective-permute-start = (bf16[3,128,128]{2,1,0:T(8,128)(2,1)S(1)}, bf16[3,128,128]{2,1,0:T(8,128)(2,1)S(1)}, u32[]{:S(2)}, u32[]{:S(2)}) collective-permute-start(bf16[3,128,128]{2,1,0:T(8,128)(2,1)S(1)} %get-tuple-element.38), channel_id=1, source_target_pairs={{0,1},{1,2},{2,3},{3,0},{4,5},{5,6},{6,7},{7,4},{8,9},{9,10},{10,1... | collective-permute-start | bytes 294920 | tf_op jit(solution)/shard_map/ppermute | solution.py:185
  5.4 2.6 %collective-permute-start.1 = (bf16[3,128,128]{2,1,0:T(8,128)(2,1)S(1)}, bf16[3,128,128]{2,1,0:T(8,128)(2,1)S(1)}, u32[]{:S(2)}, u32[]{:S(2)}) collective-permute-start(bf16[3,128,128]{2,1,0:T(8,128)(2,1)S(1)} %get-tuple-element.39), channel_id=1, source_target_pairs={{0,2},{1,3},{2,0},{3,1},{4,6},{5,7},{6,4},{7,5},{8,10},{9,11},{10,... | collective-permute-start | bytes 294920 | tf_op jit(solution)/shard_map/ppermute | solution.py:185
  8.0 1.3 %collective-permute-start.2 = (bf16[3,128,128]{2,1,0:T(8,128)(2,1)S(1)}, bf16[3,128,128]{2,1,0:T(8,128)(2,1)S(1)}, u32[]{:S(2)}, u32[]{:S(2)}) collective-permute-start(bf16[3,128,128]{2,1,0:T(8,128)(2,1)S(1)} %get-tuple-element.40), channel_id=1, source_target_pairs={{0,3},{1,0},{2,1},{3,2},{4,7},{5,4},{6,5},{7,6},{8,11},{9,8},{10,9... | collective-permute-start | bytes 294920 | tf_op jit(solution)/shard_map/ppermute | solution.py:185
  9.4 0.0 copy-done
  9.4 0.0 copy-start.1
  9.4 0.0 copy-done.4
  9.4 0.0 copy-done.5
  9.4 0.9 %copy-done.1 = bf16[512,256]{1,0:T(8,128)(2,1)S(1)} copy-done((bf16[512,256]{1,0:T(8,128)(2,1)S(1)}, bf16[512,256]{1,0:T(8,128)(2,1)}, u32[]{:S(2)}) %copy-start.1) | copy-done | bytes 262168
  10.3 0.1 copy-done.2
  10.4 0.4 %filter_spectra.1 = (f32[2,512,256]{2,1,0:T(8,128)S(1)}, bf16[128,768]{1,0:T(8,128)(2,1)S(1)}) custom-call(bf16[2,512,128]{2,1,0:T(8,128)(2,1)S(1)} %constant_dynamic-slice_fusion.filters_ref, bf16[512,256]{1,0:T(8,128)(2,1)S(1)} %copy-done.1, bf16[512,256]{1,0:T(8,128)(2,1)S(1)} %copy-done.2, bf16[128,512]{1,0:T(8,128)(2,1)S(1)} %bitcast.7, ...), custom_call_target="tpu_custom_call" | custom-call | flops 268435456 | bytes 1048576 | tf_op jit(solution)/shard_map/filter_spectra/pallas_call | solution.py:142
  10.9 0.7 %collective-permute-start.4 = (bf16[128,768]{1,0:T(8,128)(2,1)S(1)}, bf16[128,768]{1,0:T(8,128)(2,1)S(1)}, u32[]{:S(2)}, u32[]{:S(2)}) collective-permute-start(bf16[128,768]{1,0:T(8,128)(2,1)S(1)} %get-tuple-element.44), channel_id=1, source_target_pairs={{0,1},{1,0},{2,3},{3,2},{4,5},{5,4},{6,7},{7,6},{8,9},{9,8},{10,11... | collective-permute-start | bytes 589832 | tf_op jit(solution)/shard_map/ppermute | solution.py:271
  11.6 0.0 collective-permute-done.refs_1_
  11.6 3.0 %collective-permute-done.1.refs_2_ = bf16[3,128,128]{2,1,0:T(8,128)(2,1)S(1)} collective-permute-done((bf16[3,128,128]{2,1,0:T(8,128)(2,1)S(1)}, bf16[3,128,128]{2,1,0:T(8,128)(2,1)S(1)}, u32[]{:S(2)}, u32[]{:S(2)}) %collective-permute-start.1) | collective-permute-done | bytes 98336 | tf_op jit(solution)/shard_map/ppermute | solution.py:185
  14.6 0.6 %collective-permute-done.2.refs_3_ = bf16[3,128,128]{2,1,0:T(8,128)(2,1)S(1)} collective-permute-done((bf16[3,128,128]{2,1,0:T(8,128)(2,1)S(1)}, bf16[3,128,128]{2,1,0:T(8,128)(2,1)S(1)}, u32[]{:S(2)}, u32[]{:S(2)}) %collective-permute-start.2) | collective-permute-done | bytes 98336 | tf_op jit(solution)/shard_map/ppermute | solution.py:185
  15.2 0.0 copy-done.6
  15.2 1.5 %forward_convolutions.1 = (f32[512,128]{1,0:T(8,128)S(1)}, f32[512,256]{1,0:T(8,128)S(1)}, f32[512,256]{1,0:T(8,128)S(1)}, bf16[2,128,128]{2,1,0:T(8,128)(2,1)S(1)}, bf16[2,128,128]{2,1,0:T(8,128)(2,1)S(1)}) custom-call(bf16[3,128,128]{2,1,0:T(8,128)(2,1)S(1)} %get-tuple-element.37.refs_0_, bf16[3,128,128]{2,1,0:T(8,128)(2,1)S(1)} %collective-permute-done.refs_1_, ...), custom_call_target="tpu_custom_call" | custom-call | flops 402653184 | bytes 2228224 | tf_op jit(solution)/shard_map/forward_convolutions/pallas_call | solution.py:142
  16.6 1.1 %collective-permute-start.3 = (bf16[2,128,128]{2,1,0:T(8,128)(2,1)S(1)}, bf16[2,128,128]{2,1,0:T(8,128)(2,1)S(1)}, u32[]{:S(2)}, u32[]{:S(2)}) collective-permute-start(bf16[2,128,128]{2,1,0:T(8,128)(2,1)S(1)} %get-tuple-element.43), channel_id=1, source_target_pairs={{0,2},{1,3},{2,0},{3,1},{4,6},{5,7},{6,4},{7,5},{8,10},{9,11},{10,... | collective-permute-start | bytes 196616 | tf_op jit(solution)/shard_map/ppermute | solution.py:315
  17.7 1.7 %backward_convolutions.1 = (f32[2,512,128]{2,1,0:T(8,128)S(1)}, bf16[2,128,128]{2,1,0:T(8,128)(2,1)S(1)}, bf16[2,128,128]{2,1,0:T(8,128)(2,1)S(1)}, bf16[2,128,1...) custom-call(bf16[3,128,128]{2,1,0:T(8,128)(2,1)S(1)} %get-tuple-element.37.refs_0_, ...), custom_call_target="tpu_custom_call" | custom-call | flops 536870912 | bytes 3538944 | tf_op jit(solution)/shard_map/backward_convolutions/pallas_call | solution.py:142
  19.4 3.2 %collective-permute-done.3.refs_1_ = bf16[2,128,128]{2,1,0:T(8,128)(2,1)S(1)} collective-permute-done((bf16[2,128,128]{2,1,0:T(8,128)(2,1)S(1)}, bf16[2,128,128]{2,1,0:T(8,128)(2,1)S(1)}, u32[]{:S(2)}, u32[]{:S(2)}) %collective-permute-start.3) | collective-permute-done | bytes 65568 | tf_op jit(solution)/shard_map/ppermute | solution.py:315
  22.6 0.0 collective-permute-done.4.refs_4_
  22.6 0.4 %weight_partial.1 = (f32[256,512]{1,0:T(8,128)S(1)}, bf16[256,512]{1,0:T(8,128)(2,1)S(1)}, bf16[2,128,128]{2,1,0:T(8,128)(2,1)S(1)}) custom-call(bf16[2,128,128]{2,1,0:T(8,128)(2,1)S(1)} %get-tuple-element.42.refs_0_, bf16[2,128,128]{2,1,0:T(8,128)(2,1)S(1)} %collective-permute-done.3.refs_1_, bf16[128,512]{1,0:T(8,128)(2,1)S(1)} %bitcast.11, ...), custom_call_target="tpu_custom_call" | custom-call | bytes 1114112 | tf_op jit(solution)/shard_map/weight_partial/pallas_call | solution.py:142
  23.0 0.1 collective-permute-start.6
  23.1 1.5 %collective-permute-done.6.taken_ref = bf16[256,512]{1,0:T(8,128)(2,1)S(1)} collective-permute-done((bf16[256,512]{1,0:T(8,128)(2,1)S(1)}, bf16[256,512]{1,0:T(8,128)(2,1)S(1)}, u32[]{:S(2)}, u32[]{:S(2)}) %collective-permute-start.6) | collective-permute-done | bytes 262176 | tf_op jit(solution)/shard_map/ppermute | solution.py:421
  24.7 0.2 collective-permute-start.7
  24.9 1.5 %collective-permute-start.8 = (bf16[64,512]{1,0:T(8,128)(2,1)S(1)}, bf16[64,512]{1,0:T(8,128)(2,1)S(1)}, u32[]{:S(2)}, u32[]{:S(2)}) collective-permute-start(bf16[64,512]{1,0:T(8,128)(2,1)S(1)} %get-tuple-element.54), channel_id=1, source_target_pairs={{0,16},{1,25},{2,6},{3,11},{4,20},{5,29},{6,2},{7,15},{8,24},{9,17... | collective-permute-start | bytes 196616 | tf_op jit(solution)/shard_map/ppermute | solution.py:442
  26.4 3.8 %collective-permute-start.12 = (bf16[2,128,128]{2,1,0:T(8,128)(2,1)S(1)}, bf16[2,128,128]{2,1,0:T(8,128)(2,1)S(1)}, u32[]{:S(2)}, u32[]{:S(2)}) collective-permute-start(bf16[2,128,128]{2,1,0:T(8,128)(2,1)S(1)} %get-tuple-element.60), channel_id=1, source_target_pairs={{0,3},{1,0},{2,1},{3,2},{4,7},{5,4},{6,5},{7,6},{8,11},{9,8},{10,9... | collective-permute-start | bytes 196616 | tf_op jit(solution)/shard_map/ppermute | solution.py:185
  30.2 0.0 collective-permute-start.5
  30.2 0.6 %collective-permute-start.13 = (bf16[2,128,128]{2,1,0:T(8,128)(2,1)S(1)}, bf16[2,128,128]{2,1,0:T(8,128)(2,1)S(1)}, u32[]{:S(2)}, u32[]{:S(2)}) collective-permute-start(bf16[2,128,128]{2,1,0:T(8,128)(2,1)S(1)} %get-tuple-element.61), channel_id=1, source_target_pairs={{0,2},{1,3},{2,0},{3,1},{4,6},{5,7},{6,4},{7,5},{8,10},{9,11},{10,... | collective-permute-start | bytes 196616 | tf_op jit(solution)/shard_map/ppermute | solution.py:185
  30.7 0.0 collective-permute-done.8.two
  30.7 4.6 %collective-permute-start.14 = (bf16[2,128,128]{2,1,0:T(8,128)(2,1)S(1)}, bf16[2,128,128]{2,1,0:T(8,128)(2,1)S(1)}, u32[]{:S(2)}, u32[]{:S(2)}) collective-permute-start(bf16[2,128,128]{2,1,0:T(8,128)(2,1)S(1)} %get-tuple-element.62), channel_id=1, source_target_pairs={{0,1},{1,2},{2,3},{3,0},{4,5},{5,6},{6,7},{7,4},{8,9},{9,10},{10,1... | collective-permute-start | bytes 196616 | tf_op jit(solution)/shard_map/ppermute | solution.py:185
  35.4 0.0 collective-permute-done.7.one
  35.4 0.1 collective-permute-start.9
  35.5 0.0 collective-permute-done.12.refs_5_
  35.5 1.7 %collective-permute-start.10 = (bf16[192,128]{1,0:T(8,128)(2,1)S(1)}, bf16[192,128]{1,0:T(8,128)(2,1)S(1)}, u32[]{:S(2)}, u32[]{:S(2)}) collective-permute-start(bf16[192,128]{1,0:T(8,128)(2,1)S(1)} %get-tuple-element.57), channel_id=1, source_target_pairs={{0,2},{1,3},{2,0},{3,1},{4,6},{5,7},{6,4},{7,5},{8,10},{9,11},{10,... | collective-permute-start | bytes 147464 | tf_op jit(solution)/shard_map/ppermute | solution.py:185
  37.3 0.0 collective-permute-done.5.refs_2_
  37.3 2.8 %collective-permute-start.11 = (bf16[192,128]{1,0:T(8,128)(2,1)S(1)}, bf16[192,128]{1,0:T(8,128)(2,1)S(1)}, u32[]{:S(2)}, u32[]{:S(2)}) collective-permute-start(bf16[192,128]{1,0:T(8,128)(2,1)S(1)} %get-tuple-element.58), channel_id=1, source_target_pairs={{0,3},{1,0},{2,1},{3,2},{4,7},{5,4},{6,5},{7,6},{8,11},{9,8},{10,9... | collective-permute-start | bytes 147464 | tf_op jit(solution)/shard_map/ppermute | solution.py:185
  40.1 0.0 copy-done.3
  40.1 1.1 %mixed.1 = (bf16[128,512]{1,0:T(8,128)(2,1)}, bf16[128,512]{1,0:T(8,128)(2,1)}) custom-call(bf16[2,128,128]{2,1,0:T(8,128)(2,1)S(1)} %get-tuple-element.42.refs_0_, bf16[2,128,128]{2,1,0:T(8,128)(2,1)S(1)} %collective-permute-done.3.refs_1_, bf16[2,128,128]{2,1,0:T(8,128)(2,1)S(1)} %collective-permute-done.5.refs_2_, bf16[128,512]{1,0:T(8,128)(2,1)S(1)} %bitcast.12, ...), custom_call_target="tpu_custom_call" | custom-call | flops 134217728 | bytes 983040 | tf_op jit(solution)/shard_map/mixed/pallas_call | solution.py:142
  41.2 0.0 collective-permute-done.13.refs_6_
  41.2 0.0 collective-permute-done.14.refs_7_
  41.2 0.3 collective-permute-done.9.refs_1_
  41.5 0.7 %collective-permute-done.10.refs_2_ = bf16[192,128]{1,0:T(8,128)(2,1)S(1)} collective-permute-done((bf16[192,128]{1,0:T(8,128)(2,1)S(1)}, bf16[192,128]{1,0:T(8,128)(2,1)S(1)}, u32[]{:S(2)}, u32[]{:S(2)}) %collective-permute-start.10) | collective-permute-done | bytes 49184 | tf_op jit(solution)/shard_map/ppermute | solution.py:185
  42.2 0.0 collective-permute-done.11.refs_3_
  42.2 0.8 %means.1 = (f32[2,64,128]{2,1,0:T(8,128)}, f32[64,128]{1,0:T(8,128)}, bf16[128,512]{1,0:T(8,128)(2,1)}, bf16[128,512]{1,0:T(8,128)(2,1)}) custom-call(f32[192,128]{1,0:T(8,128)S(1)} %get-tuple-element.55.refs_0_, bf16[192,128]{1,0:T(8,128)(2,1)S(1)} %collective-permute-done.9.refs_1_, bf16[192,128]{1,0:T(8,128)(2,1)S(1)} %collective-permute-done.10.refs_2_, ...), custom_call_target="tpu_custom_call" | custom-call | bytes 507904 | tf_op jit(solution)/shard_map/means/pallas_call | solution.py:142
  (6 shorter events, 0.1 us)
Async XLA Ops:
  0.6 8.7 %copy-start = (bf16[2,512,512]{2,1,0:T(8,128)(2,1)S(1)}, bf16[2,512,512]{2,1,0:T(8,128)(2,1)}, u32[]{:S(2)}) copy-start(bf16[2,512,512]{2,1,0:T(8,128)(2,1)} %param.12) | copy-start | bytes 3145732
  0.6 8.8 %copy-start.4 = (bf16[1,128,512]{2,1,0:T(8,128)(2,1)S(1)}, bf16[1,128,512]{2,1,0:T(8,128)(2,1)}, u32[]{:S(2)}) copy-start(bf16[1,128,512]{2,1,0:T(8,128)(2,1)} %refs_2_.1) | copy-start | bytes 393220
  0.7 8.8 %copy-start.5 = (bf16[1,128,512]{2,1,0:T(8,128)(2,1)S(1)}, bf16[1,128,512]{2,1,0:T(8,128)(2,1)}, u32[]{:S(2)}) copy-start(bf16[1,128,512]{2,1,0:T(8,128)(2,1)} %refs_4_.2) | copy-start | bytes 393220
  2.4 9.3 %collective-permute-start = (bf16[3,128,128]{2,1,0:T(8,128)(2,1)S(1)}, bf16[3,128,128]{2,1,0:T(8,128)(2,1)S(1)}, u32[]{:S(2)}, u32[]{:S(2)}) collective-permute-start(bf16[3,128,128]{2,1,0:T(8,128)(2,1)S(1)} %get-tuple-element.38), channel_id=1, source_target_pairs={{0,1},{1,2},{2,3},{3,0},{4,5},{5,6},{6,7},{7,4},{8,9},{9,10},{10,1... | collective-permute-start | bytes 294920 | tf_op jit(solution)/shard_map/ppermute | solution.py:185
  5.4 9.2 %collective-permute-start.1 = (bf16[3,128,128]{2,1,0:T(8,128)(2,1)S(1)}, bf16[3,128,128]{2,1,0:T(8,128)(2,1)S(1)}, u32[]{:S(2)}, u32[]{:S(2)}) collective-permute-start(bf16[3,128,128]{2,1,0:T(8,128)(2,1)S(1)} %get-tuple-element.39), channel_id=1, source_target_pairs={{0,2},{1,3},{2,0},{3,1},{4,6},{5,7},{6,4},{7,5},{8,10},{9,11},{10,... | collective-permute-start | bytes 294920 | tf_op jit(solution)/shard_map/ppermute | solution.py:185
  8.0 7.1 %collective-permute-start.2 = (bf16[3,128,128]{2,1,0:T(8,128)(2,1)S(1)}, bf16[3,128,128]{2,1,0:T(8,128)(2,1)S(1)}, u32[]{:S(2)}, u32[]{:S(2)}) collective-permute-start(bf16[3,128,128]{2,1,0:T(8,128)(2,1)S(1)} %get-tuple-element.40), channel_id=1, source_target_pairs={{0,3},{1,0},{2,1},{3,2},{4,7},{5,4},{6,5},{7,6},{8,11},{9,8},{10,9... | collective-permute-start | bytes 294920 | tf_op jit(solution)/shard_map/ppermute | solution.py:185
  9.4 1.0 %copy-start.1 = (bf16[512,256]{1,0:T(8,128)(2,1)S(1)}, bf16[512,256]{1,0:T(8,128)(2,1)}, u32[]{:S(2)}) copy-start(bf16[512,256]{1,0:T(8,128)(2,1)} %constant.25.clone.high.refs_5_.refs_8_) | copy-start | bytes 786436
  9.4 1.0 %copy-start.2 = (bf16[512,256]{1,0:T(8,128)(2,1)S(1)}, bf16[512,256]{1,0:T(8,128)(2,1)}, u32[]{:S(2)}) copy-start(bf16[512,256]{1,0:T(8,128)(2,1)} %constant.26.clone.low.refs_6_.refs_9_) | copy-start | bytes 786436
  10.4 4.8 %copy-start.6 = (bf16[256,512]{1,0:T(8,128)(2,1)S(1)}, bf16[256,512]{1,0:T(8,128)(2,1)}, u32[]{:S(2)}) copy-start(bf16[256,512]{1,0:T(8,128)(2,1)} %constant.27.clone.refs_7_.refs_10_) | copy-start | bytes 786436
  10.9 11.7 %collective-permute-start.4 = (bf16[128,768]{1,0:T(8,128)(2,1)S(1)}, bf16[128,768]{1,0:T(8,128)(2,1)S(1)}, u32[]{:S(2)}, u32[]{:S(2)}) collective-permute-start(bf16[128,768]{1,0:T(8,128)(2,1)S(1)} %get-tuple-element.44), channel_id=1, source_target_pairs={{0,1},{1,0},{2,3},{3,2},{4,5},{5,4},{6,7},{7,6},{8,9},{9,8},{10,11... | collective-permute-start | bytes 589832 | tf_op jit(solution)/shard_map/ppermute | solution.py:271
  16.6 5.9 %collective-permute-start.3 = (bf16[2,128,128]{2,1,0:T(8,128)(2,1)S(1)}, bf16[2,128,128]{2,1,0:T(8,128)(2,1)S(1)}, u32[]{:S(2)}, u32[]{:S(2)}) collective-permute-start(bf16[2,128,128]{2,1,0:T(8,128)(2,1)S(1)} %get-tuple-element.43), channel_id=1, source_target_pairs={{0,2},{1,3},{2,0},{3,1},{4,6},{5,7},{6,4},{7,5},{8,10},{9,11},{10,... | collective-permute-start | bytes 196616 | tf_op jit(solution)/shard_map/ppermute | solution.py:315
  23.0 1.6 %collective-permute-start.6 = (bf16[256,512]{1,0:T(8,128)(2,1)S(1)}, bf16[256,512]{1,0:T(8,128)(2,1)S(1)}, u32[]{:S(2)}, u32[]{:S(2)}) collective-permute-start(bf16[256,512]{1,0:T(8,128)(2,1)S(1)} %get-tuple-element.52), channel_id=1, source_target_pairs={{0,4},{4,0},{8,12},{12,8},{16,20},{20,16},{24,28},{28,24},{1,5},{5... | collective-permute-start | bytes 786440 | tf_op jit(solution)/shard_map/ppermute | solution.py:421
  24.6 15.5 %copy-start.3 = (bf16[512,512]{1,0:T(8,128)(2,1)S(1)}, bf16[512,512]{1,0:T(8,128)(2,1)}, u32[]{:S(2)}) copy-start(bf16[512,512]{1,0:T(8,128)(2,1)} %refs_4_.3) | copy-start | bytes 1572868
  24.7 10.7 %collective-permute-start.7 = (bf16[192,512]{1,0:T(8,128)(2,1)S(1)}, bf16[192,512]{1,0:T(8,128)(2,1)S(1)}, u32[]{:S(2)}, u32[]{:S(2)}) collective-permute-start(bf16[192,512]{1,0:T(8,128)(2,1)S(1)} %get-tuple-element.53), channel_id=1, source_target_pairs={{0,4},{1,9},{2,18},{3,27},{4,0},{5,13},{6,22},{7,31},{8,12},{9,1},... | collective-permute-start | bytes 589832 | tf_op jit(solution)/shard_map/ppermute | solution.py:442
  24.9 5.9 %collective-permute-start.8 = (bf16[64,512]{1,0:T(8,128)(2,1)S(1)}, bf16[64,512]{1,0:T(8,128)(2,1)S(1)}, u32[]{:S(2)}, u32[]{:S(2)}) collective-permute-start(bf16[64,512]{1,0:T(8,128)(2,1)S(1)} %get-tuple-element.54), channel_id=1, source_target_pairs={{0,16},{1,25},{2,6},{3,11},{4,20},{5,29},{6,2},{7,15},{8,24},{9,17... | collective-permute-start | bytes 196616 | tf_op jit(solution)/shard_map/ppermute | solution.py:442
  26.4 9.1 %collective-permute-start.12 = (bf16[2,128,128]{2,1,0:T(8,128)(2,1)S(1)}, bf16[2,128,128]{2,1,0:T(8,128)(2,1)S(1)}, u32[]{:S(2)}, u32[]{:S(2)}) collective-permute-start(bf16[2,128,128]{2,1,0:T(8,128)(2,1)S(1)} %get-tuple-element.60), channel_id=1, source_target_pairs={{0,3},{1,0},{2,1},{3,2},{4,7},{5,4},{6,5},{7,6},{8,11},{9,8},{10,9... | collective-permute-start | bytes 196616 | tf_op jit(solution)/shard_map/ppermute | solution.py:185
  30.2 7.1 %collective-permute-start.5 = (bf16[2,128,128]{2,1,0:T(8,128)(2,1)S(1)}, bf16[2,128,128]{2,1,0:T(8,128)(2,1)S(1)}, u32[]{:S(2)}, u32[]{:S(2)}) collective-permute-start(bf16[2,128,128]{2,1,0:T(8,128)(2,1)S(1)} %get-tuple-element.49), channel_id=1, source_target_pairs={{0,1},{1,0},{2,3},{3,2},{4,5},{5,4},{6,7},{7,6},{8,9},{9,8},{10,11... | collective-permute-start | bytes 196616 | tf_op jit(solution)/shard_map/ppermute | solution.py:422
  30.2 11.0 %collective-permute-start.13 = (bf16[2,128,128]{2,1,0:T(8,128)(2,1)S(1)}, bf16[2,128,128]{2,1,0:T(8,128)(2,1)S(1)}, u32[]{:S(2)}, u32[]{:S(2)}) collective-permute-start(bf16[2,128,128]{2,1,0:T(8,128)(2,1)S(1)} %get-tuple-element.61), channel_id=1, source_target_pairs={{0,2},{1,3},{2,0},{3,1},{4,6},{5,7},{6,4},{7,5},{8,10},{9,11},{10,... | collective-permute-start | bytes 196616 | tf_op jit(solution)/shard_map/ppermute | solution.py:185
  30.7 10.4 %collective-permute-start.14 = (bf16[2,128,128]{2,1,0:T(8,128)(2,1)S(1)}, bf16[2,128,128]{2,1,0:T(8,128)(2,1)S(1)}, u32[]{:S(2)}, u32[]{:S(2)}) collective-permute-start(bf16[2,128,128]{2,1,0:T(8,128)(2,1)S(1)} %get-tuple-element.62), channel_id=1, source_target_pairs={{0,1},{1,2},{2,3},{3,0},{4,5},{5,6},{6,7},{7,4},{8,9},{9,10},{10,1... | collective-permute-start | bytes 196616 | tf_op jit(solution)/shard_map/ppermute | solution.py:185
  35.4 6.0 %collective-permute-start.9 = (bf16[192,128]{1,0:T(8,128)(2,1)S(1)}, bf16[192,128]{1,0:T(8,128)(2,1)S(1)}, u32[]{:S(2)}, u32[]{:S(2)}) collective-permute-start(bf16[192,128]{1,0:T(8,128)(2,1)S(1)} %get-tuple-element.56), channel_id=1, source_target_pairs={{0,1},{1,2},{2,3},{3,0},{4,5},{5,6},{6,7},{7,4},{8,9},{9,10},{10,1... | collective-permute-start | bytes 147464 | tf_op jit(solution)/shard_map/ppermute | solution.py:185
  35.5 6.7 %collective-permute-start.10 = (bf16[192,128]{1,0:T(8,128)(2,1)S(1)}, bf16[192,128]{1,0:T(8,128)(2,1)S(1)}, u32[]{:S(2)}, u32[]{:S(2)}) collective-permute-start(bf16[192,128]{1,0:T(8,128)(2,1)S(1)} %get-tuple-element.57), channel_id=1, source_target_pairs={{0,2},{1,3},{2,0},{3,1},{4,6},{5,7},{6,4},{7,5},{8,10},{9,11},{10,... | collective-permute-start | bytes 147464 | tf_op jit(solution)/shard_map/ppermute | solution.py:185
  37.3 4.9 %collective-permute-start.11 = (bf16[192,128]{1,0:T(8,128)(2,1)S(1)}, bf16[192,128]{1,0:T(8,128)(2,1)S(1)}, u32[]{:S(2)}, u32[]{:S(2)}) collective-permute-start(bf16[192,128]{1,0:T(8,128)(2,1)S(1)} %get-tuple-element.58), channel_id=1, source_target_pairs={{0,3},{1,0},{2,1},{3,2},{4,7},{5,4},{6,5},{7,6},{8,11},{9,8},{10,9... | collective-permute-start | bytes 147464 | tf_op jit(solution)/shard_map/ppermute | solution.py:185

commit v7 on v6

--- a/solution.py
+++ b/solution.py
@@ -320,6 +320,8 @@
         parts, refs = refs[:seq], refs[seq:]
         filt, first_ref, value_spec, mixed_spec, high, low, back = refs[:7]
         lags, *outs, stream, total = refs[7:]
+        if fast:
+            lag_kept, lag_given, *outs, packed = outs
         count = length // block
         for step, part in enumerate(parts):
             put_rows(stream, behind(step), rows, part[2])
@@ -349,11 +351,22 @@
             total[i * block : (i + 1) * block] = columns(out, i, cols)
         put_result(outs, 1, total, 2)
         put_lags(0, out)
+        if fast:
+            here, own_core = lax.axis_index("ctx"), lax.rem(lax.axis_index("dp"), 2)
+            half = jnp.where(here == 0, 1 - own_core, own_core)
+            lower = lax.broadcasted_iota(jnp.int32, (length, cols), 1) < fine
+            packed[0] = jnp.where(lower, lags[0], pltpu.roll(lags[1], fine, axis=1))
+            packed[1] = jnp.where(lower, pltpu.roll(lags[0], fine, axis=1), lags[1])
+            for index in range(seq):
+                lanes = pl.ds(index * cols, cols)
+                lag_kept[:, lanes] = packed[half, index * rows : (index + 1) * rows]
+                given = packed[1 - half, index * rows : (index + 1) * rows]
+                lag_given[:, lanes] = given.astype(BF16)
 
     with jax.named_scope("backward_convolutions"):
         lags, *sends_home = call(
             backward_kernel,
-            [((2, length, cols), F32)] + [((2, rows, cols), BF16)] * seq,
+            [((2, length, cols), F32)] + [((rows, width), F32), wide_bf16] * fast + [((2, rows, cols), BF16)] * seq,
             (
                 *parts_in,
                 filter_spectra,
@@ -364,15 +377,38 @@
                 fwd_low,
                 inv_high,
             ),
-            scratch=[pltpu.VMEM((length, cols), BF16), pltpu.VMEM((length, cols), F32)],
+            scratch=[pltpu.VMEM((2, length, cols), F32)] * fast
+            + [pltpu.VMEM((length, cols), BF16), pltpu.VMEM((length, cols), F32)],
             flops=8 * table_flops,
             limit=limit,
         )
 
     if fast:
+        def to_core(block):
+            return lax.ppermute(block, "dp", [(i, i ^ 1) for i in range(data)])
+
+        def to_chip(block, other):
+            pairs = []
+            for i in range(data):
+                for j in range(seq):
+                    pairs.append((i * seq + j, (i ^ (2 * (j ^ other) or 1)) * seq + j))
+            return lax.ppermute(block, ("dp", "ctx"), pairs)
+
+        def core_kernel(kept_ref, taken_ref, *outs):
+            summed = (kept_ref[...] + taken_ref[...].astype(F32)).astype(BF16)
+            for index, out in enumerate(outs):
+                out[...] = summed[index * out.shape[0] : (index + 1) * out.shape[0]]
+
+        lag_kept, lag_given, *sends_home = sends_home
+        with jax.named_scope("lag_core_sum"):
+            (lag_sum,) = call(
+                core_kernel, [wide_bf16], (lag_kept, to_core(lag_given)), limit=limit
+            )
+        lag_term = to_chip(lag_sum, 0)
+
         def gated_kernel(*refs):
-            stays_ref, near_ref, gate_ref, cot_ref, beside_ref, lags, *refs = refs
-            kept, given, turned, gated, cots, whole, packed = refs
+            stays_ref, near_ref, gate_ref, cot_ref, beside_ref, _, *refs = refs
+            kept, given, turned, gated, cots, whole = refs
             turned[0] = stays_ref[1]
             turned[1] = near_ref[1]
             here = lax.axis_index("ctx")
@@ -387,78 +423,55 @@
             whole[...] = lax.dot_general(
                 gated[...], cots[...], (((0,), (0,)), ((), ())), preferred_element_type=F32
             )
-            lower = lax.broadcasted_iota(jnp.int32, (length, cols), 1) < fine
-            packed[0] = jnp.where(lower, lags[0], pltpu.roll(lags[1], fine, axis=1))
-            packed[1] = jnp.where(lower, pltpu.roll(lags[0], fine, axis=1), lags[1])
             own_core = lax.rem(lax.axis_index("dp"), 2)
             first = jnp.where(here == 0, 1 - own_core, own_core)
             second = jnp.where(here == 2, 1 - own_core, own_core)
             for out, one, two in ((kept, first, second), (given, 1 - first, 1 - second)):
                 piece = whole[pl.ds(pl.multiple_of(one * own_rows, own_rows), own_rows), :]
                 out[:own_rows] = piece.astype(out.dtype)
-                for index in range(seq):
-                    piece = packed[one, index * rows : (index + 1) * rows]
-                    out[own_rows : own_rows + rows, index * cols : (index + 1) * cols] = (
-                        piece.astype(out.dtype)
-                    )
                 start = pl.multiple_of(cols + two * own_rows, own_rows)
-                out[own_rows + rows :] = whole[pl.ds(start, own_rows), :].astype(out.dtype)
-
-        term_shape = (2 * own_rows + rows, width)
+                out[own_rows:] = whole[pl.ds(start, own_rows), :].astype(out.dtype)
+
+        term_shape = (2 * own_rows, width)
         with jax.named_scope("weight_partial"):
             kept, given, goes_on = call(
                 gated_kernel,
                 [(term_shape, F32), (term_shape, BF16), ((2, rows, cols), BF16)],
-                (second_stays, second_near, gate_two[0], grad_out[0], beside_in, lags),
+                (second_stays, second_near, gate_two[0], grad_out[0], beside_in, gate_two[0]),
                 scratch=[
                     pltpu.VMEM((2 * rows, 2 * cols), BF16),
                     pltpu.VMEM((2 * rows, width), BF16),
                     pltpu.VMEM((2 * cols, width), F32),
-                    pltpu.VMEM((2, length, cols), F32),
                 ],
                 limit=limit,
             )
-        taken = lax.ppermute(given, "dp", [(i, i ^ 1) for i in range(data)])
         second_far = lax.ppermute(goes_on, "ctx", across(1))
-
-        def core_kernel(kept_ref, taken_ref, one, two):
-            summed = (kept_ref[...] + taken_ref[...].astype(F32)).astype(BF16)
-            one[...] = summed[: own_rows + rows]
-            two[...] = summed[own_rows + rows :]
 
         with jax.named_scope("core_sum"):
             sends = call(
                 core_kernel,
-                [((own_rows + rows, width), BF16), ((own_rows, width), BF16)],
-                (kept, taken),
+                [((own_rows, width), BF16)] * 2,
+                (kept, to_core(given)),
                 limit=limit,
             )
 
-        def to_chip(block, other):
-            pairs = []
-            for i in range(data):
-                for j in range(seq):
-                    pairs.append((i * seq + j, (i ^ (2 * (j ^ other) or 1)) * seq + j))
-            return lax.ppermute(block, ("dp", "ctx"), pairs)
-
         chip_terms = [to_chip(sends[0], 0), to_chip(sends[1], 2)]
 
         home = around(sends_home)
 
-        def place_kernel(one, two, *refs):
+        def place_kernel(lag_ref, one, two, *refs):
             outs, total = refs[:-1], refs[-1]
-            total[...] = one[:own_rows].astype(F32) + two[...].astype(F32)
+            total[...] = one[...].astype(F32) + two[...].astype(F32)
             for step, out in enumerate(outs):
                 out[:own_rows] = pick_columns(total, ahead(step), cols, seq).astype(out.dtype)
-                lag = pick_columns(one, ahead(step), cols, seq)[own_rows:]
-                out[own_rows:] = lag.astype(out.dtype)
+                out[own_rows:] = pick_columns(lag_ref, ahead(step), cols, seq).astype(out.dtype)
 
         small = (own_rows + rows, cols)
         with jax.named_scope("chip_sum"):
             sends = call(
                 place_kernel,
                 [(small, F32)] + [(small, BF16)] * (seq - 1),
-                chip_terms,
+                (lag_term, *chip_terms),
                 scratch=[pltpu.VMEM((own_rows, width), F32)],
             )
         last_terms = around(sends)

time: 43.1 us -> 42 us (0.974)
  starting transfers between devices: 24.2 us -> 23.1 us
  waiting for transfers between devices: 9.28 us -> 8.54 us
  Pallas kernels: 7.65 us -> 8.38 us
    ppermute x9, starting transfers between devices: 20.6 us -> 18.9 us  [around(): out.append(lax.ppermute(blocks[step], 'ctx', pairs))]
    ppermute x9, waiting for transfers between devices: 4.58 us -> 5.45 us  [around(): out.append(lax.ppermute(blocks[step], 'ctx', pairs))]
    ppermute x1, waiting for transfers between devices: 3.17 us -> 2.34 us  [on_device(): second_near = lax.ppermute(goes, 'ctx', across(2))]
    ppermute x1 -> x2, waiting for transfers between devices: 1.52 us -> 0.74 us  [to_core(): return lax.ppermute(block, 'dp', [(i, i ^ 1) for i in range(data)])]
    pallas_call x9 -> x10, Pallas kernels: 7.65 us -> 8.38 us  [call(): pl.pallas_call(kernel, out_shape=[jax.ShapeDtypeStruct(shape, dtype) for...]
    ppermute x2 -> x3, starting transfers between devices: 1.73 us -> 2.3 us  [to_chip(): return lax.ppermute(block, ('dp', 'ctx'), pairs)]
  transfers between devices with their start and end apart: 15 -> 17, of which waited for: 6 -> 6; matrix products, arithmetic and copies ran while one was open for 0% -> 0% of each run, Pallas kernels for 11% -> 14%
where the time goes in v7:
time: 42 us; the launch traced here: 41.8 us
  starting transfers between devices  23.1 us (55%)
  waiting for transfers between devices  8.54 us (20%)
  Pallas kernels  8.38 us (20%)
  local copies, waits for them, and re-layouts  1.05 us (2%)
  between operations  0.76 us (2%)
    ppermute x9, starting transfers between devices, around(): out.append(lax.ppermute(blocks[step], 'ctx', pairs))  18.9 us
    pallas_call x10, Pallas kernels, call(): pl.pallas_call(kernel, out_shape=[jax.ShapeDtypeStruct(shape, dtype) for...  8.38 us
    ppermute x9, waiting for transfers between devices, around(): out.append(lax.ppermute(blocks[step], 'ctx', pairs))  5.45 us
    ppermute x1, waiting for transfers between devices, on_device(): second_near = lax.ppermute(goes, 'ctx', across(2))  2.34 us
    ppermute x3, starting transfers between devices, to_chip(): return lax.ppermute(block, ('dp', 'ctx'), pairs)  2.3 us
    ppermute x1, starting transfers between devices, on_device(): second_near = lax.ppermute(goes, 'ctx', across(2))  1.08 us
    unnamed x14, local copies, waits for them, and re-layouts  1.01 us
  transfers between devices with their start and end apart: 17, of which 6 were waited for; matrix products, arithmetic and copies ran while one was open for 0% of the time, Pallas kernels for 14%

profile of v7, /device:TPU:0, one launch (start us, length us, event | category | flops | bytes accessed | tf_op | source)
XLA Modules:
  0.0 41.8 jit_solution(6535169630026154302)
XLA Ops:
  0.6 0.0 copy-start
  0.6 0.0 copy-start.3
  0.7 1.7 %load.1 = (bf16[3,128,128]{2,1,0:T(8,128)(2,1)S(1)}, bf16[3,128,128]{2,1,0:T(8,128)(2,1)S(1)}, bf16[3,128,128]{2,1,0:T(8,128)(2,1)S(1)}, bf16[3,128,128]{2,1,0:T(8,128)(2,1)S(1)}) custom-call(bf16[1,128,512]{2,1,0:T(8,128)(2,1)} %refs_0_.1, bf16[1,128,512]{2,1,0:T(8,128)(2,1)} %refs_1_.1, bf16[1,128,512]{2,1,0:T(8,128)(2,1)} %refs_2_.1, ...), custom_call_target="tpu_custom_call" | custom-call | flops 67108864 | bytes 1048576 | tf_op jit(solution)/shard_map/load/pallas_call | solution.py:142
  2.4 3.1 %collective-permute-start = (bf16[3,128,128]{2,1,0:T(8,128)(2,1)S(1)}, bf16[3,128,128]{2,1,0:T(8,128)(2,1)S(1)}, u32[]{:S(2)}, u32[]{:S(2)}) collective-permute-start(bf16[3,128,128]{2,1,0:T(8,128)(2,1)S(1)} %get-tuple-element.39), channel_id=1, source_target_pairs={{0,1},{1,2},{2,3},{3,0},{4,5},{5,6},{6,7},{7,4},{8,9},{9,10},{10,1... | collective-permute-start | bytes 294920 | tf_op jit(solution)/shard_map/ppermute | solution.py:185
  5.4 2.6 %collective-permute-start.1 = (bf16[3,128,128]{2,1,0:T(8,128)(2,1)S(1)}, bf16[3,128,128]{2,1,0:T(8,128)(2,1)S(1)}, u32[]{:S(2)}, u32[]{:S(2)}) collective-permute-start(bf16[3,128,128]{2,1,0:T(8,128)(2,1)S(1)} %get-tuple-element.40), channel_id=1, source_target_pairs={{0,2},{1,3},{2,0},{3,1},{4,6},{5,7},{6,4},{7,5},{8,10},{9,11},{10,... | collective-permute-start | bytes 294920 | tf_op jit(solution)/shard_map/ppermute | solution.py:185
  8.0 1.3 %collective-permute-start.2 = (bf16[3,128,128]{2,1,0:T(8,128)(2,1)S(1)}, bf16[3,128,128]{2,1,0:T(8,128)(2,1)S(1)}, u32[]{:S(2)}, u32[]{:S(2)}) collective-permute-start(bf16[3,128,128]{2,1,0:T(8,128)(2,1)S(1)} %get-tuple-element.41), channel_id=1, source_target_pairs={{0,3},{1,0},{2,1},{3,2},{4,7},{5,4},{6,5},{7,6},{8,11},{9,8},{10,9... | collective-permute-start | bytes 294920 | tf_op jit(solution)/shard_map/ppermute | solution.py:185
  9.4 0.0 copy-done
  9.4 0.8 %copy-done.1 = bf16[1,128,512]{2,1,0:T(8,128)(2,1)S(1)} copy-done((bf16[1,128,512]{2,1,0:T(8,128)(2,1)S(1)}, bf16[1,128,512]{2,1,0:T(8,128)(2,1)}, u32[]{:S(2)}) %copy-start.1) | copy-done | bytes 131096
  10.3 0.1 copy-done.2
  10.4 0.0 copy-done.5
  10.4 0.4 %filter_spectra.1 = (f32[2,512,256]{2,1,0:T(8,128)S(1)}, bf16[128,768]{1,0:T(8,128)(2,1)S(1)}) custom-call(bf16[2,512,128]{2,1,0:T(8,128)(2,1)S(1)} %constant_dynamic-slice_fusion.filters_ref, bf16[512,256]{1,0:T(8,128)(2,1)S(1)} %copy-done.3, bf16[512,256]{1,0:T(8,128)(2,1)S(1)} %copy-done.2, bf16[128,512]{1,0:T(8,128)(2,1)S(1)} %bitcast.11, ...), custom_call_target="tpu_custom_call" | custom-call | flops 268435456 | bytes 1048576 | tf_op jit(solution)/shard_map/filter_spectra/pallas_call | solution.py:142
  10.9 0.7 %collective-permute-start.4 = (bf16[128,768]{1,0:T(8,128)(2,1)S(1)}, bf16[128,768]{1,0:T(8,128)(2,1)S(1)}, u32[]{:S(2)}, u32[]{:S(2)}) collective-permute-start(bf16[128,768]{1,0:T(8,128)(2,1)S(1)} %get-tuple-element.45), channel_id=1, source_target_pairs={{0,1},{1,0},{2,3},{3,2},{4,5},{5,4},{6,7},{7,6},{8,9},{9,8},{10,11... | collective-permute-start | bytes 589832 | tf_op jit(solution)/shard_map/ppermute | solution.py:271
  11.6 0.0 collective-permute-done.refs_1_
  11.6 3.0 %collective-permute-done.1.refs_2_ = bf16[3,128,128]{2,1,0:T(8,128)(2,1)S(1)} collective-permute-done((bf16[3,128,128]{2,1,0:T(8,128)(2,1)S(1)}, bf16[3,128,128]{2,1,0:T(8,128)(2,1)S(1)}, u32[]{:S(2)}, u32[]{:S(2)}) %collective-permute-start.1) | collective-permute-done | bytes 98336 | tf_op jit(solution)/shard_map/ppermute | solution.py:185
  14.6 0.5 %collective-permute-done.2.refs_3_ = bf16[3,128,128]{2,1,0:T(8,128)(2,1)S(1)} collective-permute-done((bf16[3,128,128]{2,1,0:T(8,128)(2,1)S(1)}, bf16[3,128,128]{2,1,0:T(8,128)(2,1)S(1)}, u32[]{:S(2)}, u32[]{:S(2)}) %collective-permute-start.2) | collective-permute-done | bytes 98336 | tf_op jit(solution)/shard_map/ppermute | solution.py:185
  15.1 1.5 %forward_convolutions.1 = (f32[512,128]{1,0:T(8,128)S(1)}, f32[512,256]{1,0:T(8,128)S(1)}, f32[512,256]{1,0:T(8,128)S(1)}, bf16[2,128,128]{2,1,0:T(8,128)(2,1)S(1)}, bf16[2,128,128]{2,1,0:T(8,128)(2,1)S(1)}) custom-call(bf16[3,128,128]{2,1,0:T(8,128)(2,1)S(1)} %get-tuple-element.38.refs_0_, bf16[3,128,128]{2,1,0:T(8,128)(2,1)S(1)} %collective-permute-done.refs_1_, ...), custom_call_target="tpu_custom_call" | custom-call | flops 402653184 | bytes 2228224 | tf_op jit(solution)/shard_map/forward_convolutions/pallas_call | solution.py:142
  16.6 1.1 %collective-permute-start.3 = (bf16[2,128,128]{2,1,0:T(8,128)(2,1)S(1)}, bf16[2,128,128]{2,1,0:T(8,128)(2,1)S(1)}, u32[]{:S(2)}, u32[]{:S(2)}) collective-permute-start(bf16[2,128,128]{2,1,0:T(8,128)(2,1)S(1)} %get-tuple-element.44), channel_id=1, source_target_pairs={{0,2},{1,3},{2,0},{3,1},{4,6},{5,7},{6,4},{7,5},{8,10},{9,11},{10,... | collective-permute-start | bytes 196616 | tf_op jit(solution)/shard_map/ppermute | solution.py:315
  17.7 2.5 %backward_convolutions.1 = (f32[2,512,128]{2,1,0:T(8,128)}, f32[128,512]{1,0:T(8,128)S(1)}, bf16[128,512]{1,0:T(8,128)(2,1)S(1)}, bf16[2,128,128]{2,1,0:T(8,128)...) custom-call(bf16[3,128,128]{2,1,0:T(8,128)(2,1)S(1)} %get-tuple-elem, ...), custom_call_target="tpu_custom_call" | custom-call | flops 536870912 | bytes 3538944 | tf_op jit(solution)/shard_map/backward_convolutions/pallas_call | solution.py:142
  20.2 0.0 collective-permute-start.6
  20.2 2.3 %collective-permute-done.3.refs_1_ = bf16[2,128,128]{2,1,0:T(8,128)(2,1)S(1)} collective-permute-done((bf16[2,128,128]{2,1,0:T(8,128)(2,1)S(1)}, bf16[2,128,128]{2,1,0:T(8,128)(2,1)S(1)}, u32[]{:S(2)}, u32[]{:S(2)}) %collective-permute-start.3) | collective-permute-done | bytes 65568 | tf_op jit(solution)/shard_map/ppermute | solution.py:315
  22.5 0.0 collective-permute-done.4.refs_4_
  22.5 0.3 weight_partial.1
  22.9 0.1 collective-permute-start.8
  23.0 0.0 collective-permute-done.6.taken_ref
  23.0 0.0 copy-start.4
  23.0 0.5 %collective-permute-start.7 = (bf16[128,512]{1,0:T(8,128)(2,1)S(1)}, bf16[128,512]{1,0:T(8,128)(2,1)S(1)}, u32[]{:S(2)}, u32[]{:S(2)}) collective-permute-start(bf16[128,512]{1,0:T(8,128)(2,1)S(1)} %lag_core_sum.1), channel_id=1, source_target_pairs={{0,4},{1,9},{2,18},{3,27},{4,0},{5,13},{6,22},{7,31},{8,12},{9,1},... | collective-permute-start | bytes 393224 | tf_op jit(solution)/shard_map/ppermute | solution.py:395
  23.6 0.7 %collective-permute-done.8.taken_ref = bf16[128,512]{1,0:T(8,128)(2,1)S(1)} collective-permute-done((bf16[128,512]{1,0:T(8,128)(2,1)S(1)}, bf16[128,512]{1,0:T(8,128)(2,1)S(1)}, u32[]{:S(2)}, u32[]{:S(2)}) %collective-permute-start.8) | collective-permute-done | bytes 131104 | tf_op jit(solution)/shard_map/core_sum/ppermute | solution.py:388
  24.3 0.2 collective-permute-start.9
  24.5 1.5 %collective-permute-start.10 = (bf16[64,512]{1,0:T(8,128)(2,1)S(1)}, bf16[64,512]{1,0:T(8,128)(2,1)S(1)}, u32[]{:S(2)}, u32[]{:S(2)}) collective-permute-start(bf16[64,512]{1,0:T(8,128)(2,1)S(1)} %get-tuple-element.56), channel_id=1, source_target_pairs={{0,16},{1,25},{2,6},{3,11},{4,20},{5,29},{6,2},{7,15},{8,24},{9,17... | collective-permute-start | bytes 196616 | tf_op jit(solution)/shard_map/ppermute | solution.py:395
  26.1 4.0 %collective-permute-start.14 = (bf16[2,128,128]{2,1,0:T(8,128)(2,1)S(1)}, bf16[2,128,128]{2,1,0:T(8,128)(2,1)S(1)}, u32[]{:S(2)}, u32[]{:S(2)}) collective-permute-start(bf16[2,128,128]{2,1,0:T(8,128)(2,1)S(1)} %get-tuple-element.62), channel_id=1, source_target_pairs={{0,3},{1,0},{2,1},{3,2},{4,7},{5,4},{6,5},{7,6},{8,11},{9,8},{10,9... | collective-permute-start | bytes 196616 | tf_op jit(solution)/shard_map/ppermute | solution.py:185
  30.1 0.0 collective-permute-start.5
  30.1 0.0 collective-permute-done.7.lag_ref
  30.1 0.6 %collective-permute-start.15 = (bf16[2,128,128]{2,1,0:T(8,128)(2,1)S(1)}, bf16[2,128,128]{2,1,0:T(8,128)(2,1)S(1)}, u32[]{:S(2)}, u32[]{:S(2)}) collective-permute-start(bf16[2,128,128]{2,1,0:T(8,128)(2,1)S(1)} %get-tuple-element.63), channel_id=1, source_target_pairs={{0,2},{1,3},{2,0},{3,1},{4,6},{5,7},{6,4},{7,5},{8,10},{9,11},{10,... | collective-permute-start | bytes 196616 | tf_op jit(solution)/shard_map/ppermute | solution.py:185
  30.7 0.0 collective-permute-done.9.one
  30.7 2.7 %collective-permute-start.16 = (bf16[2,128,128]{2,1,0:T(8,128)(2,1)S(1)}, bf16[2,128,128]{2,1,0:T(8,128)(2,1)S(1)}, u32[]{:S(2)}, u32[]{:S(2)}) collective-permute-start(bf16[2,128,128]{2,1,0:T(8,128)(2,1)S(1)} %get-tuple-element.64), channel_id=1, source_target_pairs={{0,1},{1,2},{2,3},{3,0},{4,5},{5,6},{6,7},{7,4},{8,9},{9,10},{10,1... | collective-permute-start | bytes 196616 | tf_op jit(solution)/shard_map/ppermute | solution.py:185
  33.3 0.0 collective-permute-done.10.two
  33.4 0.8 %collective-permute-start.11 = (bf16[192,128]{1,0:T(8,128)(2,1)S(1)}, bf16[192,128]{1,0:T(8,128)(2,1)S(1)}, u32[]{:S(2)}, u32[]{:S(2)}) collective-permute-start(bf16[192,128]{1,0:T(8,128)(2,1)S(1)} %get-tuple-element.58), channel_id=1, source_target_pairs={{0,1},{1,2},{2,3},{3,0},{4,5},{5,6},{6,7},{7,4},{8,9},{9,10},{10,1... | collective-permute-start | bytes 147464 | tf_op jit(solution)/shard_map/ppermute | solution.py:185
  34.2 0.0 collective-permute-done.14.refs_5_
  34.2 1.7 %collective-permute-start.12 = (bf16[192,128]{1,0:T(8,128)(2,1)S(1)}, bf16[192,128]{1,0:T(8,128)(2,1)S(1)}, u32[]{:S(2)}, u32[]{:S(2)}) collective-permute-start(bf16[192,128]{1,0:T(8,128)(2,1)S(1)} %get-tuple-element.59), channel_id=1, source_target_pairs={{0,2},{1,3},{2,0},{3,1},{4,6},{5,7},{6,4},{7,5},{8,10},{9,11},{10,... | collective-permute-start | bytes 147464 | tf_op jit(solution)/shard_map/ppermute | solution.py:185
  35.9 0.0 collective-permute-done.5.refs_2_
  35.9 2.2 %collective-permute-start.13 = (bf16[192,128]{1,0:T(8,128)(2,1)S(1)}, bf16[192,128]{1,0:T(8,128)(2,1)S(1)}, u32[]{:S(2)}, u32[]{:S(2)}) collective-permute-start(bf16[192,128]{1,0:T(8,128)(2,1)S(1)} %get-tuple-element.60), channel_id=1, source_target_pairs={{0,3},{1,0},{2,1},{3,2},{4,7},{5,4},{6,5},{7,6},{8,11},{9,8},{10,9... | collective-permute-start | bytes 147464 | tf_op jit(solution)/shard_map/ppermute | solution.py:185
  38.1 1.1 %mixed.1 = (bf16[128,512]{1,0:T(8,128)(2,1)}, bf16[128,512]{1,0:T(8,128)(2,1)}) custom-call(bf16[2,128,128]{2,1,0:T(8,128)(2,1)S(1)} %get-tuple-element.43.refs_0_, bf16[2,128,128]{2,1,0:T(8,128)(2,1)S(1)} %collective-permute-done.3.refs_1_, bf16[2,128,128]{2,1,0:T(8,128)(2,1)S(1)} %collective-permute-done.5.refs_2_, bf16[128,512]{1,0:T(8,128)(2,1)S(1)} %bitcast.10, ...), custom_call_target="tpu_custom_call" | custom-call | flops 134217728 | bytes 983040 | tf_op jit(solution)/shard_map/mixed/pallas_call | solution.py:142
  39.2 0.0 collective-permute-done.15.refs_6_
  39.2 0.0 collective-permute-done.16.refs_7_
  39.2 0.4 collective-permute-done.11.refs_1_
  39.6 1.5 %collective-permute-done.12.refs_2_ = bf16[192,128]{1,0:T(8,128)(2,1)S(1)} collective-permute-done((bf16[192,128]{1,0:T(8,128)(2,1)S(1)}, bf16[192,128]{1,0:T(8,128)(2,1)S(1)}, u32[]{:S(2)}, u32[]{:S(2)}) %collective-permute-start.12) | collective-permute-done | bytes 49184 | tf_op jit(solution)/shard_map/ppermute | solution.py:185
  41.1 0.0 collective-permute-done.13.refs_3_
  41.1 0.8 %means.1 = (f32[2,64,128]{2,1,0:T(8,128)}, f32[64,128]{1,0:T(8,128)}, bf16[128,512]{1,0:T(8,128)(2,1)}, bf16[128,512]{1,0:T(8,128)(2,1)}) custom-call(f32[192,128]{1,0:T(8,128)S(1)} %get-tuple-element.57.refs_0_, bf16[192,128]{1,0:T(8,128)(2,1)S(1)} %collective-permute-done.11.refs_1_, bf16[192,128]{1,0:T(8,128)(2,1)S(1)} %collective-permute-done.12.refs_2_, ...), custom_call_target="tpu_custom_call" | custom-call | bytes 507904 | tf_op jit(solution)/shard_map/means/pallas_call | solution.py:142
  (11 shorter events, 0.2 us)
Async XLA Ops:
  0.6 8.7 %copy-start = (bf16[2,512,512]{2,1,0:T(8,128)(2,1)S(1)}, bf16[2,512,512]{2,1,0:T(8,128)(2,1)}, u32[]{:S(2)}) copy-start(bf16[2,512,512]{2,1,0:T(8,128)(2,1)} %param.12) | copy-start | bytes 3145732
  0.6 8.8 %copy-start.3 = (bf16[512,256]{1,0:T(8,128)(2,1)S(1)}, bf16[512,256]{1,0:T(8,128)(2,1)}, u32[]{:S(2)}) copy-start(bf16[512,256]{1,0:T(8,128)(2,1)} %constant.25.clone.high.refs_5_.refs_8_) | copy-start | bytes 786436
  2.4 9.3 %collective-permute-start = (bf16[3,128,128]{2,1,0:T(8,128)(2,1)S(1)}, bf16[3,128,128]{2,1,0:T(8,128)(2,1)S(1)}, u32[]{:S(2)}, u32[]{:S(2)}) collective-permute-start(bf16[3,128,128]{2,1,0:T(8,128)(2,1)S(1)} %get-tuple-element.39), channel_id=1, source_target_pairs={{0,1},{1,2},{2,3},{3,0},{4,5},{5,6},{6,7},{7,4},{8,9},{9,10},{10,1... | collective-permute-start | bytes 294920 | tf_op jit(solution)/shard_map/ppermute | solution.py:185
  5.4 9.2 %collective-permute-start.1 = (bf16[3,128,128]{2,1,0:T(8,128)(2,1)S(1)}, bf16[3,128,128]{2,1,0:T(8,128)(2,1)S(1)}, u32[]{:S(2)}, u32[]{:S(2)}) collective-permute-start(bf16[3,128,128]{2,1,0:T(8,128)(2,1)S(1)} %get-tuple-element.40), channel_id=1, source_target_pairs={{0,2},{1,3},{2,0},{3,1},{4,6},{5,7},{6,4},{7,5},{8,10},{9,11},{10,... | collective-permute-start | bytes 294920 | tf_op jit(solution)/shard_map/ppermute | solution.py:185
  8.0 7.1 %collective-permute-start.2 = (bf16[3,128,128]{2,1,0:T(8,128)(2,1)S(1)}, bf16[3,128,128]{2,1,0:T(8,128)(2,1)S(1)}, u32[]{:S(2)}, u32[]{:S(2)}) collective-permute-start(bf16[3,128,128]{2,1,0:T(8,128)(2,1)S(1)} %get-tuple-element.41), channel_id=1, source_target_pairs={{0,3},{1,0},{2,1},{3,2},{4,7},{5,4},{6,5},{7,6},{8,11},{9,8},{10,9... | collective-permute-start | bytes 294920 | tf_op jit(solution)/shard_map/ppermute | solution.py:185
  9.4 0.9 %copy-start.1 = (bf16[1,128,512]{2,1,0:T(8,128)(2,1)S(1)}, bf16[1,128,512]{2,1,0:T(8,128)(2,1)}, u32[]{:S(2)}) copy-start(bf16[1,128,512]{2,1,0:T(8,128)(2,1)} %refs_4_.2) | copy-start | bytes 393220
  9.4 1.0 %copy-start.2 = (bf16[512,256]{1,0:T(8,128)(2,1)S(1)}, bf16[512,256]{1,0:T(8,128)(2,1)}, u32[]{:S(2)}) copy-start(bf16[512,256]{1,0:T(8,128)(2,1)} %constant.26.clone.low.refs_6_.refs_9_) | copy-start | bytes 786436
  9.4 1.0 %copy-start.5 = (bf16[1,128,512]{2,1,0:T(8,128)(2,1)S(1)}, bf16[1,128,512]{2,1,0:T(8,128)(2,1)}, u32[]{:S(2)}) copy-start(bf16[1,128,512]{2,1,0:T(8,128)(2,1)} %refs_2_.1) | copy-start | bytes 393220
  10.4 4.7 %copy-start.6 = (bf16[256,512]{1,0:T(8,128)(2,1)S(1)}, bf16[256,512]{1,0:T(8,128)(2,1)}, u32[]{:S(2)}) copy-start(bf16[256,512]{1,0:T(8,128)(2,1)} %constant.27.clone.refs_7_.refs_10_) | copy-start | bytes 786436
  10.9 11.7 %collective-permute-start.4 = (bf16[128,768]{1,0:T(8,128)(2,1)S(1)}, bf16[128,768]{1,0:T(8,128)(2,1)S(1)}, u32[]{:S(2)}, u32[]{:S(2)}) collective-permute-start(bf16[128,768]{1,0:T(8,128)(2,1)S(1)} %get-tuple-element.45), channel_id=1, source_target_pairs={{0,1},{1,0},{2,3},{3,2},{4,5},{5,4},{6,7},{7,6},{8,9},{9,8},{10,11... | collective-permute-start | bytes 589832 | tf_op jit(solution)/shard_map/ppermute | solution.py:271
  16.6 5.9 %collective-permute-start.3 = (bf16[2,128,128]{2,1,0:T(8,128)(2,1)S(1)}, bf16[2,128,128]{2,1,0:T(8,128)(2,1)S(1)}, u32[]{:S(2)}, u32[]{:S(2)}) collective-permute-start(bf16[2,128,128]{2,1,0:T(8,128)(2,1)S(1)} %get-tuple-element.44), channel_id=1, source_target_pairs={{0,2},{1,3},{2,0},{3,1},{4,6},{5,7},{6,4},{7,5},{8,10},{9,11},{10,... | collective-permute-start | bytes 196616 | tf_op jit(solution)/shard_map/ppermute | solution.py:315
  20.2 2.8 %collective-permute-start.6 = (bf16[128,512]{1,0:T(8,128)(2,1)S(1)}, bf16[128,512]{1,0:T(8,128)(2,1)S(1)}, u32[]{:S(2)}, u32[]{:S(2)}) collective-permute-start(bf16[128,512]{1,0:T(8,128)(2,1)S(1)} %get-tuple-element.52), channel_id=1, source_target_pairs={{0,4},{4,0},{8,12},{12,8},{16,20},{20,16},{24,28},{28,24},{1,5},{5... | collective-permute-start | bytes 393224 | tf_op jit(solution)/shard_map/lag_core_sum/ppermute | solution.py:388
  22.9 1.4 %collective-permute-start.8 = (bf16[128,512]{1,0:T(8,128)(2,1)S(1)}, bf16[128,512]{1,0:T(8,128)(2,1)S(1)}, u32[]{:S(2)}, u32[]{:S(2)}) collective-permute-start(bf16[128,512]{1,0:T(8,128)(2,1)S(1)} %get-tuple-element.54), channel_id=1, source_target_pairs={{0,4},{4,0},{8,12},{12,8},{16,20},{20,16},{24,28},{28,24},{1,5},{5... | collective-permute-start | bytes 393224 | tf_op jit(solution)/shard_map/core_sum/ppermute | solution.py:388
  23.0 15.1 %copy-start.4 = (bf16[512,512]{1,0:T(8,128)(2,1)S(1)}, bf16[512,512]{1,0:T(8,128)(2,1)}, u32[]{:S(2)}) copy-start(bf16[512,512]{1,0:T(8,128)(2,1)} %refs_4_.3) | copy-start | bytes 1572868
  23.0 7.1 %collective-permute-start.7 = (bf16[128,512]{1,0:T(8,128)(2,1)S(1)}, bf16[128,512]{1,0:T(8,128)(2,1)S(1)}, u32[]{:S(2)}, u32[]{:S(2)}) collective-permute-start(bf16[128,512]{1,0:T(8,128)(2,1)S(1)} %lag_core_sum.1), channel_id=1, source_target_pairs={{0,4},{1,9},{2,18},{3,27},{4,0},{5,13},{6,22},{7,31},{8,12},{9,1},... | collective-permute-start | bytes 393224 | tf_op jit(solution)/shard_map/ppermute | solution.py:395
  24.3 6.3 %collective-permute-start.9 = (bf16[64,512]{1,0:T(8,128)(2,1)S(1)}, bf16[64,512]{1,0:T(8,128)(2,1)S(1)}, u32[]{:S(2)}, u32[]{:S(2)}) collective-permute-start(bf16[64,512]{1,0:T(8,128)(2,1)S(1)} %get-tuple-element.55), channel_id=1, source_target_pairs={{0,4},{1,9},{2,18},{3,27},{4,0},{5,13},{6,22},{7,31},{8,12},{9,1},... | collective-permute-start | bytes 196616 | tf_op jit(solution)/shard_map/ppermute | solution.py:395
  24.5 8.8 %collective-permute-start.10 = (bf16[64,512]{1,0:T(8,128)(2,1)S(1)}, bf16[64,512]{1,0:T(8,128)(2,1)S(1)}, u32[]{:S(2)}, u32[]{:S(2)}) collective-permute-start(bf16[64,512]{1,0:T(8,128)(2,1)S(1)} %get-tuple-element.56), channel_id=1, source_target_pairs={{0,16},{1,25},{2,6},{3,11},{4,20},{5,29},{6,2},{7,15},{8,24},{9,17... | collective-permute-start | bytes 196616 | tf_op jit(solution)/shard_map/ppermute | solution.py:395
  26.1 8.1 %collective-permute-start.14 = (bf16[2,128,128]{2,1,0:T(8,128)(2,1)S(1)}, bf16[2,128,128]{2,1,0:T(8,128)(2,1)S(1)}, u32[]{:S(2)}, u32[]{:S(2)}) collective-permute-start(bf16[2,128,128]{2,1,0:T(8,128)(2,1)S(1)} %get-tuple-element.62), channel_id=1, source_target_pairs={{0,3},{1,0},{2,1},{3,2},{4,7},{5,4},{6,5},{7,6},{8,11},{9,8},{10,9... | collective-permute-start | bytes 196616 | tf_op jit(solution)/shard_map/ppermute | solution.py:185
  30.1 5.8 %collective-permute-start.5 = (bf16[2,128,128]{2,1,0:T(8,128)(2,1)S(1)}, bf16[2,128,128]{2,1,0:T(8,128)(2,1)S(1)}, u32[]{:S(2)}, u32[]{:S(2)}) collective-permute-start(bf16[2,128,128]{2,1,0:T(8,128)(2,1)S(1)} %get-tuple-element.46), channel_id=1, source_target_pairs={{0,1},{1,0},{2,3},{3,2},{4,5},{5,4},{6,7},{7,6},{8,9},{9,8},{10,11... | collective-permute-start | bytes 196616 | tf_op jit(solution)/shard_map/ppermute | solution.py:448
  30.1 9.1 %collective-permute-start.15 = (bf16[2,128,128]{2,1,0:T(8,128)(2,1)S(1)}, bf16[2,128,128]{2,1,0:T(8,128)(2,1)S(1)}, u32[]{:S(2)}, u32[]{:S(2)}) collective-permute-start(bf16[2,128,128]{2,1,0:T(8,128)(2,1)S(1)} %get-tuple-element.63), channel_id=1, source_target_pairs={{0,2},{1,3},{2,0},{3,1},{4,6},{5,7},{6,4},{7,5},{8,10},{9,11},{10,... | collective-permute-start | bytes 196616 | tf_op jit(solution)/shard_map/ppermute | solution.py:185
  30.7 8.5 %collective-permute-start.16 = (bf16[2,128,128]{2,1,0:T(8,128)(2,1)S(1)}, bf16[2,128,128]{2,1,0:T(8,128)(2,1)S(1)}, u32[]{:S(2)}, u32[]{:S(2)}) collective-permute-start(bf16[2,128,128]{2,1,0:T(8,128)(2,1)S(1)} %get-tuple-element.64), channel_id=1, source_target_pairs={{0,1},{1,2},{2,3},{3,0},{4,5},{5,6},{6,7},{7,4},{8,9},{9,10},{10,1... | collective-permute-start | bytes 196616 | tf_op jit(solution)/shard_map/ppermute | solution.py:185
  33.4 6.2 %collective-permute-start.11 = (bf16[192,128]{1,0:T(8,128)(2,1)S(1)}, bf16[192,128]{1,0:T(8,128)(2,1)S(1)}, u32[]{:S(2)}, u32[]{:S(2)}) collective-permute-start(bf16[192,128]{1,0:T(8,128)(2,1)S(1)} %get-tuple-element.58), channel_id=1, source_target_pairs={{0,1},{1,2},{2,3},{3,0},{4,5},{5,6},{6,7},{7,4},{8,9},{9,10},{10,1... | collective-permute-start | bytes 147464 | tf_op jit(solution)/shard_map/ppermute | solution.py:185
  34.2 6.9 %collective-permute-start.12 = (bf16[192,128]{1,0:T(8,128)(2,1)S(1)}, bf16[192,128]{1,0:T(8,128)(2,1)S(1)}, u32[]{:S(2)}, u32[]{:S(2)}) collective-permute-start(bf16[192,128]{1,0:T(8,128)(2,1)S(1)} %get-tuple-element.59), channel_id=1, source_target_pairs={{0,2},{1,3},{2,0},{3,1},{4,6},{5,7},{6,4},{7,5},{8,10},{9,11},{10,... | collective-permute-start | bytes 147464 | tf_op jit(solution)/shard_map/ppermute | solution.py:185
  35.9 5.2 %collective-permute-start.13 = (bf16[192,128]{1,0:T(8,128)(2,1)S(1)}, bf16[192,128]{1,0:T(8,128)(2,1)S(1)}, u32[]{:S(2)}, u32[]{:S(2)}) collective-permute-start(bf16[192,128]{1,0:T(8,128)(2,1)S(1)} %get-tuple-element.60), channel_id=1, source_target_pairs={{0,3},{1,0},{2,1},{3,2},{4,7},{5,4},{6,5},{7,6},{8,11},{9,8},{10,9... | collective-permute-start | bytes 147464 | tf_op jit(solution)/shard_map/ppermute | solution.py:185

commit v8 on v7

--- a/solution.py
+++ b/solution.py
@@ -273,7 +273,8 @@
     def put_result(outs, index, total, arrays):
         if len(outs) == seq:
             for step, out in enumerate(outs):
-                out[index] = pick_rows(total, ahead(step), rows).astype(BF16)
+                place = lax.axis_index("ctx") ^ step if fast else ahead(step)
+                out[index] = pick_rows(total, place, rows).astype(BF16)
             return
         for far in range(4):
             piece = pick_rows(total, lax.axis_index("ctx") ^ far, rows).astype(BF16)
@@ -407,10 +408,8 @@
         lag_term = to_chip(lag_sum, 0)
 
         def gated_kernel(*refs):
-            stays_ref, near_ref, gate_ref, cot_ref, beside_ref, _, *refs = refs
-            kept, given, turned, gated, cots, whole = refs
-            turned[0] = stays_ref[1]
-            turned[1] = near_ref[1]
+            stays_ref, near_ref, gate_ref, cot_ref, beside_ref, *refs = refs
+            kept, given, gated, cots, whole = refs
             here = lax.axis_index("ctx")
             cots[:rows] = cot_ref[...]
             cots[rows:] = beside_ref[:, :width]
@@ -434,10 +433,10 @@
 
         term_shape = (2 * own_rows, width)
         with jax.named_scope("weight_partial"):
-            kept, given, goes_on = call(
+            kept, given = call(
                 gated_kernel,
-                [(term_shape, F32), (term_shape, BF16), ((2, rows, cols), BF16)],
-                (second_stays, second_near, gate_two[0], grad_out[0], beside_in, gate_two[0]),
+                [(term_shape, F32), (term_shape, BF16)],
+                (second_stays, second_near, gate_two[0], grad_out[0], beside_in),
                 scratch=[
                     pltpu.VMEM((2 * rows, 2 * cols), BF16),
                     pltpu.VMEM((2 * rows, width), BF16),
@@ -445,19 +444,25 @@
                 ],
                 limit=limit,
             )
-        second_far = lax.ppermute(goes_on, "ctx", across(1))
+
+        def terms_kernel(kept_ref, taken_ref, stays_ref, near_ref, home_ref, one, two, goes_on):
+            core_kernel(kept_ref, taken_ref, one, two)
+            goes_on[0] = stays_ref[1]
+            goes_on[1] = near_ref[1]
+            goes_on[2:] = home_ref[...]
 
         with jax.named_scope("core_sum"):
-            sends = call(
-                core_kernel,
-                [((own_rows, width), BF16)] * 2,
-                (kept, to_core(given)),
+            *sends, goes_on = call(
+                terms_kernel,
+                [((own_rows, width), BF16)] * 2 + [((4, rows, cols), BF16)],
+                (kept, to_core(given), second_stays, second_near, sends_home[1]),
                 limit=limit,
             )
+        second_far = lax.ppermute(goes_on, "ctx", across(1))
 
         chip_terms = [to_chip(sends[0], 0), to_chip(sends[1], 2)]
 
-        home = around(sends_home)
+        home = [lax.ppermute(sends_home[far], "ctx", across(far)) for far in (2, 3)]
 
         def place_kernel(lag_ref, one, two, *refs):
             outs, total = refs[:-1], refs[-1]
@@ -499,14 +504,13 @@
                 limit=limit,
             )
 
-        order = (0, 3, 2, 1)
-
         def final_kernel(*refs):
             arrived, parts, refs = refs[:seq], refs[seq : 2 * seq], refs[2 * seq :]
             filter_ref, weight_ref, gate_ref, value_ref = refs
-            for step, part in zip(order, parts):
-                put_columns(gate_ref, held(behind(step)), cols, seq, part[0])
-                put_columns(value_ref, held(behind(step)), cols, seq, part[1])
+            for part, (far, first) in zip(parts, ((0, 0), (1, 2), (2, 0), (3, 0))):
+                place = held(lax.axis_index("ctx") ^ far)
+                put_columns(gate_ref, place, cols, seq, part[first])
+                put_columns(value_ref, place, cols, seq, part[first + 1])
             total = arrived[0][...]
             for part in arrived[1:]:
                 total = total + part[...].astype(F32)
@@ -520,7 +524,7 @@
             filter_grad, weight_grad, grad_gate_one, grad_value = call(
                 final_kernel,
                 [((2, fine, rows), F32), ((own_rows, cols), F32), wide_bf16, wide_bf16],
-                (*last_terms, *(home[step] for step in order)),
+                (*last_terms, sends_home[0], second_far, *home),
             )
         filter_grad = jnp.swapaxes(filter_grad, 1, 2)
         return (

time: 42 us -> 41.5 us (0.988)
  starting transfers between devices: 23.1 us -> 21.7 us
  waiting for transfers between devices: 8.54 us -> 9.47 us
    ppermute x9 -> x6, starting transfers between devices: 18.9 us -> 10.9 us  [around(): out.append(lax.ppermute(blocks[step], 'ctx', pairs))]
    ppermute x0 -> x2, starting transfers between devices: none -> 5.19 us  [on_device(): home = [lax.ppermute(sends_home[far], 'ctx', across(far)) for far in (2, 3)]]
    ppermute x1, starting transfers between devices: 0.01 us -> 1.68 us  [on_device(): second_far = lax.ppermute(goes_on, 'ctx', across(1))]
    ppermute x9 -> x6, waiting for transfers between devices: 5.45 us -> 6.36 us  [around(): out.append(lax.ppermute(blocks[step], 'ctx', pairs))]
  transfers between devices with their start and end apart: 17 -> 16, of which waited for: 6 -> 6; matrix products, arithmetic and copies ran while one was open for 0% -> 0% of each run, Pallas kernels for 14% -> 14%
where the time goes in v8:
time: 41.5 us; the launch traced here: 41.4 us
  starting transfers between devices  21.7 us (52%)
  waiting for transfers between devices  9.47 us (23%)
  Pallas kernels  8.36 us (20%)
  local copies, waits for them, and re-layouts  1.03 us (2%)
  between operations  0.77 us (2%)
    ppermute x6, starting transfers between devices, around(): out.append(lax.ppermute(blocks[step], 'ctx', pairs))  10.9 us
    pallas_call x10, Pallas kernels, call(): pl.pallas_call(kernel, out_shape=[jax.ShapeDtypeStruct(shape, dtype) for...  8.36 us
    ppermute x6, waiting for transfers between devices, around(): out.append(lax.ppermute(blocks[step], 'ctx', pairs))  6.36 us
    ppermute x2, starting transfers between devices, on_device(): home = [lax.ppermute(sends_home[far], 'ctx', across(far)) for far in (2, 3)]  5.19 us
    ppermute x1, waiting for transfers between devices, on_device(): second_near = lax.ppermute(goes, 'ctx', across(2))  2.36 us
    ppermute x3, starting transfers between devices, to_chip(): return lax.ppermute(block, ('dp', 'ctx'), pairs)  2.07 us
    ppermute x1, starting transfers between devices, on_device(): second_far = lax.ppermute(goes_on, 'ctx', across(1))  1.68 us
    ppermute x1, starting transfers between devices, on_device(): second_near = lax.ppermute(goes, 'ctx', across(2))  1.07 us
  transfers between devices with their start and end apart: 16, of which 6 were waited for; matrix products, arithmetic and copies ran while one was open for 0% of the time, Pallas kernels for 14%

profile of v8, /device:TPU:0, one launch (start us, length us, event | category | flops | bytes accessed | tf_op | source)
XLA Modules:
  0.0 41.4 jit_solution(12988173900512777764)
XLA Ops:
  0.6 0.0 copy-start
  0.6 0.0 copy-start.4
  0.7 0.0 copy-start.5
  0.7 1.7 %load.1 = (bf16[3,128,128]{2,1,0:T(8,128)(2,1)S(1)}, bf16[3,128,128]{2,1,0:T(8,128)(2,1)S(1)}, bf16[3,128,128]{2,1,0:T(8,128)(2,1)S(1)}, bf16[3,128,128]{2,1,0:T(8,128)(2,1)S(1)}) custom-call(bf16[1,128,512]{2,1,0:T(8,128)(2,1)} %refs_0_.1, bf16[1,128,512]{2,1,0:T(8,128)(2,1)} %refs_1_.1, bf16[1,128,512]{2,1,0:T(8,128)(2,1)} %refs_2_.1, ...), custom_call_target="tpu_custom_call" | custom-call | flops 67108864 | bytes 1048576 | tf_op jit(solution)/shard_map/load/pallas_call | solution.py:142
  2.4 3.1 %collective-permute-start = (bf16[3,128,128]{2,1,0:T(8,128)(2,1)S(1)}, bf16[3,128,128]{2,1,0:T(8,128)(2,1)S(1)}, u32[]{:S(2)}, u32[]{:S(2)}) collective-permute-start(bf16[3,128,128]{2,1,0:T(8,128)(2,1)S(1)} %get-tuple-element.39), channel_id=1, source_target_pairs={{0,1},{1,2},{2,3},{3,0},{4,5},{5,6},{6,7},{7,4},{8,9},{9,10},{10,1... | collective-permute-start | bytes 294920 | tf_op jit(solution)/shard_map/ppermute | solution.py:185
  5.4 2.6 %collective-permute-start.1 = (bf16[3,128,128]{2,1,0:T(8,128)(2,1)S(1)}, bf16[3,128,128]{2,1,0:T(8,128)(2,1)S(1)}, u32[]{:S(2)}, u32[]{:S(2)}) collective-permute-start(bf16[3,128,128]{2,1,0:T(8,128)(2,1)S(1)} %get-tuple-element.40), channel_id=1, source_target_pairs={{0,2},{1,3},{2,0},{3,1},{4,6},{5,7},{6,4},{7,5},{8,10},{9,11},{10,... | collective-permute-start | bytes 294920 | tf_op jit(solution)/shard_map/ppermute | solution.py:185
  8.0 1.3 %collective-permute-start.2 = (bf16[3,128,128]{2,1,0:T(8,128)(2,1)S(1)}, bf16[3,128,128]{2,1,0:T(8,128)(2,1)S(1)}, u32[]{:S(2)}, u32[]{:S(2)}) collective-permute-start(bf16[3,128,128]{2,1,0:T(8,128)(2,1)S(1)} %get-tuple-element.41), channel_id=1, source_target_pairs={{0,3},{1,0},{2,1},{3,2},{4,7},{5,4},{6,5},{7,6},{8,11},{9,8},{10,9... | collective-permute-start | bytes 294920 | tf_op jit(solution)/shard_map/ppermute | solution.py:185
  9.4 0.0 copy-done
  9.4 0.0 copy-done.4
  9.4 0.0 copy-done.5
  9.4 0.9 %copy-done.1 = bf16[512,256]{1,0:T(8,128)(2,1)S(1)} copy-done((bf16[512,256]{1,0:T(8,128)(2,1)S(1)}, bf16[512,256]{1,0:T(8,128)(2,1)}, u32[]{:S(2)}) %copy-start.1) | copy-done | bytes 262168
  10.3 0.1 copy-done.2
  10.4 0.4 %filter_spectra.1 = (f32[2,512,256]{2,1,0:T(8,128)S(1)}, bf16[128,768]{1,0:T(8,128)(2,1)S(1)}) custom-call(bf16[2,512,128]{2,1,0:T(8,128)(2,1)S(1)} %constant_dynamic-slice_fusion.filters_ref, bf16[512,256]{1,0:T(8,128)(2,1)S(1)} %copy-done.2, bf16[512,256]{1,0:T(8,128)(2,1)S(1)} %copy-done.1, bf16[128,512]{1,0:T(8,128)(2,1)S(1)} %bitcast.7, ...), custom_call_target="tpu_custom_call" | custom-call | flops 268435456 | bytes 1048576 | tf_op jit(solution)/shard_map/filter_spectra/pallas_call | solution.py:142
  10.9 0.7 %collective-permute-start.4 = (bf16[128,768]{1,0:T(8,128)(2,1)S(1)}, bf16[128,768]{1,0:T(8,128)(2,1)S(1)}, u32[]{:S(2)}, u32[]{:S(2)}) collective-permute-start(bf16[128,768]{1,0:T(8,128)(2,1)S(1)} %get-tuple-element.45), channel_id=1, source_target_pairs={{0,1},{1,0},{2,3},{3,2},{4,5},{5,4},{6,7},{7,6},{8,9},{9,8},{10,11... | collective-permute-start | bytes 589832 | tf_op jit(solution)/shard_map/ppermute | solution.py:271
  11.6 0.0 collective-permute-done.refs_1_
  11.6 3.0 %collective-permute-done.1.refs_2_ = bf16[3,128,128]{2,1,0:T(8,128)(2,1)S(1)} collective-permute-done((bf16[3,128,128]{2,1,0:T(8,128)(2,1)S(1)}, bf16[3,128,128]{2,1,0:T(8,128)(2,1)S(1)}, u32[]{:S(2)}, u32[]{:S(2)}) %collective-permute-start.1) | collective-permute-done | bytes 98336 | tf_op jit(solution)/shard_map/ppermute | solution.py:185
  14.6 0.6 %collective-permute-done.2.refs_3_ = bf16[3,128,128]{2,1,0:T(8,128)(2,1)S(1)} collective-permute-done((bf16[3,128,128]{2,1,0:T(8,128)(2,1)S(1)}, bf16[3,128,128]{2,1,0:T(8,128)(2,1)S(1)}, u32[]{:S(2)}, u32[]{:S(2)}) %collective-permute-start.2) | collective-permute-done | bytes 98336 | tf_op jit(solution)/shard_map/ppermute | solution.py:185
  15.2 1.5 %forward_convolutions.1 = (f32[512,128]{1,0:T(8,128)S(1)}, f32[512,256]{1,0:T(8,128)S(1)}, f32[512,256]{1,0:T(8,128)S(1)}, bf16[2,128,128]{2,1,0:T(8,128)(2,1)S(1)}, bf16[2,128,128]{2,1,0:T(8,128)(2,1)S(1)}) custom-call(bf16[3,128,128]{2,1,0:T(8,128)(2,1)S(1)} %get-tuple-element.38.refs_0_, bf16[3,128,128]{2,1,0:T(8,128)(2,1)S(1)} %collective-permute-done.refs_1_, ...), custom_call_target="tpu_custom_call" | custom-call | flops 402653184 | bytes 2228224 | tf_op jit(solution)/shard_map/forward_convolutions/pallas_call | solution.py:142
  16.6 1.1 %collective-permute-start.3 = (bf16[2,128,128]{2,1,0:T(8,128)(2,1)S(1)}, bf16[2,128,128]{2,1,0:T(8,128)(2,1)S(1)}, u32[]{:S(2)}, u32[]{:S(2)}) collective-permute-start(bf16[2,128,128]{2,1,0:T(8,128)(2,1)S(1)} %get-tuple-element.44), channel_id=1, source_target_pairs={{0,2},{1,3},{2,0},{3,1},{4,6},{5,7},{6,4},{7,5},{8,10},{9,11},{10,... | collective-permute-start | bytes 196616 | tf_op jit(solution)/shard_map/ppermute | solution.py:316
  17.7 2.5 %backward_convolutions.1 = (f32[2,512,128]{2,1,0:T(8,128)}, f32[128,512]{1,0:T(8,128)S(1)}, bf16[128,512]{1,0:T(8,128)(2,1)S(1)}, bf16[2,128,128]{2,1,0:T(8,128)...) custom-call(bf16[3,128,128]{2,1,0:T(8,128)(2,1)S(1)} %get-tuple-elem, ...), custom_call_target="tpu_custom_call" | custom-call | flops 536870912 | bytes 3538944 | tf_op jit(solution)/shard_map/backward_convolutions/pallas_call | solution.py:142
  20.2 0.0 collective-permute-start.7
  20.2 2.4 %collective-permute-done.3.refs_1_.near_ref = bf16[2,128,128]{2,1,0:T(8,128)(2,1)S(1)} collective-permute-done((bf16[2,128,128]{2,1,0:T(8,128)(2,1)S(1)}, bf16[2,128,128]{2,1,0:T(8,128)(2,1)S(1)}, u32[]{:S(2)}, u32[]{:S(2)}) %collective-permute-start.3) | collective-permute-done | bytes 65568 | tf_op jit(solution)/shard_map/ppermute | solution.py:316
  22.6 0.0 collective-permute-done.4.refs_4_
  22.6 0.3 weight_partial.1
  22.9 0.1 collective-permute-start.5
  23.0 0.0 collective-permute-done.7.taken_ref
  23.0 0.0 copy-start.3
  23.1 0.5 %collective-permute-start.8 = (bf16[128,512]{1,0:T(8,128)(2,1)S(1)}, bf16[128,512]{1,0:T(8,128)(2,1)S(1)}, u32[]{:S(2)}, u32[]{:S(2)}) collective-permute-start(bf16[128,512]{1,0:T(8,128)(2,1)S(1)} %lag_core_sum.1), channel_id=1, source_target_pairs={{0,4},{1,9},{2,18},{3,27},{4,0},{5,13},{6,22},{7,31},{8,12},{9,1},... | collective-permute-start | bytes 393224 | tf_op jit(solution)/shard_map/ppermute | solution.py:396
  23.6 0.7 %collective-permute-done.5.taken_ref = bf16[128,512]{1,0:T(8,128)(2,1)S(1)} collective-permute-done((bf16[128,512]{1,0:T(8,128)(2,1)S(1)}, bf16[128,512]{1,0:T(8,128)(2,1)S(1)}, u32[]{:S(2)}, u32[]{:S(2)}) %collective-permute-start.5) | collective-permute-done | bytes 131104 | tf_op jit(solution)/shard_map/core_sum/ppermute | solution.py:389
  24.4 1.7 %collective-permute-start.6 = (bf16[4,128,128]{2,1,0:T(8,128)(2,1)S(1)}, bf16[4,128,128]{2,1,0:T(8,128)(2,1)S(1)}, u32[]{:S(2)}, u32[]{:S(2)}) collective-permute-start(bf16[4,128,128]{2,1,0:T(8,128)(2,1)S(1)} %get-tuple-element.52), channel_id=1, source_target_pairs={{0,1},{1,0},{2,3},{3,2},{4,5},{5,4},{6,7},{7,6},{8,9},{9,8},{10,11... | collective-permute-start | bytes 393224 | tf_op jit(solution)/shard_map/ppermute | solution.py:461
  26.0 0.0 collective-permute-start.9
  26.0 1.5 %collective-permute-start.10 = (bf16[64,512]{1,0:T(8,128)(2,1)S(1)}, bf16[64,512]{1,0:T(8,128)(2,1)S(1)}, u32[]{:S(2)}, u32[]{:S(2)}) collective-permute-start(bf16[64,512]{1,0:T(8,128)(2,1)S(1)} %get-tuple-element.57), channel_id=1, source_target_pairs={{0,16},{1,25},{2,6},{3,11},{4,20},{5,29},{6,2},{7,15},{8,24},{9,17... | collective-permute-start | bytes 196616 | tf_op jit(solution)/shard_map/ppermute | solution.py:396
  27.6 1.6 %collective-permute-start.14 = (bf16[2,128,128]{2,1,0:T(8,128)(2,1)S(1)}, bf16[2,128,128]{2,1,0:T(8,128)(2,1)S(1)}, u32[]{:S(2)}, u32[]{:S(2)}) collective-permute-start(bf16[2,128,128]{2,1,0:T(8,128)(2,1)S(1)} %get-tuple-element.63), channel_id=1, source_target_pairs={{0,2},{1,3},{2,0},{3,1},{4,6},{5,7},{6,4},{7,5},{8,10},{9,11},{10,... | collective-permute-start | bytes 196616 | tf_op jit(solution)/shard_map/ppermute | solution.py:465
  29.2 0.0 collective-permute-done.8.lag_ref
  29.2 3.6 %collective-permute-start.15 = (bf16[2,128,128]{2,1,0:T(8,128)(2,1)S(1)}, bf16[2,128,128]{2,1,0:T(8,128)(2,1)S(1)}, u32[]{:S(2)}, u32[]{:S(2)}) collective-permute-start(bf16[2,128,128]{2,1,0:T(8,128)(2,1)S(1)} %get-tuple-element.64), channel_id=1, source_target_pairs={{0,3},{1,2},{2,1},{3,0},{4,7},{5,6},{6,5},{7,4},{8,11},{9,10},{10,... | collective-permute-start | bytes 196616 | tf_op jit(solution)/shard_map/ppermute | solution.py:465
  32.8 0.0 collective-permute-done.9.one
  32.8 0.0 collective-permute-done.10.two
  32.8 1.4 %collective-permute-start.11 = (bf16[192,128]{1,0:T(8,128)(2,1)S(1)}, bf16[192,128]{1,0:T(8,128)(2,1)S(1)}, u32[]{:S(2)}, u32[]{:S(2)}) collective-permute-start(bf16[192,128]{1,0:T(8,128)(2,1)S(1)} %get-tuple-element.59), channel_id=1, source_target_pairs={{0,1},{1,2},{2,3},{3,0},{4,5},{5,6},{6,7},{7,4},{8,9},{9,10},{10,1... | collective-permute-start | bytes 147464 | tf_op jit(solution)/shard_map/ppermute | solution.py:185
  34.2 1.7 %collective-permute-start.12 = (bf16[192,128]{1,0:T(8,128)(2,1)S(1)}, bf16[192,128]{1,0:T(8,128)(2,1)S(1)}, u32[]{:S(2)}, u32[]{:S(2)}) collective-permute-start(bf16[192,128]{1,0:T(8,128)(2,1)S(1)} %get-tuple-element.60), channel_id=1, source_target_pairs={{0,2},{1,3},{2,0},{3,1},{4,6},{5,7},{6,4},{7,5},{8,10},{9,11},{10,... | collective-permute-start | bytes 147464 | tf_op jit(solution)/shard_map/ppermute | solution.py:185
  35.9 0.0 collective-permute-done.6.refs_2_.refs_5_
  35.9 0.8 %collective-permute-start.13 = (bf16[192,128]{1,0:T(8,128)(2,1)S(1)}, bf16[192,128]{1,0:T(8,128)(2,1)S(1)}, u32[]{:S(2)}, u32[]{:S(2)}) collective-permute-start(bf16[192,128]{1,0:T(8,128)(2,1)S(1)} %get-tuple-element.61), channel_id=1, source_target_pairs={{0,3},{1,0},{2,1},{3,2},{4,7},{5,4},{6,5},{7,6},{8,11},{9,8},{10,9... | collective-permute-start | bytes 147464 | tf_op jit(solution)/shard_map/ppermute | solution.py:185
  36.7 1.1 %mixed.1 = (bf16[128,512]{1,0:T(8,128)(2,1)}, bf16[128,512]{1,0:T(8,128)(2,1)}) custom-call(bf16[2,128,128]{2,1,0:T(8,128)(2,1)S(1)} %get-tuple-element.43.refs_0_.stays_ref, bf16[2,128,128]{2,1,0:T(8,128)(2,1)S(1)} %collective-permute-done.3.refs_1_.near_ref, bf16[4,128,128]{2,1,0:T(8,128)(2,1)S(1)} %collective-permute-done.6.refs_2_.refs_5_, ...), custom_call_target="tpu_custom_call" | custom-call | flops 134217728 | bytes 1048576 | tf_op jit(solution)/shard_map/mixed/pallas_call | solution.py:142
  37.8 0.0 collective-permute-done.14.refs_6_
  37.8 0.0 collective-permute-done.15.refs_7_
  37.8 1.4 %collective-permute-done.11.refs_1_ = bf16[192,128]{1,0:T(8,128)(2,1)S(1)} collective-permute-done((bf16[192,128]{1,0:T(8,128)(2,1)S(1)}, bf16[192,128]{1,0:T(8,128)(2,1)S(1)}, u32[]{:S(2)}, u32[]{:S(2)}) %collective-permute-start.11) | collective-permute-done | bytes 49184 | tf_op jit(solution)/shard_map/ppermute | solution.py:185
  39.2 1.4 %collective-permute-done.12.refs_2_ = bf16[192,128]{1,0:T(8,128)(2,1)S(1)} collective-permute-done((bf16[192,128]{1,0:T(8,128)(2,1)S(1)}, bf16[192,128]{1,0:T(8,128)(2,1)S(1)}, u32[]{:S(2)}, u32[]{:S(2)}) %collective-permute-start.12) | collective-permute-done | bytes 49184 | tf_op jit(solution)/shard_map/ppermute | solution.py:185
  40.6 0.0 collective-permute-done.13.refs_3_
  40.6 0.8 %means.1 = (f32[2,64,128]{2,1,0:T(8,128)}, f32[64,128]{1,0:T(8,128)}, bf16[128,512]{1,0:T(8,128)(2,1)}, bf16[128,512]{1,0:T(8,128)(2,1)}) custom-call(f32[192,128]{1,0:T(8,128)S(1)} %get-tuple-element.58.refs_0_, bf16[192,128]{1,0:T(8,128)(2,1)S(1)} %collective-permute-done.11.refs_1_, bf16[192,128]{1,0:T(8,128)(2,1)S(1)} %collective-permute-done.12.refs_2_, ...), custom_call_target="tpu_custom_call" | custom-call | bytes 573440 | tf_op jit(solution)/shard_map/means/pallas_call | solution.py:142
  (9 shorter events, 0.1 us)
Async XLA Ops:
  0.6 8.7 %copy-start = (bf16[2,512,512]{2,1,0:T(8,128)(2,1)S(1)}, bf16[2,512,512]{2,1,0:T(8,128)(2,1)}, u32[]{:S(2)}) copy-start(bf16[2,512,512]{2,1,0:T(8,128)(2,1)} %param.12) | copy-start | bytes 3145732
  0.6 8.8 %copy-start.4 = (bf16[1,128,512]{2,1,0:T(8,128)(2,1)S(1)}, bf16[1,128,512]{2,1,0:T(8,128)(2,1)}, u32[]{:S(2)}) copy-start(bf16[1,128,512]{2,1,0:T(8,128)(2,1)} %refs_2_.1) | copy-start | bytes 393220
  0.7 8.8 %copy-start.5 = (bf16[1,128,512]{2,1,0:T(8,128)(2,1)S(1)}, bf16[1,128,512]{2,1,0:T(8,128)(2,1)}, u32[]{:S(2)}) copy-start(bf16[1,128,512]{2,1,0:T(8,128)(2,1)} %refs_4_.2) | copy-start | bytes 393220
  2.4 9.3 %collective-permute-start = (bf16[3,128,128]{2,1,0:T(8,128)(2,1)S(1)}, bf16[3,128,128]{2,1,0:T(8,128)(2,1)S(1)}, u32[]{:S(2)}, u32[]{:S(2)}) collective-permute-start(bf16[3,128,128]{2,1,0:T(8,128)(2,1)S(1)} %get-tuple-element.39), channel_id=1, source_target_pairs={{0,1},{1,2},{2,3},{3,0},{4,5},{5,6},{6,7},{7,4},{8,9},{9,10},{10,1... | collective-permute-start | bytes 294920 | tf_op jit(solution)/shard_map/ppermute | solution.py:185
  5.4 9.2 %collective-permute-start.1 = (bf16[3,128,128]{2,1,0:T(8,128)(2,1)S(1)}, bf16[3,128,128]{2,1,0:T(8,128)(2,1)S(1)}, u32[]{:S(2)}, u32[]{:S(2)}) collective-permute-start(bf16[3,128,128]{2,1,0:T(8,128)(2,1)S(1)} %get-tuple-element.40), channel_id=1, source_target_pairs={{0,2},{1,3},{2,0},{3,1},{4,6},{5,7},{6,4},{7,5},{8,10},{9,11},{10,... | collective-permute-start | bytes 294920 | tf_op jit(solution)/shard_map/ppermute | solution.py:185
  8.0 7.1 %collective-permute-start.2 = (bf16[3,128,128]{2,1,0:T(8,128)(2,1)S(1)}, bf16[3,128,128]{2,1,0:T(8,128)(2,1)S(1)}, u32[]{:S(2)}, u32[]{:S(2)}) collective-permute-start(bf16[3,128,128]{2,1,0:T(8,128)(2,1)S(1)} %get-tuple-element.41), channel_id=1, source_target_pairs={{0,3},{1,0},{2,1},{3,2},{4,7},{5,4},{6,5},{7,6},{8,11},{9,8},{10,9... | collective-permute-start | bytes 294920 | tf_op jit(solution)/shard_map/ppermute | solution.py:185
  9.4 1.0 %copy-start.1 = (bf16[512,256]{1,0:T(8,128)(2,1)S(1)}, bf16[512,256]{1,0:T(8,128)(2,1)}, u32[]{:S(2)}) copy-start(bf16[512,256]{1,0:T(8,128)(2,1)} %constant.26.clone.low.refs_6_.refs_9_) | copy-start | bytes 786436
  9.4 1.0 %copy-start.2 = (bf16[512,256]{1,0:T(8,128)(2,1)S(1)}, bf16[512,256]{1,0:T(8,128)(2,1)}, u32[]{:S(2)}) copy-start(bf16[512,256]{1,0:T(8,128)(2,1)} %constant.25.clone.high.refs_5_.refs_8_) | copy-start | bytes 786436
  10.4 4.8 %copy-start.6 = (bf16[256,512]{1,0:T(8,128)(2,1)S(1)}, bf16[256,512]{1,0:T(8,128)(2,1)}, u32[]{:S(2)}) copy-start(bf16[256,512]{1,0:T(8,128)(2,1)} %constant.27.clone.refs_7_.refs_10_) | copy-start | bytes 786436
  10.9 11.7 %collective-permute-start.4 = (bf16[128,768]{1,0:T(8,128)(2,1)S(1)}, bf16[128,768]{1,0:T(8,128)(2,1)S(1)}, u32[]{:S(2)}, u32[]{:S(2)}) collective-permute-start(bf16[128,768]{1,0:T(8,128)(2,1)S(1)} %get-tuple-element.45), channel_id=1, source_target_pairs={{0,1},{1,0},{2,3},{3,2},{4,5},{5,4},{6,7},{7,6},{8,9},{9,8},{10,11... | collective-permute-start | bytes 589832 | tf_op jit(solution)/shard_map/ppermute | solution.py:271
  16.6 5.9 %collective-permute-start.3 = (bf16[2,128,128]{2,1,0:T(8,128)(2,1)S(1)}, bf16[2,128,128]{2,1,0:T(8,128)(2,1)S(1)}, u32[]{:S(2)}, u32[]{:S(2)}) collective-permute-start(bf16[2,128,128]{2,1,0:T(8,128)(2,1)S(1)} %get-tuple-element.44), channel_id=1, source_target_pairs={{0,2},{1,3},{2,0},{3,1},{4,6},{5,7},{6,4},{7,5},{8,10},{9,11},{10,... | collective-permute-start | bytes 196616 | tf_op jit(solution)/shard_map/ppermute | solution.py:316
  20.2 2.8 %collective-permute-start.7 = (bf16[128,512]{1,0:T(8,128)(2,1)S(1)}, bf16[128,512]{1,0:T(8,128)(2,1)S(1)}, u32[]{:S(2)}, u32[]{:S(2)}) collective-permute-start(bf16[128,512]{1,0:T(8,128)(2,1)S(1)} %get-tuple-element.55), channel_id=1, source_target_pairs={{0,4},{4,0},{8,12},{12,8},{16,20},{20,16},{24,28},{28,24},{1,5},{5... | collective-permute-start | bytes 393224 | tf_op jit(solution)/shard_map/lag_core_sum/ppermute | solution.py:389
  22.9 1.4 %collective-permute-start.5 = (bf16[128,512]{1,0:T(8,128)(2,1)S(1)}, bf16[128,512]{1,0:T(8,128)(2,1)S(1)}, u32[]{:S(2)}, u32[]{:S(2)}) collective-permute-start(bf16[128,512]{1,0:T(8,128)(2,1)S(1)} %get-tuple-element.47), channel_id=1, source_target_pairs={{0,4},{4,0},{8,12},{12,8},{16,20},{20,16},{24,28},{28,24},{1,5},{5... | collective-permute-start | bytes 393224 | tf_op jit(solution)/shard_map/core_sum/ppermute | solution.py:389
  23.0 13.7 %copy-start.3 = (bf16[512,512]{1,0:T(8,128)(2,1)S(1)}, bf16[512,512]{1,0:T(8,128)(2,1)}, u32[]{:S(2)}) copy-start(bf16[512,512]{1,0:T(8,128)(2,1)} %refs_4_.3) | copy-start | bytes 1572868
  23.1 6.1 %collective-permute-start.8 = (bf16[128,512]{1,0:T(8,128)(2,1)S(1)}, bf16[128,512]{1,0:T(8,128)(2,1)S(1)}, u32[]{:S(2)}, u32[]{:S(2)}) collective-permute-start(bf16[128,512]{1,0:T(8,128)(2,1)S(1)} %lag_core_sum.1), channel_id=1, source_target_pairs={{0,4},{1,9},{2,18},{3,27},{4,0},{5,13},{6,22},{7,31},{8,12},{9,1},... | collective-permute-start | bytes 393224 | tf_op jit(solution)/shard_map/ppermute | solution.py:396
  24.4 11.5 %collective-permute-start.6 = (bf16[4,128,128]{2,1,0:T(8,128)(2,1)S(1)}, bf16[4,128,128]{2,1,0:T(8,128)(2,1)S(1)}, u32[]{:S(2)}, u32[]{:S(2)}) collective-permute-start(bf16[4,128,128]{2,1,0:T(8,128)(2,1)S(1)} %get-tuple-element.52), channel_id=1, source_target_pairs={{0,1},{1,0},{2,3},{3,2},{4,5},{5,4},{6,7},{7,6},{8,9},{9,8},{10,11... | collective-permute-start | bytes 393224 | tf_op jit(solution)/shard_map/ppermute | solution.py:461
  26.0 6.7 %collective-permute-start.9 = (bf16[64,512]{1,0:T(8,128)(2,1)S(1)}, bf16[64,512]{1,0:T(8,128)(2,1)S(1)}, u32[]{:S(2)}, u32[]{:S(2)}) collective-permute-start(bf16[64,512]{1,0:T(8,128)(2,1)S(1)} %get-tuple-element.56), channel_id=1, source_target_pairs={{0,4},{1,9},{2,18},{3,27},{4,0},{5,13},{6,22},{7,31},{8,12},{9,1},... | collective-permute-start | bytes 196616 | tf_op jit(solution)/shard_map/ppermute | solution.py:396
  26.0 6.7 %collective-permute-start.10 = (bf16[64,512]{1,0:T(8,128)(2,1)S(1)}, bf16[64,512]{1,0:T(8,128)(2,1)S(1)}, u32[]{:S(2)}, u32[]{:S(2)}) collective-permute-start(bf16[64,512]{1,0:T(8,128)(2,1)S(1)} %get-tuple-element.57), channel_id=1, source_target_pairs={{0,16},{1,25},{2,6},{3,11},{4,20},{5,29},{6,2},{7,15},{8,24},{9,17... | collective-permute-start | bytes 196616 | tf_op jit(solution)/shard_map/ppermute | solution.py:396
  27.6 10.2 %collective-permute-start.14 = (bf16[2,128,128]{2,1,0:T(8,128)(2,1)S(1)}, bf16[2,128,128]{2,1,0:T(8,128)(2,1)S(1)}, u32[]{:S(2)}, u32[]{:S(2)}) collective-permute-start(bf16[2,128,128]{2,1,0:T(8,128)(2,1)S(1)} %get-tuple-element.63), channel_id=1, source_target_pairs={{0,2},{1,3},{2,0},{3,1},{4,6},{5,7},{6,4},{7,5},{8,10},{9,11},{10,... | collective-permute-start | bytes 196616 | tf_op jit(solution)/shard_map/ppermute | solution.py:465
  29.2 8.6 %collective-permute-start.15 = (bf16[2,128,128]{2,1,0:T(8,128)(2,1)S(1)}, bf16[2,128,128]{2,1,0:T(8,128)(2,1)S(1)}, u32[]{:S(2)}, u32[]{:S(2)}) collective-permute-start(bf16[2,128,128]{2,1,0:T(8,128)(2,1)S(1)} %get-tuple-element.64), channel_id=1, source_target_pairs={{0,3},{1,2},{2,1},{3,0},{4,7},{5,6},{6,5},{7,4},{8,11},{9,10},{10,... | collective-permute-start | bytes 196616 | tf_op jit(solution)/shard_map/ppermute | solution.py:465
  32.8 6.4 %collective-permute-start.11 = (bf16[192,128]{1,0:T(8,128)(2,1)S(1)}, bf16[192,128]{1,0:T(8,128)(2,1)S(1)}, u32[]{:S(2)}, u32[]{:S(2)}) collective-permute-start(bf16[192,128]{1,0:T(8,128)(2,1)S(1)} %get-tuple-element.59), channel_id=1, source_target_pairs={{0,1},{1,2},{2,3},{3,0},{4,5},{5,6},{6,7},{7,4},{8,9},{9,10},{10,1... | collective-permute-start | bytes 147464 | tf_op jit(solution)/shard_map/ppermute | solution.py:185
  34.2 6.4 %collective-permute-start.12 = (bf16[192,128]{1,0:T(8,128)(2,1)S(1)}, bf16[192,128]{1,0:T(8,128)(2,1)S(1)}, u32[]{:S(2)}, u32[]{:S(2)}) collective-permute-start(bf16[192,128]{1,0:T(8,128)(2,1)S(1)} %get-tuple-element.60), channel_id=1, source_target_pairs={{0,2},{1,3},{2,0},{3,1},{4,6},{5,7},{6,4},{7,5},{8,10},{9,11},{10,... | collective-permute-start | bytes 147464 | tf_op jit(solution)/shard_map/ppermute | solution.py:185
  35.9 4.7 %collective-permute-start.13 = (bf16[192,128]{1,0:T(8,128)(2,1)S(1)}, bf16[192,128]{1,0:T(8,128)(2,1)S(1)}, u32[]{:S(2)}, u32[]{:S(2)}) collective-permute-start(bf16[192,128]{1,0:T(8,128)(2,1)S(1)} %get-tuple-element.61), channel_id=1, source_target_pairs={{0,3},{1,0},{2,1},{3,2},{4,7},{5,4},{6,5},{7,6},{8,11},{9,8},{10,9... | collective-permute-start | bytes 147464 | tf_op jit(solution)/shard_map/ppermute | solution.py:185

commit v9 on v8

--- a/solution.py
+++ b/solution.py
@@ -190,6 +190,17 @@
             cot_ref[...], weight_ref[...], (((1,), (1,)), ((), ())), preferred_element_type=F32
         )
 
+    def across(far):
+        return [(i, i ^ far) for i in range(seq)]
+
+    in_order = (0, 3, 1, 2) if fast else range(seq)
+
+    def sent(step):
+        return lax.axis_index("ctx") ^ step if fast else ahead(step)
+
+    def came(step):
+        return lax.axis_index("ctx") ^ step if fast else behind(step)
+
     def load_kernel(*refs):
         value_ref, gate_ref, cot_arg, weight_arg, gate_arg = refs[:5]
         outs, refs = refs[5 : 5 + seq], refs[5 + seq :]
@@ -199,14 +210,8 @@
             (weight_arg, weight_ref),
             (gate_arg.at[0], gate_two_ref),
         ]
-        if cols % 128 == 0:
-            for step, out in enumerate(outs):
-                start = pl.multiple_of(held(ahead(step)) * cols, cols)
-                started.append((value_ref.at[0, :, pl.ds(start, cols)], out.at[0]))
-                started.append((gate_ref.at[0, :, pl.ds(start, cols)], out.at[1]))
-        else:
-            started.append((value_ref.at[0], whole.at[0]))
-            started.append((gate_ref.at[0], whole.at[1]))
+        started.append((value_ref.at[0], whole.at[0]))
+        started.append((gate_ref.at[0], whole.at[1]))
         started = [
             pltpu.make_async_copy(source, target, sems.at[index])
             for index, (source, target) in enumerate(started)
@@ -217,13 +222,12 @@
             copy.wait()
         second[...] = grad_gated(cot_ref, weight_ref) * gate_two_ref[...].astype(F32)
         for step, out in enumerate(outs):
-            out[2] = pick_columns(second, held(ahead(step)), cols, seq).astype(BF16)
+            out[2] = pick_columns(second, held(sent(step)), cols, seq).astype(BF16)
         for copy in started[3:]:
             copy.wait()
-        if cols % 128 != 0:
-            for step, out in enumerate(outs):
-                for index in range(2):
-                    out[index] = pick_columns(whole.at[index], held(ahead(step)), cols, seq)
+        for step, out in enumerate(outs):
+            for index in range(2):
+                out[index] = pick_columns(whole.at[index], held(sent(step)), cols, seq)
 
     triple = ((3, rows, cols), BF16)
     wide_bf16 = ((rows, width), BF16)
@@ -238,16 +242,16 @@
                 pltpu.VMEM((rows, width), BF16),
                 pltpu.VMEM((rows, width), F32),
                 pltpu.VMEM((2, rows, width), BF16),
-                pltpu.SemaphoreType.DMA((2 * seq + 3,)),
+                pltpu.SemaphoreType.DMA((5,)),
             ],
             flops=2 * rows * width * width,
             in_hbm=True,
             limit=load_limit,
         )
-    parts_in = around(sends)
-
-    def across(far):
-        return [(i, i ^ far) for i in range(seq)]
+    if fast:
+        parts_in = [sends[0]] + [lax.ppermute(sends[far], "ctx", across(far)) for far in range(1, seq)]
+    else:
+        parts_in = around(sends)
 
     def filter_kernel(filters_ref, high, low, cot_ref, gate_ref, out, *beside):
         if fast:
@@ -284,16 +288,16 @@
         parts, refs = refs[:seq], refs[seq:]
         filt, high, low, back, first_ref, value_spec, mixed_spec = refs[:7]
         outs, (stream, second) = refs[7:-2], refs[-2:]
-        for step, part in enumerate(parts):
-            put_rows(stream, behind(step), rows, part[0])
+        for step, part in zip(in_order, parts):
+            put_rows(stream, came(step), rows, part[0])
         spectra = to_spectra(high, low, stream[...])
         value_spec[...] = with_previous(spectra, cols)
         conv = from_spectra(back, causal_product(filt[0], spectra, cols))
         for i in range(length // block):
             first_ref[i * block : (i + 1) * block] = columns(conv, i, cols)
-        for step, part in enumerate(parts):
-            gated = part[1].astype(F32) * pick_rows(first_ref, behind(step), rows)
-            put_rows(stream, behind(step), rows, gated.astype(BF16))
+        for step, part in zip(in_order, parts):
+            gated = part[1].astype(F32) * pick_rows(first_ref, came(step), rows)
+            put_rows(stream, came(step), rows, gated.astype(BF16))
         spectra = to_spectra(high, low, stream[...])
         mixed_spec[...] = with_previous(spectra, cols)
         conv = from_spectra(back, causal_product(filt[1], spectra, cols))
@@ -306,7 +310,7 @@
             forward_kernel,
             [((length, cols), F32), (spectra_shape, F32), (spectra_shape, F32)]
             + ([((2, rows, cols), BF16)] * 2 if fast else [((1, rows, cols), BF16)] * seq),
-            (*parts_in, filter_spectra, fwd_high, fwd_low, inv_high),
+            (*(parts_in[step] for step in in_order), filter_spectra, fwd_high, fwd_low, inv_high),
             scratch=[pltpu.VMEM((length, cols), BF16), pltpu.VMEM((length, cols), F32)],
             flops=6 * table_flops,
             limit=limit,
@@ -324,8 +328,8 @@
         if fast:
             lag_kept, lag_given, *outs, packed = outs
         count = length // block
-        for step, part in enumerate(parts):
-            put_rows(stream, behind(step), rows, part[2])
+        for step, part in zip(in_order, parts):
+            put_rows(stream, came(step), rows, part[2])
 
         def both(left, other):
             spectra = to_spectra(high, low, stream[...])
@@ -342,9 +346,9 @@
         for i in range(count):
             total[i * block : (i + 1) * block] = columns(out, i, cols)
         put_lags(1, out)
-        for step, part in enumerate(parts):
-            grad = pick_rows(total, behind(step), rows)
-            put_rows(stream, behind(step), rows, (grad * part[1].astype(F32)).astype(BF16))
+        for step, part in zip(in_order, parts):
+            grad = pick_rows(total, came(step), rows)
+            put_rows(stream, came(step), rows, (grad * part[1].astype(F32)).astype(BF16))
         total[...] = total[...] * first_ref[...]
         put_result(outs, 0, total, 2)
         out = both(filt[0], value_spec[...])
@@ -369,7 +373,7 @@
             backward_kernel,
             [((2, length, cols), F32)] + [((rows, width), F32), wide_bf16] * fast + [((2, rows, cols), BF16)] * seq,
             (
-                *parts_in,
+                *(parts_in[step] for step in in_order),
                 filter_spectra,
                 first_conv,
                 value_spectra,

time: 41.5 us -> 41 us (0.988)
    ppermute x6 -> x3, starting transfers between devices: 10.9 us -> 4.06 us  [around(): out.append(lax.ppermute(blocks[step], 'ctx', pairs))]
    ppermute x0 -> x3, starting transfers between devices: none -> 5.76 us  [on_device(): lax.ppermute(sends[far], 'ctx', across(far))]
    ppermute x0 -> x3, waiting for transfers between devices: none -> 4.79 us  [on_device(): lax.ppermute(sends[far], 'ctx', across(far))]
    ppermute x6 -> x3, waiting for transfers between devices: 6.36 us -> 2.7 us  [around(): out.append(lax.ppermute(blocks[step], 'ctx', pairs))]
    ppermute x1, waiting for transfers between devices: 2.36 us -> 0.68 us  [on_device(): second_near = lax.ppermute(goes, 'ctx', across(2))]
    ppermute x1, starting transfers between devices: 1.07 us -> 2.49 us  [on_device(): second_near = lax.ppermute(goes, 'ctx', across(2))]
    ppermute x1, starting transfers between devices: 1.68 us -> 0.31 us  [on_device(): second_far = lax.ppermute(goes_on, 'ctx', across(1))]
    ppermute x1, starting transfers between devices: 0.74 us -> 1.45 us  [on_device(): beside_in = lax.ppermute(sends[0], 'ctx', across(1))]
  transfers between devices with their start and end apart: 16 -> 16, of which waited for: 6 -> 9; matrix products, arithmetic and copies ran while one was open for 0% -> 0% of each run, Pallas kernels for 14% -> 14%
where the time goes in v9:
time: 41 us; the launch traced here: 40.9 us
  starting transfers between devices  21.6 us (53%)
  waiting for transfers between devices  9.15 us (22%)
  Pallas kernels  8.33 us (20%)
  local copies, waits for them, and re-layouts  1.03 us (3%)
  between operations  0.75 us (2%)
    pallas_call x10, Pallas kernels, call(): pl.pallas_call(kernel, out_shape=[jax.ShapeDtypeStruct(shape, dtype) for...  8.33 us
    ppermute x3, starting transfers between devices, on_device(): lax.ppermute(sends[far], 'ctx', across(far))  5.76 us
    ppermute x2, starting transfers between devices, on_device(): home = [lax.ppermute(sends_home[far], 'ctx', across(far)) for far in (2, 3)]  5.6 us
    ppermute x3, waiting for transfers between devices, on_device(): lax.ppermute(sends[far], 'ctx', across(far))  4.79 us
    ppermute x3, starting transfers between devices, around(): out.append(lax.ppermute(blocks[step], 'ctx', pairs))  4.06 us
    ppermute x3, waiting for transfers between devices, around(): out.append(lax.ppermute(blocks[step], 'ctx', pairs))  2.7 us
    ppermute x1, starting transfers between devices, on_device(): second_near = lax.ppermute(goes, 'ctx', across(2))  2.49 us
    ppermute x3, starting transfers between devices, to_chip(): return lax.ppermute(block, ('dp', 'ctx'), pairs)  1.85 us
  transfers between devices with their start and end apart: 16, of which 9 were waited for; matrix products, arithmetic and copies ran while one was open for 0% of the time, Pallas kernels for 14%

profile of v9, /device:TPU:0, one launch (start us, length us, event | category | flops | bytes accessed | tf_op | source)
XLA Modules:
  0.0 40.9 jit_solution(3618323701447317309)
XLA Ops:
  0.6 0.0 copy-start
  0.6 0.0 copy-start.4
  0.7 0.0 copy-start.5
  0.7 1.7 %load.1 = (bf16[3,128,128]{2,1,0:T(8,128)(2,1)S(1)}, bf16[3,128,128]{2,1,0:T(8,128)(2,1)S(1)}, bf16[3,128,128]{2,1,0:T(8,128)(2,1)S(1)}, bf16[3,128,128]{2,1,0:T(8,128)(2,1)S(1)}) custom-call(bf16[1,128,512]{2,1,0:T(8,128)(2,1)} %refs_0_.1, bf16[1,128,512]{2,1,0:T(8,128)(2,1)} %refs_1_.1, bf16[1,128,512]{2,1,0:T(8,128)(2,1)} %refs_2_.1, ...), custom_call_target="tpu_custom_call" | custom-call | flops 67108864 | bytes 1048576 | tf_op jit(solution)/shard_map/load/pallas_call | solution.py:142
  2.3 5.1 %collective-permute-start = (bf16[3,128,128]{2,1,0:T(8,128)(2,1)S(1)}, bf16[3,128,128]{2,1,0:T(8,128)(2,1)S(1)}, u32[]{:S(2)}, u32[]{:S(2)}) collective-permute-start(bf16[3,128,128]{2,1,0:T(8,128)(2,1)S(1)} %get-tuple-element.39), channel_id=1, source_target_pairs={{0,3},{1,2},{2,1},{3,0},{4,7},{5,6},{6,5},{7,4},{8,11},{9,10},{10,... | collective-permute-start | bytes 294920 | tf_op jit(solution)/shard_map/ppermute | solution.py:252
  7.5 0.0 collective-permute-start.1
  7.5 0.6 %collective-permute-start.2 = (bf16[3,128,128]{2,1,0:T(8,128)(2,1)S(1)}, bf16[3,128,128]{2,1,0:T(8,128)(2,1)S(1)}, u32[]{:S(2)}, u32[]{:S(2)}) collective-permute-start(bf16[3,128,128]{2,1,0:T(8,128)(2,1)S(1)} %get-tuple-element.41), channel_id=1, source_target_pairs={{0,2},{1,3},{2,0},{3,1},{4,6},{5,7},{6,4},{7,5},{8,10},{9,11},{10,... | collective-permute-start | bytes 294920 | tf_op jit(solution)/shard_map/ppermute | solution.py:252
  8.1 0.0 copy-done
  8.1 0.0 copy-done.4
  8.2 0.9 %copy-done.1 = bf16[512,256]{1,0:T(8,128)(2,1)S(1)} copy-done((bf16[512,256]{1,0:T(8,128)(2,1)S(1)}, bf16[512,256]{1,0:T(8,128)(2,1)}, u32[]{:S(2)}) %copy-start.1) | copy-done | bytes 262168
  9.0 0.1 copy-done.2
  9.1 0.4 %filter_spectra.1 = (f32[2,512,256]{2,1,0:T(8,128)S(1)}, bf16[128,768]{1,0:T(8,128)(2,1)S(1)}) custom-call(bf16[2,512,128]{2,1,0:T(8,128)(2,1)S(1)} %constant_dynamic-slice_fusion.filters_ref, bf16[512,256]{1,0:T(8,128)(2,1)S(1)} %copy-done.2, bf16[512,256]{1,0:T(8,128)(2,1)S(1)} %copy-done.1, bf16[128,512]{1,0:T(8,128)(2,1)S(1)} %bitcast.7, ...), custom_call_target="tpu_custom_call" | custom-call | flops 268435456 | bytes 1048576 | tf_op jit(solution)/shard_map/filter_spectra/pallas_call | solution.py:142
  9.6 1.5 %collective-permute-start.4 = (bf16[128,768]{1,0:T(8,128)(2,1)S(1)}, bf16[128,768]{1,0:T(8,128)(2,1)S(1)}, u32[]{:S(2)}, u32[]{:S(2)}) collective-permute-start(bf16[128,768]{1,0:T(8,128)(2,1)S(1)} %get-tuple-element.45), channel_id=1, source_target_pairs={{0,1},{1,0},{2,3},{3,2},{4,5},{5,4},{6,7},{7,6},{8,9},{9,8},{10,11... | collective-permute-start | bytes 589832 | tf_op jit(solution)/shard_map/ppermute | solution.py:275
  11.0 0.1 collective-permute-done.refs_1_
  11.1 3.5 %collective-permute-done.1.refs_2_ = bf16[3,128,128]{2,1,0:T(8,128)(2,1)S(1)} collective-permute-done((bf16[3,128,128]{2,1,0:T(8,128)(2,1)S(1)}, bf16[3,128,128]{2,1,0:T(8,128)(2,1)S(1)}, u32[]{:S(2)}, u32[]{:S(2)}) %collective-permute-start.1) | collective-permute-done | bytes 98336 | tf_op jit(solution)/shard_map/ppermute | solution.py:252
  14.6 1.2 %collective-permute-done.2.refs_3_ = bf16[3,128,128]{2,1,0:T(8,128)(2,1)S(1)} collective-permute-done((bf16[3,128,128]{2,1,0:T(8,128)(2,1)S(1)}, bf16[3,128,128]{2,1,0:T(8,128)(2,1)S(1)}, u32[]{:S(2)}, u32[]{:S(2)}) %collective-permute-start.2) | collective-permute-done | bytes 98336 | tf_op jit(solution)/shard_map/ppermute | solution.py:252
  15.8 1.4 %forward_convolutions.1 = (f32[512,128]{1,0:T(8,128)S(1)}, f32[512,256]{1,0:T(8,128)S(1)}, f32[512,256]{1,0:T(8,128)S(1)}, bf16[2,128,128]{2,1,0:T(8,128)(2,1)S(1)}, bf16[2,128,128]{2,1,0:T(8,128)(2,1)S(1)}) custom-call(bf16[3,128,128]{2,1,0:T(8,128)(2,1)S(1)} %get-tuple-element.38.refs_0_, bf16[3,128,128]{2,1,0:T(8,128)(2,1)S(1)} %collective-permute-done.refs_1_, ...), custom_call_target="tpu_custom_call" | custom-call | flops 402653184 | bytes 2228224 | tf_op jit(solution)/shard_map/forward_convolutions/pallas_call | solution.py:142
  17.3 2.5 %collective-permute-start.3 = (bf16[2,128,128]{2,1,0:T(8,128)(2,1)S(1)}, bf16[2,128,128]{2,1,0:T(8,128)(2,1)S(1)}, u32[]{:S(2)}, u32[]{:S(2)}) collective-permute-start(bf16[2,128,128]{2,1,0:T(8,128)(2,1)S(1)} %get-tuple-element.44), channel_id=1, source_target_pairs={{0,2},{1,3},{2,0},{3,1},{4,6},{5,7},{6,4},{7,5},{8,10},{9,11},{10,... | collective-permute-start | bytes 196616 | tf_op jit(solution)/shard_map/ppermute | solution.py:320
  19.8 2.5 %backward_convolutions.1 = (f32[2,512,128]{2,1,0:T(8,128)}, f32[128,512]{1,0:T(8,128)S(1)}, bf16[128,512]{1,0:T(8,128)(2,1)S(1)}, bf16[2,128,128]{2,1,0:T(8,128)...) custom-call(bf16[3,128,128]{2,1,0:T(8,128)(2,1)S(1)} %get-tuple-elem, ...), custom_call_target="tpu_custom_call" | custom-call | flops 536870912 | bytes 3538944 | tf_op jit(solution)/shard_map/backward_convolutions/pallas_call | solution.py:142
  22.3 0.0 collective-permute-start.7
  22.3 0.7 %collective-permute-done.3.refs_1_.near_ref = bf16[2,128,128]{2,1,0:T(8,128)(2,1)S(1)} collective-permute-done((bf16[2,128,128]{2,1,0:T(8,128)(2,1)S(1)}, bf16[2,128,128]{2,1,0:T(8,128)(2,1)S(1)}, u32[]{:S(2)}, u32[]{:S(2)}) %collective-permute-start.3) | collective-permute-done | bytes 65568 | tf_op jit(solution)/shard_map/ppermute | solution.py:320
  22.9 0.0 collective-permute-done.4.refs_4_
  23.0 0.3 weight_partial.1
  23.3 0.1 collective-permute-start.5
  23.4 0.2 collective-permute-done.7.taken_ref
  23.6 0.0 copy-start.3
  23.7 0.3 collective-permute-start.8
  24.0 0.7 %collective-permute-done.5.taken_ref = bf16[128,512]{1,0:T(8,128)(2,1)S(1)} collective-permute-done((bf16[128,512]{1,0:T(8,128)(2,1)S(1)}, bf16[128,512]{1,0:T(8,128)(2,1)S(1)}, u32[]{:S(2)}, u32[]{:S(2)}) %collective-permute-start.5) | collective-permute-done | bytes 131104 | tf_op jit(solution)/shard_map/core_sum/ppermute | solution.py:393
  24.7 0.3 collective-permute-start.6
  25.1 0.0 collective-permute-start.9
  25.1 1.5 %collective-permute-start.10 = (bf16[64,512]{1,0:T(8,128)(2,1)S(1)}, bf16[64,512]{1,0:T(8,128)(2,1)S(1)}, u32[]{:S(2)}, u32[]{:S(2)}) collective-permute-start(bf16[64,512]{1,0:T(8,128)(2,1)S(1)} %get-tuple-element.57), channel_id=1, source_target_pairs={{0,16},{1,25},{2,6},{3,11},{4,20},{5,29},{6,2},{7,15},{8,24},{9,17... | collective-permute-start | bytes 196616 | tf_op jit(solution)/shard_map/ppermute | solution.py:400
  26.6 1.8 %collective-permute-start.14 = (bf16[2,128,128]{2,1,0:T(8,128)(2,1)S(1)}, bf16[2,128,128]{2,1,0:T(8,128)(2,1)S(1)}, u32[]{:S(2)}, u32[]{:S(2)}) collective-permute-start(bf16[2,128,128]{2,1,0:T(8,128)(2,1)S(1)} %get-tuple-element.63), channel_id=1, source_target_pairs={{0,2},{1,3},{2,0},{3,1},{4,6},{5,7},{6,4},{7,5},{8,10},{9,11},{10,... | collective-permute-start | bytes 196616 | tf_op jit(solution)/shard_map/ppermute | solution.py:469
  28.4 0.0 collective-permute-done.8.lag_ref
  28.4 3.8 %collective-permute-start.15 = (bf16[2,128,128]{2,1,0:T(8,128)(2,1)S(1)}, bf16[2,128,128]{2,1,0:T(8,128)(2,1)S(1)}, u32[]{:S(2)}, u32[]{:S(2)}) collective-permute-start(bf16[2,128,128]{2,1,0:T(8,128)(2,1)S(1)} %get-tuple-element.64), channel_id=1, source_target_pairs={{0,3},{1,2},{2,1},{3,0},{4,7},{5,6},{6,5},{7,4},{8,11},{9,10},{10,... | collective-permute-start | bytes 196616 | tf_op jit(solution)/shard_map/ppermute | solution.py:469
  32.2 0.0 collective-permute-done.9.one
  32.2 0.0 collective-permute-done.10.two
  32.2 1.4 %collective-permute-start.11 = (bf16[192,128]{1,0:T(8,128)(2,1)S(1)}, bf16[192,128]{1,0:T(8,128)(2,1)S(1)}, u32[]{:S(2)}, u32[]{:S(2)}) collective-permute-start(bf16[192,128]{1,0:T(8,128)(2,1)S(1)} %get-tuple-element.59), channel_id=1, source_target_pairs={{0,1},{1,2},{2,3},{3,0},{4,5},{5,6},{6,7},{7,4},{8,9},{9,10},{10,1... | collective-permute-start | bytes 147464 | tf_op jit(solution)/shard_map/ppermute | solution.py:185
  33.6 2.0 %collective-permute-start.12 = (bf16[192,128]{1,0:T(8,128)(2,1)S(1)}, bf16[192,128]{1,0:T(8,128)(2,1)S(1)}, u32[]{:S(2)}, u32[]{:S(2)}) collective-permute-start(bf16[192,128]{1,0:T(8,128)(2,1)S(1)} %get-tuple-element.60), channel_id=1, source_target_pairs={{0,2},{1,3},{2,0},{3,1},{4,6},{5,7},{6,4},{7,5},{8,10},{9,11},{10,... | collective-permute-start | bytes 147464 | tf_op jit(solution)/shard_map/ppermute | solution.py:185
  35.6 0.0 collective-permute-done.6.refs_2_.refs_5_
  35.6 0.7 %collective-permute-start.13 = (bf16[192,128]{1,0:T(8,128)(2,1)S(1)}, bf16[192,128]{1,0:T(8,128)(2,1)S(1)}, u32[]{:S(2)}, u32[]{:S(2)}) collective-permute-start(bf16[192,128]{1,0:T(8,128)(2,1)S(1)} %get-tuple-element.61), channel_id=1, source_target_pairs={{0,3},{1,0},{2,1},{3,2},{4,7},{5,4},{6,5},{7,6},{8,11},{9,8},{10,9... | collective-permute-start | bytes 147464 | tf_op jit(solution)/shard_map/ppermute | solution.py:185
  36.3 0.0 copy-done.3
  36.3 1.1 %mixed.1 = (bf16[128,512]{1,0:T(8,128)(2,1)}, bf16[128,512]{1,0:T(8,128)(2,1)}) custom-call(bf16[2,128,128]{2,1,0:T(8,128)(2,1)S(1)} %get-tuple-element.43.refs_0_.stays_ref, bf16[2,128,128]{2,1,0:T(8,128)(2,1)S(1)} %collective-permute-done.3.refs_1_.near_ref, bf16[4,128,128]{2,1,0:T(8,128)(2,1)S(1)} %collective-permute-done.6.refs_2_.refs_5_, ...), custom_call_target="tpu_custom_call" | custom-call | flops 134217728 | bytes 1048576 | tf_op jit(solution)/shard_map/mixed/pallas_call | solution.py:142
  37.4 0.0 collective-permute-done.14.refs_6_
  37.4 0.0 collective-permute-done.15.refs_7_
  37.4 1.0 %collective-permute-done.11.refs_1_ = bf16[192,128]{1,0:T(8,128)(2,1)S(1)} collective-permute-done((bf16[192,128]{1,0:T(8,128)(2,1)S(1)}, bf16[192,128]{1,0:T(8,128)(2,1)S(1)}, u32[]{:S(2)}, u32[]{:S(2)}) %collective-permute-start.11) | collective-permute-done | bytes 49184 | tf_op jit(solution)/shard_map/ppermute | solution.py:185
  38.4 1.5 %collective-permute-done.12.refs_2_ = bf16[192,128]{1,0:T(8,128)(2,1)S(1)} collective-permute-done((bf16[192,128]{1,0:T(8,128)(2,1)S(1)}, bf16[192,128]{1,0:T(8,128)(2,1)S(1)}, u32[]{:S(2)}, u32[]{:S(2)}) %collective-permute-start.12) | collective-permute-done | bytes 49184 | tf_op jit(solution)/shard_map/ppermute | solution.py:185
  39.9 0.2 collective-permute-done.13.refs_3_
  40.1 0.8 %means.1 = (f32[2,64,128]{2,1,0:T(8,128)}, f32[64,128]{1,0:T(8,128)}, bf16[128,512]{1,0:T(8,128)(2,1)}, bf16[128,512]{1,0:T(8,128)(2,1)}) custom-call(f32[192,128]{1,0:T(8,128)S(1)} %get-tuple-element.58.refs_0_, bf16[192,128]{1,0:T(8,128)(2,1)S(1)} %collective-permute-done.11.refs_1_, bf16[192,128]{1,0:T(8,128)(2,1)S(1)} %collective-permute-done.12.refs_2_, ...), custom_call_target="tpu_custom_call" | custom-call | bytes 573440 | tf_op jit(solution)/shard_map/means/pallas_call | solution.py:142
  (9 shorter events, 0.1 us)
Async XLA Ops:
  0.6 7.5 %copy-start = (bf16[2,512,512]{2,1,0:T(8,128)(2,1)S(1)}, bf16[2,512,512]{2,1,0:T(8,128)(2,1)}, u32[]{:S(2)}) copy-start(bf16[2,512,512]{2,1,0:T(8,128)(2,1)} %param.12) | copy-start | bytes 3145732
  0.6 7.5 %copy-start.4 = (bf16[1,128,512]{2,1,0:T(8,128)(2,1)S(1)}, bf16[1,128,512]{2,1,0:T(8,128)(2,1)}, u32[]{:S(2)}) copy-start(bf16[1,128,512]{2,1,0:T(8,128)(2,1)} %refs_2_.1) | copy-start | bytes 393220
  0.7 7.5 %copy-start.5 = (bf16[1,128,512]{2,1,0:T(8,128)(2,1)S(1)}, bf16[1,128,512]{2,1,0:T(8,128)(2,1)}, u32[]{:S(2)}) copy-start(bf16[1,128,512]{2,1,0:T(8,128)(2,1)} %refs_4_.2) | copy-start | bytes 393220
  2.3 8.8 %collective-permute-start = (bf16[3,128,128]{2,1,0:T(8,128)(2,1)S(1)}, bf16[3,128,128]{2,1,0:T(8,128)(2,1)S(1)}, u32[]{:S(2)}, u32[]{:S(2)}) collective-permute-start(bf16[3,128,128]{2,1,0:T(8,128)(2,1)S(1)} %get-tuple-element.39), channel_id=1, source_target_pairs={{0,3},{1,2},{2,1},{3,0},{4,7},{5,6},{6,5},{7,4},{8,11},{9,10},{10,... | collective-permute-start | bytes 294920 | tf_op jit(solution)/shard_map/ppermute | solution.py:252
  7.5 7.2 %collective-permute-start.1 = (bf16[3,128,128]{2,1,0:T(8,128)(2,1)S(1)}, bf16[3,128,128]{2,1,0:T(8,128)(2,1)S(1)}, u32[]{:S(2)}, u32[]{:S(2)}) collective-permute-start(bf16[3,128,128]{2,1,0:T(8,128)(2,1)S(1)} %get-tuple-element.40), channel_id=1, source_target_pairs={{0,1},{1,0},{2,3},{3,2},{4,5},{5,4},{6,7},{7,6},{8,9},{9,8},{10,11... | collective-permute-start | bytes 294920 | tf_op jit(solution)/shard_map/ppermute | solution.py:252
  7.5 8.4 %collective-permute-start.2 = (bf16[3,128,128]{2,1,0:T(8,128)(2,1)S(1)}, bf16[3,128,128]{2,1,0:T(8,128)(2,1)S(1)}, u32[]{:S(2)}, u32[]{:S(2)}) collective-permute-start(bf16[3,128,128]{2,1,0:T(8,128)(2,1)S(1)} %get-tuple-element.41), channel_id=1, source_target_pairs={{0,2},{1,3},{2,0},{3,1},{4,6},{5,7},{6,4},{7,5},{8,10},{9,11},{10,... | collective-permute-start | bytes 294920 | tf_op jit(solution)/shard_map/ppermute | solution.py:252
  8.1 1.0 %copy-start.1 = (bf16[512,256]{1,0:T(8,128)(2,1)S(1)}, bf16[512,256]{1,0:T(8,128)(2,1)}, u32[]{:S(2)}) copy-start(bf16[512,256]{1,0:T(8,128)(2,1)} %constant.26.clone.low.refs_6_.refs_9_) | copy-start | bytes 786436
  8.1 1.0 %copy-start.2 = (bf16[512,256]{1,0:T(8,128)(2,1)S(1)}, bf16[512,256]{1,0:T(8,128)(2,1)}, u32[]{:S(2)}) copy-start(bf16[512,256]{1,0:T(8,128)(2,1)} %constant.25.clone.high.refs_5_.refs_8_) | copy-start | bytes 786436
  9.1 6.7 %copy-start.6 = (bf16[256,512]{1,0:T(8,128)(2,1)S(1)}, bf16[256,512]{1,0:T(8,128)(2,1)}, u32[]{:S(2)}) copy-start(bf16[256,512]{1,0:T(8,128)(2,1)} %constant.27.clone.refs_7_.refs_10_) | copy-start | bytes 786436
  9.6 13.4 %collective-permute-start.4 = (bf16[128,768]{1,0:T(8,128)(2,1)S(1)}, bf16[128,768]{1,0:T(8,128)(2,1)S(1)}, u32[]{:S(2)}, u32[]{:S(2)}) collective-permute-start(bf16[128,768]{1,0:T(8,128)(2,1)S(1)} %get-tuple-element.45), channel_id=1, source_target_pairs={{0,1},{1,0},{2,3},{3,2},{4,5},{5,4},{6,7},{7,6},{8,9},{9,8},{10,11... | collective-permute-start | bytes 589832 | tf_op jit(solution)/shard_map/ppermute | solution.py:275
  17.3 5.7 %collective-permute-start.3 = (bf16[2,128,128]{2,1,0:T(8,128)(2,1)S(1)}, bf16[2,128,128]{2,1,0:T(8,128)(2,1)S(1)}, u32[]{:S(2)}, u32[]{:S(2)}) collective-permute-start(bf16[2,128,128]{2,1,0:T(8,128)(2,1)S(1)} %get-tuple-element.44), channel_id=1, source_target_pairs={{0,2},{1,3},{2,0},{3,1},{4,6},{5,7},{6,4},{7,5},{8,10},{9,11},{10,... | collective-permute-start | bytes 196616 | tf_op jit(solution)/shard_map/ppermute | solution.py:320
  22.3 1.3 %collective-permute-start.7 = (bf16[128,512]{1,0:T(8,128)(2,1)S(1)}, bf16[128,512]{1,0:T(8,128)(2,1)S(1)}, u32[]{:S(2)}, u32[]{:S(2)}) collective-permute-start(bf16[128,512]{1,0:T(8,128)(2,1)S(1)} %get-tuple-element.55), channel_id=1, source_target_pairs={{0,4},{4,0},{8,12},{12,8},{16,20},{20,16},{24,28},{28,24},{1,5},{5... | collective-permute-start | bytes 393224 | tf_op jit(solution)/shard_map/lag_core_sum/ppermute | solution.py:393
  23.3 1.4 %collective-permute-start.5 = (bf16[128,512]{1,0:T(8,128)(2,1)S(1)}, bf16[128,512]{1,0:T(8,128)(2,1)S(1)}, u32[]{:S(2)}, u32[]{:S(2)}) collective-permute-start(bf16[128,512]{1,0:T(8,128)(2,1)S(1)} %get-tuple-element.47), channel_id=1, source_target_pairs={{0,4},{4,0},{8,12},{12,8},{16,20},{20,16},{24,28},{28,24},{1,5},{5... | collective-permute-start | bytes 393224 | tf_op jit(solution)/shard_map/core_sum/ppermute | solution.py:393
  23.6 12.7 %copy-start.3 = (bf16[512,512]{1,0:T(8,128)(2,1)S(1)}, bf16[512,512]{1,0:T(8,128)(2,1)}, u32[]{:S(2)}) copy-start(bf16[512,512]{1,0:T(8,128)(2,1)} %refs_4_.3) | copy-start | bytes 1572868
  23.7 4.7 %collective-permute-start.8 = (bf16[128,512]{1,0:T(8,128)(2,1)S(1)}, bf16[128,512]{1,0:T(8,128)(2,1)S(1)}, u32[]{:S(2)}, u32[]{:S(2)}) collective-permute-start(bf16[128,512]{1,0:T(8,128)(2,1)S(1)} %lag_core_sum.1), channel_id=1, source_target_pairs={{0,4},{1,9},{2,18},{3,27},{4,0},{5,13},{6,22},{7,31},{8,12},{9,1},... | collective-permute-start | bytes 393224 | tf_op jit(solution)/shard_map/ppermute | solution.py:400
  24.7 10.9 %collective-permute-start.6 = (bf16[4,128,128]{2,1,0:T(8,128)(2,1)S(1)}, bf16[4,128,128]{2,1,0:T(8,128)(2,1)S(1)}, u32[]{:S(2)}, u32[]{:S(2)}) collective-permute-start(bf16[4,128,128]{2,1,0:T(8,128)(2,1)S(1)} %get-tuple-element.52), channel_id=1, source_target_pairs={{0,1},{1,0},{2,3},{3,2},{4,5},{5,4},{6,7},{7,6},{8,9},{9,8},{10,11... | collective-permute-start | bytes 393224 | tf_op jit(solution)/shard_map/ppermute | solution.py:465
  25.1 7.1 %collective-permute-start.9 = (bf16[64,512]{1,0:T(8,128)(2,1)S(1)}, bf16[64,512]{1,0:T(8,128)(2,1)S(1)}, u32[]{:S(2)}, u32[]{:S(2)}) collective-permute-start(bf16[64,512]{1,0:T(8,128)(2,1)S(1)} %get-tuple-element.56), channel_id=1, source_target_pairs={{0,4},{1,9},{2,18},{3,27},{4,0},{5,13},{6,22},{7,31},{8,12},{9,1},... | collective-permute-start | bytes 196616 | tf_op jit(solution)/shard_map/ppermute | solution.py:400
  25.1 7.1 %collective-permute-start.10 = (bf16[64,512]{1,0:T(8,128)(2,1)S(1)}, bf16[64,512]{1,0:T(8,128)(2,1)S(1)}, u32[]{:S(2)}, u32[]{:S(2)}) collective-permute-start(bf16[64,512]{1,0:T(8,128)(2,1)S(1)} %get-tuple-element.57), channel_id=1, source_target_pairs={{0,16},{1,25},{2,6},{3,11},{4,20},{5,29},{6,2},{7,15},{8,24},{9,17... | collective-permute-start | bytes 196616 | tf_op jit(solution)/shard_map/ppermute | solution.py:400
  26.6 10.8 %collective-permute-start.14 = (bf16[2,128,128]{2,1,0:T(8,128)(2,1)S(1)}, bf16[2,128,128]{2,1,0:T(8,128)(2,1)S(1)}, u32[]{:S(2)}, u32[]{:S(2)}) collective-permute-start(bf16[2,128,128]{2,1,0:T(8,128)(2,1)S(1)} %get-tuple-element.63), channel_id=1, source_target_pairs={{0,2},{1,3},{2,0},{3,1},{4,6},{5,7},{6,4},{7,5},{8,10},{9,11},{10,... | collective-permute-start | bytes 196616 | tf_op jit(solution)/shard_map/ppermute | solution.py:469
  28.4 9.0 %collective-permute-start.15 = (bf16[2,128,128]{2,1,0:T(8,128)(2,1)S(1)}, bf16[2,128,128]{2,1,0:T(8,128)(2,1)S(1)}, u32[]{:S(2)}, u32[]{:S(2)}) collective-permute-start(bf16[2,128,128]{2,1,0:T(8,128)(2,1)S(1)} %get-tuple-element.64), channel_id=1, source_target_pairs={{0,3},{1,2},{2,1},{3,0},{4,7},{5,6},{6,5},{7,4},{8,11},{9,10},{10,... | collective-permute-start | bytes 196616 | tf_op jit(solution)/shard_map/ppermute | solution.py:469
  32.2 6.1 %collective-permute-start.11 = (bf16[192,128]{1,0:T(8,128)(2,1)S(1)}, bf16[192,128]{1,0:T(8,128)(2,1)S(1)}, u32[]{:S(2)}, u32[]{:S(2)}) collective-permute-start(bf16[192,128]{1,0:T(8,128)(2,1)S(1)} %get-tuple-element.59), channel_id=1, source_target_pairs={{0,1},{1,2},{2,3},{3,0},{4,5},{5,6},{6,7},{7,4},{8,9},{9,10},{10,1... | collective-permute-start | bytes 147464 | tf_op jit(solution)/shard_map/ppermute | solution.py:185
  33.6 6.3 %collective-permute-start.12 = (bf16[192,128]{1,0:T(8,128)(2,1)S(1)}, bf16[192,128]{1,0:T(8,128)(2,1)S(1)}, u32[]{:S(2)}, u32[]{:S(2)}) collective-permute-start(bf16[192,128]{1,0:T(8,128)(2,1)S(1)} %get-tuple-element.60), channel_id=1, source_target_pairs={{0,2},{1,3},{2,0},{3,1},{4,6},{5,7},{6,4},{7,5},{8,10},{9,11},{10,... | collective-permute-start | bytes 147464 | tf_op jit(solution)/shard_map/ppermute | solution.py:185
  35.6 4.5 %collective-permute-start.13 = (bf16[192,128]{1,0:T(8,128)(2,1)S(1)}, bf16[192,128]{1,0:T(8,128)(2,1)S(1)}, u32[]{:S(2)}, u32[]{:S(2)}) collective-permute-start(bf16[192,128]{1,0:T(8,128)(2,1)S(1)} %get-tuple-element.61), channel_id=1, source_target_pairs={{0,3},{1,0},{2,1},{3,2},{4,7},{5,4},{6,5},{7,6},{8,11},{9,8},{10,9... | collective-permute-start | bytes 147464 | tf_op jit(solution)/shard_map/ppermute | solution.py:185

commit v10 on v9

--- a/solution.py
+++ b/solution.py
@@ -468,12 +468,17 @@
 
         home = [lax.ppermute(sends_home[far], "ctx", across(far)) for far in (2, 3)]
 
+        tables = ((0, 1, 2, 3), (1, 3, 0, 2), (3, 2, 1, 0), (2, 0, 3, 1))
+
         def place_kernel(lag_ref, one, two, *refs):
             outs, total = refs[:-1], refs[-1]
             total[...] = one[...].astype(F32) + two[...].astype(F32)
-            for step, out in enumerate(outs):
-                out[:own_rows] = pick_columns(total, ahead(step), cols, seq).astype(out.dtype)
-                out[own_rows:] = pick_columns(lag_ref, ahead(step), cols, seq).astype(out.dtype)
+            for table, out in zip(tables, outs):
+                place = table[0]
+                for index in range(1, 4):
+                    place = jnp.where(lax.axis_index("ctx") == index, table[index], place)
+                out[:own_rows] = pick_columns(total, place, cols, seq).astype(out.dtype)
+                out[own_rows:] = pick_columns(lag_ref, place, cols, seq).astype(out.dtype)
 
         small = (own_rows + rows, cols)
         with jax.named_scope("chip_sum"):
@@ -483,7 +488,9 @@
                 (lag_term, *chip_terms),
                 scratch=[pltpu.VMEM((own_rows, width), F32)],
             )
-        last_terms = around(sends)
+        last_terms = [sends[0]]
+        for table, part in zip(tables[1:], sends[1:]):
+            last_terms.append(lax.ppermute(part, "ctx", list(enumerate(table))))
 
         def mixed_kernel(*refs):
             parts, (gate_ref, weight_ref, cot_ref, mixed_ref, out, second) = refs[:3], refs[3:]
@@ -528,7 +535,7 @@
             filter_grad, weight_grad, grad_gate_one, grad_value = call(
                 final_kernel,
                 [((2, fine, rows), F32), ((own_rows, cols), F32), wide_bf16, wide_bf16],
-                (*last_terms, sends_home[0], second_far, *home),
+                (*(last_terms[step] for step in (0, 1, 2, 3)), sends_home[0], second_far, *home),
             )
         filter_grad = jnp.swapaxes(filter_grad, 1, 2)
         return (

time: 41 us -> 40.8 us (level)
  waiting for transfers between devices: 9.15 us -> 8.15 us
  starting transfers between devices: 21.6 us -> 22.4 us
    ppermute x3, waiting for transfers between devices: 2.7 us -> 1.7 us  [on_device(): last_terms.append(lax.ppermute(part, 'ctx', list(enumerate(table))))]
    ppermute x3, starting transfers between devices: 4.06 us -> 4.85 us  [on_device(): last_terms.append(lax.ppermute(part, 'ctx', list(enumerate(table))))]
  transfers between devices with their start and end apart: 16 -> 16, of which waited for: 9 -> 9; matrix products, arithmetic and copies ran while one was open for 0% -> 0% of each run, Pallas kernels for 14% -> 15%
where the time goes in v10:
time: 40.8 us; the launch traced here: 40.6 us
  starting transfers between devices  22.4 us (55%)
  Pallas kernels  8.32 us (20%)
  waiting for transfers between devices  8.15 us (20%)
  local copies, waits for them, and re-layouts  1.03 us (3%)
  between operations  0.76 us (2%)
    pallas_call x10, Pallas kernels, call(): pl.pallas_call(kernel, out_shape=[jax.ShapeDtypeStruct(shape, dtype) for...  8.32 us
    ppermute x3, starting transfers between devices, on_device(): lax.ppermute(sends[far], 'ctx', across(far))  5.76 us
    ppermute x2, starting transfers between devices, on_device(): home = [lax.ppermute(sends_home[far], 'ctx', across(far)) for far in (2, 3)]  5.6 us
    ppermute x3, starting transfers between devices, on_device(): last_terms.append(lax.ppermute(part, 'ctx', list(enumerate(table))))  4.85 us
    ppermute x3, waiting for transfers between devices, on_device(): lax.ppermute(sends[far], 'ctx', across(far))  4.79 us
    ppermute x1, starting transfers between devices, on_device(): second_near = lax.ppermute(goes, 'ctx', across(2))  2.49 us
    ppermute x3, starting transfers between devices, to_chip(): return lax.ppermute(block, ('dp', 'ctx'), pairs)  1.85 us
    ppermute x3, waiting for transfers between devices, on_device(): last_terms.append(lax.ppermute(part, 'ctx', list(enumerate(table))))  1.7 us
  transfers between devices with their start and end apart: 16, of which 9 were waited for; matrix products, arithmetic and copies ran while one was open for 0% of the time, Pallas kernels for 15%

profile of v10, /device:TPU:0, one launch (start us, length us, event | category | flops | bytes accessed | tf_op | source)
XLA Modules:
  0.0 40.6 jit_solution(13720746924509123069)
XLA Ops:
  0.6 0.0 copy-start
  0.6 0.0 copy-start.4
  0.7 0.0 copy-start.5
  0.7 1.7 %load.1 = (bf16[3,128,128]{2,1,0:T(8,128)(2,1)S(1)}, bf16[3,128,128]{2,1,0:T(8,128)(2,1)S(1)}, bf16[3,128,128]{2,1,0:T(8,128)(2,1)S(1)}, bf16[3,128,128]{2,1,0:T(8,128)(2,1)S(1)}) custom-call(bf16[1,128,512]{2,1,0:T(8,128)(2,1)} %refs_0_.1, bf16[1,128,512]{2,1,0:T(8,128)(2,1)} %refs_1_.1, bf16[1,128,512]{2,1,0:T(8,128)(2,1)} %refs_2_.1, ...), custom_call_target="tpu_custom_call" | custom-call | flops 67108864 | bytes 1048576 | tf_op jit(solution)/shard_map/load/pallas_call | solution.py:142
  2.3 5.1 %collective-permute-start = (bf16[3,128,128]{2,1,0:T(8,128)(2,1)S(1)}, bf16[3,128,128]{2,1,0:T(8,128)(2,1)S(1)}, u32[]{:S(2)}, u32[]{:S(2)}) collective-permute-start(bf16[3,128,128]{2,1,0:T(8,128)(2,1)S(1)} %get-tuple-element.39), channel_id=1, source_target_pairs={{0,3},{1,2},{2,1},{3,0},{4,7},{5,6},{6,5},{7,4},{8,11},{9,10},{10,... | collective-permute-start | bytes 294920 | tf_op jit(solution)/shard_map/ppermute | solution.py:252
  7.5 0.0 collective-permute-start.1
  7.5 0.6 %collective-permute-start.2 = (bf16[3,128,128]{2,1,0:T(8,128)(2,1)S(1)}, bf16[3,128,128]{2,1,0:T(8,128)(2,1)S(1)}, u32[]{:S(2)}, u32[]{:S(2)}) collective-permute-start(bf16[3,128,128]{2,1,0:T(8,128)(2,1)S(1)} %get-tuple-element.41), channel_id=1, source_target_pairs={{0,2},{1,3},{2,0},{3,1},{4,6},{5,7},{6,4},{7,5},{8,10},{9,11},{10,... | collective-permute-start | bytes 294920 | tf_op jit(solution)/shard_map/ppermute | solution.py:252
  8.1 0.0 copy-done
  8.1 0.0 copy-done.4
  8.2 0.0 copy-done.5
  8.2 0.9 %copy-done.1 = bf16[512,256]{1,0:T(8,128)(2,1)S(1)} copy-done((bf16[512,256]{1,0:T(8,128)(2,1)S(1)}, bf16[512,256]{1,0:T(8,128)(2,1)}, u32[]{:S(2)}) %copy-start.1) | copy-done | bytes 262168
  9.0 0.1 copy-done.2
  9.1 0.4 %filter_spectra.1 = (f32[2,512,256]{2,1,0:T(8,128)S(1)}, bf16[128,768]{1,0:T(8,128)(2,1)S(1)}) custom-call(bf16[2,512,128]{2,1,0:T(8,128)(2,1)S(1)} %constant_dynamic-slice_fusion.filters_ref, bf16[512,256]{1,0:T(8,128)(2,1)S(1)} %copy-done.2, bf16[512,256]{1,0:T(8,128)(2,1)S(1)} %copy-done.1, bf16[128,512]{1,0:T(8,128)(2,1)S(1)} %bitcast.7, ...), custom_call_target="tpu_custom_call" | custom-call | flops 268435456 | bytes 1048576 | tf_op jit(solution)/shard_map/filter_spectra/pallas_call | solution.py:142
  9.6 1.5 %collective-permute-start.4 = (bf16[128,768]{1,0:T(8,128)(2,1)S(1)}, bf16[128,768]{1,0:T(8,128)(2,1)S(1)}, u32[]{:S(2)}, u32[]{:S(2)}) collective-permute-start(bf16[128,768]{1,0:T(8,128)(2,1)S(1)} %get-tuple-element.45), channel_id=1, source_target_pairs={{0,1},{1,0},{2,3},{3,2},{4,5},{5,4},{6,7},{7,6},{8,9},{9,8},{10,11... | collective-permute-start | bytes 589832 | tf_op jit(solution)/shard_map/ppermute | solution.py:275
  11.0 0.1 collective-permute-done.refs_1_
  11.1 3.5 %collective-permute-done.1.refs_2_ = bf16[3,128,128]{2,1,0:T(8,128)(2,1)S(1)} collective-permute-done((bf16[3,128,128]{2,1,0:T(8,128)(2,1)S(1)}, bf16[3,128,128]{2,1,0:T(8,128)(2,1)S(1)}, u32[]{:S(2)}, u32[]{:S(2)}) %collective-permute-start.1) | collective-permute-done | bytes 98336 | tf_op jit(solution)/shard_map/ppermute | solution.py:252
  14.6 1.2 %collective-permute-done.2.refs_3_ = bf16[3,128,128]{2,1,0:T(8,128)(2,1)S(1)} collective-permute-done((bf16[3,128,128]{2,1,0:T(8,128)(2,1)S(1)}, bf16[3,128,128]{2,1,0:T(8,128)(2,1)S(1)}, u32[]{:S(2)}, u32[]{:S(2)}) %collective-permute-start.2) | collective-permute-done | bytes 98336 | tf_op jit(solution)/shard_map/ppermute | solution.py:252
  15.8 1.4 %forward_convolutions.1 = (f32[512,128]{1,0:T(8,128)S(1)}, f32[512,256]{1,0:T(8,128)S(1)}, f32[512,256]{1,0:T(8,128)S(1)}, bf16[2,128,128]{2,1,0:T(8,128)(2,1)S(1)}, bf16[2,128,128]{2,1,0:T(8,128)(2,1)S(1)}) custom-call(bf16[3,128,128]{2,1,0:T(8,128)(2,1)S(1)} %get-tuple-element.38.refs_0_, bf16[3,128,128]{2,1,0:T(8,128)(2,1)S(1)} %collective-permute-done.refs_1_, ...), custom_call_target="tpu_custom_call" | custom-call | flops 402653184 | bytes 2228224 | tf_op jit(solution)/shard_map/forward_convolutions/pallas_call | solution.py:142
  17.3 2.5 %collective-permute-start.3 = (bf16[2,128,128]{2,1,0:T(8,128)(2,1)S(1)}, bf16[2,128,128]{2,1,0:T(8,128)(2,1)S(1)}, u32[]{:S(2)}, u32[]{:S(2)}) collective-permute-start(bf16[2,128,128]{2,1,0:T(8,128)(2,1)S(1)} %get-tuple-element.44), channel_id=1, source_target_pairs={{0,2},{1,3},{2,0},{3,1},{4,6},{5,7},{6,4},{7,5},{8,10},{9,11},{10,... | collective-permute-start | bytes 196616 | tf_op jit(solution)/shard_map/ppermute | solution.py:320
  19.8 2.5 %backward_convolutions.1 = (f32[2,512,128]{2,1,0:T(8,128)}, f32[128,512]{1,0:T(8,128)S(1)}, bf16[128,512]{1,0:T(8,128)(2,1)S(1)}, bf16[2,128,128]{2,1,0:T(8,128)...) custom-call(bf16[3,128,128]{2,1,0:T(8,128)(2,1)S(1)} %get-tuple-elem, ...), custom_call_target="tpu_custom_call" | custom-call | flops 536870912 | bytes 3538944 | tf_op jit(solution)/shard_map/backward_convolutions/pallas_call | solution.py:142
  22.3 0.0 collective-permute-start.7
  22.3 0.7 %collective-permute-done.3.refs_1_.near_ref = bf16[2,128,128]{2,1,0:T(8,128)(2,1)S(1)} collective-permute-done((bf16[2,128,128]{2,1,0:T(8,128)(2,1)S(1)}, bf16[2,128,128]{2,1,0:T(8,128)(2,1)S(1)}, u32[]{:S(2)}, u32[]{:S(2)}) %collective-permute-start.3) | collective-permute-done | bytes 65568 | tf_op jit(solution)/shard_map/ppermute | solution.py:320
  22.9 0.0 collective-permute-done.4.refs_4_
  23.0 0.3 weight_partial.1
  23.3 0.1 collective-permute-start.5
  23.4 0.2 collective-permute-done.7.taken_ref
  23.6 0.0 copy-start.3
  23.7 0.3 collective-permute-start.8
  24.0 0.7 %collective-permute-done.5.taken_ref = bf16[128,512]{1,0:T(8,128)(2,1)S(1)} collective-permute-done((bf16[128,512]{1,0:T(8,128)(2,1)S(1)}, bf16[128,512]{1,0:T(8,128)(2,1)S(1)}, u32[]{:S(2)}, u32[]{:S(2)}) %collective-permute-start.5) | collective-permute-done | bytes 131104 | tf_op jit(solution)/shard_map/core_sum/ppermute | solution.py:393
  24.7 0.3 collective-permute-start.6
  25.1 0.0 collective-permute-start.9
  25.1 1.5 %collective-permute-start.10 = (bf16[64,512]{1,0:T(8,128)(2,1)S(1)}, bf16[64,512]{1,0:T(8,128)(2,1)S(1)}, u32[]{:S(2)}, u32[]{:S(2)}) collective-permute-start(bf16[64,512]{1,0:T(8,128)(2,1)S(1)} %get-tuple-element.57), channel_id=1, source_target_pairs={{0,16},{1,25},{2,6},{3,11},{4,20},{5,29},{6,2},{7,15},{8,24},{9,17... | collective-permute-start | bytes 196616 | tf_op jit(solution)/shard_map/ppermute | solution.py:400
  26.6 1.8 %collective-permute-start.14 = (bf16[2,128,128]{2,1,0:T(8,128)(2,1)S(1)}, bf16[2,128,128]{2,1,0:T(8,128)(2,1)S(1)}, u32[]{:S(2)}, u32[]{:S(2)}) collective-permute-start(bf16[2,128,128]{2,1,0:T(8,128)(2,1)S(1)} %get-tuple-element.63), channel_id=1, source_target_pairs={{0,2},{1,3},{2,0},{3,1},{4,6},{5,7},{6,4},{7,5},{8,10},{9,11},{10,... | collective-permute-start | bytes 196616 | tf_op jit(solution)/shard_map/ppermute | solution.py:469
  28.4 0.0 collective-permute-done.8.lag_ref
  28.4 3.8 %collective-permute-start.15 = (bf16[2,128,128]{2,1,0:T(8,128)(2,1)S(1)}, bf16[2,128,128]{2,1,0:T(8,128)(2,1)S(1)}, u32[]{:S(2)}, u32[]{:S(2)}) collective-permute-start(bf16[2,128,128]{2,1,0:T(8,128)(2,1)S(1)} %get-tuple-element.64), channel_id=1, source_target_pairs={{0,3},{1,2},{2,1},{3,0},{4,7},{5,6},{6,5},{7,4},{8,11},{9,10},{10,... | collective-permute-start | bytes 196616 | tf_op jit(solution)/shard_map/ppermute | solution.py:469
  32.2 0.0 collective-permute-done.9.one
  32.2 0.0 collective-permute-done.10.two
  32.2 1.4 %collective-permute-start.11 = (bf16[192,128]{1,0:T(8,128)(2,1)S(1)}, bf16[192,128]{1,0:T(8,128)(2,1)S(1)}, u32[]{:S(2)}, u32[]{:S(2)}) collective-permute-start(bf16[192,128]{1,0:T(8,128)(2,1)S(1)} %get-tuple-element.59), channel_id=1, source_target_pairs={{0,1},{1,3},{2,0},{3,2},{4,5},{5,7},{6,4},{7,6},{8,9},{9,11},{10,8... | collective-permute-start | bytes 147464 | tf_op jit(solution)/shard_map/ppermute | solution.py:493
  33.6 1.5 %collective-permute-start.12 = (bf16[192,128]{1,0:T(8,128)(2,1)S(1)}, bf16[192,128]{1,0:T(8,128)(2,1)S(1)}, u32[]{:S(2)}, u32[]{:S(2)}) collective-permute-start(bf16[192,128]{1,0:T(8,128)(2,1)S(1)} %get-tuple-element.60), channel_id=1, source_target_pairs={{0,3},{1,2},{2,1},{3,0},{4,7},{5,6},{6,5},{7,4},{8,11},{9,10},{10,... | collective-permute-start | bytes 147464 | tf_op jit(solution)/shard_map/ppermute | solution.py:493
  35.1 0.0 collective-permute-done.6.refs_2_.refs_5_
  35.1 1.9 %collective-permute-start.13 = (bf16[192,128]{1,0:T(8,128)(2,1)S(1)}, bf16[192,128]{1,0:T(8,128)(2,1)S(1)}, u32[]{:S(2)}, u32[]{:S(2)}) collective-permute-start(bf16[192,128]{1,0:T(8,128)(2,1)S(1)} %get-tuple-element.61), channel_id=1, source_target_pairs={{0,2},{1,0},{2,3},{3,1},{4,6},{5,4},{6,7},{7,5},{8,10},{9,8},{10,1... | collective-permute-start | bytes 147464 | tf_op jit(solution)/shard_map/ppermute | solution.py:493
  37.1 1.1 %mixed.1 = (bf16[128,512]{1,0:T(8,128)(2,1)}, bf16[128,512]{1,0:T(8,128)(2,1)}) custom-call(bf16[2,128,128]{2,1,0:T(8,128)(2,1)S(1)} %get-tuple-element.43.refs_0_.stays_ref, bf16[2,128,128]{2,1,0:T(8,128)(2,1)S(1)} %collective-permute-done.3.refs_1_.near_ref, bf16[4,128,128]{2,1,0:T(8,128)(2,1)S(1)} %collective-permute-done.6.refs_2_.refs_5_, ...), custom_call_target="tpu_custom_call" | custom-call | flops 134217728 | bytes 1048576 | tf_op jit(solution)/shard_map/mixed/pallas_call | solution.py:142
  38.2 0.0 collective-permute-done.14.refs_6_
  38.2 0.0 collective-permute-done.15.refs_7_
  38.2 0.8 %collective-permute-done.11.refs_1_ = bf16[192,128]{1,0:T(8,128)(2,1)S(1)} collective-permute-done((bf16[192,128]{1,0:T(8,128)(2,1)S(1)}, bf16[192,128]{1,0:T(8,128)(2,1)S(1)}, u32[]{:S(2)}, u32[]{:S(2)}) %collective-permute-start.11) | collective-permute-done | bytes 49184 | tf_op jit(solution)/shard_map/ppermute | solution.py:493
  38.9 0.7 %collective-permute-done.12.refs_2_ = bf16[192,128]{1,0:T(8,128)(2,1)S(1)} collective-permute-done((bf16[192,128]{1,0:T(8,128)(2,1)S(1)}, bf16[192,128]{1,0:T(8,128)(2,1)S(1)}, u32[]{:S(2)}, u32[]{:S(2)}) %collective-permute-start.12) | collective-permute-done | bytes 49184 | tf_op jit(solution)/shard_map/ppermute | solution.py:493
  39.6 0.2 collective-permute-done.13.refs_3_
  39.9 0.8 %means.1 = (f32[2,64,128]{2,1,0:T(8,128)}, f32[64,128]{1,0:T(8,128)}, bf16[128,512]{1,0:T(8,128)(2,1)}, bf16[128,512]{1,0:T(8,128)(2,1)}) custom-call(f32[192,128]{1,0:T(8,128)S(1)} %get-tuple-element.58.refs_0_, bf16[192,128]{1,0:T(8,128)(2,1)S(1)} %collective-permute-done.11.refs_1_, bf16[192,128]{1,0:T(8,128)(2,1)S(1)} %collective-permute-done.12.refs_2_, ...), custom_call_target="tpu_custom_call" | custom-call | bytes 573440 | tf_op jit(solution)/shard_map/means/pallas_call | solution.py:142
  (9 shorter events, 0.1 us)
Async XLA Ops:
  0.6 7.5 %copy-start = (bf16[2,512,512]{2,1,0:T(8,128)(2,1)S(1)}, bf16[2,512,512]{2,1,0:T(8,128)(2,1)}, u32[]{:S(2)}) copy-start(bf16[2,512,512]{2,1,0:T(8,128)(2,1)} %param.12) | copy-start | bytes 3145732
  0.6 7.5 %copy-start.4 = (bf16[1,128,512]{2,1,0:T(8,128)(2,1)S(1)}, bf16[1,128,512]{2,1,0:T(8,128)(2,1)}, u32[]{:S(2)}) copy-start(bf16[1,128,512]{2,1,0:T(8,128)(2,1)} %refs_2_.1) | copy-start | bytes 393220
  0.7 7.5 %copy-start.5 = (bf16[1,128,512]{2,1,0:T(8,128)(2,1)S(1)}, bf16[1,128,512]{2,1,0:T(8,128)(2,1)}, u32[]{:S(2)}) copy-start(bf16[1,128,512]{2,1,0:T(8,128)(2,1)} %refs_4_.2) | copy-start | bytes 393220
  2.3 8.8 %collective-permute-start = (bf16[3,128,128]{2,1,0:T(8,128)(2,1)S(1)}, bf16[3,128,128]{2,1,0:T(8,128)(2,1)S(1)}, u32[]{:S(2)}, u32[]{:S(2)}) collective-permute-start(bf16[3,128,128]{2,1,0:T(8,128)(2,1)S(1)} %get-tuple-element.39), channel_id=1, source_target_pairs={{0,3},{1,2},{2,1},{3,0},{4,7},{5,6},{6,5},{7,4},{8,11},{9,10},{10,... | collective-permute-start | bytes 294920 | tf_op jit(solution)/shard_map/ppermute | solution.py:252
  7.5 7.2 %collective-permute-start.1 = (bf16[3,128,128]{2,1,0:T(8,128)(2,1)S(1)}, bf16[3,128,128]{2,1,0:T(8,128)(2,1)S(1)}, u32[]{:S(2)}, u32[]{:S(2)}) collective-permute-start(bf16[3,128,128]{2,1,0:T(8,128)(2,1)S(1)} %get-tuple-element.40), channel_id=1, source_target_pairs={{0,1},{1,0},{2,3},{3,2},{4,5},{5,4},{6,7},{7,6},{8,9},{9,8},{10,11... | collective-permute-start | bytes 294920 | tf_op jit(solution)/shard_map/ppermute | solution.py:252
  7.5 8.4 %collective-permute-start.2 = (bf16[3,128,128]{2,1,0:T(8,128)(2,1)S(1)}, bf16[3,128,128]{2,1,0:T(8,128)(2,1)S(1)}, u32[]{:S(2)}, u32[]{:S(2)}) collective-permute-start(bf16[3,128,128]{2,1,0:T(8,128)(2,1)S(1)} %get-tuple-element.41), channel_id=1, source_target_pairs={{0,2},{1,3},{2,0},{3,1},{4,6},{5,7},{6,4},{7,5},{8,10},{9,11},{10,... | collective-permute-start | bytes 294920 | tf_op jit(solution)/shard_map/ppermute | solution.py:252
  8.1 1.0 %copy-start.1 = (bf16[512,256]{1,0:T(8,128)(2,1)S(1)}, bf16[512,256]{1,0:T(8,128)(2,1)}, u32[]{:S(2)}) copy-start(bf16[512,256]{1,0:T(8,128)(2,1)} %constant.26.clone.low.refs_6_.refs_9_) | copy-start | bytes 786436
  8.1 1.0 %copy-start.2 = (bf16[512,256]{1,0:T(8,128)(2,1)S(1)}, bf16[512,256]{1,0:T(8,128)(2,1)}, u32[]{:S(2)}) copy-start(bf16[512,256]{1,0:T(8,128)(2,1)} %constant.25.clone.high.refs_5_.refs_8_) | copy-start | bytes 786436
  9.1 6.7 %copy-start.6 = (bf16[256,512]{1,0:T(8,128)(2,1)S(1)}, bf16[256,512]{1,0:T(8,128)(2,1)}, u32[]{:S(2)}) copy-start(bf16[256,512]{1,0:T(8,128)(2,1)} %constant.27.clone.refs_7_.refs_10_) | copy-start | bytes 786436
  9.6 13.4 %collective-permute-start.4 = (bf16[128,768]{1,0:T(8,128)(2,1)S(1)}, bf16[128,768]{1,0:T(8,128)(2,1)S(1)}, u32[]{:S(2)}, u32[]{:S(2)}) collective-permute-start(bf16[128,768]{1,0:T(8,128)(2,1)S(1)} %get-tuple-element.45), channel_id=1, source_target_pairs={{0,1},{1,0},{2,3},{3,2},{4,5},{5,4},{6,7},{7,6},{8,9},{9,8},{10,11... | collective-permute-start | bytes 589832 | tf_op jit(solution)/shard_map/ppermute | solution.py:275
  17.3 5.7 %collective-permute-start.3 = (bf16[2,128,128]{2,1,0:T(8,128)(2,1)S(1)}, bf16[2,128,128]{2,1,0:T(8,128)(2,1)S(1)}, u32[]{:S(2)}, u32[]{:S(2)}) collective-permute-start(bf16[2,128,128]{2,1,0:T(8,128)(2,1)S(1)} %get-tuple-element.44), channel_id=1, source_target_pairs={{0,2},{1,3},{2,0},{3,1},{4,6},{5,7},{6,4},{7,5},{8,10},{9,11},{10,... | collective-permute-start | bytes 196616 | tf_op jit(solution)/shard_map/ppermute | solution.py:320
  22.3 1.3 %collective-permute-start.7 = (bf16[128,512]{1,0:T(8,128)(2,1)S(1)}, bf16[128,512]{1,0:T(8,128)(2,1)S(1)}, u32[]{:S(2)}, u32[]{:S(2)}) collective-permute-start(bf16[128,512]{1,0:T(8,128)(2,1)S(1)} %get-tuple-element.55), channel_id=1, source_target_pairs={{0,4},{4,0},{8,12},{12,8},{16,20},{20,16},{24,28},{28,24},{1,5},{5... | collective-permute-start | bytes 393224 | tf_op jit(solution)/shard_map/lag_core_sum/ppermute | solution.py:393
  23.3 1.4 %collective-permute-start.5 = (bf16[128,512]{1,0:T(8,128)(2,1)S(1)}, bf16[128,512]{1,0:T(8,128)(2,1)S(1)}, u32[]{:S(2)}, u32[]{:S(2)}) collective-permute-start(bf16[128,512]{1,0:T(8,128)(2,1)S(1)} %get-tuple-element.47), channel_id=1, source_target_pairs={{0,4},{4,0},{8,12},{12,8},{16,20},{20,16},{24,28},{28,24},{1,5},{5... | collective-permute-start | bytes 393224 | tf_op jit(solution)/shard_map/core_sum/ppermute | solution.py:393
  23.6 13.5 %copy-start.3 = (bf16[512,512]{1,0:T(8,128)(2,1)S(1)}, bf16[512,512]{1,0:T(8,128)(2,1)}, u32[]{:S(2)}) copy-start(bf16[512,512]{1,0:T(8,128)(2,1)} %refs_4_.3) | copy-start | bytes 1572868
  23.7 4.7 %collective-permute-start.8 = (bf16[128,512]{1,0:T(8,128)(2,1)S(1)}, bf16[128,512]{1,0:T(8,128)(2,1)S(1)}, u32[]{:S(2)}, u32[]{:S(2)}) collective-permute-start(bf16[128,512]{1,0:T(8,128)(2,1)S(1)} %lag_core_sum.1), channel_id=1, source_target_pairs={{0,4},{1,9},{2,18},{3,27},{4,0},{5,13},{6,22},{7,31},{8,12},{9,1},... | collective-permute-start | bytes 393224 | tf_op jit(solution)/shard_map/ppermute | solution.py:400
  24.7 10.4 %collective-permute-start.6 = (bf16[4,128,128]{2,1,0:T(8,128)(2,1)S(1)}, bf16[4,128,128]{2,1,0:T(8,128)(2,1)S(1)}, u32[]{:S(2)}, u32[]{:S(2)}) collective-permute-start(bf16[4,128,128]{2,1,0:T(8,128)(2,1)S(1)} %get-tuple-element.52), channel_id=1, source_target_pairs={{0,1},{1,0},{2,3},{3,2},{4,5},{5,4},{6,7},{7,6},{8,9},{9,8},{10,11... | collective-permute-start | bytes 393224 | tf_op jit(solution)/shard_map/ppermute | solution.py:465
  25.1 7.1 %collective-permute-start.9 = (bf16[64,512]{1,0:T(8,128)(2,1)S(1)}, bf16[64,512]{1,0:T(8,128)(2,1)S(1)}, u32[]{:S(2)}, u32[]{:S(2)}) collective-permute-start(bf16[64,512]{1,0:T(8,128)(2,1)S(1)} %get-tuple-element.56), channel_id=1, source_target_pairs={{0,4},{1,9},{2,18},{3,27},{4,0},{5,13},{6,22},{7,31},{8,12},{9,1},... | collective-permute-start | bytes 196616 | tf_op jit(solution)/shard_map/ppermute | solution.py:400
  25.1 7.1 %collective-permute-start.10 = (bf16[64,512]{1,0:T(8,128)(2,1)S(1)}, bf16[64,512]{1,0:T(8,128)(2,1)S(1)}, u32[]{:S(2)}, u32[]{:S(2)}) collective-permute-start(bf16[64,512]{1,0:T(8,128)(2,1)S(1)} %get-tuple-element.57), channel_id=1, source_target_pairs={{0,16},{1,25},{2,6},{3,11},{4,20},{5,29},{6,2},{7,15},{8,24},{9,17... | collective-permute-start | bytes 196616 | tf_op jit(solution)/shard_map/ppermute | solution.py:400
  26.6 11.6 %collective-permute-start.14 = (bf16[2,128,128]{2,1,0:T(8,128)(2,1)S(1)}, bf16[2,128,128]{2,1,0:T(8,128)(2,1)S(1)}, u32[]{:S(2)}, u32[]{:S(2)}) collective-permute-start(bf16[2,128,128]{2,1,0:T(8,128)(2,1)S(1)} %get-tuple-element.63), channel_id=1, source_target_pairs={{0,2},{1,3},{2,0},{3,1},{4,6},{5,7},{6,4},{7,5},{8,10},{9,11},{10,... | collective-permute-start | bytes 196616 | tf_op jit(solution)/shard_map/ppermute | solution.py:469
  28.4 9.8 %collective-permute-start.15 = (bf16[2,128,128]{2,1,0:T(8,128)(2,1)S(1)}, bf16[2,128,128]{2,1,0:T(8,128)(2,1)S(1)}, u32[]{:S(2)}, u32[]{:S(2)}) collective-permute-start(bf16[2,128,128]{2,1,0:T(8,128)(2,1)S(1)} %get-tuple-element.64), channel_id=1, source_target_pairs={{0,3},{1,2},{2,1},{3,0},{4,7},{5,6},{6,5},{7,4},{8,11},{9,10},{10,... | collective-permute-start | bytes 196616 | tf_op jit(solution)/shard_map/ppermute | solution.py:469
  32.2 6.7 %collective-permute-start.11 = (bf16[192,128]{1,0:T(8,128)(2,1)S(1)}, bf16[192,128]{1,0:T(8,128)(2,1)S(1)}, u32[]{:S(2)}, u32[]{:S(2)}) collective-permute-start(bf16[192,128]{1,0:T(8,128)(2,1)S(1)} %get-tuple-element.59), channel_id=1, source_target_pairs={{0,1},{1,3},{2,0},{3,2},{4,5},{5,7},{6,4},{7,6},{8,9},{9,11},{10,8... | collective-permute-start | bytes 147464 | tf_op jit(solution)/shard_map/ppermute | solution.py:493
  33.6 6.0 %collective-permute-start.12 = (bf16[192,128]{1,0:T(8,128)(2,1)S(1)}, bf16[192,128]{1,0:T(8,128)(2,1)S(1)}, u32[]{:S(2)}, u32[]{:S(2)}) collective-permute-start(bf16[192,128]{1,0:T(8,128)(2,1)S(1)} %get-tuple-element.60), channel_id=1, source_target_pairs={{0,3},{1,2},{2,1},{3,0},{4,7},{5,6},{6,5},{7,4},{8,11},{9,10},{10,... | collective-permute-start | bytes 147464 | tf_op jit(solution)/shard_map/ppermute | solution.py:493
  35.1 4.7 %collective-permute-start.13 = (bf16[192,128]{1,0:T(8,128)(2,1)S(1)}, bf16[192,128]{1,0:T(8,128)(2,1)S(1)}, u32[]{:S(2)}, u32[]{:S(2)}) collective-permute-start(bf16[192,128]{1,0:T(8,128)(2,1)S(1)} %get-tuple-element.61), channel_id=1, source_target_pairs={{0,2},{1,0},{2,3},{3,1},{4,6},{5,4},{6,7},{7,5},{8,10},{9,8},{10,1... | collective-permute-start | bytes 147464 | tf_op jit(solution)/shard_map/ppermute | solution.py:493

commit v11 on v10

--- a/solution.py
+++ b/solution.py
@@ -325,8 +325,6 @@
         parts, refs = refs[:seq], refs[seq:]
         filt, first_ref, value_spec, mixed_spec, high, low, back = refs[:7]
         lags, *outs, stream, total = refs[7:]
-        if fast:
-            lag_kept, lag_given, *outs, packed = outs
         count = length // block
         for step, part in zip(in_order, parts):
             put_rows(stream, came(step), rows, part[2])
@@ -356,7 +354,43 @@
             total[i * block : (i + 1) * block] = columns(out, i, cols)
         put_result(outs, 1, total, 2)
         put_lags(0, out)
-        if fast:
+
+    with jax.named_scope("backward_convolutions"):
+        lags, *sends_home = call(
+            backward_kernel,
+            [((2, length, cols), F32)] + [((2, rows, cols), BF16)] * seq,
+            (
+                *(parts_in[step] for step in in_order),
+                filter_spectra,
+                first_conv,
+                value_spectra,
+                mixed_spectra,
+                fwd_high,
+                fwd_low,
+                inv_high,
+            ),
+            scratch=[pltpu.VMEM((length, cols), BF16), pltpu.VMEM((length, cols), F32)],
+            flops=8 * table_flops,
+            limit=limit,
+        )
+
+    if fast:
+        def to_core(block):
+            return lax.ppermute(block, "dp", [(i, i ^ 1) for i in range(data)])
+
+        def to_chip(block, other):
+            pairs = []
+            for i in range(data):
+                for j in range(seq):
+                    pairs.append((i * seq + j, (i ^ (2 * (j ^ other) or 1)) * seq + j))
+            return lax.ppermute(block, ("dp", "ctx"), pairs)
+
+        def core_kernel(kept_ref, taken_ref, *outs):
+            summed = (kept_ref[...] + taken_ref[...].astype(F32)).astype(BF16)
+            for index, out in enumerate(outs):
+                out[...] = summed[index * out.shape[0] : (index + 1) * out.shape[0]]
+
+        def lag_kernel(lags, lag_kept, lag_given, packed):
             here, own_core = lax.axis_index("ctx"), lax.rem(lax.axis_index("dp"), 2)
             half = jnp.where(here == 0, 1 - own_core, own_core)
             lower = lax.broadcasted_iota(jnp.int32, (length, cols), 1) < fine
@@ -368,43 +402,15 @@
                 given = packed[1 - half, index * rows : (index + 1) * rows]
                 lag_given[:, lanes] = given.astype(BF16)
 
-    with jax.named_scope("backward_convolutions"):
-        lags, *sends_home = call(
-            backward_kernel,
-            [((2, length, cols), F32)] + [((rows, width), F32), wide_bf16] * fast + [((2, rows, cols), BF16)] * seq,
-            (
-                *(parts_in[step] for step in in_order),
-                filter_spectra,
-                first_conv,
-                value_spectra,
-                mixed_spectra,
-                fwd_high,
-                fwd_low,
-                inv_high,
-            ),
-            scratch=[pltpu.VMEM((2, length, cols), F32)] * fast
-            + [pltpu.VMEM((length, cols), BF16), pltpu.VMEM((length, cols), F32)],
-            flops=8 * table_flops,
-            limit=limit,
-        )
-
-    if fast:
-        def to_core(block):
-            return lax.ppermute(block, "dp", [(i, i ^ 1) for i in range(data)])
-
-        def to_chip(block, other):
-            pairs = []
-            for i in range(data):
-                for j in range(seq):
-                    pairs.append((i * seq + j, (i ^ (2 * (j ^ other) or 1)) * seq + j))
-            return lax.ppermute(block, ("dp", "ctx"), pairs)
-
-        def core_kernel(kept_ref, taken_ref, *outs):
-            summed = (kept_ref[...] + taken_ref[...].astype(F32)).astype(BF16)
-            for index, out in enumerate(outs):
-                out[...] = summed[index * out.shape[0] : (index + 1) * out.shape[0]]
-
-        lag_kept, lag_given, *sends_home = sends_home
+
+        with jax.named_scope("lag_halves"):
+            lag_kept, lag_given = call(
+                lag_kernel,
+                [((rows, width), F32), wide_bf16],
+                (lags,),
+                scratch=[pltpu.VMEM((2, length, cols), F32)],
+                limit=limit,
+            )
         with jax.named_scope("lag_core_sum"):
             (lag_sum,) = call(
                 core_kernel, [wide_bf16], (lag_kept, to_core(lag_given)), limit=limit

time: 40.8 us -> 40.8 us (level)
  Pallas kernels: 8.32 us -> 7.77 us
    pallas_call x10 -> x11, Pallas kernels: 8.32 us -> 7.77 us  [call(): pl.pallas_call(kernel, out_shape=[jax.ShapeDtypeStruct(shape, dtype) for...]
    ppermute x1, waiting for transfers between devices: 0.68 us -> 1.16 us  [on_device(): second_near = lax.ppermute(goes, 'ctx', across(2))]
  transfers between devices with their start and end apart: 16 -> 16, of which waited for: 9 -> 8; matrix products, arithmetic and copies ran while one was open for 0% -> 0% of each run, Pallas kernels for 15% -> 13%
where the time goes in v11:
time: 40.8 us; the launch traced here: 40.6 us
  starting transfers between devices  22.7 us (56%)
  waiting for transfers between devices  8.39 us (21%)
  Pallas kernels  7.77 us (19%)
  local copies, waits for them, and re-layouts  1.03 us (3%)
  between operations  0.78 us (2%)
    pallas_call x11, Pallas kernels, call(): pl.pallas_call(kernel, out_shape=[jax.ShapeDtypeStruct(shape, dtype) for...  7.77 us
    ppermute x3, starting transfers between devices, on_device(): lax.ppermute(sends[far], 'ctx', across(far))  5.76 us
    ppermute x2, starting transfers between devices, on_device(): home = [lax.ppermute(sends_home[far], 'ctx', across(far)) for far in (2, 3)]  5.62 us
    ppermute x3, starting transfers between devices, on_device(): last_terms.append(lax.ppermute(part, 'ctx', list(enumerate(table))))  4.85 us
    ppermute x3, waiting for transfers between devices, on_device(): lax.ppermute(sends[far], 'ctx', across(far))  4.79 us
    ppermute x1, starting transfers between devices, on_device(): second_near = lax.ppermute(goes, 'ctx', across(2))  2.49 us
    ppermute x3, starting transfers between devices, to_chip(): return lax.ppermute(block, ('dp', 'ctx'), pairs)  2.1 us
    ppermute x3, waiting for transfers between devices, on_device(): last_terms.append(lax.ppermute(part, 'ctx', list(enumerate(table))))  1.7 us
  transfers between devices with their start and end apart: 16, of which 8 were waited for; matrix products, arithmetic and copies ran while one was open for 0% of the time, Pallas kernels for 13%

profile of v11, /device:TPU:0, one launch (start us, length us, event | category | flops | bytes accessed | tf_op | source)
XLA Modules:
  0.0 40.6 jit_solution(5387115382787378220)
XLA Ops:
  0.6 0.0 copy-start
  0.6 0.0 copy-start.4
  0.7 0.0 copy-start.5
  0.7 1.7 %load.1 = (bf16[3,128,128]{2,1,0:T(8,128)(2,1)S(1)}, bf16[3,128,128]{2,1,0:T(8,128)(2,1)S(1)}, bf16[3,128,128]{2,1,0:T(8,128)(2,1)S(1)}, bf16[3,128,128]{2,1,0:T(8,128)(2,1)S(1)}) custom-call(bf16[1,128,512]{2,1,0:T(8,128)(2,1)} %refs_0_.1, bf16[1,128,512]{2,1,0:T(8,128)(2,1)} %refs_1_.1, bf16[1,128,512]{2,1,0:T(8,128)(2,1)} %refs_2_.1, ...), custom_call_target="tpu_custom_call" | custom-call | flops 67108864 | bytes 1048576 | tf_op jit(solution)/shard_map/load/pallas_call | solution.py:142
  2.3 5.1 %collective-permute-start = (bf16[3,128,128]{2,1,0:T(8,128)(2,1)S(1)}, bf16[3,128,128]{2,1,0:T(8,128)(2,1)S(1)}, u32[]{:S(2)}, u32[]{:S(2)}) collective-permute-start(bf16[3,128,128]{2,1,0:T(8,128)(2,1)S(1)} %get-tuple-element.40), channel_id=1, source_target_pairs={{0,3},{1,2},{2,1},{3,0},{4,7},{5,6},{6,5},{7,4},{8,11},{9,10},{10,... | collective-permute-start | bytes 294920 | tf_op jit(solution)/shard_map/ppermute | solution.py:252
  7.5 0.0 collective-permute-start.1
  7.5 0.6 %collective-permute-start.2 = (bf16[3,128,128]{2,1,0:T(8,128)(2,1)S(1)}, bf16[3,128,128]{2,1,0:T(8,128)(2,1)S(1)}, u32[]{:S(2)}, u32[]{:S(2)}) collective-permute-start(bf16[3,128,128]{2,1,0:T(8,128)(2,1)S(1)} %get-tuple-element.42), channel_id=1, source_target_pairs={{0,2},{1,3},{2,0},{3,1},{4,6},{5,7},{6,4},{7,5},{8,10},{9,11},{10,... | collective-permute-start | bytes 294920 | tf_op jit(solution)/shard_map/ppermute | solution.py:252
  8.1 0.0 copy-done
  8.1 0.0 copy-done.4
  8.2 0.9 %copy-done.1 = bf16[512,256]{1,0:T(8,128)(2,1)S(1)} copy-done((bf16[512,256]{1,0:T(8,128)(2,1)S(1)}, bf16[512,256]{1,0:T(8,128)(2,1)}, u32[]{:S(2)}) %copy-start.1) | copy-done | bytes 262168
  9.0 0.1 copy-done.2
  9.1 0.4 %filter_spectra.1 = (f32[2,512,256]{2,1,0:T(8,128)S(1)}, bf16[128,768]{1,0:T(8,128)(2,1)S(1)}) custom-call(bf16[2,512,128]{2,1,0:T(8,128)(2,1)S(1)} %constant_dynamic-slice_fusion.filters_ref, bf16[512,256]{1,0:T(8,128)(2,1)S(1)} %copy-done.2, bf16[512,256]{1,0:T(8,128)(2,1)S(1)} %copy-done.1, bf16[128,512]{1,0:T(8,128)(2,1)S(1)} %bitcast.7, ...), custom_call_target="tpu_custom_call" | custom-call | flops 268435456 | bytes 1048576 | tf_op jit(solution)/shard_map/filter_spectra/pallas_call | solution.py:142
  9.6 1.5 %collective-permute-start.4 = (bf16[128,768]{1,0:T(8,128)(2,1)S(1)}, bf16[128,768]{1,0:T(8,128)(2,1)S(1)}, u32[]{:S(2)}, u32[]{:S(2)}) collective-permute-start(bf16[128,768]{1,0:T(8,128)(2,1)S(1)} %get-tuple-element.46), channel_id=1, source_target_pairs={{0,1},{1,0},{2,3},{3,2},{4,5},{5,4},{6,7},{7,6},{8,9},{9,8},{10,11... | collective-permute-start | bytes 589832 | tf_op jit(solution)/shard_map/ppermute | solution.py:275
  11.0 0.1 collective-permute-done.refs_1_
  11.1 3.5 %collective-permute-done.1.refs_2_ = bf16[3,128,128]{2,1,0:T(8,128)(2,1)S(1)} collective-permute-done((bf16[3,128,128]{2,1,0:T(8,128)(2,1)S(1)}, bf16[3,128,128]{2,1,0:T(8,128)(2,1)S(1)}, u32[]{:S(2)}, u32[]{:S(2)}) %collective-permute-start.1) | collective-permute-done | bytes 98336 | tf_op jit(solution)/shard_map/ppermute | solution.py:252
  14.6 1.2 %collective-permute-done.2.refs_3_ = bf16[3,128,128]{2,1,0:T(8,128)(2,1)S(1)} collective-permute-done((bf16[3,128,128]{2,1,0:T(8,128)(2,1)S(1)}, bf16[3,128,128]{2,1,0:T(8,128)(2,1)S(1)}, u32[]{:S(2)}, u32[]{:S(2)}) %collective-permute-start.2) | collective-permute-done | bytes 98336 | tf_op jit(solution)/shard_map/ppermute | solution.py:252
  15.8 1.4 %forward_convolutions.1 = (f32[512,128]{1,0:T(8,128)S(1)}, f32[512,256]{1,0:T(8,128)S(1)}, f32[512,256]{1,0:T(8,128)S(1)}, bf16[2,128,128]{2,1,0:T(8,128)(2,1)S(1)}, bf16[2,128,128]{2,1,0:T(8,128)(2,1)S(1)}) custom-call(bf16[3,128,128]{2,1,0:T(8,128)(2,1)S(1)} %get-tuple-element.39.refs_0_, bf16[3,128,128]{2,1,0:T(8,128)(2,1)S(1)} %collective-permute-done.refs_1_, ...), custom_call_target="tpu_custom_call" | custom-call | flops 402653184 | bytes 2228224 | tf_op jit(solution)/shard_map/forward_convolutions/pallas_call | solution.py:142
  17.3 2.5 %collective-permute-start.3 = (bf16[2,128,128]{2,1,0:T(8,128)(2,1)S(1)}, bf16[2,128,128]{2,1,0:T(8,128)(2,1)S(1)}, u32[]{:S(2)}, u32[]{:S(2)}) collective-permute-start(bf16[2,128,128]{2,1,0:T(8,128)(2,1)S(1)} %get-tuple-element.45), channel_id=1, source_target_pairs={{0,2},{1,3},{2,0},{3,1},{4,6},{5,7},{6,4},{7,5},{8,10},{9,11},{10,... | collective-permute-start | bytes 196616 | tf_op jit(solution)/shard_map/ppermute | solution.py:320
  19.8 1.7 %backward_convolutions.1 = (f32[2,512,128]{2,1,0:T(8,128)S(1)}, bf16[2,128,128]{2,1,0:T(8,128)(2,1)S(1)}, bf16[2,128,128]{2,1,0:T(8,128)(2,1)S(1)}, bf16[2,128,1...) custom-call(bf16[3,128,128]{2,1,0:T(8,128)(2,1)S(1)} %get-tuple-element.39.refs_0_, ...), custom_call_target="tpu_custom_call" | custom-call | flops 536870912 | bytes 3538944 | tf_op jit(solution)/shard_map/backward_convolutions/pallas_call | solution.py:142
  21.4 0.3 lag_halves.1
  21.7 0.1 collective-permute-start.7
  21.8 1.2 %collective-permute-done.3.refs_1_.near_ref = bf16[2,128,128]{2,1,0:T(8,128)(2,1)S(1)} collective-permute-done((bf16[2,128,128]{2,1,0:T(8,128)(2,1)S(1)}, bf16[2,128,128]{2,1,0:T(8,128)(2,1)S(1)}, u32[]{:S(2)}, u32[]{:S(2)}) %collective-permute-start.3) | collective-permute-done | bytes 65568 | tf_op jit(solution)/shard_map/ppermute | solution.py:320
  22.9 0.0 collective-permute-done.4.refs_4_
  23.0 0.3 weight_partial.1
  23.3 0.1 collective-permute-start.5
  23.4 0.0 collective-permute-done.7.taken_ref
  23.4 0.0 copy-start.3
  23.4 0.5 %collective-permute-start.8 = (bf16[128,512]{1,0:T(8,128)(2,1)S(1)}, bf16[128,512]{1,0:T(8,128)(2,1)S(1)}, u32[]{:S(2)}, u32[]{:S(2)}) collective-permute-start(bf16[128,512]{1,0:T(8,128)(2,1)S(1)} %lag_core_sum.1), channel_id=1, source_target_pairs={{0,4},{1,9},{2,18},{3,27},{4,0},{5,13},{6,22},{7,31},{8,12},{9,1},... | collective-permute-start | bytes 393224 | tf_op jit(solution)/shard_map/ppermute | solution.py:386
  24.0 0.7 %collective-permute-done.5.taken_ref = bf16[128,512]{1,0:T(8,128)(2,1)S(1)} collective-permute-done((bf16[128,512]{1,0:T(8,128)(2,1)S(1)}, bf16[128,512]{1,0:T(8,128)(2,1)S(1)}, u32[]{:S(2)}, u32[]{:S(2)}) %collective-permute-start.5) | collective-permute-done | bytes 131104 | tf_op jit(solution)/shard_map/core_sum/ppermute | solution.py:379
  24.7 0.3 collective-permute-start.6
  25.0 0.0 collective-permute-start.9
  25.0 1.5 %collective-permute-start.10 = (bf16[64,512]{1,0:T(8,128)(2,1)S(1)}, bf16[64,512]{1,0:T(8,128)(2,1)S(1)}, u32[]{:S(2)}, u32[]{:S(2)}) collective-permute-start(bf16[64,512]{1,0:T(8,128)(2,1)S(1)} %get-tuple-element.59), channel_id=1, source_target_pairs={{0,16},{1,25},{2,6},{3,11},{4,20},{5,29},{6,2},{7,15},{8,24},{9,17... | collective-permute-start | bytes 196616 | tf_op jit(solution)/shard_map/ppermute | solution.py:386
  26.6 1.8 %collective-permute-start.14 = (bf16[2,128,128]{2,1,0:T(8,128)(2,1)S(1)}, bf16[2,128,128]{2,1,0:T(8,128)(2,1)S(1)}, u32[]{:S(2)}, u32[]{:S(2)}) collective-permute-start(bf16[2,128,128]{2,1,0:T(8,128)(2,1)S(1)} %get-tuple-element.65), channel_id=1, source_target_pairs={{0,2},{1,3},{2,0},{3,1},{4,6},{5,7},{6,4},{7,5},{8,10},{9,11},{10,... | collective-permute-start | bytes 196616 | tf_op jit(solution)/shard_map/ppermute | solution.py:475
  28.4 0.0 collective-permute-done.8.lag_ref
  28.4 3.8 %collective-permute-start.15 = (bf16[2,128,128]{2,1,0:T(8,128)(2,1)S(1)}, bf16[2,128,128]{2,1,0:T(8,128)(2,1)S(1)}, u32[]{:S(2)}, u32[]{:S(2)}) collective-permute-start(bf16[2,128,128]{2,1,0:T(8,128)(2,1)S(1)} %get-tuple-element.66), channel_id=1, source_target_pairs={{0,3},{1,2},{2,1},{3,0},{4,7},{5,6},{6,5},{7,4},{8,11},{9,10},{10,... | collective-permute-start | bytes 196616 | tf_op jit(solution)/shard_map/ppermute | solution.py:475
  32.2 0.0 collective-permute-done.9.one
  32.2 0.0 collective-permute-done.10.two
  32.2 1.4 %collective-permute-start.11 = (bf16[192,128]{1,0:T(8,128)(2,1)S(1)}, bf16[192,128]{1,0:T(8,128)(2,1)S(1)}, u32[]{:S(2)}, u32[]{:S(2)}) collective-permute-start(bf16[192,128]{1,0:T(8,128)(2,1)S(1)} %get-tuple-element.61), channel_id=1, source_target_pairs={{0,1},{1,3},{2,0},{3,2},{4,5},{5,7},{6,4},{7,6},{8,9},{9,11},{10,8... | collective-permute-start | bytes 147464 | tf_op jit(solution)/shard_map/ppermute | solution.py:499
  33.6 1.5 %collective-permute-start.12 = (bf16[192,128]{1,0:T(8,128)(2,1)S(1)}, bf16[192,128]{1,0:T(8,128)(2,1)S(1)}, u32[]{:S(2)}, u32[]{:S(2)}) collective-permute-start(bf16[192,128]{1,0:T(8,128)(2,1)S(1)} %get-tuple-element.62), channel_id=1, source_target_pairs={{0,3},{1,2},{2,1},{3,0},{4,7},{5,6},{6,5},{7,4},{8,11},{9,10},{10,... | collective-permute-start | bytes 147464 | tf_op jit(solution)/shard_map/ppermute | solution.py:499
  35.1 0.0 collective-permute-done.6.refs_2_.refs_5_
  35.1 1.9 %collective-permute-start.13 = (bf16[192,128]{1,0:T(8,128)(2,1)S(1)}, bf16[192,128]{1,0:T(8,128)(2,1)S(1)}, u32[]{:S(2)}, u32[]{:S(2)}) collective-permute-start(bf16[192,128]{1,0:T(8,128)(2,1)S(1)} %get-tuple-element.63), channel_id=1, source_target_pairs={{0,2},{1,0},{2,3},{3,1},{4,6},{5,4},{6,7},{7,5},{8,10},{9,8},{10,1... | collective-permute-start | bytes 147464 | tf_op jit(solution)/shard_map/ppermute | solution.py:499
  37.1 1.1 %mixed.1 = (bf16[128,512]{1,0:T(8,128)(2,1)}, bf16[128,512]{1,0:T(8,128)(2,1)}) custom-call(bf16[2,128,128]{2,1,0:T(8,128)(2,1)S(1)} %get-tuple-element.44.refs_0_.stays_ref, bf16[2,128,128]{2,1,0:T(8,128)(2,1)S(1)} %collective-permute-done.3.refs_1_.near_ref, bf16[4,128,128]{2,1,0:T(8,128)(2,1)S(1)} %collective-permute-done.6.refs_2_.refs_5_, ...), custom_call_target="tpu_custom_call" | custom-call | flops 134217728 | bytes 1048576 | tf_op jit(solution)/shard_map/mixed/pallas_call | solution.py:142
  38.2 0.0 collective-permute-done.14.refs_6_
  38.2 0.0 collective-permute-done.15.refs_7_
  38.2 0.8 %collective-permute-done.11.refs_1_ = bf16[192,128]{1,0:T(8,128)(2,1)S(1)} collective-permute-done((bf16[192,128]{1,0:T(8,128)(2,1)S(1)}, bf16[192,128]{1,0:T(8,128)(2,1)S(1)}, u32[]{:S(2)}, u32[]{:S(2)}) %collective-permute-start.11) | collective-permute-done | bytes 49184 | tf_op jit(solution)/shard_map/ppermute | solution.py:499
  38.9 0.7 %collective-permute-done.12.refs_2_ = bf16[192,128]{1,0:T(8,128)(2,1)S(1)} collective-permute-done((bf16[192,128]{1,0:T(8,128)(2,1)S(1)}, bf16[192,128]{1,0:T(8,128)(2,1)S(1)}, u32[]{:S(2)}, u32[]{:S(2)}) %collective-permute-start.12) | collective-permute-done | bytes 49184 | tf_op jit(solution)/shard_map/ppermute | solution.py:499
  39.6 0.2 collective-permute-done.13.refs_3_
  39.9 0.8 %means.1 = (f32[2,64,128]{2,1,0:T(8,128)}, f32[64,128]{1,0:T(8,128)}, bf16[128,512]{1,0:T(8,128)(2,1)}, bf16[128,512]{1,0:T(8,128)(2,1)}) custom-call(f32[192,128]{1,0:T(8,128)S(1)} %get-tuple-element.60.refs_0_, bf16[192,128]{1,0:T(8,128)(2,1)S(1)} %collective-permute-done.11.refs_1_, bf16[192,128]{1,0:T(8,128)(2,1)S(1)} %collective-permute-done.12.refs_2_, ...), custom_call_target="tpu_custom_call" | custom-call | bytes 573440 | tf_op jit(solution)/shard_map/means/pallas_call | solution.py:142
  (10 shorter events, 0.1 us)
Async XLA Ops:
  0.6 7.5 %copy-start = (bf16[2,512,512]{2,1,0:T(8,128)(2,1)S(1)}, bf16[2,512,512]{2,1,0:T(8,128)(2,1)}, u32[]{:S(2)}) copy-start(bf16[2,512,512]{2,1,0:T(8,128)(2,1)} %param.12) | copy-start | bytes 3145732
  0.6 7.5 %copy-start.4 = (bf16[1,128,512]{2,1,0:T(8,128)(2,1)S(1)}, bf16[1,128,512]{2,1,0:T(8,128)(2,1)}, u32[]{:S(2)}) copy-start(bf16[1,128,512]{2,1,0:T(8,128)(2,1)} %refs_2_.1) | copy-start | bytes 393220
  0.7 7.5 %copy-start.5 = (bf16[1,128,512]{2,1,0:T(8,128)(2,1)S(1)}, bf16[1,128,512]{2,1,0:T(8,128)(2,1)}, u32[]{:S(2)}) copy-start(bf16[1,128,512]{2,1,0:T(8,128)(2,1)} %refs_4_.2) | copy-start | bytes 393220
  2.3 8.8 %collective-permute-start = (bf16[3,128,128]{2,1,0:T(8,128)(2,1)S(1)}, bf16[3,128,128]{2,1,0:T(8,128)(2,1)S(1)}, u32[]{:S(2)}, u32[]{:S(2)}) collective-permute-start(bf16[3,128,128]{2,1,0:T(8,128)(2,1)S(1)} %get-tuple-element.40), channel_id=1, source_target_pairs={{0,3},{1,2},{2,1},{3,0},{4,7},{5,6},{6,5},{7,4},{8,11},{9,10},{10,... | collective-permute-start | bytes 294920 | tf_op jit(solution)/shard_map/ppermute | solution.py:252
  7.5 7.2 %collective-permute-start.1 = (bf16[3,128,128]{2,1,0:T(8,128)(2,1)S(1)}, bf16[3,128,128]{2,1,0:T(8,128)(2,1)S(1)}, u32[]{:S(2)}, u32[]{:S(2)}) collective-permute-start(bf16[3,128,128]{2,1,0:T(8,128)(2,1)S(1)} %get-tuple-element.41), channel_id=1, source_target_pairs={{0,1},{1,0},{2,3},{3,2},{4,5},{5,4},{6,7},{7,6},{8,9},{9,8},{10,11... | collective-permute-start | bytes 294920 | tf_op jit(solution)/shard_map/ppermute | solution.py:252
  7.5 8.4 %collective-permute-start.2 = (bf16[3,128,128]{2,1,0:T(8,128)(2,1)S(1)}, bf16[3,128,128]{2,1,0:T(8,128)(2,1)S(1)}, u32[]{:S(2)}, u32[]{:S(2)}) collective-permute-start(bf16[3,128,128]{2,1,0:T(8,128)(2,1)S(1)} %get-tuple-element.42), channel_id=1, source_target_pairs={{0,2},{1,3},{2,0},{3,1},{4,6},{5,7},{6,4},{7,5},{8,10},{9,11},{10,... | collective-permute-start | bytes 294920 | tf_op jit(solution)/shard_map/ppermute | solution.py:252
  8.1 1.0 %copy-start.1 = (bf16[512,256]{1,0:T(8,128)(2,1)S(1)}, bf16[512,256]{1,0:T(8,128)(2,1)}, u32[]{:S(2)}) copy-start(bf16[512,256]{1,0:T(8,128)(2,1)} %constant.26.clone.low.refs_6_.refs_9_) | copy-start | bytes 786436
  8.1 1.0 %copy-start.2 = (bf16[512,256]{1,0:T(8,128)(2,1)S(1)}, bf16[512,256]{1,0:T(8,128)(2,1)}, u32[]{:S(2)}) copy-start(bf16[512,256]{1,0:T(8,128)(2,1)} %constant.25.clone.high.refs_5_.refs_8_) | copy-start | bytes 786436
  9.1 6.7 %copy-start.6 = (bf16[256,512]{1,0:T(8,128)(2,1)S(1)}, bf16[256,512]{1,0:T(8,128)(2,1)}, u32[]{:S(2)}) copy-start(bf16[256,512]{1,0:T(8,128)(2,1)} %constant.27.clone.refs_7_.refs_10_) | copy-start | bytes 786436
  9.6 13.4 %collective-permute-start.4 = (bf16[128,768]{1,0:T(8,128)(2,1)S(1)}, bf16[128,768]{1,0:T(8,128)(2,1)S(1)}, u32[]{:S(2)}, u32[]{:S(2)}) collective-permute-start(bf16[128,768]{1,0:T(8,128)(2,1)S(1)} %get-tuple-element.46), channel_id=1, source_target_pairs={{0,1},{1,0},{2,3},{3,2},{4,5},{5,4},{6,7},{7,6},{8,9},{9,8},{10,11... | collective-permute-start | bytes 589832 | tf_op jit(solution)/shard_map/ppermute | solution.py:275
  17.3 5.7 %collective-permute-start.3 = (bf16[2,128,128]{2,1,0:T(8,128)(2,1)S(1)}, bf16[2,128,128]{2,1,0:T(8,128)(2,1)S(1)}, u32[]{:S(2)}, u32[]{:S(2)}) collective-permute-start(bf16[2,128,128]{2,1,0:T(8,128)(2,1)S(1)} %get-tuple-element.45), channel_id=1, source_target_pairs={{0,2},{1,3},{2,0},{3,1},{4,6},{5,7},{6,4},{7,5},{8,10},{9,11},{10,... | collective-permute-start | bytes 196616 | tf_op jit(solution)/shard_map/ppermute | solution.py:320
  21.7 1.7 %collective-permute-start.7 = (bf16[128,512]{1,0:T(8,128)(2,1)S(1)}, bf16[128,512]{1,0:T(8,128)(2,1)S(1)}, u32[]{:S(2)}, u32[]{:S(2)}) collective-permute-start(bf16[128,512]{1,0:T(8,128)(2,1)S(1)} %get-tuple-element.57), channel_id=1, source_target_pairs={{0,4},{4,0},{8,12},{12,8},{16,20},{20,16},{24,28},{28,24},{1,5},{5... | collective-permute-start | bytes 393224 | tf_op jit(solution)/shard_map/lag_core_sum/ppermute | solution.py:379
  23.3 1.4 %collective-permute-start.5 = (bf16[128,512]{1,0:T(8,128)(2,1)S(1)}, bf16[128,512]{1,0:T(8,128)(2,1)S(1)}, u32[]{:S(2)}, u32[]{:S(2)}) collective-permute-start(bf16[128,512]{1,0:T(8,128)(2,1)S(1)} %get-tuple-element.48), channel_id=1, source_target_pairs={{0,4},{4,0},{8,12},{12,8},{16,20},{20,16},{24,28},{28,24},{1,5},{5... | collective-permute-start | bytes 393224 | tf_op jit(solution)/shard_map/core_sum/ppermute | solution.py:379
  23.4 13.7 %copy-start.3 = (bf16[512,512]{1,0:T(8,128)(2,1)S(1)}, bf16[512,512]{1,0:T(8,128)(2,1)}, u32[]{:S(2)}) copy-start(bf16[512,512]{1,0:T(8,128)(2,1)} %refs_4_.3) | copy-start | bytes 1572868
  23.4 5.0 %collective-permute-start.8 = (bf16[128,512]{1,0:T(8,128)(2,1)S(1)}, bf16[128,512]{1,0:T(8,128)(2,1)S(1)}, u32[]{:S(2)}, u32[]{:S(2)}) collective-permute-start(bf16[128,512]{1,0:T(8,128)(2,1)S(1)} %lag_core_sum.1), channel_id=1, source_target_pairs={{0,4},{1,9},{2,18},{3,27},{4,0},{5,13},{6,22},{7,31},{8,12},{9,1},... | collective-permute-start | bytes 393224 | tf_op jit(solution)/shard_map/ppermute | solution.py:386
  24.7 10.4 %collective-permute-start.6 = (bf16[4,128,128]{2,1,0:T(8,128)(2,1)S(1)}, bf16[4,128,128]{2,1,0:T(8,128)(2,1)S(1)}, u32[]{:S(2)}, u32[]{:S(2)}) collective-permute-start(bf16[4,128,128]{2,1,0:T(8,128)(2,1)S(1)} %get-tuple-element.53), channel_id=1, source_target_pairs={{0,1},{1,0},{2,3},{3,2},{4,5},{5,4},{6,7},{7,6},{8,9},{9,8},{10,11... | collective-permute-start | bytes 393224 | tf_op jit(solution)/shard_map/ppermute | solution.py:471
  25.0 7.2 %collective-permute-start.9 = (bf16[64,512]{1,0:T(8,128)(2,1)S(1)}, bf16[64,512]{1,0:T(8,128)(2,1)S(1)}, u32[]{:S(2)}, u32[]{:S(2)}) collective-permute-start(bf16[64,512]{1,0:T(8,128)(2,1)S(1)} %get-tuple-element.58), channel_id=1, source_target_pairs={{0,4},{1,9},{2,18},{3,27},{4,0},{5,13},{6,22},{7,31},{8,12},{9,1},... | collective-permute-start | bytes 196616 | tf_op jit(solution)/shard_map/ppermute | solution.py:386
  25.0 7.2 %collective-permute-start.10 = (bf16[64,512]{1,0:T(8,128)(2,1)S(1)}, bf16[64,512]{1,0:T(8,128)(2,1)S(1)}, u32[]{:S(2)}, u32[]{:S(2)}) collective-permute-start(bf16[64,512]{1,0:T(8,128)(2,1)S(1)} %get-tuple-element.59), channel_id=1, source_target_pairs={{0,16},{1,25},{2,6},{3,11},{4,20},{5,29},{6,2},{7,15},{8,24},{9,17... | collective-permute-start | bytes 196616 | tf_op jit(solution)/shard_map/ppermute | solution.py:386
  26.6 11.6 %collective-permute-start.14 = (bf16[2,128,128]{2,1,0:T(8,128)(2,1)S(1)}, bf16[2,128,128]{2,1,0:T(8,128)(2,1)S(1)}, u32[]{:S(2)}, u32[]{:S(2)}) collective-permute-start(bf16[2,128,128]{2,1,0:T(8,128)(2,1)S(1)} %get-tuple-element.65), channel_id=1, source_target_pairs={{0,2},{1,3},{2,0},{3,1},{4,6},{5,7},{6,4},{7,5},{8,10},{9,11},{10,... | collective-permute-start | bytes 196616 | tf_op jit(solution)/shard_map/ppermute | solution.py:475
  28.4 9.8 %collective-permute-start.15 = (bf16[2,128,128]{2,1,0:T(8,128)(2,1)S(1)}, bf16[2,128,128]{2,1,0:T(8,128)(2,1)S(1)}, u32[]{:S(2)}, u32[]{:S(2)}) collective-permute-start(bf16[2,128,128]{2,1,0:T(8,128)(2,1)S(1)} %get-tuple-element.66), channel_id=1, source_target_pairs={{0,3},{1,2},{2,1},{3,0},{4,7},{5,6},{6,5},{7,4},{8,11},{9,10},{10,... | collective-permute-start | bytes 196616 | tf_op jit(solution)/shard_map/ppermute | solution.py:475
  32.2 6.7 %collective-permute-start.11 = (bf16[192,128]{1,0:T(8,128)(2,1)S(1)}, bf16[192,128]{1,0:T(8,128)(2,1)S(1)}, u32[]{:S(2)}, u32[]{:S(2)}) collective-permute-start(bf16[192,128]{1,0:T(8,128)(2,1)S(1)} %get-tuple-element.61), channel_id=1, source_target_pairs={{0,1},{1,3},{2,0},{3,2},{4,5},{5,7},{6,4},{7,6},{8,9},{9,11},{10,8... | collective-permute-start | bytes 147464 | tf_op jit(solution)/shard_map/ppermute | solution.py:499
  33.6 6.0 %collective-permute-start.12 = (bf16[192,128]{1,0:T(8,128)(2,1)S(1)}, bf16[192,128]{1,0:T(8,128)(2,1)S(1)}, u32[]{:S(2)}, u32[]{:S(2)}) collective-permute-start(bf16[192,128]{1,0:T(8,128)(2,1)S(1)} %get-tuple-element.62), channel_id=1, source_target_pairs={{0,3},{1,2},{2,1},{3,0},{4,7},{5,6},{6,5},{7,4},{8,11},{9,10},{10,... | collective-permute-start | bytes 147464 | tf_op jit(solution)/shard_map/ppermute | solution.py:499
  35.1 4.7 %collective-permute-start.13 = (bf16[192,128]{1,0:T(8,128)(2,1)S(1)}, bf16[192,128]{1,0:T(8,128)(2,1)S(1)}, u32[]{:S(2)}, u32[]{:S(2)}) collective-permute-start(bf16[192,128]{1,0:T(8,128)(2,1)S(1)} %get-tuple-element.63), channel_id=1, source_target_pairs={{0,2},{1,0},{2,3},{3,1},{4,6},{5,4},{6,7},{7,5},{8,10},{9,8},{10,1... | collective-permute-start | bytes 147464 | tf_op jit(solution)/shard_map/ppermute | solution.py:499
